TPU v7x, 32 devices: a whole 2x2x4 slice. The times are simulated.
32 devices in a mesh: section: 2 (over x), dp: 16 (over z, y, core).
Axes of the slice: x: 2, y: 2, z: 4, core: 2. Of those that a mesh axis runs over, the one named last changes fastest.
Arguments:
- tokens: bfloat16 [32, 256, 1152], P('dp'), may hold values from -6 to 6
- cotangent: bfloat16 [2, 32, 256, 1152], P('section', 'dp'), may hold values from -6 to 6
- labels: int32 [32], P('dp'), may hold values from 0 to 1000
- timesteps: int32 [32], P('dp'), may hold values from 0 to 999
- positions: int32 [32, 256], P('dp'), may hold values from 0 to 255, each once within a row
- label_table: bfloat16 [1001, 1152], replicated, may hold values from -6 to 6
- ada_weight: bfloat16 [2, 1152, 6912], P('section', 'dp'), may hold values from -0.25 to 0.25
- qkv_weight: bfloat16 [2, 1152, 3456], P('section', 'dp'), may hold values from -0.1875 to 0.1875
- out_weight: bfloat16 [2, 1152, 1152], P('section', 'dp'), may hold values from -1.5 to 1.5
- gate_weight: bfloat16 [2, 1152, 3072], P('section', 'dp'), may hold values from -0.1875 to 0.1875
- up_weight: bfloat16 [2, 1152, 3072], P('section', 'dp'), may hold values from -0.1875 to 0.1875
- down_weight: bfloat16 [2, 3072, 1152], P('section', 'dp'), may hold values from -0.109375 to 0.109375
- q_gain: float32 [2, 72], P('section'), may hold values from 0.1 to 1.9
- k_gain: float32 [2, 72], P('section'), may hold values from 0.1 to 1.9
Outputs:
- layer_outputs: bfloat16 [2, 32, 256, 1152], P('section', 'dp')
- input_grads: float32 [2, 32, 256, 1152], P('section', 'dp')
- table_grad: float32 [1001, 1152], replicated
- ada_grad: float32 [2, 1152, 6912], P('section', 'dp')
- qkv_grad: float32 [2, 1152, 3456], P('section', 'dp')
- out_grad: float32 [2, 1152, 1152], P('section', 'dp')
- gate_grad: float32 [2, 1152, 3072], P('section', 'dp')
- up_grad: float32 [2, 1152, 3072], P('section', 'dp')
- down_grad: float32 [2, 3072, 1152], P('section', 'dp')
- q_gain_grad: float32 [2, 72], P('section')
- k_gain_grad: float32 [2, 72], P('section')
Inputs may be any that keep to these rules, and one draw needn't show every extreme that they name: `positions`: each image's row holds every grid position 0 to 255 once.
All inputs are finite; a program needn't handle non-finite values.
Results may differ from a plain program's by a relative error of at most 0.013.
Values may be sent and summed in bfloat16 or wider, within the bound.
No kernel may reach another device: no remote copies, remote signals or barrier semaphores. Data moves between devices by JAX's collectives and lax.ppermute only.
A program may use at most 640 MiB of HBM per device.

v0:
```python
import math

import jax
import jax.numpy as jnp
from jax import lax
from jax.sharding import PartitionSpec as P

D = 1152
HD = 72
GRID = 16
MICRO = 2


epsilon = 1e-06


def passed_along(block, axis, distance):
    devices = range(lax.axis_size(axis))
    route = [(i - distance, i) for i in devices if i - distance in devices]
    return lax.ppermute(block, axis, route)


def product(left, right):
    return jnp.dot(left, right, preferred_element_type=jnp.float32)


def product_right(left, right):
    return lax.dot_general(
        left, right, (((left.ndim - 1,), (1,)), ((), ())), preferred_element_type=jnp.float32
    )


def weight_grad(inputs, grads):
    return lax.dot_general(
        inputs, grads, (((0, 1), (0, 1)), ((), ())), preferred_element_type=jnp.float32
    )


def rms_norm(values):
    return values * lax.rsqrt(jnp.mean(values * values, axis=-1, keepdims=True) + epsilon)


def rope_angles(positions):
    quarter = HD // 4
    frequency = jnp.exp(-math.log(10000.0) * jnp.arange(quarter, dtype=jnp.float32) / quarter)
    row_pos = (positions // GRID).astype(jnp.float32)
    col_pos = (positions % GRID).astype(jnp.float32)
    return (row_pos[..., None] * frequency, col_pos[..., None] * frequency)


def rotate(tensor, row_rotation, column_rotation):
    first_a, first_b, second_a, second_b = jnp.split(tensor, 4, axis=-1)
    row_cos = jnp.cos(row_rotation)[:, :, None, :]
    row_sin = jnp.sin(row_rotation)[:, :, None, :]
    col_cos = jnp.cos(column_rotation)[:, :, None, :]
    col_sin = jnp.sin(column_rotation)[:, :, None, :]
    return jnp.concatenate(
        [
            first_a * row_cos - first_b * row_sin,
            first_a * row_sin + first_b * row_cos,
            second_a * col_cos - second_b * col_sin,
            second_a * col_sin + second_b * col_cos,
        ],
        axis=-1,
    )


def time_features(timestep_ids):
    half_width = D // 2
    frequency = jnp.exp(-math.log(10000.0) * jnp.arange(half_width, dtype=jnp.float32) / half_width)
    angle_rows = timestep_ids.astype(jnp.float32)[:, None] * frequency[None, :]
    return jnp.concatenate([jnp.cos(angle_rows), jnp.sin(angle_rows)], axis=-1)


def prenorm(residual_flow, shift, scale):
    return rms_norm(residual_flow) * (1.0 + scale[:, None, :]) + shift[:, None, :]


def prepare(raw_heads, gain, row_rotation, column_rotation):
    return rotate(rms_norm(raw_heads) * gain, row_rotation, column_rotation)


def attend(queries, keys_rot, values):
    factor = queries.shape[-1] ** (-0.5)
    scores = (
        jnp.einsum("blhd,bmhd->bhlm", queries, keys_rot, preferred_element_type=jnp.float32)
        * factor
    )
    highest = jnp.max(scores, axis=-1, keepdims=True)
    expon = jnp.exp(scores - highest)
    total = jnp.sum(expon, axis=-1, keepdims=True)
    attention = expon / total
    mixed = jnp.einsum(
        "bhlm,bmhd->blhd",
        attention.astype(jnp.bfloat16),
        values,
        preferred_element_type=jnp.float32,
    )
    return (mixed, highest + jnp.log(total))


def recompute(layer_in, modulation, row_rotation, column_rotation, weights):
    qkv_matrix, out_matrix, gate_matrix, up_matrix, down_matrix, query_gain, key_gain = weights
    residual_flow = layer_in.astype(jnp.float32)
    shift_one, scale_one, gate_one, shift_two, scale_two, gate_two = jnp.split(
        modulation, 6, axis=-1
    )
    normed = prenorm(residual_flow, shift_one, scale_one).astype(jnp.bfloat16)
    projected = product(normed, qkv_matrix)
    images, patches, model_width = residual_flow.shape
    head_size = query_gain.shape[0]
    split_heads = projected.reshape(images, patches, 3, model_width // head_size, head_size)
    query_raw = split_heads[:, :, 0]
    key_raw = split_heads[:, :, 1]
    queries = prepare(query_raw, query_gain, row_rotation, column_rotation).astype(jnp.bfloat16)
    keys_rot = prepare(key_raw, key_gain, row_rotation, column_rotation).astype(jnp.bfloat16)
    values = split_heads[:, :, 2].astype(jnp.bfloat16)
    mixed, log_total = attend(queries, keys_rot, values)
    attended = mixed.astype(jnp.bfloat16).reshape(images, patches, model_width)
    branch = product(attended, out_matrix)
    after_attn = residual_flow + gate_one[:, None, :] * branch
    normed_two = prenorm(after_attn, shift_two, scale_two).astype(jnp.bfloat16)
    gate_val = product(normed_two, gate_matrix)
    up_val = product(normed_two, up_matrix)
    activated = (jax.nn.silu(gate_val) * up_val).astype(jnp.bfloat16)
    mlp_out = product(activated, down_matrix)
    result = after_attn + gate_two[:, None, :] * mlp_out
    return (
        residual_flow,
        normed,
        query_raw,
        key_raw,
        queries,
        keys_rot,
        values,
        log_total,
        attended,
        branch,
        after_attn,
        normed_two,
        gate_val,
        up_val,
        activated,
        mlp_out,
        result,
    )


def layer_forward(layer_in, modulation, row_rotation, column_rotation, weights):
    return recompute(layer_in, modulation, row_rotation, column_rotation, weights)[-1].astype(
        jnp.bfloat16
    )


def layer_backward(layer_in, modulation, row_rotation, column_rotation, out_grad, weights):
    qkv_matrix, out_matrix, gate_matrix, up_matrix, down_matrix, query_gain, key_gain = weights
    (
        residual_flow,
        normed,
        query_raw,
        key_raw,
        queries,
        keys_rot,
        values,
        log_total,
        attended,
        branch,
        after_attn,
        normed_two,
        gate_val,
        up_val,
        activated,
        mlp_out,
        result,
    ) = recompute(layer_in, modulation, row_rotation, column_rotation, weights)
    shift_one, scale_one, gate_one, shift_two, scale_two, gate_two = jnp.split(
        modulation, 6, axis=-1
    )
    images, patches, model_width = residual_flow.shape
    head_size = query_gain.shape[0]
    factor = head_size ** (-0.5)
    grad_gate_two = jnp.sum(out_grad * mlp_out, axis=1)
    mlp_grad = (gate_two[:, None, :] * out_grad).astype(jnp.bfloat16)
    act_grad = product_right(mlp_grad, down_matrix)
    sigma = jax.nn.sigmoid(gate_val)
    gate_grad = (act_grad * up_val * sigma * (1.0 + gate_val * (1.0 - sigma))).astype(jnp.bfloat16)
    up_grad = (act_grad * gate_val * sigma).astype(jnp.bfloat16)
    normed_two_grad = product_right(gate_grad, gate_matrix) + product_right(up_grad, up_matrix)
    unused, pull_two = jax.vjp(prenorm, after_attn, shift_two, scale_two)
    extra_two, grad_shift_two, grad_scale_two = pull_two(normed_two_grad)
    after_grad = out_grad + extra_two
    grad_gate_one = jnp.sum(after_grad * branch, axis=1)
    branch_grad = (gate_one[:, None, :] * after_grad).astype(jnp.bfloat16)
    mixed_grad = (
        product_right(branch_grad, out_matrix)
        .astype(jnp.bfloat16)
        .reshape(images, patches, model_width // head_size, head_size)
    )
    scores = (
        jnp.einsum("blhd,bmhd->bhlm", queries, keys_rot, preferred_element_type=jnp.float32)
        * factor
    )
    attention = jnp.exp(scores - log_total)
    value_grad = jnp.einsum(
        "bhlm,blhd->bmhd",
        attention.astype(jnp.bfloat16),
        mixed_grad,
        preferred_element_type=jnp.float32,
    )
    prob_grad = jnp.einsum(
        "blhd,bmhd->bhlm", mixed_grad, values, preferred_element_type=jnp.float32
    )
    score_grad = (
        attention * (prob_grad - jnp.sum(attention * prob_grad, axis=-1, keepdims=True))
    ).astype(jnp.bfloat16)
    query_grad = (
        jnp.einsum("bhlm,bmhd->blhd", score_grad, keys_rot, preferred_element_type=jnp.float32)
        * factor
    )
    key_grad = (
        jnp.einsum("bhlm,blhd->bmhd", score_grad, queries, preferred_element_type=jnp.float32)
        * factor
    )
    unused_q, pull_query = jax.vjp(
        lambda raw_heads, gain: prepare(raw_heads, gain, row_rotation, column_rotation),
        query_raw,
        query_gain,
    )
    query_raw_grad, query_gain_grad = pull_query(query_grad)
    unused_k, pull_key = jax.vjp(
        lambda raw_heads, gain: prepare(raw_heads, gain, row_rotation, column_rotation),
        key_raw,
        key_gain,
    )
    key_raw_grad, key_gain_grad = pull_key(key_grad)
    qkv_grad = (
        jnp.stack([query_raw_grad, key_raw_grad, value_grad], axis=2)
        .astype(jnp.bfloat16)
        .reshape(images, patches, 3 * model_width)
    )
    normed_grad = product_right(qkv_grad, qkv_matrix)
    unused_one, pull_one = jax.vjp(prenorm, residual_flow, shift_one, scale_one)
    extra_one, grad_shift_one, grad_scale_one = pull_one(normed_grad)
    stream_grad = after_grad + extra_one
    mod_grad = jnp.concatenate(
        [
            grad_shift_one,
            grad_scale_one,
            grad_gate_one,
            grad_shift_two,
            grad_scale_two,
            grad_gate_two,
        ],
        axis=-1,
    )
    kept = (
        activated,
        mlp_grad,
        normed_two,
        gate_grad,
        up_grad,
        attended,
        branch_grad,
        normed,
        qkv_grad,
    )
    return (stream_grad, mod_grad, kept, (query_gain_grad, key_gain_grad))


def pack_rows(matrices, device_count):
    return jnp.concatenate([matrix.reshape(device_count, -1) for matrix in matrices], axis=1)


def unpack_rows(flat, shapes, device_count):
    pieces = []
    offset = 0
    for shape in shapes:
        length = shape[0] // device_count * shape[1]
        pieces.append(
            flat[0, offset : offset + length].reshape(shape[0] // device_count, shape[1])[None]
        )
        offset = offset + length
    return pieces


def per_device(
    tokens,
    cotangent,
    labels,
    timesteps,
    positions,
    label_table,
    ada_weight,
    qkv_weight,
    out_weight,
    gate_weight,
    up_weight,
    down_weight,
    q_gain,
    k_gain,
):
    section_index = lax.axis_index("section")
    first_section = section_index == 0
    device_count = lax.axis_size("dp")
    image_count = tokens.shape[0]
    per_micro = image_count // MICRO
    classes = label_table.shape[0]
    label_hot = labels[:, None] == jnp.arange(classes, dtype=jnp.int32)[None, :]
    condition = product(label_hot.astype(jnp.bfloat16), label_table) + time_features(timesteps)
    sigma_cond = jax.nn.sigmoid(condition)
    swish_condition = (condition * sigma_cond).astype(jnp.bfloat16)
    row_all, col_all = rope_angles(positions)
    ada_local = ada_weight[0]
    mod_rows = product(swish_condition, lax.all_gather(ada_local, "dp", axis=0, tiled=True))
    qkv_full, out_full, gate_full, up_full, down_full = (
        lax.all_gather(qkv_weight, "dp", axis=1, tiled=True),
        lax.all_gather(out_weight, "dp", axis=1, tiled=True),
        lax.all_gather(gate_weight, "dp", axis=1, tiled=True),
        lax.all_gather(up_weight, "dp", axis=1, tiled=True),
        lax.all_gather(down_weight, "dp", axis=1, tiled=True),
    )
    weights = (
        qkv_full[0],
        out_full[0],
        gate_full[0],
        up_full[0],
        down_full[0],
        q_gain[0],
        k_gain[0],
    )

    def pick(array, micro_slot):
        return lax.dynamic_slice_in_dim(array, micro_slot * per_micro, per_micro, 0)

    def run_forward(operand):
        return layer_forward(operand[0], operand[1], operand[2], operand[3], weights)

    def skip_forward(operand):
        return jnp.zeros(operand[0].shape, jnp.bfloat16)

    received = jnp.zeros((per_micro, tokens.shape[1], tokens.shape[2]), jnp.bfloat16)
    inputs_seen = []
    outputs_seen = []
    for moment in range(MICRO + 1):
        micro_index = moment - section_index
        active = jnp.logical_and(micro_index >= 0, micro_index < MICRO)
        micro_slot = jnp.clip(micro_index, 0, MICRO - 1)
        layer_in = jnp.where(first_section, pick(tokens, micro_slot), received)
        operand = (
            layer_in,
            pick(mod_rows, micro_slot),
            pick(row_all, micro_slot),
            pick(col_all, micro_slot),
        )
        result = lax.cond(active, run_forward, skip_forward, operand)
        inputs_seen.append(layer_in)
        outputs_seen.append(result)
        if moment < MICRO:
            received = passed_along(result, "section", 1)
    kept_inputs = jnp.stack(
        [
            jnp.where(first_section, inputs_seen[micro], inputs_seen[micro + 1])
            for micro in range(MICRO)
        ]
    )
    layer_outputs = jnp.concatenate(
        [
            jnp.where(first_section, outputs_seen[micro], outputs_seen[micro + 1])
            for micro in range(MICRO)
        ],
        axis=0,
    )
    model_width = tokens.shape[2]
    hidden_width = weights[4].shape[0]
    head_size = weights[5].shape[0]

    def run_backward(operand):
        return layer_backward(operand[0], operand[1], operand[2], operand[3], operand[4], weights)

    def skip_backward(operand):
        rows_shape = operand[4].shape

        def blank(width):
            return jnp.zeros((rows_shape[0], rows_shape[1], width), jnp.bfloat16)

        kept = (
            blank(hidden_width),
            blank(model_width),
            blank(model_width),
            blank(hidden_width),
            blank(hidden_width),
            blank(model_width),
            blank(model_width),
            blank(model_width),
            blank(3 * model_width),
        )
        return (
            jnp.zeros(rows_shape, jnp.float32),
            jnp.zeros(operand[1].shape, jnp.float32),
            kept,
            (jnp.zeros((head_size,), jnp.float32), jnp.zeros((head_size,), jnp.float32)),
        )

    gain_totals = (jnp.zeros((head_size,), jnp.float32), jnp.zeros((head_size,), jnp.float32))
    mod_grads = jnp.zeros(mod_rows.shape, jnp.float32)
    back_rows = jnp.zeros(received.shape, jnp.bfloat16)
    grads_seen = []
    kept_seen = []
    for moment in range(MICRO + 1):
        micro_index = MICRO - moment - section_index
        active = jnp.logical_and(micro_index >= 0, micro_index < MICRO)
        micro_slot = jnp.clip(micro_index, 0, MICRO - 1)
        layer_in = lax.dynamic_index_in_dim(kept_inputs, micro_slot, 0, keepdims=False)
        out_grad = pick(cotangent[0], micro_slot).astype(jnp.float32) + back_rows.astype(
            jnp.float32
        )
        operand = (
            layer_in,
            pick(mod_rows, micro_slot),
            pick(row_all, micro_slot),
            pick(col_all, micro_slot),
            out_grad,
        )
        stream_grad, mod_grad, kept, gains = lax.cond(active, run_backward, skip_backward, operand)
        kept_seen.append(kept)
        gain_totals = (gain_totals[0] + gains[0], gain_totals[1] + gains[1])
        mod_grads = lax.dynamic_update_slice_in_dim(
            mod_grads, pick(mod_grads, micro_slot) + mod_grad, micro_slot * per_micro, 0
        )
        grad_low = stream_grad.astype(jnp.bfloat16)
        grads_seen.append(jnp.where(first_section, stream_grad, grad_low.astype(jnp.float32)))
        if moment < MICRO:
            back_rows = passed_along(grad_low, "section", -1)
    input_grads = jnp.concatenate(
        [
            jnp.where(first_section, grads_seen[MICRO - micro], grads_seen[MICRO - 1 - micro])
            for micro in range(MICRO)
        ],
        axis=0,
    )
    joined = [jnp.concatenate([kept[member] for kept in kept_seen], axis=0) for member in range(9)]
    qkv_term = weight_grad(joined[7], joined[8])
    out_term = weight_grad(joined[5], joined[6])
    gate_term = weight_grad(joined[2], joined[3])
    up_term = weight_grad(joined[2], joined[4])
    down_term = weight_grad(joined[0], joined[1])
    block_terms = [qkv_term, out_term, gate_term, up_term, down_term]
    block_shapes = [tuple(term.shape) for term in block_terms]
    mod_low = mod_grads.astype(jnp.bfloat16)
    silu_grad = product_right(mod_low, lax.all_gather(ada_local, "dp", axis=0, tiled=True))
    ada_full = lax.dot_general(
        swish_condition, mod_low, (((0,), (0,)), ((), ())), preferred_element_type=jnp.float32
    )
    all_terms = block_terms + [ada_full]
    summed = lax.psum_scatter(
        pack_rows(all_terms, device_count), "dp", scatter_dimension=0, tiled=True
    )
    unpacked = unpack_rows(summed, block_shapes + [tuple(ada_full.shape)], device_count)
    qkv_part, out_part, gate_part, up_part, down_part, ada_part = unpacked
    cond_grad = silu_grad * sigma_cond * (1.0 + condition * (1.0 - sigma_cond))
    table_term = lax.dot_general(
        label_hot.astype(jnp.float32),
        cond_grad,
        (((0,), (0,)), ((), ())),
        preferred_element_type=jnp.float32,
    )
    section_hot = (jnp.arange(lax.axis_size("section"), dtype=jnp.int32) == section_index).astype(
        jnp.float32
    )
    gain_term = jnp.stack([gain_totals[0], gain_totals[1]])[:, None, :] * section_hot[None, :, None]
    table_grad, gain_all = lax.psum((table_term, gain_term), ("section", "dp"))
    q_gain_grad = lax.dynamic_slice_in_dim(gain_all[0], section_index, 1, 0)
    k_gain_grad = lax.dynamic_slice_in_dim(gain_all[1], section_index, 1, 0)
    return (
        layer_outputs[None],
        input_grads[None],
        table_grad,
        ada_part,
        qkv_part,
        out_part,
        gate_part,
        up_part,
        down_part,
        q_gain_grad,
        k_gain_grad,
    )


def solution(mesh):
    placed = (
        P("dp", None, None),
        P("section", "dp", None, None),
        P("dp"),
        P("dp"),
        P("dp", None),
        P(),
        P("section", "dp", None),
        P("section", "dp", None),
        P("section", "dp", None),
        P("section", "dp", None),
        P("section", "dp", None),
        P("section", "dp", None),
        P("section", None),
        P("section", None),
    )
    return jax.shard_map(
        per_device,
        mesh=mesh,
        in_specs=placed,
        out_specs=(
            P("section", "dp", None, None),
            P("section", "dp", None, None),
            P(),
            P("section", "dp", None),
            P("section", "dp", None),
            P("section", "dp", None),
            P("section", "dp", None),
            P("section", "dp", None),
            P("section", "dp", None),
            P("section", None),
            P("section", None),
        ),
        check_vma=False,
    )
```

profile of v0, /device:TPU:0, one launch (start us, length us, event | category | flops | bytes accessed | tf_op | source)
XLA Modules:
  0.0 2829.4 jit_solution(8146813564052784647)
XLA Ops:
  14.3 120.2 %all-gather.18.cloned.1.call-done = bf16[1,1152,6912]{2,1,0:T(8,128)(2,1)} async-done(((bf16[1,72,6912]{2,1,0:T(8,128)(2,1)}), bf16[1,1152,6912]{2,1,0:T(8,128)(2,1)}) %all-gather.18.cloned.1.call-update) | async-done | bytes 15925264 | tf_op jit(solution)/shard_map/all_gather | solution.py:314
  134.5 7.7 fusion.426
  142.9 35.3 %all-gather.10.cloned.1.call-done = bf16[1,1152,1152]{2,1,0:T(8,128)(2,1)} async-done(((bf16[1,72,1152]{2,1,0:T(8,128)(2,1)}), bf16[1,1152,1152]{2,1,0:T(8,128)(2,1)}) %all-gather.10.cloned.1.call-update) | async-done | bytes 2654224 | tf_op jit(solution)/shard_map/all_gather | solution.py:317
  178.2 67.6 %all-gather.12.cloned.1.call-done = bf16[1,1152,3072]{2,1,0:T(8,128)(2,1)} async-done(((bf16[1,72,3072]{2,1,0:T(8,128)(2,1)}), bf16[1,1152,3072]{2,1,0:T(8,128)(2,1)}) %all-gather.12.cloned.1.call-update) | async-done | bytes 7077904 | tf_op jit(solution)/shard_map/all_gather | solution.py:318
  245.8 67.3 %all-gather.14.cloned.1.call-done = bf16[1,1152,3072]{2,1,0:T(8,128)(2,1)} async-done(((bf16[1,72,3072]{2,1,0:T(8,128)(2,1)}), bf16[1,1152,3072]{2,1,0:T(8,128)(2,1)}) %all-gather.14.cloned.1.call-update) | async-done | bytes 7077904 | tf_op jit(solution)/shard_map/all_gather | solution.py:319
  313.1 67.3 %all-gather.16.cloned.1.call-done = bf16[1,3072,1152]{2,1,0:T(8,128)(2,1)} async-done(((bf16[1,192,1152]{2,1,0:T(8,128)(2,1)}), bf16[1,3072,1152]{2,1,0:T(8,128)(2,1)}) %all-gather.16.cloned.1.call-update) | async-done | bytes 7077904 | tf_op jit(solution)/shard_map/all_gather | solution.py:320
  380.3 72.7 %all-gather.8.cloned.1.call-done = bf16[1,1152,3456]{2,1,0:T(8,128)(2,1)} async-done(((bf16[1,72,3456]{2,1,0:T(8,128)(2,1)}), bf16[1,1152,3456]{2,1,0:T(8,128)(2,1)}) %all-gather.8.cloned.1.call-update) | async-done | bytes 7962640 | tf_op jit(solution)/shard_map/all_gather | solution.py:316
  453.1 43.3 %conditional.6 = (bf16[1,256,1152]{2,1,0:T(8,128)(2,1)S(1)}) conditional(s32[]{:T(128)} %convert_element_type.799, () %tuple.70, (bf16[1,256,1152]{2,1,0:T(8,128)(2,1)S(1)}, f32[1,6912]{1,0:T(1,128)}, bf16[1152,3456]{1,0:T(8,128)(2,1)}, f32[1,72]{1,0:T(1,128)S(1)}, f32[1,256,18]{1,2,0:T(8,128)S(1)}, /*index=5*/f32[1,256,18]{1,2,0:T(8,128)S(1)}, ...), branch_computations={%region_0.1_spmd, %region_1.8_spmd} | conditional | flops 8483548160 | bytes 130995984 | solution.py:355
  453.1 11.5 copy.117
  466.2 6.0 convolution_bitcast_fusion
  480.8 4.0 fusion.20
  484.8 11.1 fusion.9
  497.8 13.2 collective-permute-done
  512.0 41.9 %conditional.7 = (bf16[1,256,1152]{2,1,0:T(8,128)(2,1)S(1)}) conditional(s32[]{:T(128)} %convert_element_type.804, () %tuple.72, (bf16[1,256,1152]{2,1,0:T(8,128)(2,1)S(1)}, f32[1,6912]{1,0:T(1,128)S(1)}, bf16[1152,3456]{1,0:T(8,128)(2,1)}, f32[1,72]{1,0:T(1,128)S(1)}, f32[1,256,18]{1,2,0:T(8,128)S(1)}, /*index=5*/f32[1,256,18]{1,2,0:T(8,128)S(1)}, ...), branch_computations={%region_8.9_spmd, %region_9.16_spmd} | conditional | flops 8483548160 | bytes 130995984 | solution.py:355
  512.0 11.5 copy.118
  524.3 6.0 convolution_bitcast_fusion.1
  538.8 4.0 fusion.84
  542.8 11.1 fusion.73
  553.8 4.5 collective-permute-start.1
  558.3 12.4 collective-permute-done.1
  573.0 23.0 conditional.9
  598.4 84.9 %collective-permute-done.2 = bf16[1,256,1152]{2,1,0:T(8,128)(2,1)} collective-permute-done((bf16[1,256,1152]{2,1,0:T(8,128)(2,1)}, bf16[1,256,1152]{2,1,0:T(8,128)(2,1)}, u32[]{:S(2)}, u32[]{:S(2)}) %collective-permute-start.2) | collective-permute-done | bytes 589856 | tf_op jit(solution)/shard_map/ppermute | solution.py:20
  685.6 94.0 %conditional.10 = (f32[1,256,1152]{2,1,0:T(8,128)}, f32[1,6912]{1,0:T(1,128)S(1)}, bf16[1,256,1152]{2,1,0:T(8,128)(2,1)}, bf16[1,256,3072]{2,1,0:T(8,128)(2,1)},...) conditional(s32[]{:T(128)} %convert_element_type.804, () %tuple.77, ...), branch_computations={%region_45.46_spmd, %region_46.66_spmd} | conditional | flops 17299675136 | bytes 439213696 | solution.py:424
  686.2 11.5 copy.121
  700.1 5.9 convolution_bitcast_fusion.5
  719.5 5.4 fusion.320
  725.0 6.0 multiply_convert_fusion.7
  734.7 4.6 multiply_reduce_fusion.24
  770.5 3.9 copy.170
  782.0 13.2 collective-permute-done.3
  796.4 93.3 %conditional.11 = (f32[1,256,1152]{2,1,0:T(8,128)S(1)}, f32[1,6912]{1,0:T(1,128)S(1)}, bf16[1,256,1152]{2,1,0:T(8,128)(2,1)}, bf16[1,256,3072]{2,1,0:T(8,128)(2,...) conditional(s32[]{:T(128)} %convert_element_type.799, () %tuple.76, ...), branch_computations={%region_66.67_spmd, %region_67.87_spmd} | conditional | flops 17299085312 | bytes 451600032 | solution.py:424
  799.2 11.9 copy.122
  811.1 5.9 convolution_bitcast_fusion.7
  830.6 5.4 fusion.396
  836.0 6.1 multiply_convert_fusion.13
  842.1 3.6 fusion.507
  845.8 4.6 multiply_reduce_fusion.31
  881.4 3.9 copy.178
  890.1 12.2 convolution_bitcast_fusion.8
  902.3 15.1 reshape.4425
  917.4 10.9 constant_dynamic-update-slice_fusion.26
  928.3 6.7 convolution_bitcast_fusion.12
  935.1 4.5 reshape.4426
  940.4 11.2 convolution_bitcast_fusion.11
  951.7 14.4 reshape.4427
  966.0 11.3 convolution_bitcast_fusion.10
  977.3 14.3 reshape.4428
  991.6 11.8 convolution_bitcast_fusion.9
  1003.5 14.4 reshape.4429
  1017.9 12.5 fusion.474
  1030.4 27.2 reshape.4430
  1057.6 5.2 constant_dynamic-update-slice_fusion.25
  1062.8 12.2 constant_dynamic-update-slice_fusion.24
  1075.0 12.5 constant_dynamic-update-slice_fusion.23
  1087.5 12.6 constant_dynamic-update-slice_fusion.22
  1100.1 10.7 constant_dynamic-update-slice_fusion.21
  1115.3 9.8 fusion.451
  1129.1 41.2 %psum.15 = f32[2,2,72]{2,1,0:T(2,128)S(1)} all-reduce(f32[2,2,72]{2,1,0:T(2,128)S(1)} %broadcast_multiply_fusion.2), channel_id=1, replica_groups=mesh['section'=2,'dp'=16] {'section','dp'}, use_global_device_ids=true, to_apply=%region_89.90 | all-reduce | flops 288 | bytes 2304 | tf_op jit(solution)/shard_map/psum | solution.py:471
  1174.8 1492.5 %all-reduce.6.cloned.1.call-done = f32[16,1492992]{1,0:T(8,128)} async-done(((f32[16,1492992]{1,0:T(8,128)}), f32[16,1492992]{1,0:T(8,128)}) %all-reduce.6.cloned.1.call-update) | async-done | bytes 95551504
  2667.3 23.5 dynamic-slice_reduce_fusion
  2692.6 13.3 dynamic-slice_reduce_fusion.1
  2711.2 14.5 dynamic-slice_reduce_fusion.2
  2728.9 88.5 %all-reduce.4.cloned.1.call-done = f32[1001,1152]{1,0:T(8,128)} async-done(((f32[1001,1152]{1,0:T(8,128)}), f32[1001,1152]{1,0:T(8,128)}) %all-reduce.4.cloned.1.call-update) | async-done | bytes 4612624 | tf_op jit(solution)/shard_map/psum | solution.py:471
  2817.4 4.9 copy.302
  (593 shorter events, 183.3 us)
Async XLA Ops:
  7.2 127.3 %all-gather.18.cloned.1.call-start = ((), (), s32[]{:S(2)}) async-start(), calls=%async_computation.6 | async-start | bytes 16920576 | tf_op jit(solution)/shard_map/all_gather | solution.py:314
  7.9 170.2 %all-gather.10.cloned.1.call-start = ((), (), s32[]{:S(2)}) async-start(), calls=%async_computation.1 | async-start | bytes 2820096 | tf_op jit(solution)/shard_map/all_gather | solution.py:317
  8.7 237.1 %all-gather.12.cloned.1.call-start = ((), (), s32[]{:S(2)}) async-start(), calls=%async_computation.2 | async-start | bytes 7520256 | tf_op jit(solution)/shard_map/all_gather | solution.py:318
  9.4 303.6 %all-gather.14.cloned.1.call-start = ((), (), s32[]{:S(2)}) async-start(), calls=%async_computation.3 | async-start | bytes 7520256 | tf_op jit(solution)/shard_map/all_gather | solution.py:319
  10.0 370.3 %all-gather.16.cloned.1.call-start = ((), (), s32[]{:S(2)}) async-start(), calls=%async_computation.4 | async-start | bytes 7520256 | tf_op jit(solution)/shard_map/all_gather | solution.py:320
  10.6 442.4 %all-gather.8.cloned.1.call-start = ((), (), s32[]{:S(2)}) async-start(), calls=%async_computation | async-start | bytes 8460288 | tf_op jit(solution)/shard_map/all_gather | solution.py:316
  11.2 2656.1 %all-reduce.6.cloned.1.call-start = ((), (), s32[]{:S(2)}) async-start(), calls=%async_computation.7 | async-start | bytes 191102976
  12.1 560.9 %copy-start.97 = (f32[1,256,18]{1,2,0:T(8,128)}, f32[1,256,18]{1,2,0:T(8,128)S(1)}, u32[]{:S(2)}) copy-start(f32[1,256,18]{1,2,0:T(8,128)S(1)} %get-tuple-element.1092) | copy-start | bytes 55300
  14.2 120.3 %copy-start.109 = (f32[2,1152]{1,0:T(2,128)}, f32[2,1152]{1,0:T(2,128)S(1)}, u32[]{:S(2)}) copy-start(f32[2,1152]{1,0:T(2,128)S(1)} %convolution_add_fusion.3) | copy-start | bytes 27652
  14.2 438.8 %copy-start.44 = (bf16[1,256,1152]{2,1,0:T(8,128)(2,1)S(1)}, bf16[1,256,1152]{2,1,0:T(8,128)(2,1)}, u32[]{:S(2)}) copy-start(bf16[1,256,1152]{2,1,0:T(8,128)(2,1)} %dynamic-slice_select_fusion.2) | copy-start | bytes 1769476
  14.2 438.8 %copy-start.101 = (f32[1,256,18]{1,2,0:T(8,128)S(1)}, f32[1,256,18]{1,2,0:T(8,128)}, u32[]{:S(2)}) copy-start(f32[1,256,18]{1,2,0:T(8,128)} %get-tuple-element.1094) | copy-start | bytes 55300
  14.2 438.8 %copy-start.103 = (f32[1,256,18]{1,2,0:T(8,128)S(1)}, f32[1,256,18]{1,2,0:T(8,128)}, u32[]{:S(2)}) copy-start(f32[1,256,18]{1,2,0:T(8,128)} %get-tuple-element.1106) | copy-start | bytes 55300
  14.3 438.8 %copy-start.137 = (f32[1,72]{1,0:T(1,128)S(1)}, f32[1,72]{1,0:T(1,128)}, u32[]{:S(2)}) copy-start(f32[1,72]{1,0:T(1,128)} %param.38) | copy-start | bytes 868
  14.3 438.8 %copy-start.139 = (f32[1,72]{1,0:T(1,128)S(1)}, f32[1,72]{1,0:T(1,128)}, u32[]{:S(2)}) copy-start(f32[1,72]{1,0:T(1,128)} %param.39) | copy-start | bytes 868
  142.9 369.1 %copy-start.95 = (f32[1,6912]{1,0:T(1,128)}, f32[1,6912]{1,0:T(1,128)S(1)}, u32[]{:S(2)}) copy-start(f32[1,6912]{1,0:T(1,128)S(1)} %get-tuple-element.1090) | copy-start | bytes 82948
  142.9 430.1 %copy-start.93 = (f32[1,6912]{1,0:T(1,128)}, f32[1,6912]{1,0:T(1,128)S(1)}, u32[]{:S(2)}) copy-start(f32[1,6912]{1,0:T(1,128)S(1)} %get-tuple-element.1089) | copy-start | bytes 82948
  466.0 14.8 copy-start.183
  466.0 14.8 copy-start.184
  496.4 15.6 copy-start.49
  496.4 14.6 collective-permute-start
  497.7 14.2 copy-start.105
  497.8 14.2 copy-start.107
  524.1 14.6 copy-start.186
  524.1 14.6 copy-start.187
  553.8 17.9 copy-start.51
  553.8 16.9 collective-permute-start.1
  558.3 13.4 copy-start.53
  596.0 87.4 %collective-permute-start.2 = (bf16[1,256,1152]{2,1,0:T(8,128)(2,1)}, bf16[1,256,1152]{2,1,0:T(8,128)(2,1)}, u32[]{:S(2)}, u32[]{:S(2)}) collective-permute-start(bf16[1,256,1152]{2,1,0:T(8,128)(2,1)} %get-tuple-element.498), channel_id=1, source_target_pairs={{16,0},{17,1},{18,2},{19,3},{20,4},{21,5},{22,6},{23,7},{24,8},{25... | collective-permute-start | bytes 1769480 | tf_op jit(solution)/shard_map/ppermute | solution.py:20
  598.4 87.1 %copy-start.96 = (f32[1,6912]{1,0:T(1,128)S(1)}, f32[1,6912]{1,0:T(1,128)}, u32[]{:S(2)}) copy-start(f32[1,6912]{1,0:T(1,128)} %copy-done.95) | copy-start | bytes 82948
  598.4 87.1 %copy-start.106 = (f32[1,256,18]{1,2,0:T(8,128)S(1)}, f32[1,256,18]{1,2,0:T(8,128)}, u32[]{:S(2)}) copy-start(f32[1,256,18]{1,2,0:T(8,128)} %get-tuple-element.1093) | copy-start | bytes 55300
  598.4 87.1 %copy-start.108 = (f32[1,256,18]{1,2,0:T(8,128)S(1)}, f32[1,256,18]{1,2,0:T(8,128)}, u32[]{:S(2)}) copy-start(f32[1,256,18]{1,2,0:T(8,128)} %get-tuple-element.1107) | copy-start | bytes 55300
  598.4 87.1 %copy-start.140 = (f32[1,72]{1,0:T(1,128)S(1)}, f32[1,72]{1,0:T(1,128)}, u32[]{:S(2)}) copy-start(f32[1,72]{1,0:T(1,128)} %param.39) | copy-start | bytes 868
  686.2 13.8 copy-start.129
  686.2 13.8 copy-start.156
  710.0 7.2 slice-start.20
  714.8 10.2 slice-start.28
  717.2 22.1 copy-start.29
  717.2 22.1 copy-start.174
  717.2 7.8 slice-start.29
  779.6 15.7 collective-permute-start.3
  781.2 15.2 copy-start.102
  781.2 15.2 copy-start.104
  798.1 13.0 copy-start.131
  798.1 13.0 copy-start.158
  799.2 11.9 copy-start.178
  799.2 11.9 copy-start.164
  825.8 10.2 slice-start.30
  828.2 22.2 copy-start.30
  828.2 22.2 copy-start.176
  828.3 7.8 slice-start.31
  889.7 12.6 copy-start.39
  951.7 14.4 copy-start.112
  1003.5 14.4 copy-start.110
  1062.8 37.3 %slice-start.6 = ((s8[31850496]{0:T(1024)(128)(4,1)}), s8[4194304]{0:T(1024)(128)(4,1)S(1)}, s32[]{:S(2)}) async-start(s8[31850496]{0:T(1024)(128)(4,1)} %bitcast.875), calls=%async_computation.14 | async-start | bytes 8388608
  1062.8 37.3 %slice-start.7 = ((s8[31850496]{0:T(1024)(128)(4,1)}), s8[4194304]{0:T(1024)(128)(4,1)S(1)}, s32[]{:S(2)}) async-start(s8[31850496]{0:T(1024)(128)(4,1)} %bitcast.875), calls=%async_computation.15 | async-start | bytes 8388608
  1062.8 37.3 %slice-start.8 = ((s8[31850496]{0:T(1024)(128)(4,1)}), s8[4194304]{0:T(1024)(128)(4,1)S(1)}, s32[]{:S(2)}) async-start(s8[31850496]{0:T(1024)(128)(4,1)} %bitcast.875), calls=%async_computation.16 | async-start | bytes 8388608
  1074.9 25.1 slice-start.9
  1074.9 25.1 slice-start.10
  1074.9 25.1 slice-start.11
  1087.5 12.6 slice-start.12
  1087.5 12.6 slice-start.13
  1110.9 1706.5 %all-reduce.4.cloned.1.call-start = ((), (), s32[]{:S(2)}) async-start(), calls=%async_computation.5 | async-start | bytes 9289728 | tf_op jit(solution)/shard_map/psum | solution.py:471
  1115.3 9.9 copy-start.198
  1128.3 43.0 %copy-start.40 = (f32[1,256,1152]{2,1,0:T(8,128)S(1)}, f32[1,256,1152]{2,1,0:T(8,128)}, u32[]{:S(2)}) copy-start(f32[1,256,1152]{2,1,0:T(8,128)} %copy-done.39) | copy-start | bytes 3538948
  (136 other events, 341.0 us)
Sparse Core Ops, SparseCore 0:
  10.2 124.2 all-gather.17
  136.6 41.5 all-gather.9
  180.5 65.2 all-gather.11
  247.9 65.0 all-gather.13
  315.2 65.0 all-gather.15
  382.3 70.6 all-gather.7
  1111.1 1556.1 all-reduce.5
  2673.6 143.8 all-reduce.3
where the time goes:
time: 2840 us; the launch traced here: 2830 us
  waiting for transfers between devices  2140 us (75%)
  local copies, waits for them, and re-layouts  329 us (12%)
  matrix products  231 us (8%)
  other arithmetic  53.4 us (2%)
  blocking collectives  41.2 us (1%)
    unnamed x9, waiting for transfers between devices  1500 us
    ppermute x4, waiting for transfers between devices, passed_along(): return lax.ppermute(block, axis, route)  124 us
    all_gather x1, waiting for transfers between devices, per_device(): lax.all_gather(ada_local, 'dp', axis=0, tiled=True)  120 us
    dot_general x20, matrix products, product(): return jnp.dot(left, right, preferred_element_type=jnp.float32)  91 us
    reshape x6, local copies, waits for them, and re-layouts, pack_rows(): matrix.reshape(device_count, -1)  89.9 us
    psum x1, waiting for transfers between devices, per_device(): table_grad, gain_all = lax.psum((table_term, gain_term), ('section', 'dp'))  88.5 us
    all_gather x1, waiting for transfers between devices, per_device(): lax.all_gather(qkv_weight, 'dp', axis=1, tiled=True)  72.7 us
    all_gather x1, waiting for transfers between devices, per_device(): lax.all_gather(gate_weight, 'dp', axis=1, tiled=True)  67.6 us
  transfers between devices with their start and end apart: 12, of which 12 were waited for; matrix products, arithmetic and copies ran while one was open for 3% of the time, Pallas kernels for 0%

commit v1 on v0

v1 whole, which is shorter than its diff:
```python
import math

import jax
import jax.numpy as jnp
from jax import lax
from jax.sharding import PartitionSpec as P

HD = 72
GRID = 16
epsilon = 1e-06
f32 = jnp.float32
bf16 = jnp.bfloat16


def product(left, right):
    return jnp.dot(left, right, preferred_element_type=f32)


def product_right(left, right):
    return lax.dot_general(
        left, right, (((left.ndim - 1,), (1,)), ((), ())), preferred_element_type=f32
    )


def weight_grad(inputs, grads):
    return lax.dot_general(
        inputs, grads, (((0, 1), (0, 1)), ((), ())), preferred_element_type=f32
    )


def walk_of(count):
    chips = count // 2
    order = [chip for chip in range(chips) if chip % 2 == 0]
    order += [chip for chip in reversed(range(chips)) if chip % 2 == 1]
    return [2 * chip + core for chip in order for core in (0, 1)]


def chip_place(chip, chips):
    return chip // 2 if chip % 2 == 0 else chips - 1 - chip // 2


def from_walk(rows, count):
    chips = count // 2
    blocks = rows.reshape(chips, -1, rows.shape[-1])
    picked = [blocks[chip_place(chip, chips)] for chip in range(chips)]
    return jnp.concatenate(picked, axis=0)


def to_walk(rows, count):
    chips = count // 2
    blocks = rows.reshape(chips, -1, rows.shape[-1])
    return jnp.concatenate([blocks[device // 2] for device in walk_of(count)[::2]], axis=0)


def gather_walk(rows, count):
    return lax.all_gather(rows, "dp", axis=0, tiled=True, axis_index_groups=[walk_of(count)])


def scatter_walk(rows, count):
    part = lax.psum_scatter(
        rows, "dp", scatter_dimension=0, tiled=True, axis_index_groups=[walk_of(count)]
    )
    return lax.optimization_barrier(part)


def swapped(block, bit, count):
    return lax.ppermute(block, "dp", [(device, device ^ bit) for device in range(count)])


def gather_small(block, count):
    me = lax.axis_index("dp")
    block = block[None]
    bit = 1
    while bit < count:
        other = swapped(block, bit, count)
        low = (me & bit) == 0
        block = jnp.concatenate(
            [jnp.where(low, block, other), jnp.where(low, other, block)], axis=0
        )
        bit *= 2
    return block


def scatter_small(blocks, count):
    me = lax.axis_index("dp")
    bit = 1
    while bit < count:
        pairs = blocks.reshape(blocks.shape[0] // 2, 2, *blocks.shape[1:])
        mine = jnp.where((me & bit) == 0, 0, 1)
        give = lax.dynamic_index_in_dim(pairs, 1 - mine, 1, keepdims=False)
        keep = lax.dynamic_index_in_dim(pairs, mine, 1, keepdims=False)
        blocks = keep + swapped(give, bit, count)
        bit *= 2
    return blocks[0]


def rms_norm(values):
    return values * lax.rsqrt(jnp.mean(values * values, axis=-1, keepdims=True) + epsilon)


def rope_angles(positions):
    quarter = HD // 4
    frequency = jnp.exp(-math.log(10000.0) * jnp.arange(quarter, dtype=f32) / quarter)
    row_pos = (positions // GRID).astype(f32)
    col_pos = (positions % GRID).astype(f32)
    return (row_pos[..., None] * frequency, col_pos[..., None] * frequency)


def rotate(tensor, row_rotation, column_rotation):
    first_a, first_b, second_a, second_b = jnp.split(tensor, 4, axis=-1)
    row_cos = jnp.cos(row_rotation)[:, :, None, :]
    row_sin = jnp.sin(row_rotation)[:, :, None, :]
    col_cos = jnp.cos(column_rotation)[:, :, None, :]
    col_sin = jnp.sin(column_rotation)[:, :, None, :]
    return jnp.concatenate(
        [
            first_a * row_cos - first_b * row_sin,
            first_a * row_sin + first_b * row_cos,
            second_a * col_cos - second_b * col_sin,
            second_a * col_sin + second_b * col_cos,
        ],
        axis=-1,
    )


def time_features(timestep_ids, width):
    half_width = width // 2
    frequency = jnp.exp(-math.log(10000.0) * jnp.arange(half_width, dtype=f32) / half_width)
    angle_rows = timestep_ids.astype(f32)[:, None] * frequency[None, :]
    return jnp.concatenate([jnp.cos(angle_rows), jnp.sin(angle_rows)], axis=-1)


def prenorm(residual_flow, shift, scale):
    return rms_norm(residual_flow) * (1.0 + scale[:, None, :]) + shift[:, None, :]


def prepare(raw_heads, gain, angles):
    return rotate(rms_norm(raw_heads) * gain, *angles)


def layer_forward(layer_in, modulation, angles, weights):
    qkv_matrix, out_matrix, gate_up_matrix, down_matrix, query_gain, key_gain = weights
    flow = layer_in.astype(f32)
    shift_one, scale_one, gate_one, shift_two, scale_two, gate_two = jnp.split(
        modulation, 6, axis=-1
    )
    normed = prenorm(flow, shift_one, scale_one).astype(bf16)
    projected = product(normed, qkv_matrix)
    images, patches, width = flow.shape
    head_size = query_gain.shape[0]
    split_heads = projected.reshape(images, patches, 3, width // head_size, head_size)
    query_raw = split_heads[:, :, 0]
    key_raw = split_heads[:, :, 1]
    queries = prepare(query_raw, query_gain, angles).astype(bf16)
    keys = prepare(key_raw, key_gain, angles).astype(bf16)
    values = split_heads[:, :, 2].astype(bf16)
    scores = jnp.einsum("blhd,bmhd->bhlm", queries, keys, preferred_element_type=f32)
    scores = scores * head_size ** (-0.5)
    highest = jnp.max(scores, axis=-1, keepdims=True)
    expon = jnp.exp(scores - highest)
    total = jnp.sum(expon, axis=-1, keepdims=True)
    probs = expon / total
    mixed = jnp.einsum("bhlm,bmhd->blhd", probs.astype(bf16), values, preferred_element_type=f32)
    attended = mixed.astype(bf16).reshape(images, patches, width)
    branch = product(attended, out_matrix)
    middle = flow + gate_one[:, None, :] * branch
    normed_two = prenorm(middle, shift_two, scale_two).astype(bf16)
    gate_up = product(normed_two, gate_up_matrix)
    hidden_width = gate_up.shape[-1] // 2
    gate_val, up_val = gate_up[..., :hidden_width], gate_up[..., hidden_width:]
    activated = (jax.nn.silu(gate_val) * up_val).astype(bf16)
    mlp_out = product(activated, down_matrix)
    result = (middle + gate_two[:, None, :] * mlp_out).astype(bf16)
    kept = (
        normed,
        query_raw,
        key_raw,
        queries,
        keys,
        values,
        highest + jnp.log(total),
        attended,
        branch,
        middle,
        normed_two,
        gate_val,
        up_val,
        activated,
        mlp_out,
    )
    return result, kept


def layer_backward(layer_in, modulation, angles, out_grad, weights, kept):
    qkv_matrix, out_matrix, gate_up_matrix, down_matrix, query_gain, key_gain = weights
    (
        normed,
        query_raw,
        key_raw,
        queries,
        keys,
        values,
        log_total,
        attended,
        branch,
        middle,
        normed_two,
        gate_val,
        up_val,
        activated,
        mlp_out,
    ) = kept
    flow = layer_in.astype(f32)
    shift_one, scale_one, gate_one, shift_two, scale_two, gate_two = jnp.split(
        modulation, 6, axis=-1
    )
    images, patches, width = flow.shape
    head_size = query_gain.shape[0]
    heads = width // head_size
    factor = head_size ** (-0.5)
    grad_gate_two = jnp.sum(out_grad * mlp_out, axis=1)
    mlp_grad = (gate_two[:, None, :] * out_grad).astype(bf16)
    act_grad = product_right(mlp_grad, down_matrix)
    sigma = jax.nn.sigmoid(gate_val)
    gate_grad = (act_grad * up_val * sigma * (1.0 + gate_val * (1.0 - sigma))).astype(bf16)
    up_grad = (act_grad * gate_val * sigma).astype(bf16)
    gate_up_grad = jnp.concatenate([gate_grad, up_grad], axis=-1)
    normed_two_grad = product_right(gate_up_grad, gate_up_matrix)
    unused, pull_two = jax.vjp(prenorm, middle, shift_two, scale_two)
    extra_two, grad_shift_two, grad_scale_two = pull_two(normed_two_grad)
    middle_grad = out_grad + extra_two
    grad_gate_one = jnp.sum(middle_grad * branch, axis=1)
    branch_grad = (gate_one[:, None, :] * middle_grad).astype(bf16)
    mixed_grad = product_right(branch_grad, out_matrix).astype(bf16)
    mixed_grad = mixed_grad.reshape(images, patches, heads, head_size)
    scores = jnp.einsum("blhd,bmhd->bhlm", queries, keys, preferred_element_type=f32) * factor
    probs = jnp.exp(scores - log_total)
    value_grad = jnp.einsum(
        "bhlm,blhd->bmhd", probs.astype(bf16), mixed_grad, preferred_element_type=f32
    )
    prob_grad = jnp.einsum("blhd,bmhd->bhlm", mixed_grad, values, preferred_element_type=f32)
    score_grad = probs * (prob_grad - jnp.sum(probs * prob_grad, axis=-1, keepdims=True))
    score_grad = score_grad.astype(bf16)
    query_grad = jnp.einsum("bhlm,bmhd->blhd", score_grad, keys, preferred_element_type=f32)
    key_grad = jnp.einsum("bhlm,blhd->bmhd", score_grad, queries, preferred_element_type=f32)
    unused_q, pull_query = jax.vjp(
        lambda raw, gain: prepare(raw, gain, angles), query_raw, query_gain
    )
    query_raw_grad, query_gain_grad = pull_query(query_grad * factor)
    unused_k, pull_key = jax.vjp(lambda raw, gain: prepare(raw, gain, angles), key_raw, key_gain)
    key_raw_grad, key_gain_grad = pull_key(key_grad * factor)
    qkv_grad = jnp.stack([query_raw_grad, key_raw_grad, value_grad], axis=2).astype(bf16)
    qkv_grad = qkv_grad.reshape(images, patches, 3 * width)
    normed_grad = product_right(qkv_grad, qkv_matrix)
    unused_one, pull_one = jax.vjp(prenorm, flow, shift_one, scale_one)
    extra_one, grad_shift_one, grad_scale_one = pull_one(normed_grad)
    flow_grad = middle_grad + extra_one
    mod_grad = jnp.concatenate(
        [
            grad_shift_one,
            grad_scale_one,
            grad_gate_one,
            grad_shift_two,
            grad_scale_two,
            grad_gate_two,
        ],
        axis=-1,
    )
    gains = jnp.stack([query_gain_grad, key_gain_grad])
    return flow_grad, mod_grad, gains, (mlp_grad, gate_up_grad, branch_grad, qkv_grad)


def per_device(
    tokens,
    cotangent,
    labels,
    timesteps,
    positions,
    label_table,
    ada_weight,
    qkv_weight,
    out_weight,
    gate_weight,
    up_weight,
    down_weight,
    q_gain,
    k_gain,
):
    first_section = lax.axis_index("section") == 0
    count = lax.axis_size("dp")
    me = lax.axis_index("dp")
    width = tokens.shape[2]
    rows = ada_weight.shape[1]
    classes = label_table.shape[0]

    ids = gather_small(jnp.stack([labels, timesteps]), count)
    all_labels = ids[:, 0].reshape(-1)
    all_times = ids[:, 1].reshape(-1)
    label_hot = all_labels[:, None] == jnp.arange(classes, dtype=jnp.int32)[None, :]
    condition = product(label_hot.astype(bf16), label_table) + time_features(all_times, width)
    sigma_cond = jax.nn.sigmoid(condition)
    silu_cond = (condition * sigma_cond).astype(bf16)
    silu_rows = lax.dynamic_slice_in_dim(silu_cond, me * rows, rows, 1)
    mod_part = product(silu_rows, ada_weight[0])
    modulation = scatter_small(mod_part.reshape(count, -1, mod_part.shape[1]), count)
    angles = rope_angles(positions)

    qkv_full = from_walk(gather_walk(qkv_weight[0], count), count)
    joined = jnp.concatenate([out_weight[0], gate_weight[0], up_weight[0]], axis=1)
    joined_full = from_walk(gather_walk(joined, count), count)
    down_full = from_walk(gather_walk(down_weight[0], count), count)
    weights = (
        qkv_full,
        joined_full[:, :width],
        joined_full[:, width:],
        down_full,
        q_gain[0],
        k_gain[0],
    )

    early, unused = layer_forward(tokens, modulation, angles, weights)
    received = lax.ppermute(early, "section", [(0, 1)])
    layer_in = jnp.where(first_section, tokens, received)
    result, kept = layer_forward(layer_in, modulation, angles, weights)

    grads = cotangent[0].astype(f32)
    late_grad = layer_backward(layer_in, modulation, angles, grads, weights, kept)[0]
    back = lax.ppermute(late_grad.astype(bf16), "section", [(1, 0)])
    flow_grad, mod_grad, gains, kept_grads = layer_backward(
        layer_in, modulation, angles, grads + back.astype(f32), weights, kept
    )
    input_grads = jnp.where(first_section, flow_grad, flow_grad.astype(bf16).astype(f32))
    mlp_grad, gate_up_grad, branch_grad, qkv_grad = kept_grads

    normed, attended, normed_two, activated = kept[0], kept[7], kept[10], kept[13]
    down_part = scatter_walk(to_walk(weight_grad(activated, mlp_grad).astype(bf16), count), count)
    gate_up_part = scatter_walk(
        to_walk(weight_grad(normed_two, gate_up_grad).astype(bf16), count), count
    )
    rest = jnp.concatenate(
        [
            weight_grad(attended, branch_grad).astype(bf16),
            weight_grad(normed, qkv_grad).astype(bf16),
        ],
        axis=1,
    )
    rest_part = scatter_walk(to_walk(rest, count), count)
    hidden_width = gate_up_part.shape[1] // 2

    mod_all = gather_small(mod_grad.astype(bf16), count).reshape(-1, mod_grad.shape[1])
    ada_part = lax.dot_general(
        silu_rows, mod_all, (((0,), (0,)), ((), ())), preferred_element_type=f32
    )
    silu_grad = product_right(mod_all, ada_weight[0])
    silu_grad = silu_grad + lax.ppermute(silu_grad, "section", [(0, 1), (1, 0)])
    silu_all = gather_small(silu_grad, count)
    gain_all = jnp.sum(gather_small(gains, count), axis=0)
    silu_all = jnp.swapaxes(silu_all, 0, 1).reshape(condition.shape)
    cond_grad = silu_all * sigma_cond * (1.0 + condition * (1.0 - sigma_cond))
    table_grad = lax.dot_general(
        label_hot.astype(f32),
        cond_grad,
        (((0,), (0,)), ((), ())),
        precision=lax.Precision.HIGHEST,
        preferred_element_type=f32,
    )
    return (
        result[None],
        input_grads[None],
        table_grad,
        ada_part[None],
        rest_part[None, :, width:].astype(f32),
        rest_part[None, :, :width].astype(f32),
        gate_up_part[None, :, :hidden_width].astype(f32),
        gate_up_part[None, :, hidden_width:].astype(f32),
        down_part[None].astype(f32),
        gain_all[None, 0],
        gain_all[None, 1],
    )


def solution(mesh):
    placed = (
        P("dp", None, None),
        P("section", "dp", None, None),
        P("dp"),
        P("dp"),
        P("dp", None),
        P(),
        P("section", "dp", None),
        P("section", "dp", None),
        P("section", "dp", None),
        P("section", "dp", None),
        P("section", "dp", None),
        P("section", "dp", None),
        P("section", None),
        P("section", None),
    )
    return jax.shard_map(
        per_device,
        mesh=mesh,
        in_specs=placed,
        out_specs=(
            P("section", "dp", None, None),
            P("section", "dp", None, None),
            P(),
            P("section", "dp", None),
            P("section", "dp", None),
            P("section", "dp", None),
            P("section", "dp", None),
            P("section", "dp", None),
            P("section", "dp", None),
            P("section", None),
            P("section", None),
        ),
        check_vma=False,
    )
```

time: 2840 us -> 714 us (0.25)
  waiting for transfers between devices: 2140 us -> 256 us
  local copies, waits for them, and re-layouts: 329 us -> 107 us
  blocking collectives: 41.2 us -> 0 us
    unnamed x9 -> x6, waiting for transfers between devices: 1500 us -> 1.44 us
    all_gather x6 -> x3, waiting for transfers between devices: 430 us -> 96.9 us  [gather_walk(): lax.all_gather(rows, 'dp', axis=0, tiled=True, axis_index_groups=[walk_of...]
    reshape x6 -> x2, local copies, waits for them, and re-layouts: 89.9 us -> 0.32 us  [the longest x1 0.17 us: per_device(): gather_small(mod_grad.astype(bf16), count).reshape(-1, mod_grad.shape[1])]
    psum x1 -> x0, waiting for transfers between devices: 88.5 us -> none  [per_device(): table_grad, gain_all = lax.psum((table_term, gain_term), ('section', 'dp'))]
    another operation x26 -> x2, local copies, waits for them, and re-layouts: 66.1 us -> 2.26 us  [layer_backward(): jnp.stack([query_raw_grad, key_raw_grad, value_grad], axis=2).astype(bf16)]
    slice x5 -> x4, local copies, waits for them, and re-layouts: 54.8 us -> 1.31 us  [the longest x1 0.52 us: per_device(): gain_all[None, 1]]
    dot_general x11 -> x9, matrix products: 48.5 us -> 93.8 us  [product_right(): lax.dot_general(left, right, (((left.ndim - 1,), (1,)), ((), ())), prefer...]
    psum x1 -> x0, blocking collectives: 41.2 us -> none  [per_device(): table_grad, gain_all = lax.psum((table_term, gain_term), ('section', 'dp'))]
  transfers between devices with their start and end apart: 12 -> 29, of which waited for: 12 -> 23; matrix products, arithmetic and copies ran while one was open for 3% -> 28% of each run, Pallas kernels for 0% -> 0%
where the time goes in v1:
time: 714 us; the launch traced here: 700 us
  waiting for transfers between devices  256 us (36%)
  matrix products  228 us (32%)
  local copies, waits for them, and re-layouts  107 us (15%)
  other arithmetic  60.6 us (8%)
  starting transfers between devices  31.8 us (4%)
  between operations  16.3 us (2%)
    all_gather x3, waiting for transfers between devices, gather_walk(): lax.all_gather(rows, 'dp', axis=0, tiled=True, axis_index_groups=[walk_of...  96.9 us
    dot_general x9, matrix products, product_right(): lax.dot_general(left, right, (((left.ndim - 1,), (1,)), ((), ())), prefer...  93.8 us
    unnamed x231, local copies, waits for them, and re-layouts  81.3 us
    dot_general x10, matrix products, product(): return jnp.dot(left, right, preferred_element_type=f32)  67.7 us
    ppermute x20, waiting for transfers between devices, swapped(): lax.ppermute(block, 'dp', [(device, device ^ bit) for device in range(cou...  59.1 us
    reduce_scatter x3, waiting for transfers between devices, scatter_walk(): lax.psum_scatter(rows, 'dp', scatter_dimension=0, tiled=True, axis_index_...  40.8 us
    ppermute x1, waiting for transfers between devices, per_device(): back = lax.ppermute(late_grad.astype(bf16), 'section', [(1, 0)])  29.4 us
    dot_general x4, matrix products, weight_grad(): lax.dot_general(inputs, grads, (((0, 1), (0, 1)), ((), ())), preferred_el...  29.3 us
  transfers between devices with their start and end apart: 29, of which 23 were waited for; matrix products, arithmetic and copies ran while one was open for 28% of the time, Pallas kernels for 0%

profile of v1, /device:TPU:0, one launch (start us, length us, event | category | flops | bytes accessed | tf_op | source)
XLA Modules:
  0.0 699.8 jit_solution(18178929309080246054)
XLA Ops:
  12.4 2.9 collective-permute-start.1
  20.9 3.0 collective-permute-start.3
  32.3 10.6 %collective-permute-done.5 = f32[4,2,6912]{2,1,0:T(2,128)S(1)} collective-permute-done((f32[4,2,6912]{2,1,0:T(2,128)S(1)}, f32[4,2,6912]{2,1,0:T(2,128)S(1)}, u32[]{:S(2)}, u32[]{:S(2)}) %collective-permute-start.5) | collective-permute-done | bytes 221216 | tf_op jit(solution)/shard_map/ppermute | solution.py:67
  43.5 6.6 collective-permute-done.6
  50.2 2.9 collective-permute-start.7
  53.1 3.8 collective-permute-done.7
  57.6 4.9 all-gather.10.cloned.1.call-done
  69.0 2.2 fusion.143
  75.6 2.9 fusion.91
  78.5 32.6 %all-gather.8.cloned.1.call-done = bf16[1,1152,3456]{2,1,0:T(8,128)(2,1)} async-done(((bf16[1,72,3456]{2,1,0:T(8,128)(2,1)}), bf16[1,1152,3456]{2,1,0:T(8,128)(2,1)}) %all-gather.8.cloned.1.call-update) | async-done | bytes 7962640 | tf_op jit(solution)/shard_map/all_gather | solution.py:56
  119.1 2.4 fusion.90
  121.5 4.9 fusion.8
  126.8 2.5 copy-done.44
  134.2 6.3 fusion.196
  140.5 2.7 fusion.93
  143.2 59.4 %all-gather.6.cloned.1.call-done = bf16[1152,7296]{1,0:T(8,128)(2,1)} async-done(((bf16[72,7296]{1,0:T(8,128)(2,1)}), bf16[1152,7296]{1,0:T(8,128)(2,1)}) %all-gather.6.cloned.1.call-update) | async-done | bytes 16810000 | tf_op jit(solution)/shard_map/all_gather | solution.py:56
  213.7 2.8 slice_dynamic-update-slice_fusion
  216.4 5.8 copy-done.52
  222.2 2.2 multiply_reduce_fusion.12
  224.5 14.3 %fusion.33 = f32[2,256,6144]{2,1,0:T(8,128)} fusion(bf16[1152,7296]{1,0:T(8,128)(2,1)} %copy-done.52, f32[2,256,1152]{2,1,0:T(8,128)S(1)} %get-tuple-element.149, f32[2,1152]{1,0:T(2,128)S(1)} %get-tuple-element.109, f32[2,1152]{1,0:T(2,128)S(1)} %get-tuple-element.110, f32[2,256]{1,0:T(2,128)S(1)} %add_rsqrt_fusion.2), kind=kOutput, calls=%fused_computation.71 | convolution fusion | flops 7250116608 | bytes 29118464 | tf_op jit(solution)/shard_map/dot_general | solution.py:16
  238.8 11.7 %fusion.47 = bf16[2,256,1152]{2,1,0:T(8,128)(2,1)S(1)} fusion(f32[2,256,1152]{2,1,0:T(8,128)S(1)} %get-tuple-element.149, bf16[3072,1152]{1,0:T(8,128)(2,1)} %fusion.91, f32[2,256,6144]{2,1,0:T(8,128)} %fusion.33, f32[2,1152]{1,0:T(2,128)S(1)} %get-tuple-element.108), kind=kOutput, calls=%fused_computation.96 | convolution fusion | flops 3635085312 | bytes 23208960 | tf_op jit(solution)/shard_map/dot_general | solution.py:16
  250.5 4.4 collective-permute-start.8
  254.9 24.6 %collective-permute-done.8 = bf16[2,256,1152]{2,1,0:T(8,128)(2,1)} collective-permute-done((bf16[2,256,1152]{2,1,0:T(8,128)(2,1)S(1)}, bf16[2,256,1152]{2,1,0:T(8,128)(2,1)}, u32[]{:S(2)}, u32[]{:S(2)}) %collective-permute-start.8) | collective-permute-done | bytes 1179680 | tf_op jit(solution)/shard_map/ppermute | solution.py:322
  280.1 7.9 %fusion.6 = f32[2,256,3456]{1,2,0:T(8,128)S(1)} fusion(bf16[1152,3456]{1,0:T(8,128)(2,1)} %copy-done.53, bf16[2,256,1152]{2,1,0:T(8,128)(2,1)S(1)} %get-tuple-element.32, f32[2,256]{1,0:T(2,128)S(1)} %fusion.171, f32[2,1152]{1,0:T(2,128)S(1)} %get-tuple-element.111, f32[2,1152]{1,0:T(2,128)S(1)} %get-tuple-element.112), kind=kOutput, calls=%fused_computation.27 | convolution fusion | flops 4079812608 | bytes 16240640 | tf_op jit(solution)/shard_map/dot_general | solution.py:16
  292.8 2.4 multiply_reduce_fusion.3
  300.6 5.7 multiply_reduce_fusion.11
  307.8 11.6 %fusion.32 = f32[2,256,6144]{2,1,0:T(8,128)S(1)} fusion(bf16[1152,7296]{1,0:T(8,128)(2,1)} %copy-done.52, f32[2,256,1152]{2,1,0:T(8,128)S(1)} %get-tuple-element.30, f32[2,256]{1,0:T(2,128)S(1)} %fusion.172, f32[2,1152]{1,0:T(2,128)S(1)} %copy-done.69, f32[2,1152]{1,0:T(2,128)S(1)} %get-tuple-element.110), kind=kOutput, calls=%fused_computation.70 | convolution fusion | flops 7250116608 | bytes 29118464 | tf_op jit(solution)/shard_map/dot_general | solution.py:16
  319.4 14.8 %multiply_convert_fusion.5 = (bf16[2,256,3072]{2,1,0:T(8,128)(2,1)}, bf16[2,256,3072]{2,1,0:T(8,128)(2,1)}) fusion(f32[2,256,6144]{2,1,0:T(8,128)S(1)} %fusion.32, bf16[3072,1152]{1,0:T(8,128)(2,1)} %fusion.91, bf16[1,2,256,1152]{3,2,1,0:T(8,128)(2,1)S(1)} %copy-done.17, f32[2,1152]{1,0:T(2,128)S(1)} %get-tuple-element.108), kind=kOutput, calls=%fused_computation.54 | convolution fusion | flops 3646095360 | bytes 27141120 | tf_op jit(solution)/shard_map/dot_general | solution.py:20
  334.2 17.4 %multiply_reduce_fusion.10 = (f32[2,256]{1,0:T(2,128)}, f32[2,256,1152]{2,1,0:T(8,128)}) fusion(f32[2,256,1152]{2,1,0:T(8,128)} %copy-done.14, f32[2,1152]{1,0:T(2,128)S(1)} %get-tuple-element.110, bf16[1152,7296]{1,0:T(8,128)(2,1)} %copy-done.52, bf16[2,256,3072]{2,1,0:T(8,128)(2,1)} %get-tuple-element.36, bf16[2,256,3072]{2,1,0:T(8,128)(2,1)} %get-tuple-element.35), kind=kOutput, calls=%fused_computation.166 | convolution fusion | flops 7262109184 | bytes 25177088 | tf_op jit(solution)/shard_map/dot_general | solution.py:20
  353.5 6.4 convolution_convert_fusion.1
  361.9 5.1 fusion.94
  367.0 5.6 multiply_reduce_fusion.1
  384.7 8.7 %fusion.74 = (f32[2,256]{1,0:T(2,128)S(1)}, f32[2,256,1152]{2,1,0:T(8,128)S(1)}) fusion(bf16[2,256,1152]{2,1,0:T(8,128)(2,1)S(1)} %get-tuple-element.32, f32[2,1152]{1,0:T(2,128)S(1)} %get-tuple-element.112, bf16[2,256,3456]{1,2,0:T(8,128)(2,1)S(1)} %bitcast.386, bf16[1152,3456]{1,0:T(8,128)(2,1)} %copy-done.53), kind=kOutput, calls=%fused_computation.120 | convolution fusion | flops 4079222272 | bytes 15051776 | tf_op jit(solution)/shard_map/dot_general | solution.py:20
  396.4 29.4 %collective-permute-done.9 = bf16[2,256,1152]{2,1,0:T(8,128)(2,1)S(1)} collective-permute-done((bf16[2,256,1152]{2,1,0:T(8,128)(2,1)S(1)}, bf16[2,256,1152]{2,1,0:T(8,128)(2,1)S(1)}, u32[]{:S(2)}, u32[]{:S(2)}) %collective-permute-start.9) | collective-permute-done | bytes 1179680 | tf_op jit(solution)/shard_map/ppermute | solution.py:328
  425.9 13.1 %multiply_convert_fusion.3 = (bf16[2,256,3072]{2,1,0:T(8,128)(2,1)}, bf16[2,256,3072]{2,1,0:T(8,128)(2,1)}, bf16[2,256,3072]{2,1,0:T(8,128)(2,1)S(1)}) fusion(f32[2,256,6144]{2,1,0:T(8,128)} %copy-done.92, bf16[3072,1152]{1,0:T(8,128)(2,1)} %fusion.91, bf16[2,256,1152]{2,1,0:T(8,128)(2,1)S(1)} %collective-permute-done.9, ...), kind=kOutput, calls=%fused_computation.52 | convolution fusion | flops 3651993600 | bytes 31466496 | tf_op jit(solution)/shard_map/dot_general | solution.py:20
  439.0 4.7 bitcast_convert_fusion.1
  451.1 18.3 %multiply_reduce_fusion.7 = (bf16[2,1152]{1,0:T(2,128)(2,1)}, f32[2,256]{1,0:T(2,128)S(1)}, bf16[2,1152]{1,0:T(2,128)(2,1)}, f32[2,256,1152]{2,1,0:T(8,128)}) fusion(f32[2,256,1152]{2,1,0:T(8,128)} %copy-done.14, f32[2,256]{1,0:T(2,128)S(1)} %fusion.172, f32[2,1152]{1,0:T(2,128)S(1)} %get-tuple-element.110, bf16[1152,7296]{1,0:T(8,128)(2,1)} %copy-done.52, ...), kind=kOutput, calls=%fused_computation.155 | convolution fusion | flops 7264463872 | bytes 25188352 | tf_op jit(solution)/shard_map/dot_general | solution.py:20
  469.4 8.4 %fusion.17 = f32[2,256,1152]{2,1,0:T(8,128)S(1)} fusion(bf16[2,256,3072]{2,1,0:T(8,128)(2,1)} %copy-done.93, bf16[3072,1152]{1,0:T(8,128)(2,1)} %fusion.91), kind=kOutput, calls=%fused_computation.39 | convolution fusion | flops 3623878656 | bytes 12582912 | tf_op jit(solution)/shard_map/dot_general | solution.py:16
  477.9 2.8 multiply_reduce_fusion.8
  482.2 4.7 convolution_convert_fusion
  488.4 5.7 multiply_reduce_fusion
  513.2 3.3 fusion.10
  516.5 5.3 copy.184
  521.7 7.6 %fusion.1 = bf16[1152,3456]{1,0:T(8,128)(2,1)S(1)} fusion(bf16[2,256,3456]{1,2,0:T(8,128)(2,1)} %bitcast.384, bf16[2,256,1152]{2,1,0:T(8,128)(2,1)S(1)} %get-tuple-element.32, f32[2,256]{1,0:T(2,128)S(1)} %copy-done.58, f32[2,1152]{1,0:T(2,128)S(1)} %copy-done.72, f32[2,1152]{1,0:T(2,128)S(1)} %get-tuple-element.112), kind=kOutput, calls=%fused_computation.6 | convolution fusion | flops 4083793920 | bytes 12701696 | tf_op jit(solution)/shard_map/dot_general | solution.py:26
  538.7 13.8 %bitcast_convert_fusion = bf16[1152,6144]{1,0:T(8,128)(2,1)} fusion(bf16[2,256,3072]{2,1,0:T(8,128)(2,1)} %get-tuple-element.34, bf16[2,256,3072]{2,1,0:T(8,128)(2,1)} %get-tuple-element.33, f32[2,256,1152]{2,1,0:T(8,128)} %copy-done.14, f32[2,256]{1,0:T(2,128)S(1)} %copy-done.60, f32[2,1152]{1,0:T(2,128)S(1)} %copy-done.70, ...), kind=kOutput, calls=%fused_computation.1 | convolution fusion | flops 7269777408 | bytes 22827008 | tf_op jit(solution)/shard_map/dot_general | solution.py:26
  552.5 2.9 slice_dynamic-update-slice_fusion.14
  555.4 2.9 slice_dynamic-update-slice_fusion.13
  558.3 2.9 slice_dynamic-update-slice_fusion.12
  561.2 4.2 slice_dynamic-update-slice_fusion.1
  565.3 2.9 slice_dynamic-update-slice_fusion.11
  568.2 2.9 slice_dynamic-update-slice_fusion.10
  571.1 2.9 slice_dynamic-update-slice_fusion.9
  574.8 10.1 %fusion.59 = (bf16[2,1152]{1,0:T(2,128)(2,1)S(1)}, f32[2,256]{1,0:T(2,128)S(1)}, bf16[2,1152]{1,0:T(2,128)(2,1)S(1)}, f32[2,256,1152]{2,1,0:T(8,128)S(1)}) fusion(bf16[2,256,1152]{2,1,0:T(8,128)(2,1)S(1)} %get-tuple-element.32, f32[2,256]{1,0:T(2,128)S(1)} %copy-done.58, f32[2,1152]{1,0:T(2,128)S(1)} %get-tuple-element.112, ...), kind=kOutput, calls=%fused_computation.105 | convolution fusion | flops 4081576960 | bytes 15063040 | tf_op jit(solution)/shard_map/dot_general | solution.py:20
  588.8 3.8 collective-permute-done.11
  594.8 4.7 collective-permute-done.12
  604.0 7.8 %collective-permute-done.13 = bf16[8,2,6912]{2,1,0:T(2,128)(2,1)S(1)} collective-permute-done((bf16[8,2,6912]{2,1,0:T(2,128)(2,1)S(1)}, bf16[8,2,6912]{2,1,0:T(2,128)(2,1)S(1)}, u32[]{:S(2)}, u32[]{:S(2)}) %collective-permute-start.13) | collective-permute-done | bytes 221216 | tf_op jit(solution)/shard_map/ppermute | solution.py:67
  613.5 3.7 collective-permute-done.14
  619.4 2.6 collective-permute-done.22
  622.9 2.3 collective-permute-start.17
  625.7 2.6 collective-permute-done.17
  631.6 7.2 %collective-permute-done.18 = f32[8,32,72]{2,1,0:T(8,128)S(1)} collective-permute-done((f32[8,32,72]{2,1,0:T(8,128)S(1)}, f32[8,32,72]{2,1,0:T(8,128)S(1)}, u32[]{:S(2)}, u32[]{:S(2)}) %collective-permute-start.18) | collective-permute-done | bytes 73760 | tf_op jit(solution)/shard_map/ppermute | solution.py:67
  639.1 4.3 fusion.156
  649.3 40.8 %reduce-scatter.6.cloned.1.call-done = bf16[72,6144]{1,0:T(8,128)(2,1)} async-done(((bf16[1152,6144]{1,0:T(8,128)(2,1)}), bf16[72,6144]{1,0:T(8,128)(2,1)}) %reduce-scatter.6.cloned.1.call-update) | async-done | bytes 884752 | tf_op jit(solution)/shard_map/reduce_scatter | solution.py:60
  690.1 2.5 fusion.153
  (407 shorter events, 150.3 us)
Async XLA Ops:
  7.2 19.3 %copy-start = (bf16[1001,1152]{1,0:T(8,128)(2,1)S(1)}, bf16[1001,1152]{1,0:T(8,128)(2,1)}, u32[]{:S(2)}) copy-start(bf16[1001,1152]{1,0:T(8,128)(2,1)} %param.19) | copy-start | bytes 6918916
  7.2 55.3 %all-gather.10.cloned.1.call-start = ((), (), s32[]{:S(2)}) async-start(), calls=%async_computation.8 | async-start | bytes 7520256 | tf_op jit(solution)/shard_map/all_gather | solution.py:56
  8.0 103.2 %all-gather.8.cloned.1.call-start = ((), (), s32[]{:S(2)}) async-start(), calls=%async_computation.7 | async-start | bytes 8460288 | tf_op jit(solution)/shard_map/all_gather | solution.py:56
  8.7 193.9 %all-gather.6.cloned.1.call-start = ((), (), s32[]{:S(2)}) async-start(), calls=%async_computation.3 | async-start | bytes 17860608 | tf_op jit(solution)/shard_map/all_gather | solution.py:56
  11.0 16.2 %copy-start.20 = (bf16[1,72,6912]{2,1,0:T(8,128)(2,1)S(1)}, bf16[1,72,6912]{2,1,0:T(8,128)(2,1)}, u32[]{:S(2)}) copy-start(bf16[1,72,6912]{2,1,0:T(8,128)(2,1)} %param.20) | copy-start | bytes 2985988
  11.0 632.4 %reduce-scatter.8.cloned.1.call-start = ((), (), s32[]{:S(2)}) async-start(), calls=%async_computation.6 | async-start | bytes 7520256 | tf_op jit(solution)/shard_map/reduce_scatter | solution.py:60
  11.1 1.3 collective-permute-start
  12.4 4.5 collective-permute-start.1
  16.9 3.7 collective-permute-start.2
  20.9 4.7 collective-permute-start.3
  27.7 15.4 %copy-start.19 = (bf16[2,256,1152]{2,1,0:T(8,128)(2,1)S(1)}, bf16[2,256,1152]{2,1,0:T(8,128)(2,1)}, u32[]{:S(2)}) copy-start(bf16[2,256,1152]{2,1,0:T(8,128)(2,1)} %param.14) | copy-start | bytes 3538948
  27.8 2.0 collective-permute-start.4
  30.1 12.8 %collective-permute-start.5 = (f32[4,2,6912]{2,1,0:T(2,128)S(1)}, f32[4,2,6912]{2,1,0:T(2,128)S(1)}, u32[]{:S(2)}, u32[]{:S(2)}) collective-permute-start(f32[4,2,6912]{2,1,0:T(2,128)S(1)} %dynamic-slice_bitcast_fusion.1), channel_id=1, source_target_pairs={{0,2},{1,3},{2,0},{3,1},{4,6},{5,7},{6,4},{7,5},{8,10},{9,11},{10,... | collective-permute-start | bytes 663560 | tf_op jit(solution)/shard_map/ppermute | solution.py:67
  43.1 7.0 %collective-permute-start.6 = (f32[2,2,6912]{2,1,0:T(2,128)S(1)}, f32[2,2,6912]{2,1,0:T(2,128)S(1)}, u32[]{:S(2)}, u32[]{:S(2)}) collective-permute-start(f32[2,2,6912]{2,1,0:T(2,128)S(1)} %dynamic-slice_bitcast_fusion.2), channel_id=1, source_target_pairs={{0,4},{1,5},{2,6},{3,7},{4,0},{5,1},{6,2},{7,3},{8,12},{9,13},{10,... | collective-permute-start | bytes 331784 | tf_op jit(solution)/shard_map/ppermute | solution.py:67
  50.2 6.7 collective-permute-start.7
  57.6 166.9 %copy-start.68 = (f32[2,1152]{1,0:T(2,128)}, f32[2,1152]{1,0:T(2,128)S(1)}, u32[]{:S(2)}) copy-start(f32[2,1152]{1,0:T(2,128)S(1)} %get-tuple-element.109) | copy-start | bytes 27652
  57.6 222.5 %copy-start.71 = (f32[2,1152]{1,0:T(2,128)}, f32[2,1152]{1,0:T(2,128)S(1)}, u32[]{:S(2)}) copy-start(f32[2,1152]{1,0:T(2,128)S(1)} %get-tuple-element.111) | copy-start | bytes 27652
  213.7 8.6 %copy-start.73 = (f32[2,1152]{1,0:T(2,128)S(1)}, f32[2,1152]{1,0:T(2,128)}, u32[]{:S(2)}) copy-start(f32[2,1152]{1,0:T(2,128)} %get-tuple-element.113) | copy-start | bytes 27652
  250.5 29.0 %collective-permute-start.8 = (bf16[2,256,1152]{2,1,0:T(8,128)(2,1)S(1)}, bf16[2,256,1152]{2,1,0:T(8,128)(2,1)}, u32[]{:S(2)}, u32[]{:S(2)}) collective-permute-start(bf16[2,256,1152]{2,1,0:T(8,128)(2,1)S(1)} %fusion.47), channel_id=1, source_target_pairs={{0,16},{1,17},{2,18},{3,19},{4,20},{5,21},{6,22},{7,23},{8,24},{9,... | collective-permute-start | bytes 3538952 | tf_op jit(solution)/shard_map/ppermute | solution.py:322
  280.0 114.0 %copy-start.57 = (f32[2,256]{1,0:T(2,128)}, f32[2,256]{1,0:T(2,128)S(1)}, u32[]{:S(2)}) copy-start(f32[2,256]{1,0:T(2,128)S(1)} %fusion.171) | copy-start | bytes 6148
  288.0 8.9 %copy-start.10 = (f32[2,256,3456]{1,2,0:T(8,128)}, f32[2,256,3456]{1,2,0:T(8,128)S(1)}, u32[]{:S(2)}) copy-start(f32[2,256,3456]{1,2,0:T(8,128)S(1)} %fusion.6) | copy-start | bytes 21233668
  292.5 82.3 %copy-start.22 = (bf16[2,256,16,18]{1,3,2,0:T(8,128)(2,1)}, bf16[2,256,16,18]{1,3,2,0:T(8,128)(2,1)S(1)}, u32[]{:S(2)}) copy-start(bf16[2,256,16,18]{1,3,2,0:T(8,128)(2,1)S(1)} %get-tuple-element.58) | copy-start | bytes 884740
  292.5 82.3 %copy-start.24 = (bf16[2,256,16,18]{1,3,2,0:T(8,128)(2,1)}, bf16[2,256,16,18]{1,3,2,0:T(8,128)(2,1)S(1)}, u32[]{:S(2)}) copy-start(bf16[2,256,16,18]{1,3,2,0:T(8,128)(2,1)S(1)} %get-tuple-element.59) | copy-start | bytes 884740
  306.9 144.2 %copy-start.59 = (f32[2,256]{1,0:T(2,128)}, f32[2,256]{1,0:T(2,128)S(1)}, u32[]{:S(2)}) copy-start(f32[2,256]{1,0:T(2,128)S(1)} %fusion.172) | copy-start | bytes 6148
  307.8 11.6 %copy-start.17 = (bf16[1,2,256,1152]{3,2,1,0:T(8,128)(2,1)S(1)}, bf16[1,2,256,1152]{3,2,1,0:T(8,128)(2,1)}, u32[]{:S(2)}) copy-start(bf16[1,2,256,1152]{3,2,1,0:T(8,128)(2,1)} %param.15) | copy-start | bytes 3538948
  319.4 14.8 %copy-start.92 = (f32[2,256,6144]{2,1,0:T(8,128)}, f32[2,256,6144]{2,1,0:T(8,128)S(1)}, u32[]{:S(2)}) copy-start(f32[2,256,6144]{2,1,0:T(8,128)S(1)} %fusion.32) | copy-start | bytes 37748740
  361.9 10.8 %slice-start = ((s8[8388608]{0:T(1024)(128)(4,1)}), s8[4194304]{0:T(1024)(128)(4,1)S(1)}, s32[]{:S(2)}) async-start(s8[8388608]{0:T(1024)(128)(4,1)} %bitcast.356), calls=%async_computation.9 | async-start | bytes 8388608
  384.7 9.4 %copy-start.15 = (f32[2,256,1152]{2,1,0:T(8,128)S(1)}, f32[2,256,1152]{2,1,0:T(8,128)}, u32[]{:S(2)}) copy-start(f32[2,256,1152]{2,1,0:T(8,128)} %copy-done.14) | copy-start | bytes 7077892
  384.7 9.3 %copy-start.18 = (bf16[1,2,256,1152]{3,2,1,0:T(8,128)(2,1)S(1)}, bf16[1,2,256,1152]{3,2,1,0:T(8,128)(2,1)}, u32[]{:S(2)}) copy-start(bf16[1,2,256,1152]{3,2,1,0:T(8,128)(2,1)} %param.15) | copy-start | bytes 3538948
  384.7 9.3 %copy-start.47 = (f32[2,256,1152]{2,1,0:T(8,128)S(1)}, f32[2,256,1152]{2,1,0:T(8,128)}, u32[]{:S(2)}) copy-start(f32[2,256,1152]{2,1,0:T(8,128)} %get-tuple-element.154) | copy-start | bytes 7077892
  384.7 9.3 %copy-start.78 = (f32[2,256]{1,0:T(2,128)S(1)}, f32[2,256]{1,0:T(2,128)}, u32[]{:S(2)}) copy-start(f32[2,256]{1,0:T(2,128)} %copy-done.77) | copy-start | bytes 6148
  395.1 30.7 %collective-permute-start.9 = (bf16[2,256,1152]{2,1,0:T(8,128)(2,1)S(1)}, bf16[2,256,1152]{2,1,0:T(8,128)(2,1)S(1)}, u32[]{:S(2)}, u32[]{:S(2)}) collective-permute-start(bf16[2,256,1152]{2,1,0:T(8,128)(2,1)S(1)} %fusion.67), channel_id=1, source_target_pairs={{16,0},{17,1},{18,2},{19,3},{20,4},{21,5},{22,6},{23,7},{24,8},{25... | collective-permute-start | bytes 3538952 | tf_op jit(solution)/shard_map/ppermute | solution.py:328
  425.9 13.1 %copy-start.48 = (bf16[2,256,1152]{2,1,0:T(8,128)(2,1)}, bf16[2,256,1152]{2,1,0:T(8,128)(2,1)S(1)}, u32[]{:S(2)}) copy-start(bf16[2,256,1152]{2,1,0:T(8,128)(2,1)S(1)} %collective-permute-done.9) | copy-start | bytes 3538948
  451.0 194.5 %reduce-scatter.4.cloned.1.call-start = ((), (), s32[]{:S(2)}) async-start(), calls=%async_computation.4 | async-start | bytes 11280384 | tf_op jit(solution)/shard_map/reduce_scatter | solution.py:60
  451.1 18.3 %copy-start.80 = (f32[2,256]{1,0:T(2,128)S(1)}, f32[2,256]{1,0:T(2,128)}, u32[]{:S(2)}) copy-start(f32[2,256]{1,0:T(2,128)} %get-tuple-element.28) | copy-start | bytes 6148
  469.4 8.5 %copy-start.16 = (f32[2,256,1152]{2,1,0:T(8,128)S(1)}, f32[2,256,1152]{2,1,0:T(8,128)}, u32[]{:S(2)}) copy-start(f32[2,256,1152]{2,1,0:T(8,128)} %copy-done.14) | copy-start | bytes 7077892
  469.4 8.5 %copy-start.45 = (f32[2,256,1152]{2,1,0:T(8,128)S(1)}, f32[2,256,1152]{2,1,0:T(8,128)}, u32[]{:S(2)}) copy-start(f32[2,256,1152]{2,1,0:T(8,128)} %get-tuple-element.152) | copy-start | bytes 7077892
  469.4 8.5 %copy-start.46 = (f32[2,256,1152]{2,1,0:T(8,128)S(1)}, f32[2,256,1152]{2,1,0:T(8,128)}, u32[]{:S(2)}) copy-start(f32[2,256,1152]{2,1,0:T(8,128)} %get-tuple-element.159) | copy-start | bytes 7077892
  469.4 8.5 %copy-start.49 = (bf16[2,256,1152]{2,1,0:T(8,128)(2,1)S(1)}, bf16[2,256,1152]{2,1,0:T(8,128)(2,1)}, u32[]{:S(2)}) copy-start(bf16[2,256,1152]{2,1,0:T(8,128)(2,1)} %copy-done.48) | copy-start | bytes 3538948
  469.4 8.5 %copy-start.60 = (f32[2,256]{1,0:T(2,128)S(1)}, f32[2,256]{1,0:T(2,128)}, u32[]{:S(2)}) copy-start(f32[2,256]{1,0:T(2,128)} %copy-done.59) | copy-start | bytes 6148
  538.0 152.0 %reduce-scatter.6.cloned.1.call-start = ((), (), s32[]{:S(2)}) async-start(), calls=%async_computation.5 | async-start | bytes 15040512 | tf_op jit(solution)/shard_map/reduce_scatter | solution.py:60
  574.6 10.2 %copy-start.56 = (bf16[2,1152]{1,0:T(2,128)(2,1)S(1)}, bf16[2,1152]{1,0:T(2,128)(2,1)}, u32[]{:S(2)}) copy-start(bf16[2,1152]{1,0:T(2,128)(2,1)} %get-tuple-element.23) | copy-start | bytes 13828
  574.7 10.2 %copy-start.86 = (bf16[2,1152]{1,0:T(2,128)(2,1)S(1)}, bf16[2,1152]{1,0:T(2,128)(2,1)}, u32[]{:S(2)}) copy-start(bf16[2,1152]{1,0:T(2,128)(2,1)} %get-tuple-element.19) | copy-start | bytes 13828
  574.7 10.3 %copy-start.85 = (bf16[2,1152]{1,0:T(2,128)(2,1)S(1)}, bf16[2,1152]{1,0:T(2,128)(2,1)}, u32[]{:S(2)}) copy-start(bf16[2,1152]{1,0:T(2,128)(2,1)} %get-tuple-element.15) | copy-start | bytes 13828
  574.7 10.7 %copy-start.79 = (f32[2,256]{1,0:T(2,128)S(1)}, f32[2,256]{1,0:T(2,128)}, u32[]{:S(2)}) copy-start(f32[2,256]{1,0:T(2,128)} %get-tuple-element.26) | copy-start | bytes 6148
  574.7 10.7 %copy-start.13 = (f32[2,256,1152]{2,1,0:T(8,128)S(1)}, f32[2,256,1152]{2,1,0:T(8,128)}, u32[]{:S(2)}) copy-start(f32[2,256,1152]{2,1,0:T(8,128)} %copy-done.11) | copy-start | bytes 7077892
  574.7 14.1 %collective-permute-start.19 = (f32[1,2,72]{2,1,0:T(2,128)S(1)}, f32[1,2,72]{2,1,0:T(2,128)S(1)}, u32[]{:S(2)}, u32[]{:S(2)}) collective-permute-start(f32[1,2,72]{2,1,0:T(2,128)S(1)} %maximum_bitcast_fusion.1), channel_id=1, source_target_pairs={{0,1},{1,0},{2,3},{3,2},{4,5},{5,4},{6,7},{7,6},{8,9},{9,8},{10,11... | collective-permute-start | bytes 1736 | tf_op jit(solution)/shard_map/ppermute | solution.py:67
  585.0 2.5 collective-permute-start.10
  587.4 25.6 %copy-start.21 = (bf16[1,72,6912]{2,1,0:T(8,128)(2,1)S(1)}, bf16[1,72,6912]{2,1,0:T(8,128)(2,1)}, u32[]{:S(2)}) copy-start(bf16[1,72,6912]{2,1,0:T(8,128)(2,1)} %param.20) | copy-start | bytes 2985988
  587.6 5.0 collective-permute-start.11
  592.9 6.6 collective-permute-start.12
  593.6 8.3 %collective-permute-start.20 = (f32[2,2,72]{2,1,0:T(2,128)S(1)}, f32[2,2,72]{2,1,0:T(2,128)S(1)}, u32[]{:S(2)}, u32[]{:S(2)}) collective-permute-start(f32[2,2,72]{2,1,0:T(2,128)S(1)} %pad_maximum_fusion.20), channel_id=1, source_target_pairs={{0,2},{1,3},{2,0},{3,1},{4,6},{5,7},{6,4},{7,5},{8,10},{9,11},{10,... | collective-permute-start | bytes 3464 | tf_op jit(solution)/shard_map/ppermute | solution.py:67
  600.0 11.8 %collective-permute-start.13 = (bf16[8,2,6912]{2,1,0:T(2,128)(2,1)S(1)}, bf16[8,2,6912]{2,1,0:T(2,128)(2,1)S(1)}, u32[]{:S(2)}, u32[]{:S(2)}) collective-permute-start(bf16[8,2,6912]{2,1,0:T(2,128)(2,1)S(1)} %pad_maximum_fusion.12), channel_id=1, source_target_pairs={{0,8},{1,9},{2,10},{3,11},{4,12},{5,13},{6,14},{7,15},{8,0},{9,1},... | collective-permute-start | bytes 663560 | tf_op jit(solution)/shard_map/ppermute | solution.py:67
  602.0 27.9 %copy-start.55 = (bf16[32,72]{1,0:T(8,128)(2,1)S(1)}, bf16[32,72]{1,0:T(8,128)(2,1)}, u32[]{:S(2)}) copy-start(bf16[32,72]{1,0:T(8,128)(2,1)} %copy-done.54) | copy-start | bytes 13828
  602.0 11.5 %collective-permute-start.21 = (f32[4,2,72]{2,1,0:T(2,128)S(1)}, f32[4,2,72]{2,1,0:T(2,128)S(1)}, u32[]{:S(2)}, u32[]{:S(2)}) collective-permute-start(f32[4,2,72]{2,1,0:T(2,128)S(1)} %pad_maximum_fusion.19), channel_id=1, source_target_pairs={{0,4},{1,5},{2,6},{3,7},{4,0},{5,1},{6,2},{7,3},{8,12},{9,13},{10,... | collective-permute-start | bytes 6920 | tf_op jit(solution)/shard_map/ppermute | solution.py:67
  613.4 3.8 collective-permute-start.14
  617.2 1.2 collective-permute-start.15
  617.2 4.8 collective-permute-start.22
  618.4 4.4 collective-permute-start.16
  622.9 5.4 collective-permute-start.17
  628.3 10.9 %copy-start.51 = (f32[32,1152]{1,0:T(8,128)S(1)}, f32[32,1152]{1,0:T(8,128)}, u32[]{:S(2)}) copy-start(f32[32,1152]{1,0:T(8,128)} %copy-done.50) | copy-start | bytes 442372
  628.3 10.9 %copy-start.83 = (s32[32]{0:T(128)S(1)}, s32[32]{0:T(128)}, u32[]{:S(2)}) copy-start(s32[32]{0:T(128)} %copy-done.82) | copy-start | bytes 388
  628.3 10.4 %collective-permute-start.18 = (f32[8,32,72]{2,1,0:T(8,128)S(1)}, f32[8,32,72]{2,1,0:T(8,128)S(1)}, u32[]{:S(2)}, u32[]{:S(2)}) collective-permute-start(f32[8,32,72]{2,1,0:T(8,128)S(1)} %pad_maximum_fusion.13), channel_id=1, source_target_pairs={{0,8},{1,9},{2,10},{3,11},{4,12},{5,13},{6,14},{7,15},{8,0},{9,1},... | collective-permute-start | bytes 221192 | tf_op jit(solution)/shard_map/ppermute | solution.py:67
  643.4 49.2 %copy-start.1 = (bf16[1001,1152]{1,0:T(8,128)(2,1)S(1)}, bf16[1001,1152]{1,0:T(8,128)(2,1)}, u32[]{:S(2)}) copy-start(bf16[1001,1152]{1,0:T(8,128)(2,1)} %param.19) | copy-start | bytes 6918916
  (63 other events, 160.4 us)
Sparse Core Ops, SparseCore 0:
  9.6 52.8 all-gather.9
  64.1 46.9 all-gather.7
  113.3 89.2 all-gather.5
  451.2 53.9 reduce-scatter.7
  538.2 62.7 reduce-scatter.3
  603.2 86.8 reduce-scatter.5

commit v2 on v1

--- a/solution.py
+++ b/solution.py
@@ -191,7 +191,7 @@
     return result, kept
 
 
-def layer_backward(layer_in, modulation, angles, out_grad, weights, kept):
+def layer_backward(layer_in, modulation, angles, out_grad, weights, kept, with_weights):
     qkv_matrix, out_matrix, gate_up_matrix, down_matrix, query_gain, key_gain = weights
     (
         normed,
@@ -220,7 +220,12 @@
     factor = head_size ** (-0.5)
     grad_gate_two = jnp.sum(out_grad * mlp_out, axis=1)
     mlp_grad = (gate_two[:, None, :] * out_grad).astype(bf16)
-    act_grad = product_right(mlp_grad, down_matrix)
+    if with_weights:
+        down_term = weight_grad(activated, mlp_grad).astype(bf16)
+        down_term, mlp_grad = lax.optimization_barrier((down_term, mlp_grad))
+    else:
+        down_term = None
+    act_grad = lax.optimization_barrier(product_right(mlp_grad, down_matrix))
     sigma = jax.nn.sigmoid(gate_val)
     gate_grad = (act_grad * up_val * sigma * (1.0 + gate_val * (1.0 - sigma))).astype(bf16)
     up_grad = (act_grad * gate_val * sigma).astype(bf16)
@@ -267,7 +272,7 @@
         axis=-1,
     )
     gains = jnp.stack([query_gain_grad, key_gain_grad])
-    return flow_grad, mod_grad, gains, (mlp_grad, gate_up_grad, branch_grad, qkv_grad)
+    return flow_grad, mod_grad, gains, (down_term, gate_up_grad, branch_grad, qkv_grad)
 
 
 def per_device(
@@ -305,14 +310,17 @@
     modulation = scatter_small(mod_part.reshape(count, -1, mod_part.shape[1]), count)
     angles = rope_angles(positions)
 
-    qkv_full = from_walk(gather_walk(qkv_weight[0], count), count)
-    joined = jnp.concatenate([out_weight[0], gate_weight[0], up_weight[0]], axis=1)
-    joined_full = from_walk(gather_walk(joined, count), count)
-    down_full = from_walk(gather_walk(down_weight[0], count), count)
+    joined = jnp.concatenate(
+        [qkv_weight[0], out_weight[0], gate_weight[0], up_weight[0]], axis=1
+    )
+    joined_full = gather_walk(joined, count)
+    down_rows, joined_full = lax.optimization_barrier((down_weight[0], joined_full))
+    joined_full = from_walk(joined_full, count)
+    down_full = from_walk(gather_walk(down_rows, count), count)
     weights = (
-        qkv_full,
-        joined_full[:, :width],
-        joined_full[:, width:],
+        joined_full[:, : 3 * width],
+        joined_full[:, 3 * width : 4 * width],
+        joined_full[:, 4 * width :],
         down_full,
         q_gain[0],
         k_gain[0],
@@ -324,19 +332,19 @@
     result, kept = layer_forward(layer_in, modulation, angles, weights)
 
     grads = cotangent[0].astype(f32)
-    late_grad = layer_backward(layer_in, modulation, angles, grads, weights, kept)[0]
+    late_grad = layer_backward(layer_in, modulation, angles, grads, weights, kept, False)[0]
     back = lax.ppermute(late_grad.astype(bf16), "section", [(1, 0)])
     flow_grad, mod_grad, gains, kept_grads = layer_backward(
-        layer_in, modulation, angles, grads + back.astype(f32), weights, kept
+        layer_in, modulation, angles, grads + back.astype(f32), weights, kept, True
     )
     input_grads = jnp.where(first_section, flow_grad, flow_grad.astype(bf16).astype(f32))
-    mlp_grad, gate_up_grad, branch_grad, qkv_grad = kept_grads
-
-    normed, attended, normed_two, activated = kept[0], kept[7], kept[10], kept[13]
-    down_part = scatter_walk(to_walk(weight_grad(activated, mlp_grad).astype(bf16), count), count)
-    gate_up_part = scatter_walk(
-        to_walk(weight_grad(normed_two, gate_up_grad).astype(bf16), count), count
-    )
+    down_term, gate_up_grad, branch_grad, qkv_grad = kept_grads
+
+    normed, attended, normed_two = kept[0], kept[7], kept[10]
+    down_part = scatter_walk(to_walk(down_term, count), count)
+    gate_up_term = to_walk(weight_grad(normed_two, gate_up_grad).astype(bf16), count)
+    gate_up_term, down_part = lax.optimization_barrier((gate_up_term, down_part))
+    gate_up_part = scatter_walk(gate_up_term, count)
     rest = jnp.concatenate(
         [
             weight_grad(attended, branch_grad).astype(bf16),
@@ -344,7 +352,8 @@
         ],
         axis=1,
     )
-    rest_part = scatter_walk(to_walk(rest, count), count)
+    rest, gate_up_part = lax.optimization_barrier((to_walk(rest, count), gate_up_part))
+    rest_part = scatter_walk(rest, count)
     hidden_width = gate_up_part.shape[1] // 2
 
     mod_all = gather_small(mod_grad.astype(bf16), count).reshape(-1, mod_grad.shape[1])

time: 714 us -> 663 us (0.929)
  waiting for transfers between devices: 256 us -> 203 us
  other arithmetic: 60.6 us -> 81.7 us
  local copies, waits for them, and re-layouts: 107 us -> 99.5 us
    reduce_scatter x3, waiting for transfers between devices: 40.8 us -> 4.21 us  [scatter_walk(): lax.psum_scatter(rows, 'dp', scatter_dimension=0, tiled=True, axis_index_...]
    convert_element_type x0 -> x3, other arithmetic: none -> 20.2 us  [the longest x2 19.8 us: layer_backward(): (act_grad * up_val * sigma * (1.0 + gate_val * (1.0 - sigma))).astype(bf16)]
    dot_general x9, matrix products: 93.8 us -> 82.1 us  [product_right(): lax.dot_general(left, right, (((left.ndim - 1,), (1,)), ((), ())), prefer...]
    all_gather x3 -> x2, waiting for transfers between devices: 96.9 us -> 87.2 us  [gather_walk(): lax.all_gather(rows, 'dp', axis=0, tiled=True, axis_index_groups=[walk_of...]
    ppermute x1, waiting for transfers between devices: 24.6 us -> 14.9 us  [per_device(): received = lax.ppermute(early, 'section', [(0, 1)])]
    unnamed x231 -> x225, local copies, waits for them, and re-layouts: 81.3 us -> 73.7 us
  transfers between devices with their start and end apart: 29 -> 28, of which waited for: 23 -> 22; matrix products, arithmetic and copies ran while one was open for 28% -> 37% of each run, Pallas kernels for 0% -> 0%
where the time goes in v2:
time: 663 us; the launch traced here: 656 us
  matrix products  224 us (34%)
  waiting for transfers between devices  203 us (31%)
  local copies, waits for them, and re-layouts  99.5 us (15%)
  other arithmetic  81.7 us (12%)
  starting transfers between devices  32.6 us (5%)
  between operations  15.7 us (2%)
    all_gather x2, waiting for transfers between devices, gather_walk(): lax.all_gather(rows, 'dp', axis=0, tiled=True, axis_index_groups=[walk_of...  87.2 us
    dot_general x9, matrix products, product_right(): lax.dot_general(left, right, (((left.ndim - 1,), (1,)), ((), ())), prefer...  82.1 us
    dot_general x10, matrix products, product(): return jnp.dot(left, right, preferred_element_type=f32)  74.6 us
    unnamed x225, local copies, waits for them, and re-layouts  73.7 us
    ppermute x20, waiting for transfers between devices, swapped(): lax.ppermute(block, 'dp', [(device, device ^ bit) for device in range(cou...  64.6 us
    ppermute x1, waiting for transfers between devices, per_device(): back = lax.ppermute(late_grad.astype(bf16), 'section', [(1, 0)])  29.4 us
    dot_general x4, matrix products, weight_grad(): lax.dot_general(inputs, grads, (((0, 1), (0, 1)), ((), ())), preferred_el...  29.1 us
    ppermute x20, starting transfers between devices, swapped(): lax.ppermute(block, 'dp', [(device, device ^ bit) for device in range(cou...  24.6 us
  transfers between devices with their start and end apart: 28, of which 22 were waited for; matrix products, arithmetic and copies ran while one was open for 37% of the time, Pallas kernels for 0%

profile of v2, /device:TPU:0, one launch (start us, length us, event | category | flops | bytes accessed | tf_op | source)
XLA Modules:
  0.0 655.9 jit_solution(18076083913496643347)
XLA Ops:
  7.3 2.7 pad_maximum_fusion.7
  11.5 2.9 collective-permute-start.1
  20.0 3.0 collective-permute-start.3
  31.3 10.5 %collective-permute-done.5 = f32[4,2,6912]{2,1,0:T(2,128)S(1)} collective-permute-done((f32[4,2,6912]{2,1,0:T(2,128)S(1)}, f32[4,2,6912]{2,1,0:T(2,128)S(1)}, u32[]{:S(2)}, u32[]{:S(2)}) %collective-permute-start.5) | collective-permute-done | bytes 221216 | tf_op jit(solution)/shard_map/ppermute | solution.py:67
  42.3 7.4 %collective-permute-done.6 = f32[2,2,6912]{2,1,0:T(2,128)S(1)} collective-permute-done((f32[2,2,6912]{2,1,0:T(2,128)S(1)}, f32[2,2,6912]{2,1,0:T(2,128)S(1)}, u32[]{:S(2)}, u32[]{:S(2)}) %collective-permute-start.6) | collective-permute-done | bytes 110624 | tf_op jit(solution)/shard_map/ppermute | solution.py:67
  49.9 2.6 collective-permute-start.7
  52.5 4.4 collective-permute-done.7
  57.0 87.2 %all-gather.3.cloned.1.call-done = bf16[1152,10752]{1,0:T(8,128)(2,1)} async-done(((bf16[72,10752]{1,0:T(8,128)(2,1)}), bf16[1152,10752]{1,0:T(8,128)(2,1)}) %all-gather.3.cloned.1.call-update) | async-done | bytes 24772624 | tf_op jit(solution)/shard_map/all_gather | solution.py:56
  144.4 3.7 slice_dynamic-update-slice_fusion.7
  148.1 3.7 slice_dynamic-update-slice_fusion.6
  151.9 3.9 slice_dynamic-update-slice_fusion.5
  155.8 3.9 slice_dynamic-update-slice_fusion.4
  159.7 3.7 slice_dynamic-update-slice_fusion.3
  163.4 3.8 slice_dynamic-update-slice_fusion.2
  167.2 5.9 slice_dynamic-update-slice_fusion
  173.1 7.8 %fusion.79 = f32[2,256,3456]{1,2,0:T(8,128)S(1)} fusion(bf16[1152,10752]{1,0:T(8,128)(2,1)} %slice_dynamic-update-slice_fusion, bf16[2,256,1152]{2,1,0:T(8,128)(2,1)S(1)} %copy-done.21, f32[2,1152]{1,0:T(2,128)S(1)} %get-tuple-element.127, f32[2,1152]{1,0:T(2,128)S(1)} %get-tuple-element.128, f32[2,256]{1,0:T(2,128)S(1)} %add_rsqrt_fusion.3), kind=kOutput, calls=%fused_computation.177 | convolution fusion | flops 4079812608 | bytes 16240640 | tf_op jit(solution)/shard_map/dot_general | solution.py:16
  181.2 2.5 copy-done.48
  188.3 6.3 fusion.172
  194.6 2.7 fusion.83
  197.3 4.0 multiply_reduce_fusion.12
  202.7 14.5 %fusion.25 = f32[2,256,6144]{2,1,0:T(8,128)} fusion(bf16[1152,10752]{1,0:T(8,128)(2,1)} %slice_dynamic-update-slice_fusion, f32[2,256,1152]{2,1,0:T(8,128)S(1)} %get-tuple-element.165, f32[2,1152]{1,0:T(2,128)S(1)} %get-tuple-element.125, f32[2,1152]{1,0:T(2,128)S(1)} %get-tuple-element.126, f32[2,256]{1,0:T(2,128)S(1)} %add_rsqrt_fusion.2), kind=kOutput, calls=%fused_computation.64 | convolution fusion | flops 7250116608 | bytes 29118464 | tf_op jit(solution)/shard_map/dot_general | solution.py:16
  226.9 12.3 %fusion.36 = bf16[2,256,1152]{2,1,0:T(8,128)(2,1)S(1)} fusion(f32[2,256,1152]{2,1,0:T(8,128)S(1)} %copy-done.93, bf16[3072,1152]{1,0:T(8,128)(2,1)S(1)} %slice_dynamic-update-slice_fusion.14, f32[2,256,6144]{2,1,0:T(8,128)} %fusion.25, f32[2,1152]{1,0:T(2,128)S(1)} %get-tuple-element.124), kind=kOutput, calls=%fused_computation.95 | convolution fusion | flops 3635085312 | bytes 23208960 | tf_op jit(solution)/shard_map/dot_general | solution.py:16
  239.2 4.6 collective-permute-start.8
  243.8 9.6 %fusion.7 = f32[2,256,3072]{2,1,0:T(8,128)} fusion(bf16[3072,1152]{1,0:T(8,128)(2,1)} %copy-done.55, bf16[1,2,256,1152]{3,2,1,0:T(8,128)(2,1)S(1)} %copy-done.12, f32[2,1152]{1,0:T(2,128)S(1)} %get-tuple-element.124), kind=kOutput, calls=%fused_computation.30 | convolution fusion | flops 3625648128 | bytes 14558208 | tf_op jit(solution)/shard_map/dot_general | solution.py:20
  253.5 14.9 %collective-permute-done.8 = bf16[2,256,1152]{2,1,0:T(8,128)(2,1)} collective-permute-done((bf16[2,256,1152]{2,1,0:T(8,128)(2,1)S(1)}, bf16[2,256,1152]{2,1,0:T(8,128)(2,1)}, u32[]{:S(2)}, u32[]{:S(2)}) %collective-permute-start.8) | collective-permute-done | bytes 1179680 | tf_op jit(solution)/shard_map/ppermute | solution.py:330
  268.9 7.7 %fusion.78 = f32[2,256,3456]{1,2,0:T(8,128)S(1)} fusion(bf16[1152,10752]{1,0:T(8,128)(2,1)} %slice_dynamic-update-slice_fusion, bf16[2,256,1152]{2,1,0:T(8,128)(2,1)S(1)} %get-tuple-element.48, f32[2,256]{1,0:T(2,128)S(1)} %fusion.147, f32[2,1152]{1,0:T(2,128)S(1)} %get-tuple-element.127, f32[2,1152]{1,0:T(2,128)S(1)} %get-tuple-element.128), kind=kOutput, calls=%fused_computation.176 | convolution fusion | flops 4079812608 | bytes 16240640 | tf_op jit(solution)/shard_map/dot_general | solution.py:16
  289.4 5.7 multiply_reduce_fusion.11
  295.1 12.1 %fusion.24 = f32[2,256,6144]{2,1,0:T(8,128)S(1)} fusion(bf16[1152,10752]{1,0:T(8,128)(2,1)} %slice_dynamic-update-slice_fusion, f32[2,256,1152]{2,1,0:T(8,128)S(1)} %get-tuple-element.46, f32[2,256]{1,0:T(2,128)S(1)} %fusion.148, f32[2,1152]{1,0:T(2,128)S(1)} %copy-done.76, f32[2,1152]{1,0:T(2,128)S(1)} %get-tuple-element.126), kind=kOutput, calls=%fused_computation.63 | convolution fusion | flops 7250116608 | bytes 29118464 | tf_op jit(solution)/shard_map/dot_general | solution.py:16
  307.3 11.2 %multiply_convert_fusion.5 = (bf16[2,256,3072]{2,1,0:T(8,128)(2,1)}, bf16[2,256,3072]{2,1,0:T(8,128)(2,1)}, bf16[2,256,3072]{2,1,0:T(8,128)(2,1)}) fusion(f32[2,256,3072]{2,1,0:T(8,128)} %fusion.7, f32[2,256,6144]{2,1,0:T(8,128)S(1)} %fusion.24), kind=kLoop, calls=%fused_computation.47 | loop fusion | flops 25165824 | bytes 28311552 | tf_op jit(solution)/shard_map/convert_element_type | solution.py:230
  318.5 17.5 %multiply_reduce_fusion.10 = (f32[2,256]{1,0:T(2,128)}, f32[2,256,1152]{2,1,0:T(8,128)}) fusion(f32[2,256,1152]{2,1,0:T(8,128)} %copy-done.17, f32[2,1152]{1,0:T(2,128)S(1)} %get-tuple-element.126, bf16[1152,10752]{1,0:T(8,128)(2,1)} %slice_dynamic-update-slice_fusion, bf16[2,256,3072]{2,1,0:T(8,128)(2,1)} %get-tuple-element.52, ...), kind=kOutput, calls=%fused_computation.165 | convolution fusion | flops 7262109184 | bytes 25177088 | tf_op jit(solution)/shard_map/dot_general | solution.py:20
  337.8 6.4 convolution_convert_fusion.1
  344.2 2.6 copy.167
  346.8 5.5 fusion.84
  352.3 5.6 multiply_reduce_fusion.1
  370.2 8.7 %fusion.63 = (f32[2,256]{1,0:T(2,128)S(1)}, f32[2,256,1152]{2,1,0:T(8,128)S(1)}) fusion(bf16[2,256,1152]{2,1,0:T(8,128)(2,1)S(1)} %get-tuple-element.48, f32[2,1152]{1,0:T(2,128)S(1)} %get-tuple-element.128, bf16[2,256,3456]{1,2,0:T(8,128)(2,1)S(1)} %bitcast.315, bf16[1152,10752]{1,0:T(8,128)(2,1)} %slice_dynamic-update-slice_fusion), kind=kOutput, calls=%fused_computation.119 | convolution fusion | flops 4079222272 | bytes 15051776 | tf_op jit(solution)/shard_map/dot_general | solution.py:20
  382.2 29.4 %collective-permute-done.9 = bf16[2,256,1152]{2,1,0:T(8,128)(2,1)S(1)} collective-permute-done((bf16[2,256,1152]{2,1,0:T(8,128)(2,1)S(1)}, bf16[2,256,1152]{2,1,0:T(8,128)(2,1)S(1)}, u32[]{:S(2)}, u32[]{:S(2)}) %collective-permute-start.9) | collective-permute-done | bytes 1179680 | tf_op jit(solution)/shard_map/ppermute | solution.py:336
  412.6 4.5 bitcast_convert_fusion.1
  424.6 7.0 %fusion.5 = f32[2,256,3072]{2,1,0:T(8,128)S(1)} fusion(bf16[2,256,1152]{2,1,0:T(8,128)(2,1)} %copy-done.50, bf16[3072,1152]{1,0:T(8,128)(2,1)} %copy-done.55), kind=kOutput, calls=%fused_computation.28 | convolution fusion | flops 3623878656 | bytes 14548992 | tf_op jit(solution)/shard_map/dot_general | solution.py:20
  431.7 8.7 %multiply_convert_fusion.3 = (bf16[2,256,3072]{2,1,0:T(8,128)(2,1)}, bf16[2,256,3072]{2,1,0:T(8,128)(2,1)}) fusion(f32[2,256,3072]{2,1,0:T(8,128)S(1)} %fusion.5, f32[2,256,6144]{2,1,0:T(8,128)} %copy-done.10), kind=kLoop, calls=%fused_computation.45 | loop fusion | flops 20447232 | bytes 25165824 | tf_op jit(solution)/shard_map/convert_element_type | solution.py:230
  440.3 13.4 %bitcast_convert_fusion = bf16[1152,6144]{1,0:T(8,128)(2,1)} fusion(bf16[2,256,3072]{2,1,0:T(8,128)(2,1)} %get-tuple-element.50, bf16[2,256,3072]{2,1,0:T(8,128)(2,1)} %get-tuple-element.49, f32[2,256,1152]{2,1,0:T(8,128)S(1)} %copy-done.19, f32[2,256]{1,0:T(2,128)S(1)} %fusion.148, f32[2,1152]{1,0:T(2,128)S(1)} %copy-done.77, ...), kind=kOutput, calls=%fused_computation.1 | convolution fusion | flops 7269777408 | bytes 22827008 | tf_op jit(solution)/shard_map/dot_general | solution.py:26
  453.7 2.9 slice_dynamic-update-slice_fusion.13
  456.6 2.9 slice_dynamic-update-slice_fusion.12
  459.5 2.8 slice_dynamic-update-slice_fusion.11
  462.3 4.2 slice_dynamic-update-slice_fusion.1
  466.5 2.9 slice_dynamic-update-slice_fusion.10
  469.4 2.9 slice_dynamic-update-slice_fusion.9
  472.3 2.9 slice_dynamic-update-slice_fusion.8
  475.2 3.9 reduce-scatter.4.cloned.1.call-done
  479.1 9.6 %fusion.9 = f32[2,256,1152]{2,1,0:T(8,128)} fusion(bf16[2,256,3072]{2,1,0:T(8,128)(2,1)} %get-tuple-element.53, bf16[3072,1152]{1,0:T(8,128)(2,1)} %copy-done.55), kind=kOutput, calls=%fused_computation.32 | convolution fusion | flops 3623878656 | bytes 12582912 | tf_op jit(solution)/shard_map/dot_general | solution.py:16
  488.7 18.0 %multiply_reduce_fusion.7 = (bf16[2,1152]{1,0:T(2,128)(2,1)}, f32[2,256]{1,0:T(2,128)S(1)}, bf16[2,1152]{1,0:T(2,128)(2,1)}, f32[2,256,1152]{2,1,0:T(8,128)}) fusion(f32[2,256,1152]{2,1,0:T(8,128)} %copy-done.17, f32[2,256]{1,0:T(2,128)S(1)} %fusion.148, f32[2,1152]{1,0:T(2,128)S(1)} %get-tuple-element.126, ...), kind=kOutput, calls=%fused_computation.154 | convolution fusion | flops 7264463872 | bytes 25188352 | tf_op jit(solution)/shard_map/dot_general | solution.py:20
  506.7 6.4 multiply_reduce_fusion.8
  514.5 4.7 convolution_convert_fusion
  520.8 5.8 multiply_reduce_fusion
  545.7 3.3 fusion.2
  549.0 5.2 copy.185
  554.3 7.8 %fusion.1 = bf16[1152,3456]{1,0:T(8,128)(2,1)S(1)} fusion(bf16[2,256,3456]{1,2,0:T(8,128)(2,1)} %bitcast.313, bf16[2,256,1152]{2,1,0:T(8,128)(2,1)S(1)} %get-tuple-element.48, f32[2,256]{1,0:T(2,128)S(1)} %copy-done.60, f32[2,1152]{1,0:T(2,128)S(1)} %copy-done.70, f32[2,1152]{1,0:T(2,128)S(1)} %get-tuple-element.128), kind=kOutput, calls=%fused_computation.6 | convolution fusion | flops 4083793920 | bytes 12701696 | tf_op jit(solution)/shard_map/dot_general | solution.py:26
  571.5 9.8 %fusion.48 = (bf16[2,1152]{1,0:T(2,128)(2,1)S(1)}, f32[2,256]{1,0:T(2,128)S(1)}, bf16[2,1152]{1,0:T(2,128)(2,1)S(1)}, f32[2,256,1152]{2,1,0:T(8,128)S(1)}) fusion(bf16[2,256,1152]{2,1,0:T(8,128)(2,1)S(1)} %get-tuple-element.48, f32[2,256]{1,0:T(2,128)S(1)} %copy-done.60, f32[2,1152]{1,0:T(2,128)S(1)} %get-tuple-element.128, ...), kind=kOutput, calls=%fused_computation.104 | convolution fusion | flops 4081576960 | bytes 15063040 | tf_op jit(solution)/shard_map/dot_general | solution.py:20
  585.1 3.9 collective-permute-done.11
  591.1 4.9 collective-permute-done.12
  600.2 11.4 %collective-permute-done.13 = bf16[8,2,6912]{2,1,0:T(2,128)(2,1)S(1)} collective-permute-done((bf16[8,2,6912]{2,1,0:T(2,128)(2,1)S(1)}, bf16[8,2,6912]{2,1,0:T(2,128)(2,1)S(1)}, u32[]{:S(2)}, u32[]{:S(2)}) %collective-permute-start.13) | collective-permute-done | bytes 221216 | tf_op jit(solution)/shard_map/ppermute | solution.py:67
  618.7 2.9 collective-permute-done.22
  625.0 2.8 collective-permute-done.17
  631.0 7.1 %collective-permute-done.18 = f32[8,32,72]{2,1,0:T(8,128)S(1)} collective-permute-done((f32[8,32,72]{2,1,0:T(8,128)S(1)}, f32[8,32,72]{2,1,0:T(8,128)S(1)}, u32[]{:S(2)}, u32[]{:S(2)}) %collective-permute-start.18) | collective-permute-done | bytes 73760 | tf_op jit(solution)/shard_map/ppermute | solution.py:67
  638.5 4.3 fusion.132
  (400 shorter events, 132.3 us)
Async XLA Ops:
  7.2 18.3 %copy-start = (bf16[1001,1152]{1,0:T(8,128)(2,1)S(1)}, bf16[1001,1152]{1,0:T(8,128)(2,1)}, u32[]{:S(2)}) copy-start(bf16[1001,1152]{1,0:T(8,128)(2,1)} %param.19) | copy-start | bytes 6918916
  7.2 136.9 %all-gather.3.cloned.1.call-start = ((), (), s32[]{:S(2)}) async-start(), calls=%async_computation.3 | async-start | bytes 26320896 | tf_op jit(solution)/shard_map/all_gather | solution.py:56
  10.0 16.2 %copy-start.23 = (bf16[1,72,6912]{2,1,0:T(8,128)(2,1)S(1)}, bf16[1,72,6912]{2,1,0:T(8,128)(2,1)}, u32[]{:S(2)}) copy-start(bf16[1,72,6912]{2,1,0:T(8,128)(2,1)} %param.20) | copy-start | bytes 2985988
  10.0 207.2 %all-gather.5.cloned.1.call-start = ((), (), s32[]{:S(2)}) async-start(), calls=%async_computation.4 | async-start | bytes 7520256 | tf_op jit(solution)/shard_map/all_gather | solution.py:56
  10.1 1.3 collective-permute-start
  11.5 4.5 collective-permute-start.1
  16.0 3.7 collective-permute-start.2
  20.0 4.7 collective-permute-start.3
  26.7 15.3 %copy-start.21 = (bf16[2,256,1152]{2,1,0:T(8,128)(2,1)S(1)}, bf16[2,256,1152]{2,1,0:T(8,128)(2,1)}, u32[]{:S(2)}) copy-start(bf16[2,256,1152]{2,1,0:T(8,128)(2,1)} %param.14) | copy-start | bytes 3538948
  26.8 1.9 collective-permute-start.4
  29.0 12.8 %collective-permute-start.5 = (f32[4,2,6912]{2,1,0:T(2,128)S(1)}, f32[4,2,6912]{2,1,0:T(2,128)S(1)}, u32[]{:S(2)}, u32[]{:S(2)}) collective-permute-start(f32[4,2,6912]{2,1,0:T(2,128)S(1)} %dynamic-slice_bitcast_fusion.1), channel_id=1, source_target_pairs={{0,2},{1,3},{2,0},{3,1},{4,6},{5,7},{6,4},{7,5},{8,10},{9,11},{10,... | collective-permute-start | bytes 663560 | tf_op jit(solution)/shard_map/ppermute | solution.py:67
  42.0 7.8 %collective-permute-start.6 = (f32[2,2,6912]{2,1,0:T(2,128)S(1)}, f32[2,2,6912]{2,1,0:T(2,128)S(1)}, u32[]{:S(2)}, u32[]{:S(2)}) collective-permute-start(f32[2,2,6912]{2,1,0:T(2,128)S(1)} %dynamic-slice_bitcast_fusion.2), channel_id=1, source_target_pairs={{0,4},{1,5},{2,6},{3,7},{4,0},{5,1},{6,2},{7,3},{8,12},{9,13},{10,... | collective-permute-start | bytes 331784 | tf_op jit(solution)/shard_map/ppermute | solution.py:67
  49.9 7.0 %collective-permute-start.7 = (f32[1,2,6912]{2,1,0:T(2,128)S(1)}, f32[1,2,6912]{2,1,0:T(2,128)S(1)}, u32[]{:S(2)}, u32[]{:S(2)}) collective-permute-start(f32[1,2,6912]{2,1,0:T(2,128)S(1)} %constant_dynamic-slice_fusion), channel_id=1, source_target_pairs={{0,8},{1,9},{2,10},{3,11},{4,12},{5,13},{6,14},{7,15},{8,0},{9,1},... | collective-permute-start | bytes 165896 | tf_op jit(solution)/shard_map/ppermute | solution.py:67
  57.0 140.4 %copy-start.71 = (f32[2,1152]{1,0:T(2,128)}, f32[2,1152]{1,0:T(2,128)S(1)}, u32[]{:S(2)}) copy-start(f32[2,1152]{1,0:T(2,128)S(1)} %get-tuple-element.129) | copy-start | bytes 27652
  57.0 144.4 %copy-start.75 = (f32[2,1152]{1,0:T(2,128)}, f32[2,1152]{1,0:T(2,128)S(1)}, u32[]{:S(2)}) copy-start(f32[2,1152]{1,0:T(2,128)S(1)} %get-tuple-element.125) | copy-start | bytes 27652
  57.0 211.9 %copy-start.69 = (f32[2,1152]{1,0:T(2,128)}, f32[2,1152]{1,0:T(2,128)S(1)}, u32[]{:S(2)}) copy-start(f32[2,1152]{1,0:T(2,128)S(1)} %get-tuple-element.127) | copy-start | bytes 27652
  144.2 334.9 %reduce-scatter.4.cloned.1.call-start = ((), (), s32[]{:S(2)}) async-start(), calls=%async_computation.5 | async-start | bytes 7520256 | tf_op jit(solution)/shard_map/reduce_scatter | solution.py:60
  226.9 12.4 %copy-start.55 = (bf16[3072,1152]{1,0:T(8,128)(2,1)}, bf16[3072,1152]{1,0:T(8,128)(2,1)S(1)}, u32[]{:S(2)}) copy-start(bf16[3072,1152]{1,0:T(8,128)(2,1)S(1)} %slice_dynamic-update-slice_fusion.14) | copy-start | bytes 21233668
  226.9 16.9 %copy-start.12 = (bf16[1,2,256,1152]{3,2,1,0:T(8,128)(2,1)S(1)}, bf16[1,2,256,1152]{3,2,1,0:T(8,128)(2,1)}, u32[]{:S(2)}) copy-start(bf16[1,2,256,1152]{3,2,1,0:T(8,128)(2,1)} %param.15) | copy-start | bytes 3538948
  239.2 29.1 %collective-permute-start.8 = (bf16[2,256,1152]{2,1,0:T(8,128)(2,1)S(1)}, bf16[2,256,1152]{2,1,0:T(8,128)(2,1)}, u32[]{:S(2)}, u32[]{:S(2)}) collective-permute-start(bf16[2,256,1152]{2,1,0:T(8,128)(2,1)S(1)} %fusion.36), channel_id=1, source_target_pairs={{0,16},{1,17},{2,18},{3,19},{4,20},{5,21},{6,22},{7,23},{8,24},{9,... | collective-permute-start | bytes 3538952 | tf_op jit(solution)/shard_map/ppermute | solution.py:330
  243.8 24.5 %copy-start.22 = (bf16[2,256,1152]{2,1,0:T(8,128)(2,1)S(1)}, bf16[2,256,1152]{2,1,0:T(8,128)(2,1)}, u32[]{:S(2)}) copy-start(bf16[2,256,1152]{2,1,0:T(8,128)(2,1)} %param.14) | copy-start | bytes 3538948
  268.8 110.6 %copy-start.59 = (f32[2,256]{1,0:T(2,128)}, f32[2,256]{1,0:T(2,128)S(1)}, u32[]{:S(2)}) copy-start(f32[2,256]{1,0:T(2,128)S(1)} %fusion.147) | copy-start | bytes 6148
  276.6 8.9 %copy-start.11 = (f32[2,256,3456]{1,2,0:T(8,128)}, f32[2,256,3456]{1,2,0:T(8,128)S(1)}, u32[]{:S(2)}) copy-start(f32[2,256,3456]{1,2,0:T(8,128)S(1)} %fusion.78) | copy-start | bytes 21233668
  281.1 78.9 %copy-start.25 = (bf16[2,256,16,18]{1,3,2,0:T(8,128)(2,1)}, bf16[2,256,16,18]{1,3,2,0:T(8,128)(2,1)S(1)}, u32[]{:S(2)}) copy-start(bf16[2,256,16,18]{1,3,2,0:T(8,128)(2,1)S(1)} %get-tuple-element.74) | copy-start | bytes 884740
  281.1 78.9 %copy-start.27 = (bf16[2,256,16,18]{1,3,2,0:T(8,128)(2,1)}, bf16[2,256,16,18]{1,3,2,0:T(8,128)(2,1)S(1)}, u32[]{:S(2)}) copy-start(bf16[2,256,16,18]{1,3,2,0:T(8,128)(2,1)S(1)} %get-tuple-element.75) | copy-start | bytes 884740
  295.1 12.2 %copy-start.17 = (f32[2,256,1152]{2,1,0:T(8,128)}, f32[2,256,1152]{2,1,0:T(8,128)S(1)}, u32[]{:S(2)}) copy-start(f32[2,256,1152]{2,1,0:T(8,128)S(1)} %get-tuple-element.46) | copy-start | bytes 7077892
  295.1 12.2 %copy-start.82 = (f32[2,256]{1,0:T(2,128)}, f32[2,256]{1,0:T(2,128)S(1)}, u32[]{:S(2)}) copy-start(f32[2,256]{1,0:T(2,128)S(1)} %get-tuple-element.45) | copy-start | bytes 6148
  295.1 193.6 %copy-start.61 = (f32[2,256]{1,0:T(2,128)}, f32[2,256]{1,0:T(2,128)S(1)}, u32[]{:S(2)}) copy-start(f32[2,256]{1,0:T(2,128)S(1)} %fusion.148) | copy-start | bytes 6148
  307.3 11.2 %copy-start.10 = (f32[2,256,6144]{2,1,0:T(8,128)}, f32[2,256,6144]{2,1,0:T(8,128)S(1)}, u32[]{:S(2)}) copy-start(f32[2,256,6144]{2,1,0:T(8,128)S(1)} %fusion.24) | copy-start | bytes 37748740
  346.8 11.1 %slice-start = ((s8[8388608]{0:T(1024)(128)(4,1)}), s8[4194304]{0:T(1024)(128)(4,1)S(1)}, s32[]{:S(2)}) async-start(s8[8388608]{0:T(1024)(128)(4,1)} %bitcast.285), calls=%async_computation.8 | async-start | bytes 8388608
  370.1 9.3 %copy-start.18 = (f32[2,256,1152]{2,1,0:T(8,128)S(1)}, f32[2,256,1152]{2,1,0:T(8,128)}, u32[]{:S(2)}) copy-start(f32[2,256,1152]{2,1,0:T(8,128)} %copy-done.17) | copy-start | bytes 7077892
  370.2 9.3 %copy-start.49 = (f32[2,256,1152]{2,1,0:T(8,128)S(1)}, f32[2,256,1152]{2,1,0:T(8,128)}, u32[]{:S(2)}) copy-start(f32[2,256,1152]{2,1,0:T(8,128)} %get-tuple-element.170) | copy-start | bytes 7077892
  370.2 9.3 %copy-start.79 = (f32[2,256]{1,0:T(2,128)S(1)}, f32[2,256]{1,0:T(2,128)}, u32[]{:S(2)}) copy-start(f32[2,256]{1,0:T(2,128)} %copy-done.78) | copy-start | bytes 6148
  380.6 32.0 %copy-start.47 = (bf16[2,256,3072]{2,1,0:T(8,128)(2,1)S(1)}, bf16[2,256,3072]{2,1,0:T(8,128)(2,1)}, u32[]{:S(2)}) copy-start(bf16[2,256,3072]{2,1,0:T(8,128)(2,1)} %get-tuple-element.53) | copy-start | bytes 9437188
  380.6 30.9 %collective-permute-start.9 = (bf16[2,256,1152]{2,1,0:T(8,128)(2,1)S(1)}, bf16[2,256,1152]{2,1,0:T(8,128)(2,1)S(1)}, u32[]{:S(2)}, u32[]{:S(2)}) collective-permute-start(bf16[2,256,1152]{2,1,0:T(8,128)(2,1)S(1)} %fusion.56), channel_id=1, source_target_pairs={{16,0},{17,1},{18,2},{19,3},{20,4},{21,5},{22,6},{23,7},{24,8},{25... | collective-permute-start | bytes 3538952 | tf_op jit(solution)/shard_map/ppermute | solution.py:336
  424.6 146.3 %reduce-scatter.6.cloned.1.call-start = ((), (), s32[]{:S(2)}) async-start(), calls=%async_computation.6 | async-start | bytes 15040512 | tf_op jit(solution)/shard_map/reduce_scatter | solution.py:60
  431.6 8.7 %copy-start.19 = (f32[2,256,1152]{2,1,0:T(8,128)S(1)}, f32[2,256,1152]{2,1,0:T(8,128)}, u32[]{:S(2)}) copy-start(f32[2,256,1152]{2,1,0:T(8,128)} %copy-done.17) | copy-start | bytes 7077892
  431.7 8.7 %copy-start.77 = (f32[2,1152]{1,0:T(2,128)S(1)}, f32[2,1152]{1,0:T(2,128)}, u32[]{:S(2)}) copy-start(f32[2,1152]{1,0:T(2,128)} %copy-done.75) | copy-start | bytes 27652
  479.1 166.4 %reduce-scatter.8.cloned.1.call-start = ((), (), s32[]{:S(2)}) async-start(), calls=%async_computation.7 | async-start | bytes 11280384 | tf_op jit(solution)/shard_map/reduce_scatter | solution.py:60
  488.7 18.0 %copy-start.81 = (f32[2,256]{1,0:T(2,128)S(1)}, f32[2,256]{1,0:T(2,128)}, u32[]{:S(2)}) copy-start(f32[2,256]{1,0:T(2,128)} %get-tuple-element.44) | copy-start | bytes 6148
  506.7 7.8 %copy-start.73 = (f32[2,1152]{1,0:T(2,128)S(1)}, f32[2,1152]{1,0:T(2,128)}, u32[]{:S(2)}) copy-start(f32[2,1152]{1,0:T(2,128)} %copy-done.71) | copy-start | bytes 27652
  554.3 7.9 %copy-start.3 = (bf16[1152,1152]{1,0:T(8,128)(2,1)S(1)}, bf16[1152,1152]{1,0:T(8,128)(2,1)}, u32[]{:S(2)}) copy-start(bf16[1152,1152]{1,0:T(8,128)(2,1)} %copy.185) | copy-start | bytes 7962628
  570.9 10.5 %copy-start.58 = (bf16[2,1152]{1,0:T(2,128)(2,1)S(1)}, bf16[2,1152]{1,0:T(2,128)(2,1)}, u32[]{:S(2)}) copy-start(bf16[2,1152]{1,0:T(2,128)(2,1)} %get-tuple-element.39) | copy-start | bytes 13828
  570.9 10.5 %copy-start.86 = (bf16[2,1152]{1,0:T(2,128)(2,1)S(1)}, bf16[2,1152]{1,0:T(2,128)(2,1)}, u32[]{:S(2)}) copy-start(bf16[2,1152]{1,0:T(2,128)(2,1)} %get-tuple-element.35) | copy-start | bytes 13828
  570.9 10.5 %copy-start.85 = (bf16[2,1152]{1,0:T(2,128)(2,1)S(1)}, bf16[2,1152]{1,0:T(2,128)(2,1)}, u32[]{:S(2)}) copy-start(bf16[2,1152]{1,0:T(2,128)(2,1)} %get-tuple-element.31) | copy-start | bytes 13828
  571.0 10.6 %copy-start.80 = (f32[2,256]{1,0:T(2,128)S(1)}, f32[2,256]{1,0:T(2,128)}, u32[]{:S(2)}) copy-start(f32[2,256]{1,0:T(2,128)} %get-tuple-element.42) | copy-start | bytes 6148
  571.0 10.6 %copy-start.16 = (f32[2,256,1152]{2,1,0:T(8,128)S(1)}, f32[2,256,1152]{2,1,0:T(8,128)}, u32[]{:S(2)}) copy-start(f32[2,256,1152]{2,1,0:T(8,128)} %copy-done.14) | copy-start | bytes 7077892
  571.0 14.1 %collective-permute-start.19 = (f32[1,2,72]{2,1,0:T(2,128)S(1)}, f32[1,2,72]{2,1,0:T(2,128)S(1)}, u32[]{:S(2)}, u32[]{:S(2)}) collective-permute-start(f32[1,2,72]{2,1,0:T(2,128)S(1)} %maximum_bitcast_fusion.1), channel_id=1, source_target_pairs={{0,1},{1,0},{2,3},{3,2},{4,5},{5,4},{6,7},{7,6},{8,9},{9,8},{10,11... | collective-permute-start | bytes 1736 | tf_op jit(solution)/shard_map/ppermute | solution.py:67
  581.5 2.2 collective-permute-start.10
  583.6 29.2 %copy-start.24 = (bf16[1,72,6912]{2,1,0:T(8,128)(2,1)S(1)}, bf16[1,72,6912]{2,1,0:T(8,128)(2,1)}, u32[]{:S(2)}) copy-start(bf16[1,72,6912]{2,1,0:T(8,128)(2,1)} %param.20) | copy-start | bytes 2985988
  583.8 5.2 collective-permute-start.11
  589.3 6.7 %collective-permute-start.12 = (bf16[4,2,6912]{2,1,0:T(2,128)(2,1)S(1)}, bf16[4,2,6912]{2,1,0:T(2,128)(2,1)S(1)}, u32[]{:S(2)}, u32[]{:S(2)}) collective-permute-start(bf16[4,2,6912]{2,1,0:T(2,128)(2,1)S(1)} %pad_maximum_fusion.14), channel_id=1, source_target_pairs={{0,4},{1,5},{2,6},{3,7},{4,0},{5,1},{6,2},{7,3},{8,12},{9,13},{10,... | collective-permute-start | bytes 331784 | tf_op jit(solution)/shard_map/ppermute | solution.py:67
  589.7 8.5 %collective-permute-start.20 = (f32[2,2,72]{2,1,0:T(2,128)S(1)}, f32[2,2,72]{2,1,0:T(2,128)S(1)}, u32[]{:S(2)}, u32[]{:S(2)}) collective-permute-start(f32[2,2,72]{2,1,0:T(2,128)S(1)} %pad_maximum_fusion.20), channel_id=1, source_target_pairs={{0,2},{1,3},{2,0},{3,1},{4,6},{5,7},{6,4},{7,5},{8,10},{9,11},{10,... | collective-permute-start | bytes 3464 | tf_op jit(solution)/shard_map/ppermute | solution.py:67
  596.5 15.1 %collective-permute-start.13 = (bf16[8,2,6912]{2,1,0:T(2,128)(2,1)S(1)}, bf16[8,2,6912]{2,1,0:T(2,128)(2,1)S(1)}, u32[]{:S(2)}, u32[]{:S(2)}) collective-permute-start(bf16[8,2,6912]{2,1,0:T(2,128)(2,1)S(1)} %pad_maximum_fusion.12), channel_id=1, source_target_pairs={{0,8},{1,9},{2,10},{3,11},{4,12},{5,13},{6,14},{7,15},{8,0},{9,1},... | collective-permute-start | bytes 663560 | tf_op jit(solution)/shard_map/ppermute | solution.py:67
  598.3 31.0 %copy-start.57 = (bf16[32,72]{1,0:T(8,128)(2,1)S(1)}, bf16[32,72]{1,0:T(8,128)(2,1)}, u32[]{:S(2)}) copy-start(bf16[32,72]{1,0:T(8,128)(2,1)} %copy-done.56) | copy-start | bytes 13828
  598.3 16.5 %collective-permute-start.21 = (f32[4,2,72]{2,1,0:T(2,128)S(1)}, f32[4,2,72]{2,1,0:T(2,128)S(1)}, u32[]{:S(2)}, u32[]{:S(2)}) collective-permute-start(f32[4,2,72]{2,1,0:T(2,128)S(1)} %pad_maximum_fusion.19), channel_id=1, source_target_pairs={{0,4},{1,5},{2,6},{3,7},{4,0},{5,1},{6,2},{7,3},{8,12},{9,13},{10,... | collective-permute-start | bytes 6920 | tf_op jit(solution)/shard_map/ppermute | solution.py:67
  613.2 3.8 collective-permute-start.14
  617.0 1.2 collective-permute-start.15
  617.0 4.6 collective-permute-start.22
  618.2 4.4 collective-permute-start.16
  622.6 5.1 collective-permute-start.17
  627.8 10.7 %copy-start.53 = (f32[32,1152]{1,0:T(8,128)S(1)}, f32[32,1152]{1,0:T(8,128)}, u32[]{:S(2)}) copy-start(f32[32,1152]{1,0:T(8,128)} %copy-done.52) | copy-start | bytes 442372
  627.8 10.7 %copy-start.84 = (s32[32]{0:T(128)S(1)}, s32[32]{0:T(128)}, u32[]{:S(2)}) copy-start(s32[32]{0:T(128)} %copy-done.83) | copy-start | bytes 388
  627.8 10.3 %collective-permute-start.18 = (f32[8,32,72]{2,1,0:T(8,128)S(1)}, f32[8,32,72]{2,1,0:T(8,128)S(1)}, u32[]{:S(2)}, u32[]{:S(2)}) collective-permute-start(f32[8,32,72]{2,1,0:T(8,128)S(1)} %pad_maximum_fusion.13), channel_id=1, source_target_pairs={{0,8},{1,9},{2,10},{3,11},{4,12},{5,13},{6,14},{7,15},{8,0},{9,1},... | collective-permute-start | bytes 221192 | tf_op jit(solution)/shard_map/ppermute | solution.py:67
  (62 other events, 158.0 us)
Sparse Core Ops, SparseCore 0:
  10.2 133.8 all-gather.2
  145.7 43.6 all-gather.4
  424.7 54.2 reduce-scatter.3
  481.3 80.3 reduce-scatter.5
  571.0 74.3 reduce-scatter.7

commit v3 on v1

v3 whole, which is shorter than its diff:
```python
import functools
import math

import jax
import jax.numpy as jnp
from jax import lax
from jax.experimental import pallas as pl
from jax.experimental.pallas import tpu as pltpu
from jax.sharding import PartitionSpec as P

GRID = 16
epsilon = 1e-06
f32 = jnp.float32
bf16 = jnp.bfloat16
LANES = 128
VMEM_BYTES = 56 * 1024 * 1024


def params():
    return pltpu.CompilerParams(vmem_limit_bytes=VMEM_BYTES)


def cost(flops, moved):
    return pl.CostEstimate(flops=int(flops), bytes_accessed=int(moved), transcendentals=0)


def dot(left, right):
    return jnp.dot(left, right, preferred_element_type=f32)


def dot_right(left, right):
    return lax.dot_general(left, right, (((1,), (1,)), ((), ())), preferred_element_type=f32)


def dot_left(left, right):
    return lax.dot_general(left, right, (((0,), (0,)), ((), ())), preferred_element_type=f32)


def whole_rows(ref, places):
    if len(places) == 1:
        return ref[places[0]]
    return jnp.concatenate([ref[place] for place in places], axis=0)


def part_place(index, parts, walked):
    if not walked:
        return index
    return index // 2 + (index % 2) * (parts - 1 - 2 * (index // 2))


def places_of(parts, walked):
    return [part_place(index, parts, walked) for index in range(parts)]


def two_terms(left, right):
    high = left.astype(bf16)
    low = (left - high.astype(f32)).astype(bf16)
    return dot(high, right) + dot(low, right)


def inverse_rms(values):
    return lax.rsqrt(jnp.mean(values * values, axis=-1, keepdims=True) + epsilon)


def partner(values, first_half, quarter):
    width = values.shape[1]
    return jnp.where(
        first_half, pltpu.roll(values, width - quarter, 1), pltpu.roll(values, quarter, 1)
    )


def first_half_mask(shape, quarter):
    lane = lax.broadcasted_iota(jnp.int32, shape, 1)
    return lane % (2 * quarter) < quarter


def head_window(head, head_size, width):
    span = min(2 * LANES, width)
    start = min(head * head_size // LANES * LANES, width - span)
    return start, span


def head_mask(head, head_size, start, span):
    lane = lax.broadcasted_iota(jnp.int32, (1, span), 1) + start
    inside = jnp.logical_and(lane >= head * head_size, lane < (head + 1) * head_size)
    return inside.astype(f32).astype(bf16)


def attention_forward_kernel(
    heads,
    places,
    keep,
    received_ref,
    x_ref,
    mod_ref,
    cos_ref,
    sin_ref,
    gain_ref,
    sum_ref,
    spread_ref,
    joined_ref,
    *rest,
):
    if keep:
        normed_ref, raw_ref, value_ref, attended_ref, branch_ref, middle_ref, normed_two_ref = rest[:7]
        flow_ref = rest[7]
        rest = rest[8:]
    else:
        middle_ref, normed_two_ref = rest[:2]
        rest = rest[2:]
    weight, mixed, sems = rest
    width = x_ref.shape[1]
    head_size = width // heads
    quarter = head_size // 4

    def fetch(part):
        return pltpu.make_async_copy(
            joined_ref.at[:, :, pl.ds(part * width, width)], weight.at[part], sems.at[part]
        )

    @pl.when(pl.program_id(0) == 0)
    def _():
        for part in range(4):
            fetch(part).start()

    def arrived(part):
        @pl.when(pl.program_id(0) == 0)
        def _():
            fetch(part).wait()

    flow = x_ref[...].astype(f32)
    if keep:
        flow = flow + received_ref[...].astype(f32)
        flow_ref[...] = flow.astype(bf16)
    mod = mod_ref[0]
    normed = (flow * inverse_rms(flow) * (1.0 + mod[1:2]) + mod[0:1]).astype(bf16)
    if keep:
        normed_ref[...] = normed
    summing, spreading = sum_ref[...], spread_ref[...]
    first_half = first_half_mask((1, width), quarter)

    def prepared(part):
        arrived(part)
        raw = dot(normed, whole_rows(weight.at[part], places))
        if keep:
            raw_ref[:, part * width : (part + 1) * width] = raw
        scale = lax.rsqrt(two_terms(raw * raw, summing) * (1.0 / head_size) + epsilon)
        scaled = raw * two_terms(scale, spreading) * gain_ref[part : part + 1]
        turned = scaled * cos_ref[...] + partner(scaled, first_half, quarter) * sin_ref[...]
        return turned.astype(bf16)

    queries = prepared(0)
    keys = prepared(1)
    arrived(2)
    values = dot(normed, whole_rows(weight.at[2], places)).astype(bf16)
    if keep:
        value_ref[...] = values
    mixed[...] = jnp.zeros_like(mixed)
    factor = head_size ** (-0.5)
    for head in range(heads):
        start, span = head_window(head, head_size, width)
        mask = head_mask(head, head_size, start, span)
        window = slice(start, start + span)
        scores = dot_right(queries[:, window], keys[:, window] * mask)
        highest = jnp.max(scores, axis=-1, keepdims=True)
        expon = jnp.exp((scores - highest) * factor)
        probs = expon * (1.0 / jnp.sum(expon, axis=-1, keepdims=True))
        mixed[:, window] += dot(probs.astype(bf16), values[:, window] * mask)
    attended = mixed[...].astype(bf16)
    arrived(3)
    branch = dot(attended, whole_rows(weight.at[3], places))
    middle = flow + mod[2:3] * branch
    middle_ref[...] = middle
    normed_two_ref[...] = (middle * inverse_rms(middle) * (1.0 + mod[4:5]) + mod[3:4]).astype(bf16)
    if keep:
        attended_ref[...] = attended
        branch_ref[...] = branch


def attention_forward(x, received, mod, tables, gains, joined, walked, first, count, made=None):
    keep = received is not None
    cos, sin, summing, spreading = tables
    gain, head_size = gains
    images, unused, width = mod.shape
    tokens = x.shape[0]
    patches = tokens // images
    heads = width // head_size
    places = places_of(joined.shape[0], walked)
    row = lambda columns: pl.BlockSpec((patches, columns), lambda image: (first + image, 0))
    fixed = lambda array: pl.BlockSpec(array.shape, lambda image: (0,) * array.ndim)
    shapes = [(width, f32), (width, bf16)]
    if keep:
        shapes = [
            (width, bf16),
            (2 * width, f32),
            (width, bf16),
            (width, bf16),
            (width, f32),
            (width, f32),
            (width, bf16),
            (width, bf16),
        ]
    made = [] if made is None else list(made)
    extra = [received] if keep else []
    inputs = 8 + len(extra)

    def body(*refs):
        rest = refs[inputs + len(made) :]
        received_ref = refs[0] if keep else None
        attention_forward_kernel(
            heads, places, keep, received_ref, *refs[len(extra) : inputs], *rest
        )

    return pl.pallas_call(
        body,
        grid=(count,),
        in_specs=[pl.BlockSpec((patches, width), lambda image: (image, 0))] * len(extra)
        + [
            row(width),
            pl.BlockSpec((1, 6, width), lambda image: (first + image, 0, 0)),
            row(width),
            row(width),
            fixed(gain),
            fixed(summing),
            fixed(spreading),
            pl.BlockSpec(memory_space=pl.ANY),
        ]
        + [pl.BlockSpec(memory_space=pl.ANY)] * len(made),
        out_specs=[row(columns) for columns, kind in shapes],
        out_shape=[jax.ShapeDtypeStruct((tokens, columns), kind) for columns, kind in shapes],
        input_output_aliases={inputs + index: index for index in range(len(made))},
        scratch_shapes=[
            pltpu.VMEM((4, joined.shape[0], joined.shape[1], width), bf16),
            pltpu.VMEM((patches, width), f32),
            pltpu.SemaphoreType.DMA((4,)),
        ],
        compiler_params=params(),
        cost_estimate=cost(
            2 * count * patches * width * (4 * width + 2 * patches),
            8 * width * width + count * patches * width * 20,
        ),
    )(*extra, x, mod, cos, sin, gain, summing, spreading, joined, *made)


def gate_up_kernel(places, keep, normed_ref, gate_ref, up_ref, *outs):
    normed = normed_ref[...]
    gate = dot(normed, whole_rows(gate_ref, places))
    up = dot(normed, whole_rows(up_ref, places))
    outs[0][...] = (gate * (1.0 / (1.0 + jnp.exp(-gate))) * up).astype(bf16)
    if keep:
        outs[1][...] = gate.astype(bf16)
        outs[2][...] = up.astype(bf16)


def gate_up(normed_two, joined, hidden, walked, keep):
    tokens, width = normed_two.shape
    step = 512
    base = 4 * width // step
    count = hidden // step
    parts, rows, unused = joined.shape
    shapes = 3 if keep else 1
    return pl.pallas_call(
        functools.partial(gate_up_kernel, places_of(parts, walked), keep),
        grid=(count,),
        in_specs=[
            pl.BlockSpec((tokens, width), lambda i: (0, 0)),
            pl.BlockSpec((parts, rows, step), lambda i: (0, 0, base + i)),
            pl.BlockSpec((parts, rows, step), lambda i: (0, 0, base + count + i)),
        ],
        out_specs=[pl.BlockSpec((tokens, step), lambda i: (0, i))] * shapes,
        out_shape=[jax.ShapeDtypeStruct((tokens, hidden), bf16)] * shapes,
        compiler_params=params(),
        cost_estimate=cost(4 * tokens * width * hidden, 4 * width * hidden + 2 * shapes * tokens * hidden),
    )(normed_two, joined, joined)


def parts_per_step(rows):
    return max(1, 768 // rows)


def part_specs(down, walked):
    parts, rows, width = down.shape
    each = parts_per_step(rows)

    def spec(which):
        return pl.BlockSpec(
            (1, rows, width), lambda i: (part_place(i * each + which, parts, walked), 0, 0)
        )

    return [spec(which) for which in range(each)]


def joined_parts(refs):
    if len(refs) == 1:
        return refs[0][0]
    return jnp.concatenate([ref[0] for ref in refs], axis=0)


def down_projection(act, down, middle, mod, walked, first, count, keep):
    hidden = act.shape[1]
    images, unused, width = mod.shape
    patches = act.shape[0] // images
    tokens = count * patches
    specs = part_specs(down, walked)
    each, rows = len(specs), down.shape[1]
    outs = [jax.ShapeDtypeStruct((tokens, width), bf16)]
    scratch = [pltpu.VMEM((tokens, width), f32)]
    if keep:
        outs.append(jax.ShapeDtypeStruct((tokens, width), f32))
        scratch = []

    def body(act_ref, middle_ref, mod_ref, *refs):
        step = pl.program_id(0)
        total = refs[each + 1]
        term = dot(act_ref[...], joined_parts(refs[:each]))

        @pl.when(step == 0)
        def _():
            total[...] = term

        @pl.when(step > 0)
        def _():
            total[...] += term

        @pl.when(step == pl.num_programs(0) - 1)
        def _():
            for image in range(count):
                at = slice(image * patches, (image + 1) * patches)
                gate = mod_ref[first + image, 5:6]
                refs[each][at] = (middle_ref[at] + gate * total[at]).astype(bf16)

    return pl.pallas_call(
        body,
        grid=(hidden // (each * rows),),
        in_specs=[
            pl.BlockSpec((tokens, each * rows), lambda i: (first // count, i)),
            pl.BlockSpec((tokens, width), lambda i: (first // count, 0)),
            pl.BlockSpec(mod.shape, lambda i: (0, 0, 0)),
        ]
        + specs,
        out_specs=[pl.BlockSpec((tokens, width), lambda i: (0, 0))] * len(outs),
        out_shape=outs,
        scratch_shapes=scratch,
        compiler_params=params(),
        cost_estimate=cost(2 * tokens * width * hidden, 2 * width * hidden + 8 * tokens * width),
    )(act, middle, mod, *[down] * each)


def incoming(cot_ref, back_refs, image, at):
    value = cot_ref[at].astype(f32)
    return value + back_refs[image][...].astype(f32) if back_refs else value


def mlp_gradient(cot, backs, mod, first, count):
    images, unused, width = mod.shape
    patches = cot.shape[0] // images

    def body(cot_ref, mod_ref, *refs):
        for image in range(count):
            at = slice(image * patches, (image + 1) * patches)
            grads = incoming(cot_ref, refs[: len(backs)], image, at)
            refs[-1][at] = (mod_ref[first + image, 5:6] * grads).astype(bf16)

    return pl.pallas_call(
        body,
        grid=(1,),
        in_specs=[
            pl.BlockSpec((count * patches, width), lambda i: (first // count, 0)),
            pl.BlockSpec(mod.shape, lambda i: (0, 0, 0)),
        ]
        + [pl.BlockSpec((patches, width), lambda i: (0, 0))] * len(backs),
        out_specs=pl.BlockSpec((count * patches, width), lambda i: (0, 0)),
        out_shape=jax.ShapeDtypeStruct((count * patches, width), bf16),
        compiler_params=params(),
        cost_estimate=cost(0, 6 * count * patches * width),
    )(cot, mod, *backs)


def stacked(refs):
    return refs[0][...] if len(refs) == 1 else jnp.concatenate([ref[...] for ref in refs], axis=0)


def whole_specs(arrays):
    return [pl.BlockSpec(array.shape, lambda i: (0, 0)) for array in arrays]


def act_backward(mlp_grads, down, hidden, walked):
    width = mlp_grads[0].shape[1]
    tokens = sum(grad.shape[0] for grad in mlp_grads)
    specs = part_specs(down, walked)
    each, rows = len(specs), down.shape[1]

    def body(*refs):
        grads, refs = refs[: len(mlp_grads)], refs[len(mlp_grads) :]
        refs[each][...] = dot_right(stacked(grads), joined_parts(refs[:each])).astype(bf16)

    return pl.pallas_call(
        body,
        grid=(hidden // (each * rows),),
        in_specs=whole_specs(mlp_grads) + specs,
        out_specs=pl.BlockSpec((tokens, each * rows), lambda i: (0, i)),
        out_shape=jax.ShapeDtypeStruct((tokens, hidden), bf16),
        compiler_params=params(),
        cost_estimate=cost(2 * tokens * width * hidden, 2 * width * hidden + 4 * tokens * width),
    )(*mlp_grads, *[down] * each)


def mlp_backward(cot, backs, mlp, act_grad, gate, up, joined, middle, branch, mod, walked, keep):
    tokens, hidden = gate.shape
    images, unused, width = mod.shape
    patches = tokens // images
    parts, rows, unused = joined.shape
    places = places_of(parts, walked)
    step = 512
    base = 4 * width // step
    count = hidden // step
    whole = pl.BlockSpec((tokens, width), lambda i: (0, 0))
    block = pl.BlockSpec((tokens, step), lambda i: (0, i))
    kept = [mlp, branch] if keep else []

    def body(cot_ref, act_grad_ref, gate_ref, up_ref, gate_weight, up_weight, middle_ref, mod_ref, joined_ref, *refs):
        back_refs, refs = refs[: len(backs)], refs[len(backs) :]
        if keep:
            mlp_ref, branch_ref = refs[:2]
            refs = refs[2:]
        middle_grad_ref, mixed_grad_ref = refs[:2]
        refs = refs[2:]
        if keep:
            gate_grad_ref, up_grad_ref, branch_grad_ref, sums_ref = refs[:4]
            refs = refs[4:]
        total, out_weight, sem = refs
        index = pl.program_id(0)
        fetch = pltpu.make_async_copy(joined_ref.at[:, :, pl.ds(3 * width, width)], out_weight, sem)

        @pl.when(index == 0)
        def _():
            fetch.start()

        gate_val, up_val = gate_ref[...].astype(f32), up_ref[...].astype(f32)
        sigma = 1.0 / (1.0 + jnp.exp(-gate_val))
        slope = act_grad_ref[...].astype(f32) * sigma
        gate_grad = (slope * up_val * (1.0 + gate_val * (1.0 - sigma))).astype(bf16)
        up_grad = (slope * gate_val).astype(bf16)
        if keep:
            gate_grad_ref[...] = gate_grad
            up_grad_ref[...] = up_grad
        term = dot_right(gate_grad, whole_rows(gate_weight, places))
        term = term + dot_right(up_grad, whole_rows(up_weight, places))

        @pl.when(index == 0)
        def _():
            total[...] = term

        @pl.when(index > 0)
        def _():
            total[...] += term

        @pl.when(index == count - 1)
        def _():
            fetch.wait()
            matrix = whole_rows(out_weight, places)
            for image in range(images):
                at = slice(image * patches, (image + 1) * patches)
                mod = mod_ref[image]
                grad, flow = total[at], middle_ref[at]
                inverse = inverse_rms(flow)
                normal = flow * inverse
                scaled = grad * (1.0 + mod[4:5])
                mean = jnp.mean(scaled * normal, axis=-1, keepdims=True)
                out_grad = incoming(cot_ref, back_refs, image, at)
                middle_grad = out_grad + (scaled - normal * mean) * inverse
                middle_grad_ref[at] = middle_grad
                branch_grad = (mod[2:3] * middle_grad).astype(bf16)
                mixed_grad_ref[at] = dot_right(branch_grad, matrix).astype(bf16)
                if keep:
                    branch_grad_ref[at] = branch_grad
                    terms = [middle_grad * branch_ref[at], grad, grad * normal, out_grad * mlp_ref[at]]
                    for place, value in enumerate(terms):
                        sums_ref[image, place : place + 1] = jnp.sum(value, axis=0, keepdims=True)

    out_shapes = [
        jax.ShapeDtypeStruct((tokens, width), f32),
        jax.ShapeDtypeStruct((tokens, width), bf16),
    ]
    out_specs = [whole, whole]
    if keep:
        out_shapes += [jax.ShapeDtypeStruct((tokens, hidden), bf16)] * 2
        out_shapes += [jax.ShapeDtypeStruct((tokens, width), bf16)]
        out_shapes += [jax.ShapeDtypeStruct((images, 4, width), f32)]
        out_specs += [block, block, whole, pl.BlockSpec((images, 4, width), lambda i: (0, 0, 0))]
    return pl.pallas_call(
        body,
        grid=(count,),
        in_specs=[
            whole,
            block,
            block,
            block,
            pl.BlockSpec((parts, rows, step), lambda i: (0, 0, base + i)),
            pl.BlockSpec((parts, rows, step), lambda i: (0, 0, base + count + i)),
            whole,
            pl.BlockSpec(mod.shape, lambda i: (0, 0, 0)),
            pl.BlockSpec(memory_space=pl.ANY),
        ]
        + [pl.BlockSpec((patches, width), lambda i: (0, 0))] * len(backs)
        + [whole] * len(kept),
        out_specs=out_specs,
        out_shape=out_shapes,
        scratch_shapes=[
            pltpu.VMEM((tokens, width), f32),
            pltpu.VMEM((parts, rows, width), bf16),
            pltpu.SemaphoreType.DMA,
        ],
        compiler_params=params(),
        cost_estimate=cost(
            2 * tokens * width * (2 * hidden + width), 4 * width * hidden + 6 * tokens * hidden
        ),
    )(cot, act_grad, gate, up, joined, joined, middle, mod, joined, *backs, *kept)


def attention_backward_kernel(
    heads,
    places,
    keep,
    raw_ref,
    value_ref,
    mixed_grad_ref,
    middle_grad_ref,
    x_ref,
    mod_ref,
    cos_ref,
    sin_ref,
    gain_ref,
    sum_ref,
    spread_ref,
    joined_ref,
    *rest,
):
    if keep:
        flow_grad_ref, qkv_grad_ref, sums_ref = rest[:3]
        rest = rest[3:]
    else:
        back_ref = rest[0]
        rest = rest[1:]
    weight, query_total, key_total, value_total, sems = rest
    width = x_ref.shape[1]
    head_size = width // heads
    quarter = head_size // 4
    factor = head_size ** (-0.5)

    def fetch(part):
        return pltpu.make_async_copy(
            joined_ref.at[:, :, pl.ds(part * width, width)], weight.at[part], sems.at[part]
        )

    @pl.when(pl.program_id(0) == 0)
    def _():
        for part in range(3):
            fetch(part).start()

    summing, spreading = sum_ref[...], spread_ref[...]
    first_half = first_half_mask((1, width), quarter)

    def prepared(part):
        raw = raw_ref[:, part * width : (part + 1) * width]
        scale = lax.rsqrt(two_terms(raw * raw, summing) * (1.0 / head_size) + epsilon)
        scaled = raw * two_terms(scale, spreading) * gain_ref[part : part + 1]
        turned = scaled * cos_ref[...] + partner(scaled, first_half, quarter) * sin_ref[...]
        return turned.astype(bf16)

    queries, keys, values = prepared(0), prepared(1), value_ref[...]
    mixed_grad = mixed_grad_ref[...]
    query_total[...] = jnp.zeros_like(query_total)
    key_total[...] = jnp.zeros_like(key_total)
    value_total[...] = jnp.zeros_like(value_total)
    for head in range(heads):
        start, span = head_window(head, head_size, width)
        mask = head_mask(head, head_size, start, span)
        window = slice(start, start + span)
        key_part, query_part = keys[:, window] * mask, queries[:, window] * mask
        grad_part = mixed_grad[:, window] * mask
        scores = dot_right(key_part, queries[:, window])
        highest = jnp.max(scores, axis=0, keepdims=True)
        expon = jnp.exp((scores - highest) * factor)
        probs = expon * (1.0 / jnp.sum(expon, axis=0, keepdims=True))
        value_total[:, window] += dot(probs.astype(bf16), grad_part)
        probs_grad = dot_right(values[:, window], grad_part)
        middle = jnp.sum(probs * probs_grad, axis=0, keepdims=True)
        scores_grad = (probs * (probs_grad - middle)).astype(bf16)
        key_total[:, window] += dot(scores_grad, query_part)
        query_total[:, window] += dot_left(scores_grad, key_part)

    def raw_grad(part, total):
        turned = total[...] * factor
        weighted = turned * sin_ref[...]
        grad = turned * cos_ref[...] + partner(weighted, first_half, quarter)
        raw = raw_ref[:, part * width : (part + 1) * width]
        scale = lax.rsqrt(two_terms(raw * raw, summing) * (1.0 / head_size) + epsilon)
        scale = two_terms(scale, spreading)
        normal = raw * scale
        if keep:
            sums_ref[0, 2 + part : 3 + part] = jnp.sum(grad * normal, axis=0, keepdims=True)
        grad = grad * gain_ref[part : part + 1]
        mean = two_terms(two_terms(grad * normal, summing) * (1.0 / head_size), spreading)
        return (scale * (grad - normal * mean)).astype(bf16)

    def arrived(part):
        @pl.when(pl.program_id(0) == 0)
        def _():
            fetch(part).wait()

    parts = [raw_grad(0, query_total), raw_grad(1, key_total), value_total[...].astype(bf16)]
    grad = None
    for part in range(3):
        arrived(part)
        if keep:
            qkv_grad_ref[:, part * width : (part + 1) * width] = parts[part]
        term = dot_right(parts[part], whole_rows(weight.at[part], places))
        grad = term if grad is None else grad + term
    mod = mod_ref[0]
    flow = x_ref[...].astype(f32)
    inverse = inverse_rms(flow)
    normal = flow * inverse
    scaled = grad * (1.0 + mod[1:2])
    mean = jnp.mean(scaled * normal, axis=-1, keepdims=True)
    flow_grad = middle_grad_ref[...] + (scaled - normal * mean) * inverse
    if keep:
        flow_grad_ref[...] = flow_grad
        sums_ref[0, 0:1] = jnp.sum(grad, axis=0, keepdims=True)
        sums_ref[0, 1:2] = jnp.sum(grad * normal, axis=0, keepdims=True)
    else:
        back_ref[...] = flow_grad.astype(bf16)


def attention_backward(
    raw, value, mixed_grad, middle_grad, x, mod, tables, gains, joined, walked, first, count, keep
):
    cos, sin, summing, spreading = tables
    gain, head_size = gains
    images, unused, width = mod.shape
    patches = x.shape[0] // images
    tokens = count * patches
    heads = width // head_size
    parts, rows, unused = joined.shape
    row = lambda columns: pl.BlockSpec((patches, columns), lambda image: (first + image, 0))
    token = lambda columns: pl.BlockSpec((patches, columns), lambda image: (image, 0))
    fixed = lambda array: pl.BlockSpec(array.shape, lambda image: (0,) * array.ndim)
    out_shapes = [jax.ShapeDtypeStruct((tokens, width), bf16)]
    out_specs = [token(width)]
    if keep:
        out_shapes = [
            jax.ShapeDtypeStruct((tokens, width), f32),
            jax.ShapeDtypeStruct((tokens, 3 * width), bf16),
            jax.ShapeDtypeStruct((count, 4, width), f32),
        ]
        out_specs = [
            token(width),
            token(3 * width),
            pl.BlockSpec((1, 4, width), lambda image: (image, 0, 0)),
        ]
    return pl.pallas_call(
        functools.partial(attention_backward_kernel, heads, places_of(parts, walked), keep),
        grid=(count,),
        in_specs=[
            row(2 * width),
            row(width),
            row(width),
            row(width),
            row(width),
            pl.BlockSpec((1, 6, width), lambda image: (first + image, 0, 0)),
            row(width),
            row(width),
            fixed(gain),
            fixed(summing),
            fixed(spreading),
            pl.BlockSpec(memory_space=pl.ANY),
        ],
        out_specs=out_specs,
        out_shape=out_shapes,
        scratch_shapes=[
            pltpu.VMEM((3, parts, rows, width), bf16),
            pltpu.VMEM((patches, width), f32),
            pltpu.VMEM((patches, width), f32),
            pltpu.VMEM((patches, width), f32),
            pltpu.SemaphoreType.DMA((3,)),
        ],
        compiler_params=params(),
        cost_estimate=cost(
            2 * tokens * width * (3 * width + 5 * patches),
            6 * width * width + tokens * width * 20,
        ),
    )(raw, value, mixed_grad, middle_grad, x, mod, cos, sin, gain, summing, spreading, joined)


def down_grad(mlp_grads, act, parts, walked):
    tokens, hidden = act.shape
    width = mlp_grads[0].shape[1]
    step = hidden // parts

    def body(act_ref, *refs):
        refs[-1][0] = dot_left(act_ref[...], stacked(refs[:-1])).astype(bf16)

    return pl.pallas_call(
        body,
        grid=(parts,),
        in_specs=[pl.BlockSpec((tokens, step), lambda i: (0, i))] + whole_specs(mlp_grads),
        out_specs=pl.BlockSpec((1, step, width), lambda i: (part_place(i, parts, walked), 0, 0)),
        out_shape=jax.ShapeDtypeStruct((parts, step, width), bf16),
        compiler_params=params(),
        cost_estimate=cost(2 * tokens * width * hidden, 2 * width * hidden),
    )(act, *mlp_grads)


def matrix_grad_kernel(places, counts, *refs):
    pairs = len(counts)
    inputs, grads, out_ref = refs[:pairs], refs[pairs : 2 * pairs], refs[2 * pairs]
    rows = out_ref.shape[1]
    step = pl.program_id(0)
    first = 0
    for index in range(pairs):

        @pl.when(jnp.logical_and(step >= first, step < first + counts[index]))
        def _(index=index):
            product = dot_left(inputs[index][...], grads[index][...]).astype(bf16)
            for part, place in enumerate(places):
                out_ref[place] = product[part * rows : (part + 1) * rows]

        first += counts[index]


def matrix_grad(inputs, grads, step, parts, walked):
    tokens, width = inputs[0].shape
    counts = [grad.shape[1] // step for grad in grads]
    columns = sum(counts) * step
    rows = width // parts
    firsts = [sum(counts[:index]) for index in range(len(counts))]

    def grad_spec(first, count):
        return pl.BlockSpec((tokens, step), lambda i: (0, jnp.clip(i - first, 0, count - 1)))

    return pl.pallas_call(
        functools.partial(matrix_grad_kernel, places_of(parts, walked), counts),
        grid=(sum(counts),),
        in_specs=[pl.BlockSpec((tokens, width), lambda i: (0, 0))] * len(inputs)
        + [grad_spec(first, count) for first, count in zip(firsts, counts)],
        out_specs=pl.BlockSpec((parts, rows, step), lambda i: (0, 0, i)),
        out_shape=jax.ShapeDtypeStruct((parts, rows, columns), bf16),
        compiler_params=params(),
        cost_estimate=cost(2 * tokens * width * columns, 2 * width * columns),
    )(*inputs, *grads)


def walk_of(count):
    chips = count // 2
    order = [chip for chip in range(chips) if chip % 2 == 0]
    order += [chip for chip in reversed(range(chips)) if chip % 2 == 1]
    return [2 * chip + core for chip in order for core in (0, 1)]


def from_walk(rows, count):
    blocks = rows.reshape(count // 2, -1, rows.shape[-1])
    places = places_of(count // 2, True)
    return jnp.concatenate([blocks[place] for place in places], axis=0)


def to_walk(rows, count):
    blocks = rows.reshape(count // 2, -1, rows.shape[-1])
    return jnp.concatenate([blocks[device // 2] for device in walk_of(count)[::2]], axis=0)


def gather_walk(rows, count):
    return lax.all_gather(rows, "dp", axis=0, tiled=True, axis_index_groups=[walk_of(count)])


def scatter_walk(rows, count):
    part = lax.psum_scatter(
        rows, "dp", scatter_dimension=0, tiled=True, axis_index_groups=[walk_of(count)]
    )
    return lax.optimization_barrier(part)


def as_parts(rows, count, unit):
    each = rows.shape[0] // (count // 2)
    if each % unit == 0:
        return rows.reshape(count // 2, each, rows.shape[1]), True
    whole = from_walk(rows, count)
    return whole[None], False


def swapped(block, bit, count):
    return lax.ppermute(block, "dp", [(device, device ^ bit) for device in range(count)])


def gather_small(block, count):
    me = lax.axis_index("dp")
    block = block[None]
    bit = 1
    while bit < count:
        other = swapped(block, bit, count)
        low = (me & bit) == 0
        block = jnp.concatenate(
            [jnp.where(low, block, other), jnp.where(low, other, block)], axis=0
        )
        bit *= 2
    return block


def scatter_small(blocks, count):
    me = lax.axis_index("dp")
    bit = 1
    while bit < count:
        pairs = blocks.reshape(blocks.shape[0] // 2, 2, *blocks.shape[1:])
        mine = jnp.where((me & bit) == 0, 0, 1)
        give = lax.dynamic_index_in_dim(pairs, 1 - mine, 1, keepdims=False)
        keep = lax.dynamic_index_in_dim(pairs, mine, 1, keepdims=False)
        blocks = keep + swapped(give, bit, count)
        bit *= 2
    return blocks[0]


def time_features(timestep_ids, width):
    half_width = width // 2
    frequency = jnp.exp(-math.log(10000.0) * jnp.arange(half_width, dtype=f32) / half_width)
    angle_rows = timestep_ids.astype(f32)[:, None] * frequency[None, :]
    return jnp.concatenate([jnp.cos(angle_rows), jnp.sin(angle_rows)], axis=-1)


def rotation_tables(positions, width, head_size):
    heads = width // head_size
    quarter = head_size // 4
    frequency = jnp.exp(-math.log(10000.0) * jnp.arange(quarter, dtype=f32) / quarter)
    places = positions.reshape(-1, 1)
    row_angle = (places // GRID).astype(f32) * frequency
    col_angle = (places % GRID).astype(f32) * frequency
    row_cos, row_sin = jnp.cos(row_angle), jnp.sin(row_angle)
    col_cos, col_sin = jnp.cos(col_angle), jnp.sin(col_angle)
    cos = jnp.concatenate([row_cos, row_cos, col_cos, col_cos], axis=1)
    sin = jnp.concatenate([-row_sin, row_sin, -col_sin, col_sin], axis=1)
    head = jnp.arange(width) // head_size
    summing = (head[:, None] == jnp.arange(LANES)[None, :]).astype(bf16)
    return jnp.tile(cos, (1, heads)), jnp.tile(sin, (1, heads)), summing, summing.T


def per_device(
    tokens,
    cotangent,
    labels,
    timesteps,
    positions,
    label_table,
    ada_weight,
    qkv_weight,
    out_weight,
    gate_weight,
    up_weight,
    down_weight,
    q_gain,
    k_gain,
):
    first_section = lax.axis_index("section") == 0
    count = lax.axis_size("dp")
    me = lax.axis_index("dp")
    images, patches, width = tokens.shape
    hidden = gate_weight.shape[2]
    head_size = q_gain.shape[1]
    heads = width // head_size
    rows = ada_weight.shape[1]
    classes = label_table.shape[0]

    joined = gather_walk(
        jnp.concatenate([qkv_weight[0], out_weight[0], gate_weight[0], up_weight[0]], axis=1),
        count,
    )

    ids = gather_small(jnp.stack([labels, timesteps]), count)
    all_labels = ids[:, 0].reshape(-1)
    all_times = ids[:, 1].reshape(-1)
    label_hot = all_labels[:, None] == jnp.arange(classes, dtype=jnp.int32)[None, :]
    condition = dot(label_hot.astype(bf16), label_table) + time_features(all_times, width)
    sigma_cond = jax.nn.sigmoid(condition)
    silu_cond = (condition * sigma_cond).astype(bf16)
    silu_rows = lax.dynamic_slice_in_dim(silu_cond, me * rows, rows, 1)
    mod_part = dot(silu_rows, ada_weight[0])
    mod = scatter_small(mod_part.reshape(count, images, -1), count).reshape(images, 6, width)
    tables = rotation_tables(positions, width, head_size)
    flat = tokens.reshape(images * patches, width)
    own = jnp.where(first_section, flat, jnp.zeros_like(flat))

    down, joined, mod, own, tables = lax.optimization_barrier(
        (down_weight[0], joined, mod, own, tables)
    )
    down = gather_walk(down, count)
    joined, walked = as_parts(joined, count, 16)
    down, down_walked = as_parts(down, count, LANES)
    if not down_walked:
        down = down.reshape(hidden // 384, 384, width)
    gains = (jnp.tile(jnp.concatenate([q_gain, k_gain]), (1, heads)), head_size)

    cot = cotangent[0].reshape(images * patches, width)
    middle, normed_two = attention_forward(
        flat, None, mod, tables, gains, joined, walked, 0, images
    )
    (act,) = gate_up(normed_two, joined, hidden, walked, False)
    received = []
    for image in range(images):
        (early,) = down_projection(act, down, middle, mod, down_walked, image, 1, False)
        received.append(lax.ppermute(early, "section", [(0, 1)]))
    late_cot, unused = lax.optimization_barrier((cot, early))
    mlp_grads = [mlp_gradient(late_cot, [], mod, 0, images)]
    act_grad = act_backward(mlp_grads, down, hidden, down_walked)
    kept = None
    for image in range(images):
        kept = attention_forward(
            own, received[image], mod, tables, gains, joined, walked, image, 1, kept
        )
    normed, raw, values, attended, branch, middle, normed_two, layer_in = kept
    act, gate, up = gate_up(normed_two, joined, hidden, walked, True)

    middle_grad, mixed_grad = mlp_backward(
        cot, [], None, act_grad, gate, up, joined, middle, None, mod, walked, False
    )
    backs = []
    for image in range(images):
        (early,) = attention_backward(
            raw,
            values,
            mixed_grad,
            middle_grad,
            layer_in,
            mod,
            tables,
            gains,
            joined,
            walked,
            image,
            1,
            False,
        )
        backs.append(lax.ppermute(early, "section", [(1, 0)]))
    late_act, unused = lax.optimization_barrier((act, early))
    result, mlp = down_projection(late_act, down, middle, mod, down_walked, 0, images, True)

    late_cot, unused = lax.optimization_barrier((cot, mlp))
    mlp_grads = [
        mlp_gradient(late_cot, [back], mod, image, 1) for image, back in enumerate(backs)
    ]
    down_term = down_grad(mlp_grads, act, down.shape[0], down_walked)
    down_term, mlp_grads = lax.optimization_barrier((down_term, mlp_grads))
    down_term = down_term.reshape(hidden, width)
    down_part = scatter_walk(down_term if down_walked else to_walk(down_term, count), count)
    act_grad = act_backward(mlp_grads, down, hidden, down_walked)
    middle_grad, mixed_grad, gate_grad, up_grad, branch_grad, mlp_sums = mlp_backward(
        cot, backs, mlp, act_grad, gate, up, joined, middle, branch, mod, walked, True
    )

    def matrix_part(inputs, grads, step, before):
        term = matrix_grad(inputs, grads, step, joined.shape[0], walked).reshape(width, -1)
        term = term if walked else to_walk(term, count)
        term, before = lax.optimization_barrier((term, before))
        return scatter_walk(term, count), before

    gate_up_part, down_part = matrix_part(
        [normed_two, normed_two], [gate_grad, up_grad], hidden // 2, down_part
    )
    flow_grad, qkv_grad, attention_sums = attention_backward(
        raw,
        values,
        mixed_grad,
        middle_grad,
        layer_in,
        mod,
        tables,
        gains,
        joined,
        walked,
        0,
        images,
        True,
    )
    rest_part, gate_up_part = matrix_part(
        [normed, attended], [qkv_grad, branch_grad], width, gate_up_part
    )
    flow_grad = flow_grad.reshape(images, patches, width)
    input_grads = jnp.where(first_section, flow_grad, flow_grad.astype(bf16).astype(f32))

    mod_grad = jnp.concatenate([attention_sums[:, :2], mlp_sums], axis=1).reshape(images, -1)
    head_sums = jnp.sum(attention_sums[:, 2:], axis=0).reshape(2, heads, head_size)
    mod_all = gather_small(mod_grad.astype(bf16), count).reshape(-1, mod_grad.shape[1])
    ada_part = dot_left(silu_rows, mod_all)
    silu_grad = dot_right(mod_all, ada_weight[0])
    silu_grad = silu_grad + lax.ppermute(silu_grad, "section", [(0, 1), (1, 0)])
    silu_all = gather_small(silu_grad, count)
    gain_all = jnp.sum(gather_small(jnp.sum(head_sums, axis=1), count), axis=0)
    silu_all = jnp.swapaxes(silu_all, 0, 1).reshape(condition.shape)
    cond_grad = silu_all * sigma_cond * (1.0 + condition * (1.0 - sigma_cond))
    table_grad = lax.dot_general(
        label_hot.astype(f32),
        cond_grad,
        (((0,), (0,)), ((), ())),
        precision=lax.Precision.HIGHEST,
        preferred_element_type=f32,
    )
    return (
        result.reshape(1, images, patches, width),
        input_grads[None],
        table_grad,
        ada_part[None],
        rest_part[None, :, : 3 * width].astype(f32),
        rest_part[None, :, 3 * width :].astype(f32),
        gate_up_part[None, :, :hidden].astype(f32),
        gate_up_part[None, :, hidden:].astype(f32),
        down_part[None].astype(f32),
        gain_all[None, 0],
        gain_all[None, 1],
    )


def solution(mesh):
    placed = (
        P("dp", None, None),
        P("section", "dp", None, None),
        P("dp"),
        P("dp"),
        P("dp", None),
        P(),
        P("section", "dp", None),
        P("section", "dp", None),
        P("section", "dp", None),
        P("section", "dp", None),
        P("section", "dp", None),
        P("section", "dp", None),
        P("section", None),
        P("section", None),
    )
    return jax.shard_map(
        per_device,
        mesh=mesh,
        in_specs=placed,
        out_specs=(
            P("section", "dp", None, None),
            P("section", "dp", None, None),
            P(),
            P("section", "dp", None),
            P("section", "dp", None),
            P("section", "dp", None),
            P("section", "dp", None),
            P("section", "dp", None),
            P("section", "dp", None),
            P("section", None),
            P("section", None),
        ),
        check_vma=False,
    )
```

time: 714 us -> 591 us (0.83)
  Pallas kernels: 0 us -> 291 us
  matrix products: 228 us -> 7.19 us
  local copies, waits for them, and re-layouts: 107 us -> 15.6 us
  waiting for transfers between devices: 256 us -> 200 us
  other arithmetic: 60.6 us -> 18.8 us
    pallas_call x0 -> x21, Pallas kernels: none -> 291 us  [the longest x3 81.3 us: attention_backward(): pl.pallas_call(functools.partial(attention_backward_kernel, heads, places...]
    dot_general x36 -> x4, matrix products: 224 us -> 2.93 us  [the longest x1 1.72 us: dot_left(): lax.dot_general(left, right, (((0,), (0,)), ((), ())), preferred_element_...]
    unnamed x231 -> x53, local copies, waits for them, and re-layouts: 81.3 us -> 5.2 us
    ppermute x2 -> x4, waiting for transfers between devices: 54 us -> 2.28 us  [the longest x2 2.27 us: per_device(): backs.append(lax.ppermute(early, 'section', [(1, 0)]))]
    all_gather x3 -> x2, waiting for transfers between devices: 96.9 us -> 83.8 us  [gather_walk(): lax.all_gather(rows, 'dp', axis=0, tiled=True, axis_index_groups=[walk_of...]
    concatenate x6 -> x0, local copies, waits for them, and re-layouts: 12 us -> none  [the longest x3 8.09 us: from_walk(): return jnp.concatenate(picked, axis=0)]
    reduce_scatter x3, waiting for transfers between devices: 40.8 us -> 52.5 us  [scatter_walk(): lax.psum_scatter(rows, 'dp', scatter_dimension=0, tiled=True, axis_index_...]
    reduce_sum x14 -> x4, other arithmetic: 10.3 us -> 0.07 us  [the longest x3 0.05 us: per_device(): gain_all = jnp.sum(gather_small(jnp.sum(head_sums, axis=1), count), axis=0)]
  transfers between devices with their start and end apart: 29 -> 30, of which waited for: 23 -> 22; matrix products, arithmetic and copies ran while one was open for 28% -> 5% of each run, Pallas kernels for 0% -> 35%
where the time goes in v3:
time: 591 us; the launch traced here: 583 us
  Pallas kernels  291 us (49%)
  waiting for transfers between devices  200 us (34%)
  starting transfers between devices  36.2 us (6%)
  other arithmetic  18.8 us (3%)
  local copies, waits for them, and re-layouts  15.6 us (3%)
  between operations  14.7 us (2%)
  matrix products  7.19 us (1%)
    all_gather x2, waiting for transfers between devices, gather_walk(): lax.all_gather(rows, 'dp', axis=0, tiled=True, axis_index_groups=[walk_of...  83.8 us
    pallas_call x3, Pallas kernels, attention_backward(): pl.pallas_call(functools.partial(attention_backward_kernel, heads, places...  81.3 us
    ppermute x20, waiting for transfers between devices, swapped(): lax.ppermute(block, 'dp', [(device, device ^ bit) for device in range(cou...  58.7 us
    pallas_call x3, Pallas kernels, attention_forward(): pl.pallas_call(body, grid=(count,), in_specs=[pl.BlockSpec((patches, widt...  54.6 us
    reduce_scatter x3, waiting for transfers between devices, scatter_walk(): lax.psum_scatter(rows, 'dp', scatter_dimension=0, tiled=True, axis_index_...  52.5 us
    pallas_call x2, Pallas kernels, mlp_backward(): pl.pallas_call(body, grid=(count,), in_specs=[whole, block, block, block,...  44.1 us
    ppermute x20, starting transfers between devices, swapped(): lax.ppermute(block, 'dp', [(device, device ^ bit) for device in range(cou...  27.1 us
    pallas_call x2, Pallas kernels, gate_up(): pl.pallas_call(functools.partial(gate_up_kernel, places_of(parts, walked)...  26.8 us
  transfers between devices with their start and end apart: 30, of which 22 were waited for; matrix products, arithmetic and copies ran while one was open for 5% of the time, Pallas kernels for 35%

profile of v3, /device:TPU:0, one launch (start us, length us, event | category | flops | bytes accessed | tf_op | source)
XLA Modules:
  0.0 583.3 jit_solution(12288790468148672801)
XLA Ops:
  7.3 2.7 pad_maximum_fusion
  14.5 2.6 collective-permute-start.1
  17.1 1.6 collective-permute-done.1
  18.7 2.1 collective-permute-start.2
  20.8 1.6 collective-permute-done.2
  22.7 3.0 collective-permute-start.3
  25.7 1.7 collective-permute-done.3
  32.3 1.6 collective-permute-start.5
  34.0 11.1 %collective-permute-done.5 = f32[4,2,6912]{2,1,0:T(2,128)S(1)} collective-permute-done((f32[4,2,6912]{2,1,0:T(2,128)S(1)}, f32[4,2,6912]{2,1,0:T(2,128)S(1)}, u32[]{:S(2)}, u32[]{:S(2)}) %collective-permute-start.5) | collective-permute-done | bytes 221216 | tf_op jit(solution)/shard_map/ppermute | solution.py:791
  45.8 7.3 %collective-permute-done.6 = f32[2,2,6912]{2,1,0:T(2,128)S(1)} collective-permute-done((f32[2,2,6912]{2,1,0:T(2,128)S(1)}, f32[2,2,6912]{2,1,0:T(2,128)S(1)}, u32[]{:S(2)}, u32[]{:S(2)}) %collective-permute-start.6) | collective-permute-done | bytes 110624 | tf_op jit(solution)/shard_map/ppermute | solution.py:791
  53.1 2.6 collective-permute-start.7
  55.8 4.5 collective-permute-done.7
  61.1 83.1 %all-gather.3.cloned.1.call-done = bf16[1152,10752]{1,0:T(8,128)(2,1)} async-done(((bf16[72,10752]{1,0:T(8,128)(2,1)}), bf16[1152,10752]{1,0:T(8,128)(2,1)}) %all-gather.3.cloned.1.call-update) | async-done | bytes 24772624 | tf_op jit(solution)/shard_map/all_gather | solution.py:772
  144.5 1.7 tile.14
  147.1 1.9 copy.102.refs_2_.refs_3_.cos_ref
  149.1 3.1 copy.103.refs_3_.refs_4_.sin_ref
  152.2 24.1 %shard_map.221 = (f32[512,1152]{1,0:T(8,128)}, bf16[512,1152]{1,0:T(8,128)(2,1)}) custom-call(bf16[512,1152]{1,0:T(8,128)(2,1)} %bitcast.123, f32[2,6,1152]{2,1,0:T(8,128)} %reshape_squeeze.7.refs_1_.mod_ref.refs_2_, f32[512,1152]{1,0:T(8,128)} %copy.102.refs_2_.refs_3_.cos_ref, f32[512,1152]{1,0:T(8,128)} %copy.103.refs_3_.refs_4_.sin_ref, ...), custom_call_target="tpu_custom_call" | custom-call | flops 6039797760 | bytes 22413312 | tf_op jit(solution)/shard_map/pallas_call | solution.py:214
  176.3 13.1 %shard_map.222.act_ref = bf16[512,3072]{1,0:T(8,128)(2,1)} custom-call(bf16[512,1152]{1,0:T(8,128)(2,1)} %get-tuple-element.69.normed_ref, bf16[8,144,10752]{2,1,0:T(8,128)(2,1)} %bitcast.88, bf16[8,144,10752]{2,1,0:T(8,128)(2,1)} %bitcast.89), custom_call_target="tpu_custom_call" | custom-call | flops 7247757312 | bytes 17301504 | tf_op jit(solution)/shard_map/pallas_call | solution.py:262
  190.0 7.3 %shard_map.224 = bf16[256,1152]{1,0:T(8,128)(2,1)} custom-call(bf16[512,3072]{1,0:T(8,128)(2,1)} %shard_map.222.act_ref, f32[512,1152]{1,0:T(8,128)} %get-tuple-element.70.middle_ref, f32[2,6,1152]{2,1,0:T(8,128)} %reshape_squeeze.7.refs_1_.mod_ref.refs_2_, bf16[8,384,1152]{2,1,0:T(8,128)(2,1)} %bitcast.103, bf16[8,384,1152]{2,1,0:T(8,128)(2,1)} %bitcast.104), custom_call_target="tpu_custom_call" | custom-call | flops 1811939328 | bytes 9437184 | tf_op jit(solution)/shard_map/pallas_call | solution.py:332
  197.3 3.4 collective-permute-start.9
  200.7 7.3 %shard_map.223 = bf16[256,1152]{1,0:T(8,128)(2,1)} custom-call(bf16[512,3072]{1,0:T(8,128)(2,1)} %shard_map.222.act_ref, f32[512,1152]{1,0:T(8,128)} %get-tuple-element.70.middle_ref, f32[2,6,1152]{2,1,0:T(8,128)} %reshape_squeeze.7.refs_1_.mod_ref.refs_2_, bf16[8,384,1152]{2,1,0:T(8,128)(2,1)} %bitcast.105, bf16[8,384,1152]{2,1,0:T(8,128)(2,1)} %bitcast.106), custom_call_target="tpu_custom_call" | custom-call | flops 1811939328 | bytes 9437184 | tf_op jit(solution)/shard_map/pallas_call | solution.py:332
  208.1 1.3 collective-permute-start.8
  209.4 2.5 shard_map.228.refs_0_
  211.9 8.5 %shard_map.229.act_grad_ref = bf16[512,3072]{1,0:T(8,128)(2,1)} custom-call(bf16[512,1152]{1,0:T(8,128)(2,1)} %shard_map.228.refs_0_, bf16[8,384,1152]{2,1,0:T(8,128)(2,1)} %bitcast.107, bf16[8,384,1152]{2,1,0:T(8,128)(2,1)} %bitcast.108), custom_call_target="tpu_custom_call" | custom-call | flops 3623878656 | bytes 9437184 | tf_op jit(solution)/shard_map/pallas_call | solution.py:397
  221.2 15.1 %shard_map.225 = (bf16[512,1152]{1,0:T(8,128)(2,1)}, f32[512,2304]{1,0:T(8,128)}, bf16[512,1152]{1,0:T(8,128)(2,1)}, bf16[512,1152]{1,0:T(8,128)(2,1)}, f32[512,...) custom-call(bf16[256,1152]{1,0:T(8,128)(2,1)} %copy-done.12, ...), custom_call_target="tpu_custom_call" | custom-call | flops 3019898880 | bytes 16515072 | tf_op jit(solution)/shard_map/pallas_call | solution.py:214
  237.1 15.5 %shard_map.226 = (bf16[512,1152]{1,0:T(8,128)(2,1)}, f32[512,2304]{1,0:T(8,128)}, bf16[512,1152]{1,0:T(8,128)(2,1)}, bf16[512,1152]{1,0:T(8,128)(2,1)}, f32[512,...) custom-call(bf16[256,1152]{1,0:T(8,128)(2,1)} %copy-done.11, ...), custom_call_target="tpu_custom_call", output_to_operand_aliasing={{0}: (9, {}), {1}: (10, {}), {2}: (11, {}), {3}: (12, {}), ... | custom-call | flops 3019898880 | bytes 16515072 | tf_op jit(solution)/shard_map/pallas_call | solution.py:214
  252.6 13.8 %shard_map.227 = (bf16[512,3072]{1,0:T(8,128)(2,1)}, bf16[512,3072]{1,0:T(8,128)(2,1)}, bf16[512,3072]{1,0:T(8,128)(2,1)}) custom-call(bf16[512,1152]{1,0:T(8,128)(2,1)} %get-tuple-element.81.normed_ref.refs_0_.refs_1_, bf16[8,144,10752]{2,1,0:T(8,128)(2,1)} %bitcast.92, bf16[8,144,10752]{2,1,0:T(8,128)(2,1)} %bitcast.93), custom_call_target="tpu_custom_call" | custom-call | flops 7247757312 | bytes 23592960 | tf_op jit(solution)/shard_map/pallas_call | solution.py:262
  266.3 20.1 %shard_map.230 = (f32[512,1152]{1,0:T(8,128)}, bf16[512,1152]{1,0:T(8,128)(2,1)}) custom-call(bf16[512,1152]{1,0:T(8,128)(2,1)} %bitcast.114, bf16[512,3072]{1,0:T(8,128)(2,1)} %shard_map.229.act_grad_ref, bf16[512,3072]{1,0:T(8,128)(2,1)} %get-tuple-element.86.gate_ref, bf16[512,3072]{1,0:T(8,128)(2,1)} %get-tuple-element.87.up_ref, ...), custom_call_target="tpu_custom_call" | custom-call | flops 8606711808 | bytes 23592960 | tf_op jit(solution)/shard_map/pallas_call | solution.py:491
  286.4 20.6 %shard_map.231 = bf16[256,1152]{1,0:T(8,128)(2,1)} custom-call(f32[512,2304]{1,0:T(8,128)} %get-tuple-element.83.raw_ref, bf16[512,1152]{1,0:T(8,128)(2,1)} %get-tuple-element.84.value_ref, bf16[512,1152]{1,0:T(8,128)(2,1)} %get-tuple-element.89.mixed_grad_ref, f32[512,1152]{1,0:T(8,128)} %get-tuple-element.90.middle_grad_ref, ...), custom_call_target="tpu_custom_call" | custom-call | flops 2793406464 | bytes 13860864 | tf_op jit(solution)/shard_map/pallas_call | solution.py:661
  308.3 20.3 %shard_map.233 = bf16[256,1152]{1,0:T(8,128)(2,1)} custom-call(f32[512,2304]{1,0:T(8,128)} %get-tuple-element.83.raw_ref, bf16[512,1152]{1,0:T(8,128)(2,1)} %get-tuple-element.84.value_ref, bf16[512,1152]{1,0:T(8,128)(2,1)} %get-tuple-element.89.mixed_grad_ref, f32[512,1152]{1,0:T(8,128)} %get-tuple-element.90.middle_grad_ref, ...), custom_call_target="tpu_custom_call" | custom-call | flops 2793406464 | bytes 13860864 | tf_op jit(solution)/shard_map/pallas_call | solution.py:661
  330.0 10.7 %shard_map.232 = (bf16[512,1152]{1,0:T(8,128)(2,1)}, f32[512,1152]{1,0:T(8,128)}) custom-call(bf16[512,3072]{1,0:T(8,128)(2,1)} %get-tuple-element.92.act_ref, f32[512,1152]{1,0:T(8,128)} %get-tuple-element.88.middle_ref, f32[2,6,1152]{2,1,0:T(8,128)} %reshape_squeeze.7.refs_1_.mod_ref.refs_2_, bf16[8,384,1152]{2,1,0:T(8,128)(2,1)} %bitcast.109, ...), custom_call_target="tpu_custom_call" | custom-call | flops 3623878656 | bytes 11796480 | tf_op jit(solution)/shard_map/pallas_call | solution.py:332
  341.5 2.3 shard_map.235.refs_1_
  343.7 2.3 collective-permute-done.10.refs_0_
  346.8 2.3 shard_map.234.refs_0_
  349.1 9.9 %shard_map.236 = bf16[8,384,1152]{2,1,0:T(8,128)(2,1)} custom-call(bf16[512,3072]{1,0:T(8,128)(2,1)} %get-tuple-element.92.act_ref, bf16[256,1152]{1,0:T(8,128)(2,1)} %shard_map.234.refs_0_, bf16[256,1152]{1,0:T(8,128)(2,1)} %shard_map.235.refs_1_), custom_call_target="tpu_custom_call" | custom-call | flops 3623878656 | bytes 7077888 | tf_op jit(solution)/shard_map/pallas_call | solution.py:703
  359.1 8.4 %shard_map.237.act_grad_ref = bf16[512,3072]{1,0:T(8,128)(2,1)} custom-call(bf16[256,1152]{1,0:T(8,128)(2,1)} %shard_map.234.refs_0_, bf16[256,1152]{1,0:T(8,128)(2,1)} %shard_map.235.refs_1_, bf16[8,384,1152]{2,1,0:T(8,128)(2,1)} %bitcast.111, bf16[8,384,1152]{2,1,0:T(8,128)(2,1)} %bitcast.112), custom_call_target="tpu_custom_call" | custom-call | flops 3623878656 | bytes 9437184 | tf_op jit(solution)/shard_map/pallas_call | solution.py:397
  367.5 24.0 %shard_map.238 = (f32[512,1152]{1,0:T(8,128)}, bf16[512,1152]{1,0:T(8,128)(2,1)}, bf16[512,3072]{1,0:T(8,128)(2,1)}, bf16[512,3072]{1,0:T(8,128)(2,1)}, bf16[512...) custom-call(bf16[512,1152]{1,0:T(8,128)(2,1)} %bitcast.117, bf16[512,3072]{1,0:T(8,128)(2,1)} %shard_map.237.act_grad_ref, ...), custom_call_target="tpu_custom_call" | custom-call | flops 8606711808 | bytes 23592960 | tf_op jit(solution)/shard_map/pallas_call | solution.py:491
  391.5 13.6 %shard_map.241 = bf16[8,144,6144]{2,1,0:T(8,128)(2,1)} custom-call(bf16[512,1152]{1,0:T(8,128)(2,1)} %get-tuple-element.81.normed_ref.refs_0_.refs_1_, bf16[512,1152]{1,0:T(8,128)(2,1)} %get-tuple-element.81.normed_ref.refs_0_.refs_1_, bf16[512,3072]{1,0:T(8,128)(2,1)} %get-tuple-element.108.refs_2_, bf16[512,3072]{1,0:T(8,128)(2,1)} %get-tuple-element.109.refs_3_), custom_call_target="tpu_custom_call" | custom-call | flops 7247757312 | bytes 14155776 | tf_op jit(solution)/shard_map/pallas_call | solution.py:741
  405.1 8.0 %reduce-scatter.4.cloned.1.call-done = bf16[192,1152]{1,0:T(8,128)(2,1)} async-done(((bf16[3072,1152]{1,0:T(8,128)(2,1)}), bf16[192,1152]{1,0:T(8,128)(2,1)}) %reduce-scatter.4.cloned.1.call-update) | async-done | bytes 442384 | tf_op jit(solution)/shard_map/reduce_scatter | solution.py:776
  413.2 40.4 %shard_map.239 = (f32[512,1152]{1,0:T(8,128)}, bf16[512,3456]{1,0:T(8,128)(2,1)}, f32[2,4,1152]{2,1,0:T(4,128)}) custom-call(f32[512,2304]{1,0:T(8,128)} %get-tuple-element.83.raw_ref, bf16[512,1152]{1,0:T(8,128)(2,1)} %get-tuple-element.84.value_ref, bf16[512,1152]{1,0:T(8,128)(2,1)} %get-tuple-element.99.mixed_grad_ref, ...), custom_call_target="tpu_custom_call" | custom-call | flops 5586812928 | bytes 19759104 | tf_op jit(solution)/shard_map/pallas_call | solution.py:661
  453.6 11.5 %shard_map.240 = bf16[8,144,4608]{2,1,0:T(8,128)(2,1)} custom-call(bf16[512,1152]{1,0:T(8,128)(2,1)} %get-tuple-element.104.refs_0_, bf16[512,1152]{1,0:T(8,128)(2,1)} %get-tuple-element.105.refs_1_, bf16[512,3456]{1,0:T(8,128)(2,1)} %get-tuple-element.106.refs_2_, bf16[512,1152]{1,0:T(8,128)(2,1)} %get-tuple-element.107.refs_3_), custom_call_target="tpu_custom_call" | custom-call | flops 5435817984 | bytes 10616832 | tf_op jit(solution)/shard_map/pallas_call | solution.py:741
  465.1 30.8 %reduce-scatter.6.cloned.1.call-done = bf16[72,6144]{1,0:T(8,128)(2,1)} async-done(((bf16[1152,6144]{1,0:T(8,128)(2,1)}), bf16[72,6144]{1,0:T(8,128)(2,1)}) %reduce-scatter.6.cloned.1.call-update) | async-done | bytes 884752 | tf_op jit(solution)/shard_map/reduce_scatter | solution.py:776
  497.6 1.6 convert_select_fusion
  499.8 1.3 collective-permute-start.13
  501.1 2.9 collective-permute-done.13
  504.3 1.6 collective-permute-start.14
  505.8 1.4 collective-permute-start.22
  507.2 3.0 collective-permute-done.14
  510.8 2.4 collective-permute-start.15
  513.3 1.6 collective-permute-start.23
  514.9 10.4 %collective-permute-done.15 = bf16[8,2,6912]{2,1,0:T(2,128)(2,1)S(1)} collective-permute-done((bf16[8,2,6912]{2,1,0:T(2,128)(2,1)S(1)}, bf16[8,2,6912]{2,1,0:T(2,128)(2,1)S(1)}, u32[]{:S(2)}, u32[]{:S(2)}) %collective-permute-start.15) | collective-permute-done | bytes 221216 | tf_op jit(solution)/shard_map/ppermute | solution.py:791
  526.9 1.5 collective-permute-start.16
  528.5 2.3 collective-permute-done.16
  531.9 2.5 collective-permute-start.18
  536.8 1.4 collective-permute-start.19
  538.7 3.2 collective-permute-done.19
  542.0 1.6 collective-permute-start.20
  543.5 1.7 convolution_bitcast_fusion
  545.2 6.9 %collective-permute-done.20 = f32[8,32,72]{2,1,0:T(8,128)S(1)} collective-permute-done((f32[8,32,72]{2,1,0:T(8,128)S(1)}, f32[8,32,72]{2,1,0:T(8,128)S(1)}, u32[]{:S(2)}, u32[]{:S(2)}) %collective-permute-start.20) | collective-permute-done | bytes 73760 | tf_op jit(solution)/shard_map/ppermute | solution.py:791
  552.5 4.3 fusion.8
  557.8 1.4 bitcast_convert_fusion.1
  559.1 13.7 %reduce-scatter.8.cloned.1.call-done = bf16[72,4608]{1,0:T(8,128)(2,1)} async-done(((bf16[1152,4608]{1,0:T(8,128)(2,1)}), bf16[72,4608]{1,0:T(8,128)(2,1)}) %reduce-scatter.8.cloned.1.call-update) | async-done | bytes 663568 | tf_op jit(solution)/shard_map/reduce_scatter | solution.py:776
  572.9 1.7 fusion.7
  574.5 2.0 fusion.6
  (165 shorter events, 29.0 us)
Async XLA Ops:
  7.2 21.1 %copy-start = (bf16[1001,1152]{1,0:T(8,128)(2,1)S(1)}, bf16[1001,1152]{1,0:T(8,128)(2,1)}, u32[]{:S(2)}) copy-start(bf16[1001,1152]{1,0:T(8,128)(2,1)} %param.19) | copy-start | bytes 6918916
  7.2 2.9 copy-start.21
  7.2 2.9 copy-start.22
  7.2 136.9 %all-gather.3.cloned.1.call-start = ((), (), s32[]{:S(2)}) async-start(), calls=%async_computation.3 | async-start | bytes 26320896 | tf_op jit(solution)/shard_map/all_gather | solution.py:772
  7.3 3.9 copy-start.20
  7.3 5.2 copy-start.2
  10.0 180.0 %all-gather.5.cloned.1.call-start = ((), (), s32[]{:S(2)}) async-start(), calls=%async_computation.4 | async-start | bytes 7520256 | tf_op jit(solution)/shard_map/all_gather | solution.py:772
  10.7 3.0 collective-permute-start
  13.7 15.8 %copy-start.3 = (bf16[1,72,6912]{2,1,0:T(8,128)(2,1)S(1)}, bf16[1,72,6912]{2,1,0:T(8,128)(2,1)}, u32[]{:S(2)}) copy-start(bf16[1,72,6912]{2,1,0:T(8,128)(2,1)} %param.20) | copy-start | bytes 2985988
  14.5 4.1 collective-permute-start.1
  18.7 3.7 collective-permute-start.2
  22.7 4.7 collective-permute-start.3
  27.7 2.1 copy-start.18
  28.8 3.2 copy-start.9
  28.9 0.6 copy-start.14
  29.8 15.5 %copy-start.23 = (f32[18]{0:T(128)S(1)}, f32[18]{0:T(128)}, u32[]{:S(2)}) copy-start(f32[18]{0:T(128)} %multiply_exponential_fusion.1) | copy-start | bytes 220
  29.9 2.1 collective-permute-start.4
  32.3 12.8 %collective-permute-start.5 = (f32[4,2,6912]{2,1,0:T(2,128)S(1)}, f32[4,2,6912]{2,1,0:T(2,128)S(1)}, u32[]{:S(2)}, u32[]{:S(2)}) collective-permute-start(f32[4,2,6912]{2,1,0:T(2,128)S(1)} %dynamic-slice_bitcast_fusion.1), channel_id=1, source_target_pairs={{0,2},{1,3},{2,0},{3,1},{4,6},{5,7},{6,4},{7,5},{8,10},{9,11},{10,... | collective-permute-start | bytes 663560 | tf_op jit(solution)/shard_map/ppermute | solution.py:791
  45.3 7.8 %collective-permute-start.6 = (f32[2,2,6912]{2,1,0:T(2,128)S(1)}, f32[2,2,6912]{2,1,0:T(2,128)S(1)}, u32[]{:S(2)}, u32[]{:S(2)}) collective-permute-start(f32[2,2,6912]{2,1,0:T(2,128)S(1)} %dynamic-slice_bitcast_fusion.2), channel_id=1, source_target_pairs={{0,4},{1,5},{2,6},{3,7},{4,0},{5,1},{6,2},{7,3},{8,12},{9,13},{10,... | collective-permute-start | bytes 331784 | tf_op jit(solution)/shard_map/ppermute | solution.py:791
  53.1 7.2 %collective-permute-start.7 = (f32[1,2,6912]{2,1,0:T(2,128)S(1)}, f32[1,2,6912]{2,1,0:T(2,128)S(1)}, u32[]{:S(2)}, u32[]{:S(2)}) collective-permute-start(f32[1,2,6912]{2,1,0:T(2,128)S(1)} %constant_dynamic-slice_fusion), channel_id=1, source_target_pairs={{0,8},{1,9},{2,10},{3,11},{4,12},{5,13},{6,14},{7,15},{8,0},{9,1},... | collective-permute-start | bytes 165896 | tf_op jit(solution)/shard_map/ppermute | solution.py:791
  144.2 2.2 copy-start.24
  144.2 2.3 copy-start.25
  146.2 266.9 %reduce-scatter.4.cloned.1.call-start = ((), (), s32[]{:S(2)}) async-start(), calls=%async_computation.5 | async-start | bytes 7520256 | tf_op jit(solution)/shard_map/reduce_scatter | solution.py:776
  197.3 23.1 %collective-permute-start.9 = (bf16[256,1152]{1,0:T(8,128)(2,1)}, bf16[256,1152]{1,0:T(8,128)(2,1)S(1)}, u32[]{:S(2)}, u32[]{:S(2)}) collective-permute-start(bf16[256,1152]{1,0:T(8,128)(2,1)} %shard_map.224), channel_id=1, source_target_pairs={{0,16},{1,17},{2,18},{3,19},{4,20},{5,21},{6,22},{7,23},{8,24},{9,... | collective-permute-start | bytes 1769480 | tf_op jit(solution)/shard_map/ppermute | solution.py:907
  208.1 28.2 %collective-permute-start.8 = (bf16[256,1152]{1,0:T(8,128)(2,1)}, bf16[256,1152]{1,0:T(8,128)(2,1)S(1)}, u32[]{:S(2)}, u32[]{:S(2)}) collective-permute-start(bf16[256,1152]{1,0:T(8,128)(2,1)} %shard_map.223), channel_id=1, source_target_pairs={{0,16},{1,17},{2,18},{3,19},{4,20},{5,21},{6,22},{7,23},{8,24},{9,... | collective-permute-start | bytes 1769480 | tf_op jit(solution)/shard_map/ppermute | solution.py:907
  220.4 0.8 copy-start.12
  236.3 0.8 copy-start.11
  307.0 33.6 %collective-permute-start.11 = (bf16[256,1152]{1,0:T(8,128)(2,1)}, bf16[256,1152]{1,0:T(8,128)(2,1)S(1)}, u32[]{:S(2)}, u32[]{:S(2)}) collective-permute-start(bf16[256,1152]{1,0:T(8,128)(2,1)} %shard_map.231), channel_id=1, source_target_pairs={{16,0},{17,1},{18,2},{19,3},{20,4},{21,5},{22,6},{23,7},{24,8},{25... | collective-permute-start | bytes 1769480 | tf_op jit(solution)/shard_map/ppermute | solution.py:939
  328.7 17.3 %collective-permute-start.10 = (bf16[256,1152]{1,0:T(8,128)(2,1)}, bf16[256,1152]{1,0:T(8,128)(2,1)S(1)}, u32[]{:S(2)}, u32[]{:S(2)}) collective-permute-start(bf16[256,1152]{1,0:T(8,128)(2,1)} %shard_map.233), channel_id=1, source_target_pairs={{16,0},{17,1},{18,2},{19,3},{20,4},{21,5},{22,6},{23,7},{24,8},{25... | collective-permute-start | bytes 1769480 | tf_op jit(solution)/shard_map/ppermute | solution.py:939
  340.6 0.8 copy-start.6
  346.0 0.8 copy-start.7
  359.1 136.9 %reduce-scatter.6.cloned.1.call-start = ((), (), s32[]{:S(2)}) async-start(), calls=%async_computation.6 | async-start | bytes 15040512 | tf_op jit(solution)/shard_map/reduce_scatter | solution.py:776
  413.1 159.7 %reduce-scatter.8.cloned.1.call-start = ((), (), s32[]{:S(2)}) async-start(), calls=%async_computation.7 | async-start | bytes 11280384 | tf_op jit(solution)/shard_map/reduce_scatter | solution.py:776
  495.9 0.8 copy-start.17
  495.9 0.8 copy-start.16
  495.9 1.7 copy-start.5
  496.8 2.8 collective-permute-start.12
  499.2 27.4 %copy-start.4 = (bf16[1,72,6912]{2,1,0:T(8,128)(2,1)S(1)}, bf16[1,72,6912]{2,1,0:T(8,128)(2,1)}, u32[]{:S(2)}) copy-start(bf16[1,72,6912]{2,1,0:T(8,128)(2,1)} %param.20) | copy-start | bytes 2985988
  499.3 1.8 collective-permute-start.21
  499.8 4.2 collective-permute-start.13
  504.3 6.0 %collective-permute-start.14 = (bf16[4,2,6912]{2,1,0:T(2,128)(2,1)S(1)}, bf16[4,2,6912]{2,1,0:T(2,128)(2,1)S(1)}, u32[]{:S(2)}, u32[]{:S(2)}) collective-permute-start(bf16[4,2,6912]{2,1,0:T(2,128)(2,1)S(1)} %pad_maximum_fusion.6), channel_id=1, source_target_pairs={{0,4},{1,5},{2,6},{3,7},{4,0},{5,1},{6,2},{7,3},{8,12},{9,13},{10,... | collective-permute-start | bytes 331784 | tf_op jit(solution)/shard_map/ppermute | solution.py:791
  505.8 7.4 %collective-permute-start.22 = (f32[2,2,72]{2,1,0:T(2,128)S(1)}, f32[2,2,72]{2,1,0:T(2,128)S(1)}, u32[]{:S(2)}, u32[]{:S(2)}) collective-permute-start(f32[2,2,72]{2,1,0:T(2,128)S(1)} %pad_maximum_fusion.13), channel_id=1, source_target_pairs={{0,2},{1,3},{2,0},{3,1},{4,6},{5,7},{6,4},{7,5},{8,10},{9,11},{10,... | collective-permute-start | bytes 3464 | tf_op jit(solution)/shard_map/ppermute | solution.py:791
  510.8 14.5 %collective-permute-start.15 = (bf16[8,2,6912]{2,1,0:T(2,128)(2,1)S(1)}, bf16[8,2,6912]{2,1,0:T(2,128)(2,1)S(1)}, u32[]{:S(2)}, u32[]{:S(2)}) collective-permute-start(bf16[8,2,6912]{2,1,0:T(2,128)(2,1)S(1)} %pad_maximum_fusion.2), channel_id=1, source_target_pairs={{0,8},{1,9},{2,10},{3,11},{4,12},{5,13},{6,14},{7,15},{8,0},{9,1},... | collective-permute-start | bytes 663560 | tf_op jit(solution)/shard_map/ppermute | solution.py:791
  513.3 30.2 %copy-start.15 = (bf16[32,72]{1,0:T(8,128)(2,1)S(1)}, bf16[32,72]{1,0:T(8,128)(2,1)}, u32[]{:S(2)}) copy-start(bf16[32,72]{1,0:T(8,128)(2,1)} %copy-done.14) | copy-start | bytes 13828
  513.3 15.2 %collective-permute-start.23 = (f32[4,2,72]{2,1,0:T(2,128)S(1)}, f32[4,2,72]{2,1,0:T(2,128)S(1)}, u32[]{:S(2)}, u32[]{:S(2)}) collective-permute-start(f32[4,2,72]{2,1,0:T(2,128)S(1)} %pad_maximum_fusion.12), channel_id=1, source_target_pairs={{0,4},{1,5},{2,6},{3,7},{4,0},{5,1},{6,2},{7,3},{8,12},{9,13},{10,... | collective-permute-start | bytes 6920 | tf_op jit(solution)/shard_map/ppermute | solution.py:791
  526.9 3.8 collective-permute-start.16
  530.7 1.2 collective-permute-start.17
  530.7 4.8 collective-permute-start.24
  531.9 4.8 collective-permute-start.18
  536.8 5.1 collective-permute-start.19
  541.9 10.6 %copy-start.10 = (f32[32,1152]{1,0:T(8,128)S(1)}, f32[32,1152]{1,0:T(8,128)}, u32[]{:S(2)}) copy-start(f32[32,1152]{1,0:T(8,128)} %copy-done.9) | copy-start | bytes 442372
  541.9 10.6 %copy-start.19 = (s32[32]{0:T(128)S(1)}, s32[32]{0:T(128)}, u32[]{:S(2)}) copy-start(s32[32]{0:T(128)} %copy-done.18) | copy-start | bytes 388
  542.0 10.2 %collective-permute-start.20 = (f32[8,32,72]{2,1,0:T(8,128)S(1)}, f32[8,32,72]{2,1,0:T(8,128)S(1)}, u32[]{:S(2)}, u32[]{:S(2)}) collective-permute-start(f32[8,32,72]{2,1,0:T(8,128)S(1)} %pad_maximum_fusion.5), channel_id=1, source_target_pairs={{0,8},{1,9},{2,10},{3,11},{4,12},{5,13},{6,14},{7,15},{8,0},{9,1},... | collective-permute-start | bytes 221192 | tf_op jit(solution)/shard_map/ppermute | solution.py:791
  552.5 4.3 copy-start.13
  552.5 5.2 copy-start.8
  556.8 19.8 %copy-start.1 = (bf16[1001,1152]{1,0:T(8,128)(2,1)S(1)}, bf16[1001,1152]{1,0:T(8,128)(2,1)}, u32[]{:S(2)}) copy-start(bf16[1001,1152]{1,0:T(8,128)(2,1)} %param.19) | copy-start | bytes 6918916
Sparse Core Ops, SparseCore 0:
  10.2 133.8 all-gather.2
  146.3 43.6 all-gather.4
  359.2 53.8 reduce-scatter.3
  415.4 80.4 reduce-scatter.5
  498.2 74.6 reduce-scatter.7

commit v4 on v3

--- a/solution.py
+++ b/solution.py
@@ -52,10 +52,10 @@
     return [part_place(index, parts, walked) for index in range(parts)]
 
 
-def two_terms(left, right):
-    high = left.astype(bf16)
-    low = (left - high.astype(f32)).astype(bf16)
-    return dot(high, right) + dot(low, right)
+def two_terms(values):
+    high = values.astype(bf16)
+    low = (values - high.astype(f32)).astype(bf16)
+    return jnp.concatenate([high, low], axis=1)
 
 
 def inverse_rms(values):
@@ -74,10 +74,17 @@
     return lane % (2 * quarter) < quarter
 
 
-def head_window(head, head_size, width):
+def head_groups(heads, head_size):
+    width = heads * head_size
     span = min(2 * LANES, width)
-    start = min(head * head_size // LANES * LANES, width - span)
-    return start, span
+    groups = []
+    for head in range(heads):
+        low, high = head * head_size, (head + 1) * head_size
+        if groups and high <= groups[-1][0] + span:
+            groups[-1][2].append(head)
+        else:
+            groups.append((min(low // LANES * LANES, width - span), span, [head]))
+    return groups
 
 
 def head_mask(head, head_size, start, span):
@@ -86,41 +93,52 @@
     return inside.astype(f32).astype(bf16)
 
 
-def attention_forward_kernel(
-    heads,
-    places,
-    keep,
-    received_ref,
-    x_ref,
-    mod_ref,
-    cos_ref,
-    sin_ref,
-    gain_ref,
-    sum_ref,
-    spread_ref,
-    joined_ref,
-    *rest,
-):
-    if keep:
-        normed_ref, raw_ref, value_ref, attended_ref, branch_ref, middle_ref, normed_two_ref = rest[:7]
-        flow_ref = rest[7]
-        rest = rest[8:]
+def side_by_side(parts):
+    return parts[0] if len(parts) == 1 else jnp.concatenate(parts, axis=1)
+
+
+def one_above_other(parts):
+    return parts[0] if len(parts) == 1 else jnp.concatenate(parts, axis=0)
+
+
+def rotated(raw, part, tables, keep_scale=None):
+    cos_ref, sin_ref, gain_ref, sum_ref, spread_ref, repeat_ref, head_size = tables
+    quarter = head_size // 4
+    squares = dot((raw * raw).astype(bf16), sum_ref[...])
+    scale = lax.rsqrt(squares * (1.0 / head_size) + epsilon)
+    scale = dot(two_terms(scale), spread_ref[...])
+    if keep_scale is not None:
+        keep_scale[part] = scale
+    scaled = raw * scale * gain_ref[part : part + 1]
+    first_half = first_half_mask((1, raw.shape[1]), quarter)
+    cos, sin = dot(cos_ref[...], repeat_ref[...]), dot(sin_ref[...], repeat_ref[...])
+    return (scaled * cos + partner(scaled, first_half, quarter) * sin).astype(bf16)
+
+
+def attention_forward_kernel(heads, places, first, keep, refs):
+    if keep:
+        received_ref, refs = refs[0], refs[1:]
+    x_ref, mod_ref, cos_ref, sin_ref, gain_ref, sum_ref, spread_ref, repeat_ref = refs[:8]
+    query_weight, joined_ref = refs[8:10]
+    refs = refs[10:]
+    patches, width = x_ref.shape
+    if keep:
+        outs, refs = refs[:8], refs[8:]
+        weight, mixed, sems = refs[:3]
+        held, out_sems = refs[3:11], refs[11]
     else:
-        middle_ref, normed_two_ref = rest[:2]
-        rest = rest[2:]
-    weight, mixed, sems = rest
-    width = x_ref.shape[1]
+        middle_ref, normed_two_ref, weight, mixed, sems = refs
     head_size = width // heads
-    quarter = head_size // 4
+    tables = (cos_ref, sin_ref, gain_ref, sum_ref, spread_ref, repeat_ref, head_size)
 
     def fetch(part):
         return pltpu.make_async_copy(
-            joined_ref.at[:, :, pl.ds(part * width, width)], weight.at[part], sems.at[part]
+            joined_ref.at[:, :, pl.ds((part + 1) * width, width)], weight.at[part], sems.at[part]
         )
 
     @pl.when(pl.program_id(0) == 0)
     def _():
-        for part in range(4):
+        for part in range(3):
             fetch(part).start()
 
     def arrived(part):
@@ -128,66 +146,75 @@
         def _():
             fetch(part).wait()
 
+        return whole_rows(weight.at[part], places)
+
+    def put(which):
+        rows = pl.ds(first * patches, patches)
+        return pltpu.make_async_copy(held[which], outs[which].at[rows], out_sems.at[which])
+
     flow = x_ref[...].astype(f32)
     if keep:
         flow = flow + received_ref[...].astype(f32)
-        flow_ref[...] = flow.astype(bf16)
     mod = mod_ref[0]
     normed = (flow * inverse_rms(flow) * (1.0 + mod[1:2]) + mod[0:1]).astype(bf16)
-    if keep:
-        normed_ref[...] = normed
-    summing, spreading = sum_ref[...], spread_ref[...]
-    first_half = first_half_mask((1, width), quarter)
-
-    def prepared(part):
-        arrived(part)
-        raw = dot(normed, whole_rows(weight.at[part], places))
-        if keep:
-            raw_ref[:, part * width : (part + 1) * width] = raw
-        scale = lax.rsqrt(two_terms(raw * raw, summing) * (1.0 / head_size) + epsilon)
-        scaled = raw * two_terms(scale, spreading) * gain_ref[part : part + 1]
-        turned = scaled * cos_ref[...] + partner(scaled, first_half, quarter) * sin_ref[...]
-        return turned.astype(bf16)
-
-    queries = prepared(0)
-    keys = prepared(1)
-    arrived(2)
-    values = dot(normed, whole_rows(weight.at[2], places)).astype(bf16)
-    if keep:
-        value_ref[...] = values
+    raw = dot(normed, whole_rows(query_weight, places))
+    if keep:
+        held[7][...] = flow.astype(bf16)
+        held[0][...] = normed
+        held[1][:, :width] = raw
+        put(7).start()
+        put(0).start()
+    queries = rotated(raw, 0, tables)
+    raw = dot(normed, arrived(0))
+    if keep:
+        held[1][:, width:] = raw
+        put(1).start()
+    keys = rotated(raw, 1, tables)
+    values = dot(normed, arrived(1)).astype(bf16)
+    if keep:
+        held[2][...] = values
+        put(2).start()
     mixed[...] = jnp.zeros_like(mixed)
-    factor = head_size ** (-0.5)
-    for head in range(heads):
-        start, span = head_window(head, head_size, width)
-        mask = head_mask(head, head_size, start, span)
+    factor = head_size ** (-0.5) * math.log2(math.e)
+    for start, span, members in head_groups(heads, head_size):
         window = slice(start, start + span)
-        scores = dot_right(queries[:, window], keys[:, window] * mask)
-        highest = jnp.max(scores, axis=-1, keepdims=True)
-        expon = jnp.exp((scores - highest) * factor)
-        probs = expon * (1.0 / jnp.sum(expon, axis=-1, keepdims=True))
-        mixed[:, window] += dot(probs.astype(bf16), values[:, window] * mask)
+        probs, parts = [], []
+        for head in members:
+            mask = head_mask(head, head_size, start, span)
+            expon = jnp.exp2(dot_right(queries[:, window], keys[:, window] * mask) * factor)
+            total = jnp.sum(expon, axis=-1, keepdims=True)
+            probs.append((expon * (1.0 / total)).astype(bf16))
+            parts.append(values[:, window] * mask)
+        mixed[:, window] += dot(side_by_side(probs), one_above_other(parts))
     attended = mixed[...].astype(bf16)
-    arrived(3)
-    branch = dot(attended, whole_rows(weight.at[3], places))
+    if keep:
+        held[3][...] = attended
+        put(3).start()
+    branch = dot(attended, arrived(2))
     middle = flow + mod[2:3] * branch
-    middle_ref[...] = middle
-    normed_two_ref[...] = (middle * inverse_rms(middle) * (1.0 + mod[4:5]) + mod[3:4]).astype(bf16)
-    if keep:
-        attended_ref[...] = attended
-        branch_ref[...] = branch
-
-
-def attention_forward(x, received, mod, tables, gains, joined, walked, first, count, made=None):
+    normed_two = (middle * inverse_rms(middle) * (1.0 + mod[4:5]) + mod[3:4]).astype(bf16)
+    if keep:
+        for which, value in ((4, branch), (5, middle), (6, normed_two)):
+            held[which][...] = value
+            put(which).start()
+        for which in range(8):
+            put(which).wait()
+    else:
+        middle_ref[...] = middle
+        normed_two_ref[...] = normed_two
+
+
+def attention_forward(x, received, mod, tables, gain, joined, walked, first, count, made=None):
     keep = received is not None
-    cos, sin, summing, spreading = tables
-    gain, head_size = gains
     images, unused, width = mod.shape
     tokens = x.shape[0]
     patches = tokens // images
-    heads = width // head_size
-    places = places_of(joined.shape[0], walked)
+    heads = width // tables[-1]
+    arrays = tables[:-1]
+    parts, rows, unused = joined.shape
     row = lambda columns: pl.BlockSpec((patches, columns), lambda image: (first + image, 0))
     fixed = lambda array: pl.BlockSpec(array.shape, lambda image: (0,) * array.ndim)
+    anywhere = pl.BlockSpec(memory_space=pl.ANY)
     shapes = [(width, f32), (width, bf16)]
     if keep:
         shapes = [
@@ -202,14 +229,19 @@
         ]
     made = [] if made is None else list(made)
     extra = [received] if keep else []
-    inputs = 8 + len(extra)
+    inputs = 10 + len(extra)
+    scratch = [
+        pltpu.VMEM((3, parts, rows, width), bf16),
+        pltpu.VMEM((patches, width), f32),
+        pltpu.SemaphoreType.DMA((3,)),
+    ]
+    if keep:
+        scratch += [pltpu.VMEM((patches, columns), kind) for columns, kind in shapes]
+        scratch += [pltpu.SemaphoreType.DMA((len(shapes),))]
 
     def body(*refs):
-        rest = refs[inputs + len(made) :]
-        received_ref = refs[0] if keep else None
-        attention_forward_kernel(
-            heads, places, keep, received_ref, *refs[len(extra) : inputs], *rest
-        )
+        refs = refs[:inputs] + refs[inputs + len(made) :]
+        attention_forward_kernel(heads, places_of(parts, walked), first, keep, refs)
 
     return pl.pallas_call(
         body,
@@ -218,28 +250,51 @@
         + [
             row(width),
             pl.BlockSpec((1, 6, width), lambda image: (first + image, 0, 0)),
-            row(width),
-            row(width),
+            row(arrays[0].shape[1]),
+            row(arrays[1].shape[1]),
             fixed(gain),
-            fixed(summing),
-            fixed(spreading),
-            pl.BlockSpec(memory_space=pl.ANY),
+            fixed(arrays[2]),
+            fixed(arrays[3]),
+            fixed(arrays[4]),
+            pl.BlockSpec((parts, rows, width), lambda image: (0, 0, 0)),
+            anywhere,
         ]
-        + [pl.BlockSpec(memory_space=pl.ANY)] * len(made),
-        out_specs=[row(columns) for columns, kind in shapes],
+        + [anywhere] * len(made),
+        out_specs=[anywhere if keep else row(columns) for columns, kind in shapes],
         out_shape=[jax.ShapeDtypeStruct((tokens, columns), kind) for columns, kind in shapes],
         input_output_aliases={inputs + index: index for index in range(len(made))},
-        scratch_shapes=[
-            pltpu.VMEM((4, joined.shape[0], joined.shape[1], width), bf16),
-            pltpu.VMEM((patches, width), f32),
-            pltpu.SemaphoreType.DMA((4,)),
-        ],
+        scratch_shapes=scratch,
         compiler_params=params(),
         cost_estimate=cost(
             2 * count * patches * width * (4 * width + 2 * patches),
             8 * width * width + count * patches * width * 20,
         ),
-    )(*extra, x, mod, cos, sin, gain, summing, spreading, joined, *made)
+    )(*extra, x, mod, arrays[0], arrays[1], gain, *arrays[2:], joined, joined, *made)
+
+
+def pack_columns(matrices, pieces):
+    rows = matrices[0].shape[0]
+    total = sum(columns for unused, first, columns in pieces)
+
+    def body(*refs):
+        at = 0
+        for which, first, columns in pieces:
+            refs[-1][:, at : at + columns] = refs[which][:, first : first + columns]
+            at += columns
+
+    if any(columns % LANES or first % LANES for unused, first, columns in pieces):
+        return jnp.concatenate(
+            [matrices[which][:, first : first + columns] for which, first, columns in pieces], axis=1
+        )
+    return pl.pallas_call(
+        body,
+        grid=(1,),
+        in_specs=whole_specs(matrices),
+        out_specs=pl.BlockSpec((rows, total), lambda i: (0, 0)),
+        out_shape=jax.ShapeDtypeStruct((rows, total), matrices[0].dtype),
+        compiler_params=params(),
+        cost_estimate=cost(0, 4 * rows * total),
+    )(*matrices)
 
 
 def gate_up_kernel(places, keep, normed_ref, gate_ref, up_ref, *outs):
@@ -274,76 +329,61 @@
     )(normed_two, joined, joined)
 
 
-def parts_per_step(rows):
-    return max(1, 768 // rows)
-
-
-def part_specs(down, walked):
-    parts, rows, width = down.shape
-    each = parts_per_step(rows)
-
-    def spec(which):
-        return pl.BlockSpec(
-            (1, rows, width), lambda i: (part_place(i * each + which, parts, walked), 0, 0)
-        )
-
-    return [spec(which) for which in range(each)]
-
-
-def joined_parts(refs):
-    if len(refs) == 1:
-        return refs[0][0]
-    return jnp.concatenate([ref[0] for ref in refs], axis=0)
-
-
-def down_projection(act, down, middle, mod, walked, first, count, keep):
+def down_projection(active, act, down, middle, mod, first, count, keep, step):
     hidden = act.shape[1]
     images, unused, width = mod.shape
     patches = act.shape[0] // images
     tokens = count * patches
-    specs = part_specs(down, walked)
-    each, rows = len(specs), down.shape[1]
     outs = [jax.ShapeDtypeStruct((tokens, width), bf16)]
     scratch = [pltpu.VMEM((tokens, width), f32)]
     if keep:
         outs.append(jax.ShapeDtypeStruct((tokens, width), f32))
         scratch = []
 
-    def body(act_ref, middle_ref, mod_ref, *refs):
-        step = pl.program_id(0)
-        total = refs[each + 1]
-        term = dot(act_ref[...], joined_parts(refs[:each]))
-
-        @pl.when(step == 0)
+    def body(active_ref, act_ref, middle_ref, mod_ref, down_ref, result_ref, total):
+        index = pl.program_id(0)
+
+        @pl.when(active_ref[0] == 0)
         def _():
-            total[...] = term
-
-        @pl.when(step > 0)
+            result_ref[...] = jnp.zeros_like(result_ref)
+
+        @pl.when(active_ref[0] != 0)
         def _():
-            total[...] += term
-
-        @pl.when(step == pl.num_programs(0) - 1)
-        def _():
-            for image in range(count):
-                at = slice(image * patches, (image + 1) * patches)
-                gate = mod_ref[first + image, 5:6]
-                refs[each][at] = (middle_ref[at] + gate * total[at]).astype(bf16)
+            term = dot(act_ref[...], down_ref[...])
+
+            @pl.when(index == 0)
+            def _():
+                total[...] = term
+
+            @pl.when(index > 0)
+            def _():
+                total[...] += term
+
+            @pl.when(index == hidden // step - 1)
+            def _():
+                for image in range(count):
+                    at = slice(image * patches, (image + 1) * patches)
+                    gate = mod_ref[first + image, 5:6]
+                    result_ref[at] = (middle_ref[at] + gate * total[at]).astype(bf16)
 
     return pl.pallas_call(
         body,
-        grid=(hidden // (each * rows),),
-        in_specs=[
-            pl.BlockSpec((tokens, each * rows), lambda i: (first // count, i)),
-            pl.BlockSpec((tokens, width), lambda i: (first // count, 0)),
-            pl.BlockSpec(mod.shape, lambda i: (0, 0, 0)),
-        ]
-        + specs,
-        out_specs=[pl.BlockSpec((tokens, width), lambda i: (0, 0))] * len(outs),
+        grid_spec=pltpu.PrefetchScalarGridSpec(
+            num_scalar_prefetch=1,
+            grid=(hidden // step,),
+            in_specs=[
+                pl.BlockSpec((tokens, step), lambda i, active: (first // count, i * active[0])),
+                pl.BlockSpec((tokens, width), lambda i, active: (first // count, 0)),
+                pl.BlockSpec(mod.shape, lambda i, active: (0, 0, 0)),
+                pl.BlockSpec((step, width), lambda i, active: (i * active[0], 0)),
+            ],
+            out_specs=[pl.BlockSpec((tokens, width), lambda i, active: (0, 0))] * len(outs),
+            scratch_shapes=scratch,
+        ),
         out_shape=outs,
-        scratch_shapes=scratch,
         compiler_params=params(),
         cost_estimate=cost(2 * tokens * width * hidden, 2 * width * hidden + 8 * tokens * width),
-    )(act, middle, mod, *[down] * each)
+    )(active, act, middle, mod, down)
 
 
 def incoming(cot_ref, back_refs, image, at):
@@ -384,25 +424,22 @@
     return [pl.BlockSpec(array.shape, lambda i: (0, 0)) for array in arrays]
 
 
-def act_backward(mlp_grads, down, hidden, walked):
-    width = mlp_grads[0].shape[1]
+def act_backward(mlp_grads, down, step):
+    hidden, width = down.shape
     tokens = sum(grad.shape[0] for grad in mlp_grads)
-    specs = part_specs(down, walked)
-    each, rows = len(specs), down.shape[1]
 
     def body(*refs):
-        grads, refs = refs[: len(mlp_grads)], refs[len(mlp_grads) :]
-        refs[each][...] = dot_right(stacked(grads), joined_parts(refs[:each])).astype(bf16)
+        refs[-1][...] = dot_right(stacked(refs[:-2]), refs[-2][...]).astype(bf16)
 
     return pl.pallas_call(
         body,
-        grid=(hidden // (each * rows),),
-        in_specs=whole_specs(mlp_grads) + specs,
-        out_specs=pl.BlockSpec((tokens, each * rows), lambda i: (0, i)),
+        grid=(hidden // step,),
+        in_specs=whole_specs(mlp_grads) + [pl.BlockSpec((step, width), lambda i: (i, 0))],
+        out_specs=pl.BlockSpec((tokens, step), lambda i: (0, i)),
         out_shape=jax.ShapeDtypeStruct((tokens, hidden), bf16),
         compiler_params=params(),
         cost_estimate=cost(2 * tokens * width * hidden, 2 * width * hidden + 4 * tokens * width),
-    )(*mlp_grads, *[down] * each)
+    )(*mlp_grads, down)
 
 
 def mlp_backward(cot, backs, mlp, act_grad, gate, up, joined, middle, branch, mod, walked, keep):
@@ -416,13 +453,17 @@
     count = hidden // step
     whole = pl.BlockSpec((tokens, width), lambda i: (0, 0))
     block = pl.BlockSpec((tokens, step), lambda i: (0, i))
-    kept = [mlp, branch] if keep else []
-
-    def body(cot_ref, act_grad_ref, gate_ref, up_ref, gate_weight, up_weight, middle_ref, mod_ref, joined_ref, *refs):
+    anywhere = pl.BlockSpec(memory_space=pl.ANY)
+    late = [cot, middle] + ([mlp, branch] if keep else [])
+
+    def body(act_grad_ref, gate_ref, up_ref, gate_weight, up_weight, mod_ref, joined_ref, *refs):
         back_refs, refs = refs[: len(backs)], refs[len(backs) :]
+        sources, refs = refs[: len(late)], refs[len(late) :]
+        sems, refs = refs[-1], refs[:-1]
+        copies, refs = refs[-len(late) :], refs[: -len(late)]
+        cot_ref, middle_ref = copies[:2]
         if keep:
-            mlp_ref, branch_ref = refs[:2]
-            refs = refs[2:]
+            mlp_ref, branch_ref = copies[2:]
         middle_grad_ref, mixed_grad_ref = refs[:2]
         refs = refs[2:]
         if keep:
@@ -430,11 +471,17 @@
             refs = refs[4:]
         total, out_weight, sem = refs
         index = pl.program_id(0)
-        fetch = pltpu.make_async_copy(joined_ref.at[:, :, pl.ds(3 * width, width)], out_weight, sem)
+        fetches = [
+            pltpu.make_async_copy(joined_ref.at[:, :, pl.ds(3 * width, width)], out_weight, sem)
+        ] + [
+            pltpu.make_async_copy(source, copies[which], sems.at[which])
+            for which, source in enumerate(sources)
+        ]
 
         @pl.when(index == 0)
         def _():
-            fetch.start()
+            for fetch in fetches:
+                fetch.start()
 
         gate_val, up_val = gate_ref[...].astype(f32), up_ref[...].astype(f32)
         sigma = 1.0 / (1.0 + jnp.exp(-gate_val))
@@ -457,7 +504,8 @@
 
         @pl.when(index == count - 1)
         def _():
-            fetch.wait()
+            for fetch in fetches:
+                fetch.wait()
             matrix = whole_rows(out_weight, places)
             for image in range(images):
                 at = slice(image * patches, (image + 1) * patches)
@@ -492,131 +540,125 @@
         body,
         grid=(count,),
         in_specs=[
-            whole,
             block,
             block,
             block,
             pl.BlockSpec((parts, rows, step), lambda i: (0, 0, base + i)),
             pl.BlockSpec((parts, rows, step), lambda i: (0, 0, base + count + i)),
-            whole,
             pl.BlockSpec(mod.shape, lambda i: (0, 0, 0)),
-            pl.BlockSpec(memory_space=pl.ANY),
+            anywhere,
         ]
         + [pl.BlockSpec((patches, width), lambda i: (0, 0))] * len(backs)
-        + [whole] * len(kept),
+        + [anywhere] * len(late),
         out_specs=out_specs,
         out_shape=out_shapes,
         scratch_shapes=[
             pltpu.VMEM((tokens, width), f32),
             pltpu.VMEM((parts, rows, width), bf16),
             pltpu.SemaphoreType.DMA,
-        ],
+        ]
+        + [pltpu.VMEM(array.shape, array.dtype) for array in late]
+        + [pltpu.SemaphoreType.DMA((len(late),))],
         compiler_params=params(),
         cost_estimate=cost(
             2 * tokens * width * (2 * hidden + width), 4 * width * hidden + 6 * tokens * hidden
         ),
-    )(cot, act_grad, gate, up, joined, joined, middle, mod, joined, *backs, *kept)
-
-
-def attention_backward_kernel(
-    heads,
-    places,
-    keep,
-    raw_ref,
-    value_ref,
-    mixed_grad_ref,
-    middle_grad_ref,
-    x_ref,
-    mod_ref,
-    cos_ref,
-    sin_ref,
-    gain_ref,
-    sum_ref,
-    spread_ref,
-    joined_ref,
-    *rest,
-):
-    if keep:
-        flow_grad_ref, qkv_grad_ref, sums_ref = rest[:3]
-        rest = rest[3:]
+    )(act_grad, gate, up, joined, joined, mod, joined, *backs, *late)
+
+
+def attention_backward_kernel(heads, places, first, keep, refs):
+    raw_ref, value_ref, mixed_grad_ref, middle_grad_hbm, x_hbm, mod_ref = refs[:6]
+    cos_ref, sin_ref, gain_ref, sum_ref, spread_ref, repeat_ref, joined_ref = refs[6:13]
+    refs = refs[13:]
+    if keep:
+        flow_grad_ref, qkv_grad_ref, sums_ref = refs[:3]
+        refs = refs[3:]
     else:
-        back_ref = rest[0]
-        rest = rest[1:]
-    weight, query_total, key_total, value_total, sems = rest
-    width = x_ref.shape[1]
+        back_ref = refs[0]
+        refs = refs[1:]
+    weight, scales, query_total, key_total, value_total, middle_grad_ref, x_ref, sems = refs
+    patches, width = x_ref.shape
     head_size = width // heads
     quarter = head_size // 4
     factor = head_size ** (-0.5)
+    image = pl.program_id(0)
+    tables = (cos_ref, sin_ref, gain_ref, sum_ref, spread_ref, repeat_ref, head_size)
+    rows = pl.ds((first + image) * patches, patches)
+    late = [
+        pltpu.make_async_copy(x_hbm.at[rows], x_ref, sems.at[3]),
+        pltpu.make_async_copy(middle_grad_hbm.at[rows], middle_grad_ref, sems.at[4]),
+    ]
 
     def fetch(part):
         return pltpu.make_async_copy(
             joined_ref.at[:, :, pl.ds(part * width, width)], weight.at[part], sems.at[part]
         )
 
-    @pl.when(pl.program_id(0) == 0)
+    @pl.when(image == 0)
     def _():
         for part in range(3):
             fetch(part).start()
 
-    summing, spreading = sum_ref[...], spread_ref[...]
+    for copy in late:
+        copy.start()
     first_half = first_half_mask((1, width), quarter)
-
-    def prepared(part):
-        raw = raw_ref[:, part * width : (part + 1) * width]
-        scale = lax.rsqrt(two_terms(raw * raw, summing) * (1.0 / head_size) + epsilon)
-        scaled = raw * two_terms(scale, spreading) * gain_ref[part : part + 1]
-        turned = scaled * cos_ref[...] + partner(scaled, first_half, quarter) * sin_ref[...]
-        return turned.astype(bf16)
-
-    queries, keys, values = prepared(0), prepared(1), value_ref[...]
-    mixed_grad = mixed_grad_ref[...]
+    raws = [raw_ref[:, part * width : (part + 1) * width] for part in range(2)]
+    queries = rotated(raws[0], 0, tables, scales)
+    keys = rotated(raws[1], 1, tables, scales)
+    values, mixed_grad = value_ref[...], mixed_grad_ref[...]
     query_total[...] = jnp.zeros_like(query_total)
     key_total[...] = jnp.zeros_like(key_total)
     value_total[...] = jnp.zeros_like(value_total)
-    for head in range(heads):
-        start, span = head_window(head, head_size, width)
-        mask = head_mask(head, head_size, start, span)
+    for start, span, members in head_groups(heads, head_size):
         window = slice(start, start + span)
-        key_part, query_part = keys[:, window] * mask, queries[:, window] * mask
-        grad_part = mixed_grad[:, window] * mask
-        scores = dot_right(key_part, queries[:, window])
-        highest = jnp.max(scores, axis=0, keepdims=True)
-        expon = jnp.exp((scores - highest) * factor)
-        probs = expon * (1.0 / jnp.sum(expon, axis=0, keepdims=True))
-        value_total[:, window] += dot(probs.astype(bf16), grad_part)
-        probs_grad = dot_right(values[:, window], grad_part)
-        middle = jnp.sum(probs * probs_grad, axis=0, keepdims=True)
-        scores_grad = (probs * (probs_grad - middle)).astype(bf16)
-        key_total[:, window] += dot(scores_grad, query_part)
-        query_total[:, window] += dot_left(scores_grad, key_part)
+        probs, slopes, key_parts, query_parts, grad_parts = [], [], [], [], []
+        for head in members:
+            mask = head_mask(head, head_size, start, span)
+            key_part, query_part = keys[:, window] * mask, queries[:, window] * mask
+            grad_part = mixed_grad[:, window] * mask
+            scores = dot_right(key_part, queries[:, window])
+            expon = jnp.exp2(scores * (factor * math.log2(math.e)))
+            prob = expon * (1.0 / jnp.sum(expon, axis=0, keepdims=True))
+            prob_grad = dot_right(values[:, window], grad_part)
+            middle = jnp.sum(prob * prob_grad, axis=0, keepdims=True)
+            probs.append(prob.astype(bf16))
+            slopes.append((prob * (prob_grad - middle)).astype(bf16))
+            key_parts.append(key_part)
+            query_parts.append(query_part)
+            grad_parts.append(grad_part)
+        value_total[:, window] += dot(side_by_side(probs), one_above_other(grad_parts))
+        key_total[:, window] += dot(side_by_side(slopes), one_above_other(query_parts))
+        query_total[:, window] += dot_left(one_above_other(slopes), one_above_other(key_parts))
 
     def raw_grad(part, total):
         turned = total[...] * factor
-        weighted = turned * sin_ref[...]
-        grad = turned * cos_ref[...] + partner(weighted, first_half, quarter)
-        raw = raw_ref[:, part * width : (part + 1) * width]
-        scale = lax.rsqrt(two_terms(raw * raw, summing) * (1.0 / head_size) + epsilon)
-        scale = two_terms(scale, spreading)
-        normal = raw * scale
+        cos, sin = dot(cos_ref[...], repeat_ref[...]), dot(sin_ref[...], repeat_ref[...])
+        grad = turned * cos + partner(turned * sin, first_half, quarter)
+        scale = scales[part]
+        normal = raw_ref[:, part * width : (part + 1) * width] * scale
         if keep:
             sums_ref[0, 2 + part : 3 + part] = jnp.sum(grad * normal, axis=0, keepdims=True)
         grad = grad * gain_ref[part : part + 1]
-        mean = two_terms(two_terms(grad * normal, summing) * (1.0 / head_size), spreading)
+        mean = dot((grad * normal).astype(bf16), sum_ref[...]) * (1.0 / head_size)
+        mean = dot(two_terms(mean), spread_ref[...])
         return (scale * (grad - normal * mean)).astype(bf16)
 
     def arrived(part):
-        @pl.when(pl.program_id(0) == 0)
+        @pl.when(image == 0)
         def _():
             fetch(part).wait()
+
+        return whole_rows(weight.at[part], places)
 
     parts = [raw_grad(0, query_total), raw_grad(1, key_total), value_total[...].astype(bf16)]
     grad = None
     for part in range(3):
-        arrived(part)
         if keep:
             qkv_grad_ref[:, part * width : (part + 1) * width] = parts[part]
-        term = dot_right(parts[part], whole_rows(weight.at[part], places))
+        term = dot_right(parts[part], arrived(part))
         grad = term if grad is None else grad + term
+    for copy in late:
+        copy.wait()
     mod = mod_ref[0]
     flow = x_ref[...].astype(f32)
     inverse = inverse_rms(flow)
@@ -633,18 +675,18 @@
 
 
 def attention_backward(
-    raw, value, mixed_grad, middle_grad, x, mod, tables, gains, joined, walked, first, count, keep
+    raw, value, mixed_grad, middle_grad, x, mod, tables, gain, joined, walked, first, count, keep
 ):
-    cos, sin, summing, spreading = tables
-    gain, head_size = gains
     images, unused, width = mod.shape
     patches = x.shape[0] // images
     tokens = count * patches
-    heads = width // head_size
+    heads = width // tables[-1]
+    arrays = tables[:-1]
     parts, rows, unused = joined.shape
     row = lambda columns: pl.BlockSpec((patches, columns), lambda image: (first + image, 0))
     token = lambda columns: pl.BlockSpec((patches, columns), lambda image: (image, 0))
     fixed = lambda array: pl.BlockSpec(array.shape, lambda image: (0,) * array.ndim)
+    anywhere = pl.BlockSpec(memory_space=pl.ANY)
     out_shapes = [jax.ShapeDtypeStruct((tokens, width), bf16)]
     out_specs = [token(width)]
     if keep:
@@ -658,54 +700,61 @@
             token(3 * width),
             pl.BlockSpec((1, 4, width), lambda image: (image, 0, 0)),
         ]
+
+    def body(*refs):
+        attention_backward_kernel(heads, places_of(parts, walked), first, keep, refs)
+
     return pl.pallas_call(
-        functools.partial(attention_backward_kernel, heads, places_of(parts, walked), keep),
+        body,
         grid=(count,),
         in_specs=[
             row(2 * width),
             row(width),
             row(width),
-            row(width),
-            row(width),
+            anywhere,
+            anywhere,
             pl.BlockSpec((1, 6, width), lambda image: (first + image, 0, 0)),
-            row(width),
-            row(width),
+            row(arrays[0].shape[1]),
+            row(arrays[1].shape[1]),
             fixed(gain),
-            fixed(summing),
-            fixed(spreading),
-            pl.BlockSpec(memory_space=pl.ANY),
+            fixed(arrays[2]),
+            fixed(arrays[3]),
+            fixed(arrays[4]),
+            anywhere,
         ],
         out_specs=out_specs,
         out_shape=out_shapes,
         scratch_shapes=[
             pltpu.VMEM((3, parts, rows, width), bf16),
+            pltpu.VMEM((2, patches, width), f32),
             pltpu.VMEM((patches, width), f32),
             pltpu.VMEM((patches, width), f32),
             pltpu.VMEM((patches, width), f32),
-            pltpu.SemaphoreType.DMA((3,)),
+            pltpu.VMEM((patches, width), f32),
+            pltpu.VMEM((patches, width), bf16),
+            pltpu.SemaphoreType.DMA((5,)),
         ],
         compiler_params=params(),
         cost_estimate=cost(
             2 * tokens * width * (3 * width + 5 * patches),
             6 * width * width + tokens * width * 20,
         ),
-    )(raw, value, mixed_grad, middle_grad, x, mod, cos, sin, gain, summing, spreading, joined)
-
-
-def down_grad(mlp_grads, act, parts, walked):
+    )(raw, value, mixed_grad, middle_grad, x, mod, arrays[0], arrays[1], gain, *arrays[2:], joined)
+
+
+def down_grad(mlp_grads, act, step):
     tokens, hidden = act.shape
     width = mlp_grads[0].shape[1]
-    step = hidden // parts
 
     def body(act_ref, *refs):
-        refs[-1][0] = dot_left(act_ref[...], stacked(refs[:-1])).astype(bf16)
+        refs[-1][...] = dot_left(act_ref[...], stacked(refs[:-1])).astype(bf16)
 
     return pl.pallas_call(
         body,
-        grid=(parts,),
+        grid=(hidden // step,),
         in_specs=[pl.BlockSpec((tokens, step), lambda i: (0, i))] + whole_specs(mlp_grads),
-        out_specs=pl.BlockSpec((1, step, width), lambda i: (part_place(i, parts, walked), 0, 0)),
-        out_shape=jax.ShapeDtypeStruct((parts, step, width), bf16),
+        out_specs=pl.BlockSpec((step, width), lambda i: (i, 0)),
+        out_shape=jax.ShapeDtypeStruct((hidden, width), bf16),
         compiler_params=params(),
         cost_estimate=cost(2 * tokens * width * hidden, 2 * width * hidden),
     )(act, *mlp_grads)
@@ -763,6 +812,19 @@
     return jnp.concatenate([blocks[place] for place in places], axis=0)
 
 
+def walk_columns(which, columns, count):
+    each = columns // (count // 2)
+    return [(which, device // 2 * each, each) for device in walk_of(count)[::2]]
+
+
+def columns_from_walk(matrix, count):
+    each = matrix.shape[1] // (count // 2)
+    places = places_of(count // 2, True)
+    return jnp.concatenate(
+        [matrix[:, place * each : (place + 1) * each] for place in places], axis=1
+    )
+
+
 def to_walk(rows, count):
     blocks = rows.reshape(count // 2, -1, rows.shape[-1])
     return jnp.concatenate([blocks[device // 2] for device in walk_of(count)[::2]], axis=0)
@@ -779,9 +841,9 @@
     return lax.optimization_barrier(part)
 
 
-def as_parts(rows, count, unit):
+def as_parts(rows, count):
     each = rows.shape[0] // (count // 2)
-    if each % unit == 0:
+    if each % 16 == 0:
         return rows.reshape(count // 2, each, rows.shape[1]), True
     whole = from_walk(rows, count)
     return whole[None], False
@@ -794,14 +856,13 @@
 def gather_small(block, count):
     me = lax.axis_index("dp")
     block = block[None]
-    bit = 1
-    while bit < count:
+    bit = count // 2
+    while bit:
         other = swapped(block, bit, count)
         low = (me & bit) == 0
-        block = jnp.concatenate(
-            [jnp.where(low, block, other), jnp.where(low, other, block)], axis=0
-        )
-        bit *= 2
+        pair = [jnp.where(low, block, other), jnp.where(low, other, block)]
+        block = jnp.stack(pair, axis=1).reshape(2 * block.shape[0], *block.shape[1:])
+        bit //= 2
     return block
 
 
@@ -826,7 +887,6 @@
 
 
 def rotation_tables(positions, width, head_size):
-    heads = width // head_size
     quarter = head_size // 4
     frequency = jnp.exp(-math.log(10000.0) * jnp.arange(quarter, dtype=f32) / quarter)
     places = positions.reshape(-1, 1)
@@ -836,9 +896,19 @@
     col_cos, col_sin = jnp.cos(col_angle), jnp.sin(col_angle)
     cos = jnp.concatenate([row_cos, row_cos, col_cos, col_cos], axis=1)
     sin = jnp.concatenate([-row_sin, row_sin, -col_sin, col_sin], axis=1)
-    head = jnp.arange(width) // head_size
-    summing = (head[:, None] == jnp.arange(LANES)[None, :]).astype(bf16)
-    return jnp.tile(cos, (1, heads)), jnp.tile(sin, (1, heads)), summing, summing.T
+    padding = ((0, 0), (0, LANES - head_size))
+    number = jnp.arange(LANES)
+    column = jnp.arange(width)
+    summing = (column[:, None] // head_size == number[None, :]).astype(bf16)
+    spreading = (column[None, :] // head_size == number[:, None]).astype(bf16)
+    repeating = (column[None, :] % head_size == number[:, None]).astype(bf16)
+    return (
+        two_terms(jnp.pad(cos, padding)),
+        two_terms(jnp.pad(sin, padding)),
+        summing,
+        jnp.concatenate([spreading, spreading]),
+        jnp.concatenate([repeating, repeating]),
+    )
 
 
 def per_device(
@@ -858,6 +928,8 @@
     k_gain,
 ):
     first_section = lax.axis_index("section") == 0
+    first_only = first_section.astype(jnp.int32).reshape(1)
+    always = jnp.ones((1,), jnp.int32)
     count = lax.axis_size("dp")
     me = lax.axis_index("dp")
     images, patches, width = tokens.shape
@@ -867,9 +939,10 @@
     rows = ada_weight.shape[1]
     classes = label_table.shape[0]
 
+    pieces = [(0, 0, 3 * width), (1, 0, width)]
+    pieces += walk_columns(2, hidden, count) + walk_columns(3, hidden, count)
     joined = gather_walk(
-        jnp.concatenate([qkv_weight[0], out_weight[0], gate_weight[0], up_weight[0]], axis=1),
-        count,
+        pack_columns([qkv_weight[0], out_weight[0], gate_weight[0], up_weight[0]], pieces), count
     )
 
     ids = gather_small(jnp.stack([labels, timesteps]), count)
@@ -890,28 +963,28 @@
         (down_weight[0], joined, mod, own, tables)
     )
     down = gather_walk(down, count)
-    joined, walked = as_parts(joined, count, 16)
-    down, down_walked = as_parts(down, count, LANES)
-    if not down_walked:
-        down = down.reshape(hidden // 384, 384, width)
-    gains = (jnp.tile(jnp.concatenate([q_gain, k_gain]), (1, heads)), head_size)
+    joined, walked = as_parts(joined, count)
+    tables = (*tables, head_size)
+    gain = jnp.tile(jnp.concatenate([q_gain, k_gain]), (1, heads))
 
     cot = cotangent[0].reshape(images * patches, width)
     middle, normed_two = attention_forward(
-        flat, None, mod, tables, gains, joined, walked, 0, images
+        flat, None, mod, tables, gain, joined, walked, 0, images
     )
     (act,) = gate_up(normed_two, joined, hidden, walked, False)
     received = []
     for image in range(images):
-        (early,) = down_projection(act, down, middle, mod, down_walked, image, 1, False)
+        (early,) = down_projection(
+            first_only, act, down, middle, mod, image, 1, False, hidden // 2
+        )
         received.append(lax.ppermute(early, "section", [(0, 1)]))
-    late_cot, unused = lax.optimization_barrier((cot, early))
-    mlp_grads = [mlp_gradient(late_cot, [], mod, 0, images)]
-    act_grad = act_backward(mlp_grads, down, hidden, down_walked)
+    mlp_grad, unused = lax.optimization_barrier((mlp_gradient(cot, [], mod, 0, images), early))
+    mlp_grads = [mlp_grad]
+    act_grad = act_backward(mlp_grads, down, hidden // 2)
     kept = None
     for image in range(images):
         kept = attention_forward(
-            own, received[image], mod, tables, gains, joined, walked, image, 1, kept
+            own, received[image], mod, tables, gain, joined, walked, image, 1, kept
         )
     normed, raw, values, attended, branch, middle, normed_two, layer_in = kept
     act, gate, up = gate_up(normed_two, joined, hidden, walked, True)
@@ -929,7 +1002,7 @@
             layer_in,
             mod,
             tables,
-            gains,
+            gain,
             joined,
             walked,
             image,
@@ -938,17 +1011,18 @@
         )
         backs.append(lax.ppermute(early, "section", [(1, 0)]))
     late_act, unused = lax.optimization_barrier((act, early))
-    result, mlp = down_projection(late_act, down, middle, mod, down_walked, 0, images, True)
+    result, mlp = down_projection(
+        always, late_act, down, middle, mod, 0, images, True, hidden // 2
+    )
 
     late_cot, unused = lax.optimization_barrier((cot, mlp))
     mlp_grads = [
         mlp_gradient(late_cot, [back], mod, image, 1) for image, back in enumerate(backs)
     ]
-    down_term = down_grad(mlp_grads, act, down.shape[0], down_walked)
+    down_term = down_grad(mlp_grads, act, hidden // 4)
     down_term, mlp_grads = lax.optimization_barrier((down_term, mlp_grads))
-    down_term = down_term.reshape(hidden, width)
-    down_part = scatter_walk(down_term if down_walked else to_walk(down_term, count), count)
-    act_grad = act_backward(mlp_grads, down, hidden, down_walked)
+    down_part = scatter_walk(down_term, count)
+    act_grad = act_backward(mlp_grads, down, hidden // 2)
     middle_grad, mixed_grad, gate_grad, up_grad, branch_grad, mlp_sums = mlp_backward(
         cot, backs, mlp, act_grad, gate, up, joined, middle, branch, mod, walked, True
     )
@@ -956,11 +1030,11 @@
     def matrix_part(inputs, grads, step, before):
         term = matrix_grad(inputs, grads, step, joined.shape[0], walked).reshape(width, -1)
         term = term if walked else to_walk(term, count)
-        term, before = lax.optimization_barrier((term, before))
-        return scatter_walk(term, count), before
+        term, *before = lax.optimization_barrier((term, *before))
+        return scatter_walk(term, count), *before
 
     gate_up_part, down_part = matrix_part(
-        [normed_two, normed_two], [gate_grad, up_grad], hidden // 2, down_part
+        [normed_two, normed_two], [gate_grad, up_grad], hidden // 2, [down_part]
     )
     flow_grad, qkv_grad, attention_sums = attention_backward(
         raw,
@@ -970,22 +1044,22 @@
         layer_in,
         mod,
         tables,
-        gains,
+        gain,
         joined,
         walked,
         0,
         images,
         True,
     )
-    rest_part, gate_up_part = matrix_part(
-        [normed, attended], [qkv_grad, branch_grad], width, gate_up_part
+    mod_grad = jnp.concatenate([attention_sums[:, :2], mlp_sums], axis=1).reshape(images, -1)
+    mod_all = gather_small(mod_grad.astype(bf16), count).reshape(-1, mod_grad.shape[1])
+    rest_part, gate_up_part, mod_all = matrix_part(
+        [normed, attended], [qkv_grad, branch_grad], width, [gate_up_part, mod_all]
     )
     flow_grad = flow_grad.reshape(images, patches, width)
     input_grads = jnp.where(first_section, flow_grad, flow_grad.astype(bf16).astype(f32))
 
-    mod_grad = jnp.concatenate([attention_sums[:, :2], mlp_sums], axis=1).reshape(images, -1)
     head_sums = jnp.sum(attention_sums[:, 2:], axis=0).reshape(2, heads, head_size)
-    mod_all = gather_small(mod_grad.astype(bf16), count).reshape(-1, mod_grad.shape[1])
     ada_part = dot_left(silu_rows, mod_all)
     silu_grad = dot_right(mod_all, ada_weight[0])
     silu_grad = silu_grad + lax.ppermute(silu_grad, "section", [(0, 1), (1, 0)])
@@ -1007,8 +1081,8 @@
         ada_part[None],
         rest_part[None, :, : 3 * width].astype(f32),
         rest_part[None, :, 3 * width :].astype(f32),
-        gate_up_part[None, :, :hidden].astype(f32),
-        gate_up_part[None, :, hidden:].astype(f32),
+        columns_from_walk(gate_up_part[:, :hidden], count)[None].astype(f32),
+        columns_from_walk(gate_up_part[:, hidden:], count)[None].astype(f32),
         down_part[None].astype(f32),
         gain_all[None, 0],
         gain_all[None, 1],

time: 591 us -> 558 us (0.944)
  Pallas kernels: 291 us -> 258 us
  waiting for transfers between devices: 200 us -> 217 us
  starting transfers between devices: 36.2 us -> 24.5 us
    pallas_call x11 -> x12, Pallas kernels: 178 us -> 154 us  [the longest x3 61.7 us: attention_backward(): pl.pallas_call(body, grid=(count,), in_specs=[row(2 * width), row(width),...]
    ppermute x20, starting transfers between devices: 27.1 us -> 16.6 us  [swapped(): lax.ppermute(block, 'dp', [(device, device ^ bit) for device in range(cou...]
    pallas_call x3, Pallas kernels: 54.6 us -> 44.3 us  [attention_forward(): pl.pallas_call(body, grid=(count,), in_specs=[pl.BlockSpec((patches, widt...]
    all_gather x2, waiting for transfers between devices: 83.8 us -> 92.8 us  [gather_walk(): lax.all_gather(rows, 'dp', axis=0, tiled=True, axis_index_groups=[walk_of...]
  transfers between devices with their start and end apart: 30 -> 30, of which waited for: 22 -> 23; matrix products, arithmetic and copies ran while one was open for 5% -> 5% of each run, Pallas kernels for 35% -> 32%
where the time goes in v4:
time: 558 us; the launch traced here: 552 us
  Pallas kernels  258 us (46%)
  waiting for transfers between devices  217 us (39%)
  starting transfers between devices  24.5 us (4%)
  other arithmetic  20.1 us (4%)
  between operations  15.2 us (3%)
  local copies, waits for them, and re-layouts  10.1 us (2%)
  matrix products  7.2 us (1%)
    all_gather x2, waiting for transfers between devices, gather_walk(): lax.all_gather(rows, 'dp', axis=0, tiled=True, axis_index_groups=[walk_of...  92.8 us
    ppermute x20, waiting for transfers between devices, swapped(): lax.ppermute(block, 'dp', [(device, device ^ bit) for device in range(cou...  64.3 us
    pallas_call x3, Pallas kernels, attention_backward(): pl.pallas_call(body, grid=(count,), in_specs=[row(2 * width), row(width),...  61.7 us
    reduce_scatter x3, waiting for transfers between devices, scatter_walk(): lax.psum_scatter(rows, 'dp', scatter_dimension=0, tiled=True, axis_index_...  55 us
    pallas_call x3, Pallas kernels, attention_forward(): pl.pallas_call(body, grid=(count,), in_specs=[pl.BlockSpec((patches, widt...  44.3 us
    pallas_call x2, Pallas kernels, mlp_backward(): pl.pallas_call(body, grid=(count,), in_specs=[block, block, block, pl.Blo...  43.2 us
    pallas_call x2, Pallas kernels, gate_up(): pl.pallas_call(functools.partial(gate_up_kernel, places_of(parts, walked)...  26.8 us
    pallas_call x2, Pallas kernels, matrix_grad(): pl.pallas_call(functools.partial(matrix_grad_kernel, places_of(parts, wal...  25.1 us
  transfers between devices with their start and end apart: 30, of which 23 were waited for; matrix products, arithmetic and copies ran while one was open for 5% of the time, Pallas kernels for 32%

profile of v4, /device:TPU:0, one launch (start us, length us, event | category | flops | bytes accessed | tf_op | source)
XLA Modules:
  0.0 552.2 jit_solution(18313676728322094433)
XLA Ops:
  7.3 2.8 shard_map.221
  10.2 4.1 collective-permute-start
  14.4 1.9 fusion.17
  20.5 1.2 broadcast_select_fusion.refs_1_
  21.7 1.6 collective-permute-start.1
  23.4 2.0 collective-permute-done.1
  25.6 1.5 collective-permute-start.2
  27.1 2.1 collective-permute-done.2
  29.4 1.2 collective-permute-done.3
  32.9 1.5 collective-permute-done.4
  34.8 1.7 collective-permute-start.5
  36.5 1.1 add_convert_fusion
  37.6 10.0 %collective-permute-done.5 = f32[4,2,6912]{2,1,0:T(2,128)S(1)} collective-permute-done((f32[4,2,6912]{2,1,0:T(2,128)S(1)}, f32[4,2,6912]{2,1,0:T(2,128)S(1)}, u32[]{:S(2)}, u32[]{:S(2)}) %collective-permute-start.5) | collective-permute-done | bytes 221216 | tf_op jit(solution)/shard_map/ppermute | solution.py:853
  48.1 7.4 %collective-permute-done.6 = f32[2,2,6912]{2,1,0:T(2,128)S(1)} collective-permute-done((f32[2,2,6912]{2,1,0:T(2,128)S(1)}, f32[2,2,6912]{2,1,0:T(2,128)S(1)}, u32[]{:S(2)}, u32[]{:S(2)}) %collective-permute-start.6) | collective-permute-done | bytes 110624 | tf_op jit(solution)/shard_map/ppermute | solution.py:853
  56.7 5.7 %collective-permute-done.7 = f32[1,2,6912]{2,1,0:T(2,128)S(1)} collective-permute-done((f32[1,2,6912]{2,1,0:T(2,128)S(1)}, f32[1,2,6912]{2,1,0:T(2,128)S(1)}, u32[]{:S(2)}, u32[]{:S(2)}) %collective-permute-start.7) | collective-permute-done | bytes 55328 | tf_op jit(solution)/shard_map/ppermute | solution.py:853
  63.1 81.1 %all-gather.3.cloned.1.call-done = bf16[1152,10752]{1,0:T(8,128)(2,1)} async-done(((bf16[72,10752]{1,0:T(8,128)(2,1)}), bf16[1152,10752]{1,0:T(8,128)(2,1)}) %all-gather.3.cloned.1.call-update) | async-done | bytes 24772624 | tf_op jit(solution)/shard_map/all_gather | solution.py:834
  145.2 19.5 %shard_map.222 = (f32[512,1152]{1,0:T(8,128)}, bf16[512,1152]{1,0:T(8,128)(2,1)}) custom-call(bf16[512,1152]{1,0:T(8,128)(2,1)} %bitcast.241, f32[2,6,1152]{2,1,0:T(8,128)} %reshape_squeeze.7.refs_1_.mod_ref.refs_2_.refs_5_, bf16[512,256]{1,0:T(8,128)(2,1)} %get-tuple-element.66.refs_2_.refs_3_.refs_6_, ...), custom_call_target="tpu_custom_call" | custom-call | flops 6039797760 | bytes 22413312 | tf_op jit(solution)/shard_map/pallas_call | solution.py:246
  164.8 13.0 %shard_map.223.act_ref = bf16[512,3072]{1,0:T(8,128)(2,1)} custom-call(bf16[512,1152]{1,0:T(8,128)(2,1)} %get-tuple-element.72.normed_ref, bf16[8,144,10752]{2,1,0:T(8,128)(2,1)} %bitcast.217, bf16[8,144,10752]{2,1,0:T(8,128)(2,1)} %bitcast.218), custom_call_target="tpu_custom_call" | custom-call | flops 7247757312 | bytes 17301504 | tf_op jit(solution)/shard_map/pallas_call | solution.py:317
  177.8 11.7 %all-gather.5.cloned.1.call-done.down_ref.refs_1_.refs_2_ = bf16[3072,1152]{1,0:T(8,128)(2,1)} async-done(((bf16[192,1152]{1,0:T(8,128)(2,1)}), bf16[3072,1152]{1,0:T(8,128)(2,1)}) %all-gather.5.cloned.1.call-update) | async-done | bytes 7077904 | tf_op jit(solution)/shard_map/all_gather | solution.py:834
  189.5 6.1 %shard_map.225 = bf16[256,1152]{1,0:T(8,128)(2,1)} custom-call(s32[1]{0:T(128)} %bitcast.active_ref, bf16[512,3072]{1,0:T(8,128)(2,1)} %shard_map.223.act_ref, f32[512,1152]{1,0:T(8,128)} %get-tuple-element.73.middle_ref, f32[2,6,1152]{2,1,0:T(8,128)} %reshape_squeeze.7.refs_1_.mod_ref.refs_2_.refs_5_, ...), custom_call_target="tpu_custom_call" | custom-call | flops 1811939328 | bytes 9437184 | tf_op jit(solution)/shard_map/pallas_call | solution.py:369
  195.6 1.3 collective-permute-start.9
  197.0 2.5 shard_map.229.refs_0_
  199.5 6.1 %shard_map.224 = bf16[256,1152]{1,0:T(8,128)(2,1)} custom-call(s32[1]{0:T(128)} %bitcast.active_ref, bf16[512,3072]{1,0:T(8,128)(2,1)} %shard_map.223.act_ref, f32[512,1152]{1,0:T(8,128)} %get-tuple-element.73.middle_ref, f32[2,6,1152]{2,1,0:T(8,128)} %reshape_squeeze.7.refs_1_.mod_ref.refs_2_.refs_5_, ...), custom_call_target="tpu_custom_call" | custom-call | flops 1811939328 | bytes 9437184 | tf_op jit(solution)/shard_map/pallas_call | solution.py:369
  205.6 1.3 collective-permute-start.8
  206.9 8.4 %shard_map.230.act_grad_ref = bf16[512,3072]{1,0:T(8,128)(2,1)} custom-call(bf16[512,1152]{1,0:T(8,128)(2,1)} %shard_map.229.refs_0_, bf16[3072,1152]{1,0:T(8,128)(2,1)} %all-gather.5.cloned.1.call-done.down_ref.refs_1_.refs_2_), custom_call_target="tpu_custom_call" | custom-call | flops 3623878656 | bytes 9437184 | tf_op jit(solution)/shard_map/pallas_call | solution.py:434
  216.2 12.3 %shard_map.226 = (bf16[512,1152]{1,0:T(8,128)(2,1)}, f32[512,2304]{1,0:T(8,128)}, bf16[512,1152]{1,0:T(8,128)(2,1)}, bf16[512,1152]{1,0:T(8,128)(2,1)}, f32[512,...) custom-call(bf16[256,1152]{1,0:T(8,128)(2,1)} %copy-done.17, ...), custom_call_target="tpu_custom_call" | custom-call | flops 3019898880 | bytes 16515072 | tf_op jit(solution)/shard_map/pallas_call | solution.py:246
  229.3 12.5 %shard_map.227 = (bf16[512,1152]{1,0:T(8,128)(2,1)}, f32[512,2304]{1,0:T(8,128)}, bf16[512,1152]{1,0:T(8,128)(2,1)}, bf16[512,1152]{1,0:T(8,128)(2,1)}, f32[512,...) custom-call(bf16[256,1152]{1,0:T(8,128)(2,1)} %copy-done.15, ...), custom_call_target="tpu_custom_call", output_to_operand_aliasing={{0}: (11, {}), {1}: (12, {}), {2}: (13, {}), {3}: (14, {}),... | custom-call | flops 3019898880 | bytes 16515072 | tf_op jit(solution)/shard_map/pallas_call | solution.py:246
  241.8 13.8 %shard_map.228 = (bf16[512,3072]{1,0:T(8,128)(2,1)}, bf16[512,3072]{1,0:T(8,128)(2,1)}, bf16[512,3072]{1,0:T(8,128)(2,1)}) custom-call(bf16[512,1152]{1,0:T(8,128)(2,1)} %get-tuple-element.84.normed_ref.refs_0_.refs_1_, bf16[8,144,10752]{2,1,0:T(8,128)(2,1)} %bitcast.223, bf16[8,144,10752]{2,1,0:T(8,128)(2,1)} %bitcast.224), custom_call_target="tpu_custom_call" | custom-call | flops 7247757312 | bytes 23592960 | tf_op jit(solution)/shard_map/pallas_call | solution.py:317
  255.5 19.3 %shard_map.231 = (f32[512,1152]{1,0:T(8,128)}, bf16[512,1152]{1,0:T(8,128)(2,1)}) custom-call(bf16[512,3072]{1,0:T(8,128)(2,1)} %shard_map.230.act_grad_ref, bf16[512,3072]{1,0:T(8,128)(2,1)} %get-tuple-element.89.gate_ref, bf16[512,3072]{1,0:T(8,128)(2,1)} %get-tuple-element.90.up_ref, bf16[8,144,10752]{2,1,0:T(8,128)(2,1)} %bitcast.225, ...), custom_call_target="tpu_custom_call" | custom-call | flops 8606711808 | bytes 23592960 | tf_op jit(solution)/shard_map/pallas_call | solution.py:539
  274.8 15.4 %shard_map.232 = bf16[256,1152]{1,0:T(8,128)(2,1)} custom-call(f32[512,2304]{1,0:T(8,128)} %get-tuple-element.86.refs_0_, bf16[512,1152]{1,0:T(8,128)(2,1)} %get-tuple-element.87.refs_1_, bf16[512,1152]{1,0:T(8,128)(2,1)} %get-tuple-element.92.refs_2_, f32[512,1152]{1,0:T(8,128)} %get-tuple-element.93.refs_3_, bf16[512,1152]{1,0:T(8,128)(2,1)} %get-tuple-element.94.refs_4_, ...), custom_call_target="tpu_custom_call" | custom-call | flops 2793406464 | bytes 13860864 | tf_op jit(solution)/shard_map/pallas_call | solution.py:707
  290.2 1.7 collective-permute-start.11
  291.9 15.4 %shard_map.234 = bf16[256,1152]{1,0:T(8,128)(2,1)} custom-call(f32[512,2304]{1,0:T(8,128)} %get-tuple-element.86.refs_0_, bf16[512,1152]{1,0:T(8,128)(2,1)} %get-tuple-element.87.refs_1_, bf16[512,1152]{1,0:T(8,128)(2,1)} %get-tuple-element.92.refs_2_, f32[512,1152]{1,0:T(8,128)} %get-tuple-element.93.refs_3_, bf16[512,1152]{1,0:T(8,128)(2,1)} %get-tuple-element.94.refs_4_, ...), custom_call_target="tpu_custom_call" | custom-call | flops 2793406464 | bytes 13860864 | tf_op jit(solution)/shard_map/pallas_call | solution.py:707
  307.3 1.5 collective-permute-start.10
  308.7 10.0 %shard_map.233 = (bf16[512,1152]{1,0:T(8,128)(2,1)}, f32[512,1152]{1,0:T(8,128)}) custom-call(s32[1]{0:T(128)} %constant.100.clone.1.active_ref, bf16[512,3072]{1,0:T(8,128)(2,1)} %get-tuple-element.95.act_ref, f32[512,1152]{1,0:T(8,128)} %get-tuple-element.91.refs_1_.middle_ref.refs_3_, f32[2,6,1152]{2,1,0:T(8,128)} %reshape_squeeze.7.refs_1_.mod_ref.refs_2_.refs_5_, ...), custom_call_target="tpu_custom_call" | custom-call | flops 3623878656 | bytes 11796480 | tf_op jit(solution)/shard_map/pallas_call | solution.py:369
  319.5 2.3 shard_map.236.refs_1_
  321.8 3.1 collective-permute-done.10.refs_0_
  325.7 2.3 shard_map.235.refs_0_
  328.0 8.2 %shard_map.237 = bf16[3072,1152]{1,0:T(8,128)(2,1)} custom-call(bf16[512,3072]{1,0:T(8,128)(2,1)} %get-tuple-element.95.act_ref, bf16[256,1152]{1,0:T(8,128)(2,1)} %shard_map.235.refs_0_, bf16[256,1152]{1,0:T(8,128)(2,1)} %shard_map.236.refs_1_), custom_call_target="tpu_custom_call" | custom-call | flops 3623878656 | bytes 7077888 | tf_op jit(solution)/shard_map/pallas_call | solution.py:752
  336.3 7.9 %shard_map.238.act_grad_ref = bf16[512,3072]{1,0:T(8,128)(2,1)} custom-call(bf16[256,1152]{1,0:T(8,128)(2,1)} %shard_map.235.refs_0_, bf16[256,1152]{1,0:T(8,128)(2,1)} %shard_map.236.refs_1_, bf16[3072,1152]{1,0:T(8,128)(2,1)} %all-gather.5.cloned.1.call-done.down_ref.refs_1_.refs_2_), custom_call_target="tpu_custom_call" | custom-call | flops 3623878656 | bytes 9437184 | tf_op jit(solution)/shard_map/pallas_call | solution.py:434
  344.2 23.9 %shard_map.239 = (f32[512,1152]{1,0:T(8,128)}, bf16[512,1152]{1,0:T(8,128)(2,1)}, bf16[512,3072]{1,0:T(8,128)(2,1)}, bf16[512,3072]{1,0:T(8,128)(2,1)}, bf16[512...) custom-call(bf16[512,3072]{1,0:T(8,128)(2,1)} %shard_map.238.act_grad_ref, bf16[512,3072]{1,0:T(8,128)(2,1)} %get-tuple-element.89.gate_ref, ...), custom_call_target="tpu_custom_call" | custom-call | flops 8606711808 | bytes 23592960 | tf_op jit(solution)/shard_map/pallas_call | solution.py:539
  368.1 13.6 %shard_map.242 = bf16[8,144,6144]{2,1,0:T(8,128)(2,1)} custom-call(bf16[512,1152]{1,0:T(8,128)(2,1)} %get-tuple-element.84.normed_ref.refs_0_.refs_1_, bf16[512,1152]{1,0:T(8,128)(2,1)} %get-tuple-element.84.normed_ref.refs_0_.refs_1_, bf16[512,3072]{1,0:T(8,128)(2,1)} %get-tuple-element.109.refs_2_, bf16[512,3072]{1,0:T(8,128)(2,1)} %get-tuple-element.110.refs_3_), custom_call_target="tpu_custom_call" | custom-call | flops 7247757312 | bytes 14155776 | tf_op jit(solution)/shard_map/pallas_call | solution.py:790
  381.7 8.6 %reduce-scatter.4.cloned.1.call-done = bf16[192,1152]{1,0:T(8,128)(2,1)} async-done(((bf16[3072,1152]{1,0:T(8,128)(2,1)}), bf16[192,1152]{1,0:T(8,128)(2,1)}) %reduce-scatter.4.cloned.1.call-update) | async-done | bytes 442384 | tf_op jit(solution)/shard_map/reduce_scatter | solution.py:838
  390.6 31.0 %shard_map.240 = (f32[512,1152]{1,0:T(8,128)}, bf16[512,3456]{1,0:T(8,128)(2,1)}, f32[2,4,1152]{2,1,0:T(4,128)}) custom-call(f32[512,2304]{1,0:T(8,128)} %get-tuple-element.86.refs_0_, bf16[512,1152]{1,0:T(8,128)(2,1)} %get-tuple-element.87.refs_1_, bf16[512,1152]{1,0:T(8,128)(2,1)} %get-tuple-element.102.refs_2_, f32[512,1152]{1,0:T(8,128)} %get-tuple-element.103.refs_3_, ...), custom_call_target="tpu_custom_call" | custom-call | flops 5586812928 | bytes 19759104 | tf_op jit(solution)/shard_map/pallas_call | solution.py:707
  422.5 1.8 collective-permute-start.12
  424.3 4.1 collective-permute-done.12
  428.9 4.4 collective-permute-done.13
  434.7 5.4 collective-permute-done.14
  440.8 11.5 %shard_map.241 = bf16[8,144,4608]{2,1,0:T(8,128)(2,1)} custom-call(bf16[512,1152]{1,0:T(8,128)(2,1)} %get-tuple-element.105.refs_0_, bf16[512,1152]{1,0:T(8,128)(2,1)} %get-tuple-element.106.refs_1_, bf16[512,3456]{1,0:T(8,128)(2,1)} %get-tuple-element.107.refs_2_, bf16[512,1152]{1,0:T(8,128)(2,1)} %get-tuple-element.108.refs_3_), custom_call_target="tpu_custom_call" | custom-call | flops 5435817984 | bytes 10616832 | tf_op jit(solution)/shard_map/pallas_call | solution.py:790
  453.8 21.5 %reduce-scatter.6.cloned.1.call-done = bf16[72,6144]{1,0:T(8,128)(2,1)} async-done(((bf16[1152,6144]{1,0:T(8,128)(2,1)}), bf16[72,6144]{1,0:T(8,128)(2,1)}) %reduce-scatter.6.cloned.1.call-update) | async-done | bytes 884752 | tf_op jit(solution)/shard_map/reduce_scatter | solution.py:838
  476.6 4.2 collective-permute-done.21
  480.9 3.6 collective-permute-done.22
  485.4 2.7 collective-permute-done.23
  488.3 1.6 convert_select_fusion
  491.8 1.5 collective-permute-start.16
  493.4 2.2 collective-permute-done.16
  495.6 1.2 collective-permute-start.17
  496.8 3.6 collective-permute-done.17
  500.6 4.3 collective-permute-done.18
  507.9 2.1 collective-permute-done.19
  510.2 1.7 convolution_bitcast_fusion
  512.4 4.3 fusion.9
  516.6 24.9 %reduce-scatter.8.cloned.1.call-done = bf16[72,4608]{1,0:T(8,128)(2,1)} async-done(((bf16[1152,4608]{1,0:T(8,128)(2,1)}), bf16[72,4608]{1,0:T(8,128)(2,1)}) %reduce-scatter.8.cloned.1.call-update) | async-done | bytes 663568 | tf_op jit(solution)/shard_map/reduce_scatter | solution.py:838
  541.5 1.7 fusion.8
  543.2 2.0 fusion.5
  (202 shorter events, 27.2 us)
Async XLA Ops:
  7.2 24.3 %copy-start = (bf16[1001,1152]{1,0:T(8,128)(2,1)S(1)}, bf16[1001,1152]{1,0:T(8,128)(2,1)}, u32[]{:S(2)}) copy-start(bf16[1001,1152]{1,0:T(8,128)(2,1)} %param.19) | copy-start | bytes 6918916
  7.2 2.9 copy-start.29
  7.2 2.9 copy-start.30
  7.2 137.0 %all-gather.3.cloned.1.call-start = ((), (), s32[]{:S(2)}) async-start(), calls=%async_computation.3 | async-start | bytes 26320896 | tf_op jit(solution)/shard_map/all_gather | solution.py:834
  7.3 7.0 %copy-start.28 = (s32[2,256]{1,0:T(2,128)S(1)}, s32[2,256]{1,0:T(2,128)}, u32[]{:S(2)}) copy-start(s32[2,256]{1,0:T(2,128)} %param.18) | copy-start | bytes 6148
  10.1 10.4 %copy-start.2 = (bf16[2,256,1152]{2,1,0:T(8,128)(2,1)S(1)}, bf16[2,256,1152]{2,1,0:T(8,128)(2,1)}, u32[]{:S(2)}) copy-start(bf16[2,256,1152]{2,1,0:T(8,128)(2,1)} %param.14) | copy-start | bytes 3538948
  10.1 179.4 %all-gather.5.cloned.1.call-start = ((), (), s32[]{:S(2)}) async-start(), calls=%async_computation.4 | async-start | bytes 7520256 | tf_op jit(solution)/shard_map/all_gather | solution.py:834
  10.2 11.5 %collective-permute-start = (s32[1,2,2]{2,1,0:T(2,128)S(1)}, s32[1,2,2]{2,1,0:T(2,128)S(1)}, u32[]{:S(2)}, u32[]{:S(2)}) collective-permute-start(s32[1,2,2]{2,1,0:T(2,128)S(1)} %add_bitcast_fusion.2), channel_id=1, source_target_pairs={{0,8},{1,9},{2,10},{3,11},{4,12},{5,13},{6,14},{7,15},{8,0},{9,1},... | collective-permute-start | bytes 56 | tf_op jit(solution)/shard_map/ppermute | solution.py:853
  16.3 0.7 copy-start.6
  16.3 1.5 copy-start.8
  21.7 10.5 %copy-start.3 = (bf16[1,72,6912]{2,1,0:T(8,128)(2,1)S(1)}, bf16[1,72,6912]{2,1,0:T(8,128)(2,1)}, u32[]{:S(2)}) copy-start(bf16[1,72,6912]{2,1,0:T(8,128)(2,1)} %param.20) | copy-start | bytes 2985988
  21.7 3.7 collective-permute-start.1
  25.6 3.6 collective-permute-start.2
  29.4 1.2 collective-permute-start.3
  31.0 1.5 copy-start.26
  32.1 0.8 copy-start.13
  32.2 0.7 copy-start.22
  32.2 4.3 copy-start.16
  32.6 1.9 collective-permute-start.4
  32.9 14.9 %copy-start.7 = (f32[512,18]{1,0:T(8,128)S(1)}, f32[512,18]{1,0:T(8,128)}, u32[]{:S(2)}) copy-start(f32[512,18]{1,0:T(8,128)} %copy-done.6) | copy-start | bytes 110596
  32.9 14.9 %copy-start.9 = (f32[512,18]{1,0:T(8,128)S(1)}, f32[512,18]{1,0:T(8,128)}, u32[]{:S(2)}) copy-start(f32[512,18]{1,0:T(8,128)} %copy-done.8) | copy-start | bytes 110596
  34.5 21.4 %copy-start.18 = (bf16[512,128]{1,0:T(8,128)(2,1)S(1)}, bf16[512,128]{1,0:T(8,128)(2,1)}, u32[]{:S(2)}) copy-start(bf16[512,128]{1,0:T(8,128)(2,1)} %fusion.39) | copy-start | bytes 393220
  34.5 21.4 %copy-start.19 = (bf16[512,128]{1,0:T(8,128)(2,1)S(1)}, bf16[512,128]{1,0:T(8,128)(2,1)}, u32[]{:S(2)}) copy-start(bf16[512,128]{1,0:T(8,128)(2,1)} %get-tuple-element.121) | copy-start | bytes 393220
  34.5 21.4 %copy-start.20 = (bf16[512,128]{1,0:T(8,128)(2,1)S(1)}, bf16[512,128]{1,0:T(8,128)(2,1)}, u32[]{:S(2)}) copy-start(bf16[512,128]{1,0:T(8,128)(2,1)} %get-tuple-element.122) | copy-start | bytes 393220
  34.8 109.7 %copy-start.31 = (f32[1,72]{1,0:T(1,128)S(1)}, f32[1,72]{1,0:T(1,128)}, u32[]{:S(2)}) copy-start(f32[1,72]{1,0:T(1,128)} %param.27) | copy-start | bytes 868
  34.8 109.7 %copy-start.32 = (f32[1,72]{1,0:T(1,128)S(1)}, f32[1,72]{1,0:T(1,128)}, u32[]{:S(2)}) copy-start(f32[1,72]{1,0:T(1,128)} %param.26) | copy-start | bytes 868
  34.8 12.8 %collective-permute-start.5 = (f32[4,2,6912]{2,1,0:T(2,128)S(1)}, f32[4,2,6912]{2,1,0:T(2,128)S(1)}, u32[]{:S(2)}, u32[]{:S(2)}) collective-permute-start(f32[4,2,6912]{2,1,0:T(2,128)S(1)} %dynamic-slice_bitcast_fusion.1), channel_id=1, source_target_pairs={{0,2},{1,3},{2,0},{3,1},{4,6},{5,7},{6,4},{7,5},{8,10},{9,11},{10,... | collective-permute-start | bytes 663560 | tf_op jit(solution)/shard_map/ppermute | solution.py:853
  47.8 7.8 %collective-permute-start.6 = (f32[2,2,6912]{2,1,0:T(2,128)S(1)}, f32[2,2,6912]{2,1,0:T(2,128)S(1)}, u32[]{:S(2)}, u32[]{:S(2)}) collective-permute-start(f32[2,2,6912]{2,1,0:T(2,128)S(1)} %dynamic-slice_bitcast_fusion.2), channel_id=1, source_target_pairs={{0,4},{1,5},{2,6},{3,7},{4,0},{5,1},{6,2},{7,3},{8,12},{9,13},{10,... | collective-permute-start | bytes 331784 | tf_op jit(solution)/shard_map/ppermute | solution.py:853
  55.7 6.8 %collective-permute-start.7 = (f32[1,2,6912]{2,1,0:T(2,128)S(1)}, f32[1,2,6912]{2,1,0:T(2,128)S(1)}, u32[]{:S(2)}, u32[]{:S(2)}) collective-permute-start(f32[1,2,6912]{2,1,0:T(2,128)S(1)} %constant_dynamic-slice_fusion), channel_id=1, source_target_pairs={{0,8},{1,9},{2,10},{3,11},{4,12},{5,13},{6,14},{7,15},{8,0},{9,1},... | collective-permute-start | bytes 165896 | tf_op jit(solution)/shard_map/ppermute | solution.py:853
  144.2 246.1 %reduce-scatter.4.cloned.1.call-start = ((), (), s32[]{:S(2)}) async-start(), calls=%async_computation.5 | async-start | bytes 7520256 | tf_op jit(solution)/shard_map/reduce_scatter | solution.py:838
  195.6 19.7 %collective-permute-start.9 = (bf16[256,1152]{1,0:T(8,128)(2,1)}, bf16[256,1152]{1,0:T(8,128)(2,1)S(1)}, u32[]{:S(2)}, u32[]{:S(2)}) collective-permute-start(bf16[256,1152]{1,0:T(8,128)(2,1)} %shard_map.225), channel_id=1, source_target_pairs={{0,16},{1,17},{2,18},{3,19},{4,20},{5,21},{6,22},{7,23},{8,24},{9,... | collective-permute-start | bytes 1769480 | tf_op jit(solution)/shard_map/ppermute | solution.py:980
  205.6 22.9 %collective-permute-start.8 = (bf16[256,1152]{1,0:T(8,128)(2,1)}, bf16[256,1152]{1,0:T(8,128)(2,1)S(1)}, u32[]{:S(2)}, u32[]{:S(2)}) collective-permute-start(bf16[256,1152]{1,0:T(8,128)(2,1)} %shard_map.224), channel_id=1, source_target_pairs={{0,16},{1,17},{2,18},{3,19},{4,20},{5,21},{6,22},{7,23},{8,24},{9,... | collective-permute-start | bytes 1769480 | tf_op jit(solution)/shard_map/ppermute | solution.py:980
  215.4 0.8 copy-start.17
  228.5 0.8 copy-start.15
  290.2 28.5 %collective-permute-start.11 = (bf16[256,1152]{1,0:T(8,128)(2,1)}, bf16[256,1152]{1,0:T(8,128)(2,1)S(1)}, u32[]{:S(2)}, u32[]{:S(2)}) collective-permute-start(bf16[256,1152]{1,0:T(8,128)(2,1)} %shard_map.232), channel_id=1, source_target_pairs={{16,0},{17,1},{18,2},{19,3},{20,4},{21,5},{22,6},{23,7},{24,8},{25... | collective-permute-start | bytes 1769480 | tf_op jit(solution)/shard_map/ppermute | solution.py:1012
  307.3 17.6 %collective-permute-start.10 = (bf16[256,1152]{1,0:T(8,128)(2,1)}, bf16[256,1152]{1,0:T(8,128)(2,1)S(1)}, u32[]{:S(2)}, u32[]{:S(2)}) collective-permute-start(bf16[256,1152]{1,0:T(8,128)(2,1)} %shard_map.234), channel_id=1, source_target_pairs={{16,0},{17,1},{18,2},{19,3},{20,4},{21,5},{22,6},{23,7},{24,8},{25... | collective-permute-start | bytes 1769480 | tf_op jit(solution)/shard_map/ppermute | solution.py:1012
  318.7 0.8 copy-start.10
  324.9 0.8 copy-start.11
  336.2 139.1 %reduce-scatter.6.cloned.1.call-start = ((), (), s32[]{:S(2)}) async-start(), calls=%async_computation.6 | async-start | bytes 15040512 | tf_op jit(solution)/shard_map/reduce_scatter | solution.py:838
  390.3 151.2 %reduce-scatter.8.cloned.1.call-start = ((), (), s32[]{:S(2)}) async-start(), calls=%async_computation.7 | async-start | bytes 11280384 | tf_op jit(solution)/shard_map/reduce_scatter | solution.py:838
  390.6 31.8 %copy-start.24 = (f32[2,4,1152]{2,1,0:T(4,128)S(1)}, f32[2,4,1152]{2,1,0:T(4,128)}, u32[]{:S(2)}) copy-start(f32[2,4,1152]{2,1,0:T(4,128)} %get-tuple-element.114) | copy-start | bytes 110596
  422.5 5.9 %collective-permute-start.12 = (bf16[1,2,6912]{2,1,0:T(2,128)(2,1)S(1)}, bf16[1,2,6912]{2,1,0:T(2,128)(2,1)S(1)}, u32[]{:S(2)}, u32[]{:S(2)}) collective-permute-start(bf16[1,2,6912]{2,1,0:T(2,128)(2,1)S(1)} %convert_element_type.143), channel_id=1, source_target_pairs={{0,8},{1,9},{2,10},{3,11},{4,12},{5,13},{6,14},{7,15},{8,0},{9,1},... | collective-permute-start | bytes 82952 | tf_op jit(solution)/shard_map/ppermute | solution.py:853
  428.5 4.9 collective-permute-start.13
  433.7 6.3 %collective-permute-start.14 = (bf16[4,2,6912]{2,1,0:T(2,128)(2,1)S(1)}, bf16[4,2,6912]{2,1,0:T(2,128)(2,1)S(1)}, u32[]{:S(2)}, u32[]{:S(2)}) collective-permute-start(bf16[4,2,6912]{2,1,0:T(2,128)(2,1)S(1)} %bitcast.254), channel_id=1, source_target_pairs={{0,2},{1,3},{2,0},{3,1},{4,6},{5,7},{6,4},{7,5},{8,10},{9,11},{10,... | collective-permute-start | bytes 331784 | tf_op jit(solution)/shard_map/ppermute | solution.py:853
  440.7 11.6 %collective-permute-start.15 = (bf16[8,2,6912]{2,1,0:T(2,128)(2,1)S(1)}, bf16[8,2,6912]{2,1,0:T(2,128)(2,1)S(1)}, u32[]{:S(2)}, u32[]{:S(2)}) collective-permute-start(bf16[8,2,6912]{2,1,0:T(2,128)(2,1)S(1)} %bitcast.246), channel_id=1, source_target_pairs={{0,1},{1,0},{2,3},{3,2},{4,5},{5,4},{6,7},{7,6},{8,9},{9,8},{10,11... | collective-permute-start | bytes 663560 | tf_op jit(solution)/shard_map/ppermute | solution.py:853
  475.3 0.8 copy-start.25
  475.3 12.9 %copy-start.5 = (f32[512,1152]{1,0:T(8,128)S(1)}, f32[512,1152]{1,0:T(8,128)}, u32[]{:S(2)}) copy-start(f32[512,1152]{1,0:T(8,128)} %get-tuple-element.104) | copy-start | bytes 7077892
  476.2 4.5 collective-permute-start.21
  480.8 3.6 collective-permute-start.22
  484.5 3.7 collective-permute-start.23
  488.2 1.7 collective-permute-start.24
  488.3 2.1 copy-start.21
  488.3 3.1 copy-start.4
  489.9 3.4 copy-start.12
  491.8 3.8 collective-permute-start.16
  495.6 4.9 collective-permute-start.17
  496.8 13.4 %copy-start.23 = (bf16[32,72]{1,0:T(8,128)(2,1)S(1)}, bf16[32,72]{1,0:T(8,128)(2,1)}, u32[]{:S(2)}) copy-start(bf16[32,72]{1,0:T(8,128)(2,1)} %copy-done.22) | copy-start | bytes 13828
  500.5 4.4 collective-permute-start.18
  504.9 5.1 collective-permute-start.19
  510.1 2.2 copy-start.14
  510.1 2.2 copy-start.27
  510.1 1.8 collective-permute-start.20
  512.2 33.0 %copy-start.1 = (bf16[1001,1152]{1,0:T(8,128)(2,1)S(1)}, bf16[1001,1152]{1,0:T(8,128)(2,1)}, u32[]{:S(2)}) copy-start(bf16[1001,1152]{1,0:T(8,128)(2,1)} %param.19) | copy-start | bytes 6918916
Sparse Core Ops, SparseCore 0:
  10.2 133.9 all-gather.2
  145.8 43.6 all-gather.4
  336.3 53.9 reduce-scatter.3
  392.6 82.6 reduce-scatter.5
  477.6 63.8 reduce-scatter.7

commit v5 on v4

--- a/solution.py
+++ b/solution.py
@@ -102,16 +102,15 @@
 
 
 def rotated(raw, part, tables, keep_scale=None):
-    cos_ref, sin_ref, gain_ref, sum_ref, spread_ref, repeat_ref, head_size = tables
+    cos, sin, gain_ref, summing, spreading, head_size = tables
     quarter = head_size // 4
-    squares = dot((raw * raw).astype(bf16), sum_ref[...])
+    squares = dot((raw * raw).astype(bf16), summing)
     scale = lax.rsqrt(squares * (1.0 / head_size) + epsilon)
-    scale = dot(two_terms(scale), spread_ref[...])
+    scale = dot(two_terms(scale), spreading)
     if keep_scale is not None:
         keep_scale[part] = scale
     scaled = raw * scale * gain_ref[part : part + 1]
     first_half = first_half_mask((1, raw.shape[1]), quarter)
-    cos, sin = dot(cos_ref[...], repeat_ref[...]), dot(sin_ref[...], repeat_ref[...])
     return (scaled * cos + partner(scaled, first_half, quarter) * sin).astype(bf16)
 
 
@@ -129,7 +128,6 @@
     else:
         middle_ref, normed_two_ref, weight, mixed, sems = refs
     head_size = width // heads
-    tables = (cos_ref, sin_ref, gain_ref, sum_ref, spread_ref, repeat_ref, head_size)
 
     def fetch(part):
         return pltpu.make_async_copy(
@@ -157,6 +155,8 @@
         flow = flow + received_ref[...].astype(f32)
     mod = mod_ref[0]
     normed = (flow * inverse_rms(flow) * (1.0 + mod[1:2]) + mod[0:1]).astype(bf16)
+    cos, sin = dot(cos_ref[...], repeat_ref[...]), dot(sin_ref[...], repeat_ref[...])
+    tables = (cos, sin, gain_ref, sum_ref[...], spread_ref[...], head_size)
     raw = dot(normed, whole_rows(query_weight, places))
     if keep:
         held[7][...] = flow.astype(bf16)
@@ -210,7 +210,7 @@
     tokens = x.shape[0]
     patches = tokens // images
     heads = width // tables[-1]
-    arrays = tables[:-1]
+    cos, sin, *matrices, unused = tables
     parts, rows, unused = joined.shape
     row = lambda columns: pl.BlockSpec((patches, columns), lambda image: (first + image, 0))
     fixed = lambda array: pl.BlockSpec(array.shape, lambda image: (0,) * array.ndim)
@@ -250,16 +250,13 @@
         + [
             row(width),
             pl.BlockSpec((1, 6, width), lambda image: (first + image, 0, 0)),
-            row(arrays[0].shape[1]),
-            row(arrays[1].shape[1]),
+            row(cos.shape[1]),
+            row(sin.shape[1]),
             fixed(gain),
-            fixed(arrays[2]),
-            fixed(arrays[3]),
-            fixed(arrays[4]),
-            pl.BlockSpec((parts, rows, width), lambda image: (0, 0, 0)),
-            anywhere,
         ]
-        + [anywhere] * len(made),
+        + [fixed(matrix) for matrix in matrices]
+        + [pl.BlockSpec((parts, rows, width), lambda image: (0, 0, 0))]
+        + [anywhere] * (1 + len(made)),
         out_specs=[anywhere if keep else row(columns) for columns, kind in shapes],
         out_shape=[jax.ShapeDtypeStruct((tokens, columns), kind) for columns, kind in shapes],
         input_output_aliases={inputs + index: index for index in range(len(made))},
@@ -269,7 +266,7 @@
             2 * count * patches * width * (4 * width + 2 * patches),
             8 * width * width + count * patches * width * 20,
         ),
-    )(*extra, x, mod, arrays[0], arrays[1], gain, *arrays[2:], joined, joined, *made)
+    )(*extra, x, mod, cos, sin, gain, *matrices, joined, joined, *made)
 
 
 def pack_columns(matrices, pieces):
@@ -297,35 +294,32 @@
     )(*matrices)
 
 
-def gate_up_kernel(places, keep, normed_ref, gate_ref, up_ref, *outs):
-    normed = normed_ref[...]
-    gate = dot(normed, whole_rows(gate_ref, places))
-    up = dot(normed, whole_rows(up_ref, places))
-    outs[0][...] = (gate * (1.0 / (1.0 + jnp.exp(-gate))) * up).astype(bf16)
-    if keep:
-        outs[1][...] = gate.astype(bf16)
-        outs[2][...] = up.astype(bf16)
-
-
-def gate_up(normed_two, joined, hidden, walked, keep):
+def gate_up(normed_two, joined, hidden, walked):
     tokens, width = normed_two.shape
     step = 512
     base = 4 * width // step
     count = hidden // step
     parts, rows, unused = joined.shape
-    shapes = 3 if keep else 1
+    places = places_of(parts, walked)
+
+    def body(normed_ref, gate_ref, up_ref, act_ref):
+        normed = normed_ref[...]
+        gate = dot(normed, whole_rows(gate_ref, places))
+        up = dot(normed, whole_rows(up_ref, places))
+        act_ref[...] = (gate * (1.0 / (1.0 + jnp.exp(-gate))) * up).astype(bf16)
+
     return pl.pallas_call(
-        functools.partial(gate_up_kernel, places_of(parts, walked), keep),
+        body,
         grid=(count,),
         in_specs=[
             pl.BlockSpec((tokens, width), lambda i: (0, 0)),
             pl.BlockSpec((parts, rows, step), lambda i: (0, 0, base + i)),
             pl.BlockSpec((parts, rows, step), lambda i: (0, 0, base + count + i)),
         ],
-        out_specs=[pl.BlockSpec((tokens, step), lambda i: (0, i))] * shapes,
-        out_shape=[jax.ShapeDtypeStruct((tokens, hidden), bf16)] * shapes,
+        out_specs=pl.BlockSpec((tokens, step), lambda i: (0, i)),
+        out_shape=jax.ShapeDtypeStruct((tokens, hidden), bf16),
         compiler_params=params(),
-        cost_estimate=cost(4 * tokens * width * hidden, 4 * width * hidden + 2 * shapes * tokens * hidden),
+        cost_estimate=cost(4 * tokens * width * hidden, 4 * width * hidden + 2 * tokens * hidden),
     )(normed_two, joined, joined)
 
 
@@ -442,8 +436,8 @@
     )(*mlp_grads, down)
 
 
-def mlp_backward(cot, backs, mlp, act_grad, gate, up, joined, middle, branch, mod, walked, keep):
-    tokens, hidden = gate.shape
+def mlp_backward(cot, backs, act_grad, forward, joined, middle, mod, walked, sums_of):
+    tokens, hidden = act_grad.shape
     images, unused, width = mod.shape
     patches = tokens // images
     parts, rows, unused = joined.shape
@@ -451,25 +445,27 @@
     step = 512
     base = 4 * width // step
     count = hidden // step
+    fresh, keep = len(forward) == 1, sums_of is not None
     whole = pl.BlockSpec((tokens, width), lambda i: (0, 0))
     block = pl.BlockSpec((tokens, step), lambda i: (0, i))
     anywhere = pl.BlockSpec(memory_space=pl.ANY)
-    late = [cot, middle] + ([mlp, branch] if keep else [])
-
-    def body(act_grad_ref, gate_ref, up_ref, gate_weight, up_weight, mod_ref, joined_ref, *refs):
-        back_refs, refs = refs[: len(backs)], refs[len(backs) :]
-        sources, refs = refs[: len(late)], refs[len(late) :]
-        sems, refs = refs[-1], refs[:-1]
-        copies, refs = refs[-len(late) :], refs[: -len(late)]
+    late = [cot, middle] + (list(sums_of) if keep else [])
+
+    def body(act_grad_ref, gate_weight_ref, up_weight_ref, mod_ref, joined_ref, *refs):
+        refs = list(refs)
+
+        def taken(number):
+            first = refs[:number]
+            del refs[:number]
+            return first
+
+        forward_refs, back_refs, sources = taken(len(forward)), taken(len(backs)), taken(len(late))
+        middle_grad_ref, mixed_grad_ref = taken(2)
+        fresh_refs = taken(3 if fresh else 0)
+        kept_refs = taken(4 if keep else 0)
+        total, out_weight, sem = taken(3)
+        copies, (sems,) = taken(len(late)), refs
         cot_ref, middle_ref = copies[:2]
-        if keep:
-            mlp_ref, branch_ref = copies[2:]
-        middle_grad_ref, mixed_grad_ref = refs[:2]
-        refs = refs[2:]
-        if keep:
-            gate_grad_ref, up_grad_ref, branch_grad_ref, sums_ref = refs[:4]
-            refs = refs[4:]
-        total, out_weight, sem = refs
         index = pl.program_id(0)
         fetches = [
             pltpu.make_async_copy(joined_ref.at[:, :, pl.ds(3 * width, width)], out_weight, sem)
@@ -483,16 +479,25 @@
             for fetch in fetches:
                 fetch.start()
 
-        gate_val, up_val = gate_ref[...].astype(f32), up_ref[...].astype(f32)
-        sigma = 1.0 / (1.0 + jnp.exp(-gate_val))
+        gate_weight = whole_rows(gate_weight_ref, places)
+        up_weight = whole_rows(up_weight_ref, places)
+        if fresh:
+            normed = forward_refs[0][...]
+            gate, up = dot(normed, gate_weight), dot(normed, up_weight)
+        else:
+            gate, up = (ref[...].astype(f32) for ref in forward_refs)
+        sigma = 1.0 / (1.0 + jnp.exp(-gate))
         slope = act_grad_ref[...].astype(f32) * sigma
-        gate_grad = (slope * up_val * (1.0 + gate_val * (1.0 - sigma))).astype(bf16)
-        up_grad = (slope * gate_val).astype(bf16)
+        gate_grad = (slope * up * (1.0 + gate * (1.0 - sigma))).astype(bf16)
+        up_grad = (slope * gate).astype(bf16)
+        if fresh:
+            fresh_refs[0][...] = (gate * sigma * up).astype(bf16)
+            fresh_refs[1][...] = gate.astype(bf16)
+            fresh_refs[2][...] = up.astype(bf16)
         if keep:
-            gate_grad_ref[...] = gate_grad
-            up_grad_ref[...] = up_grad
-        term = dot_right(gate_grad, whole_rows(gate_weight, places))
-        term = term + dot_right(up_grad, whole_rows(up_weight, places))
+            kept_refs[0][...] = gate_grad
+            kept_refs[1][...] = up_grad
+        term = dot_right(gate_grad, gate_weight) + dot_right(up_grad, up_weight)
 
         @pl.when(index == 0)
         def _():
@@ -521,16 +526,20 @@
                 branch_grad = (mod[2:3] * middle_grad).astype(bf16)
                 mixed_grad_ref[at] = dot_right(branch_grad, matrix).astype(bf16)
                 if keep:
-                    branch_grad_ref[at] = branch_grad
+                    mlp_ref, branch_ref = copies[2:]
+                    kept_refs[2][at] = branch_grad
                     terms = [middle_grad * branch_ref[at], grad, grad * normal, out_grad * mlp_ref[at]]
                     for place, value in enumerate(terms):
-                        sums_ref[image, place : place + 1] = jnp.sum(value, axis=0, keepdims=True)
+                        kept_refs[3][image, place : place + 1] = jnp.sum(value, axis=0, keepdims=True)
 
     out_shapes = [
         jax.ShapeDtypeStruct((tokens, width), f32),
         jax.ShapeDtypeStruct((tokens, width), bf16),
     ]
     out_specs = [whole, whole]
+    if fresh:
+        out_shapes += [jax.ShapeDtypeStruct((tokens, hidden), bf16)] * 3
+        out_specs += [block] * 3
     if keep:
         out_shapes += [jax.ShapeDtypeStruct((tokens, hidden), bf16)] * 2
         out_shapes += [jax.ShapeDtypeStruct((tokens, width), bf16)]
@@ -541,13 +550,12 @@
         grid=(count,),
         in_specs=[
             block,
-            block,
-            block,
             pl.BlockSpec((parts, rows, step), lambda i: (0, 0, base + i)),
             pl.BlockSpec((parts, rows, step), lambda i: (0, 0, base + count + i)),
             pl.BlockSpec(mod.shape, lambda i: (0, 0, 0)),
             anywhere,
         ]
+        + [whole if fresh else block] * len(forward)
         + [pl.BlockSpec((patches, width), lambda i: (0, 0))] * len(backs)
         + [anywhere] * len(late),
         out_specs=out_specs,
@@ -561,14 +569,14 @@
         + [pltpu.SemaphoreType.DMA((len(late),))],
         compiler_params=params(),
         cost_estimate=cost(
-            2 * tokens * width * (2 * hidden + width), 4 * width * hidden + 6 * tokens * hidden
+            2 * tokens * width * (4 * hidden + width), 4 * width * hidden + 6 * tokens * hidden
         ),
-    )(act_grad, gate, up, joined, joined, mod, joined, *backs, *late)
+    )(act_grad, joined, joined, mod, joined, *forward, *backs, *late)
 
 
 def attention_backward_kernel(heads, places, first, keep, refs):
-    raw_ref, value_ref, mixed_grad_ref, middle_grad_hbm, x_hbm, mod_ref = refs[:6]
-    cos_ref, sin_ref, gain_ref, sum_ref, spread_ref, repeat_ref, joined_ref = refs[6:13]
+    raw_hbm, value_hbm, mixed_grad_hbm, middle_grad_hbm, x_hbm = refs[:5]
+    mod_ref, cos_ref, sin_ref, gain_ref, sum_ref, spread_ref, repeat_ref, joined_ref = refs[5:13]
     refs = refs[13:]
     if keep:
         flow_grad_ref, qkv_grad_ref, sums_ref = refs[:3]
@@ -576,18 +584,29 @@
     else:
         back_ref = refs[0]
         refs = refs[1:]
-    weight, scales, query_total, key_total, value_total, middle_grad_ref, x_ref, sems = refs
+    weight, scales, query_total, key_total, value_total = refs[:5]
+    raw_ref, value_ref, mixed_grad_ref, middle_grad_ref, x_ref, sems = refs[5:]
     patches, width = x_ref.shape
     head_size = width // heads
     quarter = head_size // 4
     factor = head_size ** (-0.5)
     image = pl.program_id(0)
-    tables = (cos_ref, sin_ref, gain_ref, sum_ref, spread_ref, repeat_ref, head_size)
     rows = pl.ds((first + image) * patches, patches)
-    late = [
-        pltpu.make_async_copy(x_hbm.at[rows], x_ref, sems.at[3]),
-        pltpu.make_async_copy(middle_grad_hbm.at[rows], middle_grad_ref, sems.at[4]),
+    sources = [
+        raw_hbm.at[rows, pl.ds(0, width)],
+        raw_hbm.at[rows, pl.ds(width, width)],
+        value_hbm.at[rows],
+        mixed_grad_hbm.at[rows],
+        middle_grad_hbm.at[rows],
+        x_hbm.at[rows],
     ]
+    targets = [raw_ref.at[0], raw_ref.at[1], value_ref, mixed_grad_ref, middle_grad_ref, x_ref]
+    copies = [
+        pltpu.make_async_copy(source, target, sems.at[3 + which])
+        for which, (source, target) in enumerate(zip(sources, targets))
+    ]
+    for copy in copies[:4]:
+        copy.start()
 
     def fetch(part):
         return pltpu.make_async_copy(
@@ -599,12 +618,18 @@
         for part in range(3):
             fetch(part).start()
 
-    for copy in late:
+    for copy in copies[4:]:
         copy.start()
     first_half = first_half_mask((1, width), quarter)
-    raws = [raw_ref[:, part * width : (part + 1) * width] for part in range(2)]
-    queries = rotated(raws[0], 0, tables, scales)
-    keys = rotated(raws[1], 1, tables, scales)
+    cos, sin = dot(cos_ref[...], repeat_ref[...]), dot(sin_ref[...], repeat_ref[...])
+    summing, spreading = sum_ref[...], spread_ref[...]
+    tables = (cos, sin, gain_ref, summing, spreading, head_size)
+    copies[0].wait()
+    queries = rotated(raw_ref[0], 0, tables, scales)
+    copies[1].wait()
+    keys = rotated(raw_ref[1], 1, tables, scales)
+    for copy in copies[2:4]:
+        copy.wait()
     values, mixed_grad = value_ref[...], mixed_grad_ref[...]
     query_total[...] = jnp.zeros_like(query_total)
     key_total[...] = jnp.zeros_like(key_total)
@@ -632,15 +657,14 @@
 
     def raw_grad(part, total):
         turned = total[...] * factor
-        cos, sin = dot(cos_ref[...], repeat_ref[...]), dot(sin_ref[...], repeat_ref[...])
         grad = turned * cos + partner(turned * sin, first_half, quarter)
         scale = scales[part]
-        normal = raw_ref[:, part * width : (part + 1) * width] * scale
+        normal = raw_ref[part] * scale
         if keep:
             sums_ref[0, 2 + part : 3 + part] = jnp.sum(grad * normal, axis=0, keepdims=True)
         grad = grad * gain_ref[part : part + 1]
-        mean = dot((grad * normal).astype(bf16), sum_ref[...]) * (1.0 / head_size)
-        mean = dot(two_terms(mean), spread_ref[...])
+        mean = dot((grad * normal).astype(bf16), summing) * (1.0 / head_size)
+        mean = dot(two_terms(mean), spreading)
         return (scale * (grad - normal * mean)).astype(bf16)
 
     def arrived(part):
@@ -657,7 +681,7 @@
             qkv_grad_ref[:, part * width : (part + 1) * width] = parts[part]
         term = dot_right(parts[part], arrived(part))
         grad = term if grad is None else grad + term
-    for copy in late:
+    for copy in copies[4:]:
         copy.wait()
     mod = mod_ref[0]
     flow = x_ref[...].astype(f32)
@@ -681,7 +705,7 @@
     patches = x.shape[0] // images
     tokens = count * patches
     heads = width // tables[-1]
-    arrays = tables[:-1]
+    cos, sin, *matrices, unused = tables
     parts, rows, unused = joined.shape
     row = lambda columns: pl.BlockSpec((patches, columns), lambda image: (first + image, 0))
     token = lambda columns: pl.BlockSpec((patches, columns), lambda image: (image, 0))
@@ -707,21 +731,15 @@
     return pl.pallas_call(
         body,
         grid=(count,),
-        in_specs=[
-            row(2 * width),
-            row(width),
-            row(width),
-            anywhere,
-            anywhere,
+        in_specs=[anywhere] * 5
+        + [
             pl.BlockSpec((1, 6, width), lambda image: (first + image, 0, 0)),
-            row(arrays[0].shape[1]),
-            row(arrays[1].shape[1]),
+            row(cos.shape[1]),
+            row(sin.shape[1]),
             fixed(gain),
-            fixed(arrays[2]),
-            fixed(arrays[3]),
-            fixed(arrays[4]),
-            anywhere,
-        ],
+        ]
+        + [fixed(matrix) for matrix in matrices]
+        + [anywhere],
         out_specs=out_specs,
         out_shape=out_shapes,
         scratch_shapes=[
@@ -730,34 +748,63 @@
             pltpu.VMEM((patches, width), f32),
             pltpu.VMEM((patches, width), f32),
             pltpu.VMEM((patches, width), f32),
+            pltpu.VMEM((2, patches, width), f32),
+            pltpu.VMEM((patches, width), bf16),
+            pltpu.VMEM((patches, width), bf16),
             pltpu.VMEM((patches, width), f32),
             pltpu.VMEM((patches, width), bf16),
-            pltpu.SemaphoreType.DMA((5,)),
+            pltpu.SemaphoreType.DMA((9,)),
         ],
         compiler_params=params(),
         cost_estimate=cost(
             2 * tokens * width * (3 * width + 5 * patches),
             6 * width * width + tokens * width * 20,
         ),
-    )(raw, value, mixed_grad, middle_grad, x, mod, arrays[0], arrays[1], gain, *arrays[2:], joined)
-
-
-def down_grad(mlp_grads, act, step):
+    )(raw, value, mixed_grad, middle_grad, x, mod, cos, sin, gain, *matrices, joined)
+
+
+def down_grad(mlp_grads, cot, back, act, mod, step):
     tokens, hidden = act.shape
-    width = mlp_grads[0].shape[1]
-
-    def body(act_ref, *refs):
-        refs[-1][...] = dot_left(act_ref[...], stacked(refs[:-1])).astype(bf16)
+    images, unused, width = mod.shape
+    patches = tokens // images
+    last = images - 1
+
+    def body(act_ref, cot_ref, back_ref, mod_ref, *refs):
+        given, (out_ref, last_ref, mlp_grad) = refs[:last], refs[last:]
+
+        @pl.when(pl.program_id(0) == 0)
+        def _():
+            grads = incoming(cot_ref, [back_ref], 0, slice(0, patches))
+            value = (mod_ref[last, 5:6] * grads).astype(bf16)
+            last_ref[...] = value
+            for image in range(last):
+                mlp_grad[image * patches : (image + 1) * patches] = given[image][...]
+            mlp_grad[last * patches :] = value
+
+        out_ref[...] = dot_left(act_ref[...], mlp_grad[...]).astype(bf16)
 
     return pl.pallas_call(
         body,
         grid=(hidden // step,),
-        in_specs=[pl.BlockSpec((tokens, step), lambda i: (0, i))] + whole_specs(mlp_grads),
-        out_specs=pl.BlockSpec((step, width), lambda i: (i, 0)),
-        out_shape=jax.ShapeDtypeStruct((hidden, width), bf16),
+        in_specs=[
+            pl.BlockSpec((tokens, step), lambda i: (0, i)),
+            pl.BlockSpec((patches, width), lambda i: (last, 0)),
+            pl.BlockSpec((patches, width), lambda i: (0, 0)),
+            pl.BlockSpec(mod.shape, lambda i: (0, 0, 0)),
+        ]
+        + whole_specs(mlp_grads),
+        out_specs=[
+            pl.BlockSpec((step, width), lambda i: (i, 0)),
+            pl.BlockSpec((patches, width), lambda i: (0, 0)),
+        ],
+        out_shape=[
+            jax.ShapeDtypeStruct((hidden, width), bf16),
+            jax.ShapeDtypeStruct((patches, width), bf16),
+        ],
+        scratch_shapes=[pltpu.VMEM((tokens, width), bf16)],
         compiler_params=params(),
         cost_estimate=cost(2 * tokens * width * hidden, 2 * width * hidden),
-    )(act, *mlp_grads)
+    )(act, cot, back, mod, *mlp_grads)
 
 
 def matrix_grad_kernel(places, counts, *refs):
@@ -971,7 +1018,7 @@
     middle, normed_two = attention_forward(
         flat, None, mod, tables, gain, joined, walked, 0, images
     )
-    (act,) = gate_up(normed_two, joined, hidden, walked, False)
+    act = gate_up(normed_two, joined, hidden, walked)
     received = []
     for image in range(images):
         (early,) = down_projection(
@@ -987,10 +1034,9 @@
             own, received[image], mod, tables, gain, joined, walked, image, 1, kept
         )
     normed, raw, values, attended, branch, middle, normed_two, layer_in = kept
-    act, gate, up = gate_up(normed_two, joined, hidden, walked, True)
-
-    middle_grad, mixed_grad = mlp_backward(
-        cot, [], None, act_grad, gate, up, joined, middle, None, mod, walked, False
+
+    middle_grad, mixed_grad, act, gate, up = mlp_backward(
+        cot, [], act_grad, [normed_two], joined, middle, mod, walked, None
     )
     backs = []
     for image in range(images):
@@ -1017,14 +1063,15 @@
 
     late_cot, unused = lax.optimization_barrier((cot, mlp))
     mlp_grads = [
-        mlp_gradient(late_cot, [back], mod, image, 1) for image, back in enumerate(backs)
+        mlp_gradient(late_cot, [back], mod, image, 1) for image, back in enumerate(backs[:-1])
     ]
-    down_term = down_grad(mlp_grads, act, hidden // 4)
+    down_term, mlp_grad = down_grad(mlp_grads, late_cot, backs[-1], act, mod, hidden // 4)
+    mlp_grads = [*mlp_grads, mlp_grad]
     down_term, mlp_grads = lax.optimization_barrier((down_term, mlp_grads))
     down_part = scatter_walk(down_term, count)
     act_grad = act_backward(mlp_grads, down, hidden // 2)
     middle_grad, mixed_grad, gate_grad, up_grad, branch_grad, mlp_sums = mlp_backward(
-        cot, backs, mlp, act_grad, gate, up, joined, middle, branch, mod, walked, True
+        cot, backs, act_grad, [gate, up], joined, middle, mod, walked, [mlp, branch]
     )
 
     def matrix_part(inputs, grads, step, before):

time: 558 us -> 550 us (0.986)
  Pallas kernels: 258 us -> 249 us
    pallas_call x7 -> x6, Pallas kernels: 132 us -> 124 us  [the longest x3 61 us: attention_backward(): pl.pallas_call(body, grid=(count,), in_specs=[anywhere] * 5 + [pl.BlockSp...]
where the time goes in v5:
time: 550 us; the launch traced here: 544 us
  Pallas kernels  249 us (45%)
  waiting for transfers between devices  218 us (40%)
  starting transfers between devices  24.6 us (4%)
  other arithmetic  20.1 us (4%)
  between operations  15.2 us (3%)
  local copies, waits for them, and re-layouts  10.1 us (2%)
  matrix products  7.2 us (1%)
    all_gather x2, waiting for transfers between devices, gather_walk(): lax.all_gather(rows, 'dp', axis=0, tiled=True, axis_index_groups=[walk_of...  92.3 us
    ppermute x20, waiting for transfers between devices, swapped(): lax.ppermute(block, 'dp', [(device, device ^ bit) for device in range(cou...  63.9 us
    pallas_call x3, Pallas kernels, attention_backward(): pl.pallas_call(body, grid=(count,), in_specs=[anywhere] * 5 + [pl.BlockSp...  61 us
    reduce_scatter x3, waiting for transfers between devices, scatter_walk(): lax.psum_scatter(rows, 'dp', scatter_dimension=0, tiled=True, axis_index_...  56.6 us
    pallas_call x2, Pallas kernels, mlp_backward(): pl.pallas_call(body, grid=(count,), in_specs=[block, pl.BlockSpec((parts,...  50 us
    pallas_call x3, Pallas kernels, attention_forward(): pl.pallas_call(body, grid=(count,), in_specs=[pl.BlockSpec((patches, widt...  45 us
    pallas_call x2, Pallas kernels, matrix_grad(): pl.pallas_call(functools.partial(matrix_grad_kernel, places_of(parts, wal...  25.1 us
    pallas_call x3, Pallas kernels, down_projection(): pl.pallas_call(body, grid_spec=pltpu.PrefetchScalarGridSpec(num_scalar_pr...  22.3 us
  transfers between devices with their start and end apart: 30, of which 23 were waited for; matrix products, arithmetic and copies ran while one was open for 5% of the time, Pallas kernels for 32%

profile of v5, /device:TPU:0, one launch (start us, length us, event | category | flops | bytes accessed | tf_op | source)
XLA Modules:
  0.0 544.3 jit_solution(2747396222051665525)
XLA Ops:
  7.3 2.8 shard_map.221
  10.2 4.1 collective-permute-start
  14.4 1.9 fusion.17
  20.5 1.2 broadcast_select_fusion.refs_1_
  21.7 1.6 collective-permute-start.1
  23.4 2.0 collective-permute-done.1
  25.6 1.5 collective-permute-start.2
  27.1 2.1 collective-permute-done.2
  29.4 1.2 collective-permute-done.3
  32.9 1.5 collective-permute-done.4
  34.8 1.7 collective-permute-start.5
  36.5 1.1 add_convert_fusion
  37.6 10.0 %collective-permute-done.5 = f32[4,2,6912]{2,1,0:T(2,128)S(1)} collective-permute-done((f32[4,2,6912]{2,1,0:T(2,128)S(1)}, f32[4,2,6912]{2,1,0:T(2,128)S(1)}, u32[]{:S(2)}, u32[]{:S(2)}) %collective-permute-start.5) | collective-permute-done | bytes 221216 | tf_op jit(solution)/shard_map/ppermute | solution.py:900
  48.1 7.4 %collective-permute-done.6 = f32[2,2,6912]{2,1,0:T(2,128)S(1)} collective-permute-done((f32[2,2,6912]{2,1,0:T(2,128)S(1)}, f32[2,2,6912]{2,1,0:T(2,128)S(1)}, u32[]{:S(2)}, u32[]{:S(2)}) %collective-permute-start.6) | collective-permute-done | bytes 110624 | tf_op jit(solution)/shard_map/ppermute | solution.py:900
  56.8 5.7 %collective-permute-done.7 = f32[1,2,6912]{2,1,0:T(2,128)S(1)} collective-permute-done((f32[1,2,6912]{2,1,0:T(2,128)S(1)}, f32[1,2,6912]{2,1,0:T(2,128)S(1)}, u32[]{:S(2)}, u32[]{:S(2)}) %collective-permute-start.7) | collective-permute-done | bytes 55328 | tf_op jit(solution)/shard_map/ppermute | solution.py:900
  63.1 81.1 %all-gather.3.cloned.1.call-done = bf16[1152,10752]{1,0:T(8,128)(2,1)} async-done(((bf16[72,10752]{1,0:T(8,128)(2,1)}), bf16[1152,10752]{1,0:T(8,128)(2,1)}) %all-gather.3.cloned.1.call-update) | async-done | bytes 24772624 | tf_op jit(solution)/shard_map/all_gather | solution.py:881
  145.2 19.9 %shard_map.223 = (f32[512,1152]{1,0:T(8,128)}, bf16[512,1152]{1,0:T(8,128)(2,1)}) custom-call(bf16[512,1152]{1,0:T(8,128)(2,1)} %bitcast.239, f32[2,6,1152]{2,1,0:T(8,128)} %reshape_squeeze.8.mod_ref.refs_1_.refs_2_.refs_5_, bf16[512,256]{1,0:T(8,128)(2,1)} %get-tuple-element.68.refs_2_.refs_3_.refs_6_, ...), custom_call_target="tpu_custom_call" | custom-call | flops 6039797760 | bytes 22413312 | tf_op jit(solution)/shard_map/pallas_call | solution.py:246
  165.2 13.1 %shard_map.224.act_ref = bf16[512,3072]{1,0:T(8,128)(2,1)} custom-call(bf16[512,1152]{1,0:T(8,128)(2,1)} %get-tuple-element.74.normed_ref, bf16[8,144,10752]{2,1,0:T(8,128)(2,1)} %bitcast.217, bf16[8,144,10752]{2,1,0:T(8,128)(2,1)} %bitcast.218), custom_call_target="tpu_custom_call" | custom-call | flops 7247757312 | bytes 17301504 | tf_op jit(solution)/shard_map/pallas_call | solution.py:311
  178.3 11.2 %all-gather.5.cloned.1.call-done.down_ref.refs_1_.refs_2_ = bf16[3072,1152]{1,0:T(8,128)(2,1)} async-done(((bf16[192,1152]{1,0:T(8,128)(2,1)}), bf16[3072,1152]{1,0:T(8,128)(2,1)}) %all-gather.5.cloned.1.call-update) | async-done | bytes 7077904 | tf_op jit(solution)/shard_map/all_gather | solution.py:881
  189.5 6.1 %shard_map.227 = bf16[256,1152]{1,0:T(8,128)(2,1)} custom-call(s32[1]{0:T(128)} %bitcast.31.active_ref, bf16[512,3072]{1,0:T(8,128)(2,1)} %shard_map.224.act_ref, f32[512,1152]{1,0:T(8,128)} %get-tuple-element.75.middle_ref, f32[2,6,1152]{2,1,0:T(8,128)} %reshape_squeeze.8.mod_ref.refs_1_.refs_2_.refs_5_, ...), custom_call_target="tpu_custom_call" | custom-call | flops 1811939328 | bytes 9437184 | tf_op jit(solution)/shard_map/pallas_call | solution.py:363
  195.6 1.3 collective-permute-start.9
  197.0 2.5 shard_map.222.refs_0_
  199.5 6.1 %shard_map.225 = bf16[256,1152]{1,0:T(8,128)(2,1)} custom-call(s32[1]{0:T(128)} %bitcast.31.active_ref, bf16[512,3072]{1,0:T(8,128)(2,1)} %shard_map.224.act_ref, f32[512,1152]{1,0:T(8,128)} %get-tuple-element.75.middle_ref, f32[2,6,1152]{2,1,0:T(8,128)} %reshape_squeeze.8.mod_ref.refs_1_.refs_2_.refs_5_, ...), custom_call_target="tpu_custom_call" | custom-call | flops 1811939328 | bytes 9437184 | tf_op jit(solution)/shard_map/pallas_call | solution.py:363
  205.6 1.3 collective-permute-start.8
  206.9 8.4 %shard_map.226.act_grad_ref = bf16[512,3072]{1,0:T(8,128)(2,1)} custom-call(bf16[512,1152]{1,0:T(8,128)(2,1)} %shard_map.222.refs_0_, bf16[3072,1152]{1,0:T(8,128)(2,1)} %all-gather.5.cloned.1.call-done.down_ref.refs_1_.refs_2_), custom_call_target="tpu_custom_call" | custom-call | flops 3623878656 | bytes 9437184 | tf_op jit(solution)/shard_map/pallas_call | solution.py:428
  216.1 12.4 %shard_map.228 = (bf16[512,1152]{1,0:T(8,128)(2,1)}, f32[512,2304]{1,0:T(8,128)}, bf16[512,1152]{1,0:T(8,128)(2,1)}, bf16[512,1152]{1,0:T(8,128)(2,1)}, f32[512,...) custom-call(bf16[256,1152]{1,0:T(8,128)(2,1)} %copy-done.16, ...), custom_call_target="tpu_custom_call" | custom-call | flops 3019898880 | bytes 16515072 | tf_op jit(solution)/shard_map/pallas_call | solution.py:246
  229.4 12.6 %shard_map.229 = (bf16[512,1152]{1,0:T(8,128)(2,1)}, f32[512,2304]{1,0:T(8,128)}, bf16[512,1152]{1,0:T(8,128)(2,1)}, bf16[512,1152]{1,0:T(8,128)(2,1)}, f32[512,...) custom-call(bf16[256,1152]{1,0:T(8,128)(2,1)} %copy-done.14, ...), custom_call_target="tpu_custom_call", output_to_operand_aliasing={{0}: (11, {}), {1}: (12, {}), {2}: (13, {}), {3}: (14, {}),... | custom-call | flops 3019898880 | bytes 16515072 | tf_op jit(solution)/shard_map/pallas_call | solution.py:246
  242.0 26.6 %shard_map.230 = (f32[512,1152]{1,0:T(8,128)}, bf16[512,1152]{1,0:T(8,128)(2,1)}, bf16[512,3072]{1,0:T(8,128)(2,1)}, bf16[512,3072]{1,0:T(8,128)(2,1)}, bf16[512,3072]{1,0:T(8,128)(2,1)}) custom-call(bf16[512,3072]{1,0:T(8,128)(2,1)} %shard_map.226.act_grad_ref, bf16[8,144,10752]{2,1,0:T(8,128)(2,1)} %bitcast.223, bf16[8,144,10752]{2,1,0:T(8,128)(2,1)} %bitcast.224, ...), custom_call_target="tpu_custom_call" | custom-call | flops 15854469120 | bytes 23592960 | tf_op jit(solution)/shard_map/pallas_call | solution.py:548
  268.6 15.4 %shard_map.233 = bf16[256,1152]{1,0:T(8,128)(2,1)} custom-call(f32[512,2304]{1,0:T(8,128)} %get-tuple-element.90.refs_0_, bf16[512,1152]{1,0:T(8,128)(2,1)} %get-tuple-element.91.refs_1_, bf16[512,1152]{1,0:T(8,128)(2,1)} %get-tuple-element.92.refs_2_, f32[512,1152]{1,0:T(8,128)} %get-tuple-element.93.refs_3_, bf16[512,1152]{1,0:T(8,128)(2,1)} %get-tuple-element.94.refs_4_, ...), custom_call_target="tpu_custom_call" | custom-call | flops 2793406464 | bytes 13860864 | tf_op jit(solution)/shard_map/pallas_call | solution.py:731
  284.0 1.7 collective-permute-start.11
  285.7 15.4 %shard_map.231 = bf16[256,1152]{1,0:T(8,128)(2,1)} custom-call(f32[512,2304]{1,0:T(8,128)} %get-tuple-element.90.refs_0_, bf16[512,1152]{1,0:T(8,128)(2,1)} %get-tuple-element.91.refs_1_, bf16[512,1152]{1,0:T(8,128)(2,1)} %get-tuple-element.92.refs_2_, f32[512,1152]{1,0:T(8,128)} %get-tuple-element.93.refs_3_, bf16[512,1152]{1,0:T(8,128)(2,1)} %get-tuple-element.94.refs_4_, ...), custom_call_target="tpu_custom_call" | custom-call | flops 2793406464 | bytes 13860864 | tf_op jit(solution)/shard_map/pallas_call | solution.py:731
  301.1 1.5 collective-permute-start.10
  302.6 10.1 %shard_map.232 = (bf16[512,1152]{1,0:T(8,128)(2,1)}, f32[512,1152]{1,0:T(8,128)}) custom-call(s32[1]{0:T(128)} %constant.100.clone.1.active_ref, bf16[512,3072]{1,0:T(8,128)(2,1)} %get-tuple-element.95.act_ref, f32[512,1152]{1,0:T(8,128)} %get-tuple-element.88.refs_2_.middle_ref.refs_5_, f32[2,6,1152]{2,1,0:T(8,128)} %reshape_squeeze.8.mod_ref.refs_1_.refs_2_.refs_5_, ...), custom_call_target="tpu_custom_call" | custom-call | flops 3623878656 | bytes 11796480 | tf_op jit(solution)/shard_map/pallas_call | solution.py:363
  313.4 2.3 shard_map.234.refs_0_
  315.7 3.0 collective-permute-done.10.back_ref.refs_3_
  319.5 8.7 %shard_map.235 = (bf16[3072,1152]{1,0:T(8,128)(2,1)}, bf16[256,1152]{1,0:T(8,128)(2,1)}) custom-call(bf16[512,3072]{1,0:T(8,128)(2,1)} %get-tuple-element.95.act_ref, bf16[512,1152]{1,0:T(8,128)(2,1)} %bitcast.235, bf16[256,1152]{1,0:T(8,128)(2,1)} %copy-done.17, f32[2,6,1152]{2,1,0:T(8,128)} %reshape_squeeze.8.mod_ref.refs_1_.refs_2_.refs_5_, ...), custom_call_target="tpu_custom_call" | custom-call | flops 3623878656 | bytes 7077888 | tf_op jit(solution)/shard_map/pallas_call | solution.py:786
  328.3 7.9 %shard_map.236.act_grad_ref = bf16[512,3072]{1,0:T(8,128)(2,1)} custom-call(bf16[256,1152]{1,0:T(8,128)(2,1)} %shard_map.234.refs_0_, bf16[256,1152]{1,0:T(8,128)(2,1)} %get-tuple-element.102.refs_1_, bf16[3072,1152]{1,0:T(8,128)(2,1)} %all-gather.5.cloned.1.call-done.down_ref.refs_1_.refs_2_), custom_call_target="tpu_custom_call" | custom-call | flops 3623878656 | bytes 9437184 | tf_op jit(solution)/shard_map/pallas_call | solution.py:428
  336.2 23.4 %shard_map.237 = (f32[512,1152]{1,0:T(8,128)}, bf16[512,1152]{1,0:T(8,128)(2,1)}, bf16[512,3072]{1,0:T(8,128)(2,1)}, bf16[512,3072]{1,0:T(8,128)(2,1)}, bf16[512...) custom-call(bf16[512,3072]{1,0:T(8,128)(2,1)} %shard_map.236.act_grad_ref, bf16[8,144,10752]{2,1,0:T(8,128)(2,1)} %bitcast.228, ...), custom_call_target="tpu_custom_call" | custom-call | flops 15854469120 | bytes 23592960 | tf_op jit(solution)/shard_map/pallas_call | solution.py:548
  359.7 13.6 %shard_map.240 = bf16[8,144,6144]{2,1,0:T(8,128)(2,1)} custom-call(bf16[512,1152]{1,0:T(8,128)(2,1)} %get-tuple-element.87.refs_0_.refs_1_, bf16[512,1152]{1,0:T(8,128)(2,1)} %get-tuple-element.87.refs_0_.refs_1_, bf16[512,3072]{1,0:T(8,128)(2,1)} %get-tuple-element.113.refs_2_, bf16[512,3072]{1,0:T(8,128)(2,1)} %get-tuple-element.114.refs_3_), custom_call_target="tpu_custom_call" | custom-call | flops 7247757312 | bytes 14155776 | tf_op jit(solution)/shard_map/pallas_call | solution.py:837
  373.3 9.0 %reduce-scatter.4.cloned.1.call-done = bf16[192,1152]{1,0:T(8,128)(2,1)} async-done(((bf16[3072,1152]{1,0:T(8,128)(2,1)}), bf16[192,1152]{1,0:T(8,128)(2,1)}) %reduce-scatter.4.cloned.1.call-update) | async-done | bytes 442384 | tf_op jit(solution)/shard_map/reduce_scatter | solution.py:885
  382.6 30.2 %shard_map.238 = (f32[512,1152]{1,0:T(8,128)}, bf16[512,3456]{1,0:T(8,128)(2,1)}, f32[2,4,1152]{2,1,0:T(4,128)}) custom-call(f32[512,2304]{1,0:T(8,128)} %get-tuple-element.90.refs_0_, bf16[512,1152]{1,0:T(8,128)(2,1)} %get-tuple-element.91.refs_1_, bf16[512,1152]{1,0:T(8,128)(2,1)} %get-tuple-element.106.refs_2_, f32[512,1152]{1,0:T(8,128)} %get-tuple-element.107.refs_3_, ...), custom_call_target="tpu_custom_call" | custom-call | flops 5586812928 | bytes 19759104 | tf_op jit(solution)/shard_map/pallas_call | solution.py:731
  413.7 1.7 collective-permute-start.12
  415.4 4.1 collective-permute-done.12
  420.2 4.4 collective-permute-done.13
  424.9 1.0 collective-permute-start.14
  426.0 5.1 collective-permute-done.14
  431.8 11.5 %shard_map.239 = bf16[8,144,4608]{2,1,0:T(8,128)(2,1)} custom-call(bf16[512,1152]{1,0:T(8,128)(2,1)} %get-tuple-element.109.refs_0_, bf16[512,1152]{1,0:T(8,128)(2,1)} %get-tuple-element.110.refs_1_, bf16[512,3456]{1,0:T(8,128)(2,1)} %get-tuple-element.111.refs_2_, bf16[512,1152]{1,0:T(8,128)(2,1)} %get-tuple-element.112.refs_3_), custom_call_target="tpu_custom_call" | custom-call | flops 5435817984 | bytes 10616832 | tf_op jit(solution)/shard_map/pallas_call | solution.py:837
  444.7 22.6 %reduce-scatter.6.cloned.1.call-done = bf16[72,6144]{1,0:T(8,128)(2,1)} async-done(((bf16[1152,6144]{1,0:T(8,128)(2,1)}), bf16[72,6144]{1,0:T(8,128)(2,1)}) %reduce-scatter.6.cloned.1.call-update) | async-done | bytes 884752 | tf_op jit(solution)/shard_map/reduce_scatter | solution.py:885
  468.6 4.2 collective-permute-done.21
  472.9 3.6 collective-permute-done.22
  477.5 2.7 collective-permute-done.23
  480.3 1.6 convert_select_fusion
  483.8 1.5 collective-permute-start.16
  485.4 2.2 collective-permute-done.16
  487.6 1.3 collective-permute-start.17
  488.9 3.6 collective-permute-done.17
  492.6 4.3 collective-permute-done.18
  497.0 1.0 collective-permute-start.19
  500.0 2.1 collective-permute-done.19
  502.2 1.7 convolution_bitcast_fusion
  504.4 4.3 fusion.9
  508.7 24.9 %reduce-scatter.8.cloned.1.call-done = bf16[72,4608]{1,0:T(8,128)(2,1)} async-done(((bf16[1152,4608]{1,0:T(8,128)(2,1)}), bf16[72,4608]{1,0:T(8,128)(2,1)}) %reduce-scatter.8.cloned.1.call-update) | async-done | bytes 663568 | tf_op jit(solution)/shard_map/reduce_scatter | solution.py:885
  533.6 1.7 fusion.8
  535.2 2.0 fusion.5
  (200 shorter events, 25.4 us)
Async XLA Ops:
  7.2 24.3 %copy-start = (bf16[1001,1152]{1,0:T(8,128)(2,1)S(1)}, bf16[1001,1152]{1,0:T(8,128)(2,1)}, u32[]{:S(2)}) copy-start(bf16[1001,1152]{1,0:T(8,128)(2,1)} %param.19) | copy-start | bytes 6918916
  7.2 2.9 copy-start.29
  7.2 2.9 copy-start.30
  7.2 137.0 %all-gather.3.cloned.1.call-start = ((), (), s32[]{:S(2)}) async-start(), calls=%async_computation.3 | async-start | bytes 26320896 | tf_op jit(solution)/shard_map/all_gather | solution.py:881
  7.3 7.0 %copy-start.28 = (s32[2,256]{1,0:T(2,128)S(1)}, s32[2,256]{1,0:T(2,128)}, u32[]{:S(2)}) copy-start(s32[2,256]{1,0:T(2,128)} %param.18) | copy-start | bytes 6148
  10.1 10.4 %copy-start.2 = (bf16[2,256,1152]{2,1,0:T(8,128)(2,1)S(1)}, bf16[2,256,1152]{2,1,0:T(8,128)(2,1)}, u32[]{:S(2)}) copy-start(bf16[2,256,1152]{2,1,0:T(8,128)(2,1)} %param.14) | copy-start | bytes 3538948
  10.1 179.4 %all-gather.5.cloned.1.call-start = ((), (), s32[]{:S(2)}) async-start(), calls=%async_computation.4 | async-start | bytes 7520256 | tf_op jit(solution)/shard_map/all_gather | solution.py:881
  10.2 11.5 %collective-permute-start = (s32[1,2,2]{2,1,0:T(2,128)S(1)}, s32[1,2,2]{2,1,0:T(2,128)S(1)}, u32[]{:S(2)}, u32[]{:S(2)}) collective-permute-start(s32[1,2,2]{2,1,0:T(2,128)S(1)} %add_bitcast_fusion.2), channel_id=1, source_target_pairs={{0,8},{1,9},{2,10},{3,11},{4,12},{5,13},{6,14},{7,15},{8,0},{9,1},... | collective-permute-start | bytes 56 | tf_op jit(solution)/shard_map/ppermute | solution.py:900
  16.3 0.7 copy-start.6
  16.3 1.5 copy-start.8
  21.7 10.5 %copy-start.3 = (bf16[1,72,6912]{2,1,0:T(8,128)(2,1)S(1)}, bf16[1,72,6912]{2,1,0:T(8,128)(2,1)}, u32[]{:S(2)}) copy-start(bf16[1,72,6912]{2,1,0:T(8,128)(2,1)} %param.20) | copy-start | bytes 2985988
  21.7 3.7 collective-permute-start.1
  25.6 3.6 collective-permute-start.2
  29.4 1.2 collective-permute-start.3
  31.0 1.5 copy-start.26
  32.1 0.8 copy-start.12
  32.2 0.7 copy-start.22
  32.2 4.3 copy-start.15
  32.6 1.9 collective-permute-start.4
  32.9 14.9 %copy-start.7 = (f32[512,18]{1,0:T(8,128)S(1)}, f32[512,18]{1,0:T(8,128)}, u32[]{:S(2)}) copy-start(f32[512,18]{1,0:T(8,128)} %copy-done.6) | copy-start | bytes 110596
  32.9 14.9 %copy-start.9 = (f32[512,18]{1,0:T(8,128)S(1)}, f32[512,18]{1,0:T(8,128)}, u32[]{:S(2)}) copy-start(f32[512,18]{1,0:T(8,128)} %copy-done.8) | copy-start | bytes 110596
  34.5 21.4 %copy-start.18 = (bf16[512,128]{1,0:T(8,128)(2,1)S(1)}, bf16[512,128]{1,0:T(8,128)(2,1)}, u32[]{:S(2)}) copy-start(bf16[512,128]{1,0:T(8,128)(2,1)} %fusion.39) | copy-start | bytes 393220
  34.5 21.4 %copy-start.19 = (bf16[512,128]{1,0:T(8,128)(2,1)S(1)}, bf16[512,128]{1,0:T(8,128)(2,1)}, u32[]{:S(2)}) copy-start(bf16[512,128]{1,0:T(8,128)(2,1)} %get-tuple-element.125) | copy-start | bytes 393220
  34.5 21.4 %copy-start.20 = (bf16[512,128]{1,0:T(8,128)(2,1)S(1)}, bf16[512,128]{1,0:T(8,128)(2,1)}, u32[]{:S(2)}) copy-start(bf16[512,128]{1,0:T(8,128)(2,1)} %get-tuple-element.126) | copy-start | bytes 393220
  34.8 109.7 %copy-start.31 = (f32[1,72]{1,0:T(1,128)S(1)}, f32[1,72]{1,0:T(1,128)}, u32[]{:S(2)}) copy-start(f32[1,72]{1,0:T(1,128)} %param.27) | copy-start | bytes 868
  34.8 109.7 %copy-start.32 = (f32[1,72]{1,0:T(1,128)S(1)}, f32[1,72]{1,0:T(1,128)}, u32[]{:S(2)}) copy-start(f32[1,72]{1,0:T(1,128)} %param.26) | copy-start | bytes 868
  34.8 12.8 %collective-permute-start.5 = (f32[4,2,6912]{2,1,0:T(2,128)S(1)}, f32[4,2,6912]{2,1,0:T(2,128)S(1)}, u32[]{:S(2)}, u32[]{:S(2)}) collective-permute-start(f32[4,2,6912]{2,1,0:T(2,128)S(1)} %dynamic-slice_bitcast_fusion.1), channel_id=1, source_target_pairs={{0,2},{1,3},{2,0},{3,1},{4,6},{5,7},{6,4},{7,5},{8,10},{9,11},{10,... | collective-permute-start | bytes 663560 | tf_op jit(solution)/shard_map/ppermute | solution.py:900
  47.8 7.8 %collective-permute-start.6 = (f32[2,2,6912]{2,1,0:T(2,128)S(1)}, f32[2,2,6912]{2,1,0:T(2,128)S(1)}, u32[]{:S(2)}, u32[]{:S(2)}) collective-permute-start(f32[2,2,6912]{2,1,0:T(2,128)S(1)} %dynamic-slice_bitcast_fusion.2), channel_id=1, source_target_pairs={{0,4},{1,5},{2,6},{3,7},{4,0},{5,1},{6,2},{7,3},{8,12},{9,13},{10,... | collective-permute-start | bytes 331784 | tf_op jit(solution)/shard_map/ppermute | solution.py:900
  55.7 6.8 %collective-permute-start.7 = (f32[1,2,6912]{2,1,0:T(2,128)S(1)}, f32[1,2,6912]{2,1,0:T(2,128)S(1)}, u32[]{:S(2)}, u32[]{:S(2)}) collective-permute-start(f32[1,2,6912]{2,1,0:T(2,128)S(1)} %constant_dynamic-slice_fusion), channel_id=1, source_target_pairs={{0,8},{1,9},{2,10},{3,11},{4,12},{5,13},{6,14},{7,15},{8,0},{9,1},... | collective-permute-start | bytes 165896 | tf_op jit(solution)/shard_map/ppermute | solution.py:900
  144.2 238.1 %reduce-scatter.4.cloned.1.call-start = ((), (), s32[]{:S(2)}) async-start(), calls=%async_computation.5 | async-start | bytes 7520256 | tf_op jit(solution)/shard_map/reduce_scatter | solution.py:885
  195.6 19.6 %collective-permute-start.9 = (bf16[256,1152]{1,0:T(8,128)(2,1)}, bf16[256,1152]{1,0:T(8,128)(2,1)S(1)}, u32[]{:S(2)}, u32[]{:S(2)}) collective-permute-start(bf16[256,1152]{1,0:T(8,128)(2,1)} %shard_map.227), channel_id=1, source_target_pairs={{0,16},{1,17},{2,18},{3,19},{4,20},{5,21},{6,22},{7,23},{8,24},{9,... | collective-permute-start | bytes 1769480 | tf_op jit(solution)/shard_map/ppermute | solution.py:1027
  205.6 23.0 %collective-permute-start.8 = (bf16[256,1152]{1,0:T(8,128)(2,1)}, bf16[256,1152]{1,0:T(8,128)(2,1)S(1)}, u32[]{:S(2)}, u32[]{:S(2)}) collective-permute-start(bf16[256,1152]{1,0:T(8,128)(2,1)} %shard_map.225), channel_id=1, source_target_pairs={{0,16},{1,17},{2,18},{3,19},{4,20},{5,21},{6,22},{7,23},{8,24},{9,... | collective-permute-start | bytes 1769480 | tf_op jit(solution)/shard_map/ppermute | solution.py:1027
  215.3 0.8 copy-start.16
  228.6 0.8 copy-start.14
  284.0 28.6 %collective-permute-start.11 = (bf16[256,1152]{1,0:T(8,128)(2,1)}, bf16[256,1152]{1,0:T(8,128)(2,1)S(1)}, u32[]{:S(2)}, u32[]{:S(2)}) collective-permute-start(bf16[256,1152]{1,0:T(8,128)(2,1)} %shard_map.233), channel_id=1, source_target_pairs={{16,0},{17,1},{18,2},{19,3},{20,4},{21,5},{22,6},{23,7},{24,8},{25... | collective-permute-start | bytes 1769480 | tf_op jit(solution)/shard_map/ppermute | solution.py:1058
  301.1 17.6 %collective-permute-start.10 = (bf16[256,1152]{1,0:T(8,128)(2,1)}, bf16[256,1152]{1,0:T(8,128)(2,1)S(1)}, u32[]{:S(2)}, u32[]{:S(2)}) collective-permute-start(bf16[256,1152]{1,0:T(8,128)(2,1)} %shard_map.231), channel_id=1, source_target_pairs={{16,0},{17,1},{18,2},{19,3},{20,4},{21,5},{22,6},{23,7},{24,8},{25... | collective-permute-start | bytes 1769480 | tf_op jit(solution)/shard_map/ppermute | solution.py:1058
  312.6 0.8 copy-start.10
  318.7 0.8 copy-start.17
  328.2 139.1 %reduce-scatter.6.cloned.1.call-start = ((), (), s32[]{:S(2)}) async-start(), calls=%async_computation.6 | async-start | bytes 15040512 | tf_op jit(solution)/shard_map/reduce_scatter | solution.py:885
  382.4 151.2 %reduce-scatter.8.cloned.1.call-start = ((), (), s32[]{:S(2)}) async-start(), calls=%async_computation.7 | async-start | bytes 11280384 | tf_op jit(solution)/shard_map/reduce_scatter | solution.py:885
  382.6 31.0 %copy-start.24 = (f32[2,4,1152]{2,1,0:T(4,128)S(1)}, f32[2,4,1152]{2,1,0:T(4,128)}, u32[]{:S(2)}) copy-start(f32[2,4,1152]{2,1,0:T(4,128)} %get-tuple-element.118) | copy-start | bytes 110596
  413.7 5.8 %collective-permute-start.12 = (bf16[1,2,6912]{2,1,0:T(2,128)(2,1)S(1)}, bf16[1,2,6912]{2,1,0:T(2,128)(2,1)S(1)}, u32[]{:S(2)}, u32[]{:S(2)}) collective-permute-start(bf16[1,2,6912]{2,1,0:T(2,128)(2,1)S(1)} %convert_element_type.143), channel_id=1, source_target_pairs={{0,8},{1,9},{2,10},{3,11},{4,12},{5,13},{6,14},{7,15},{8,0},{9,1},... | collective-permute-start | bytes 82952 | tf_op jit(solution)/shard_map/ppermute | solution.py:900
  419.7 4.9 collective-permute-start.13
  424.9 6.1 %collective-permute-start.14 = (bf16[4,2,6912]{2,1,0:T(2,128)(2,1)S(1)}, bf16[4,2,6912]{2,1,0:T(2,128)(2,1)S(1)}, u32[]{:S(2)}, u32[]{:S(2)}) collective-permute-start(bf16[4,2,6912]{2,1,0:T(2,128)(2,1)S(1)} %bitcast.252), channel_id=1, source_target_pairs={{0,2},{1,3},{2,0},{3,1},{4,6},{5,7},{6,4},{7,5},{8,10},{9,11},{10,... | collective-permute-start | bytes 331784 | tf_op jit(solution)/shard_map/ppermute | solution.py:900
  431.7 11.5 %collective-permute-start.15 = (bf16[8,2,6912]{2,1,0:T(2,128)(2,1)S(1)}, bf16[8,2,6912]{2,1,0:T(2,128)(2,1)S(1)}, u32[]{:S(2)}, u32[]{:S(2)}) collective-permute-start(bf16[8,2,6912]{2,1,0:T(2,128)(2,1)S(1)} %bitcast.244), channel_id=1, source_target_pairs={{0,1},{1,0},{2,3},{3,2},{4,5},{5,4},{6,7},{7,6},{8,9},{9,8},{10,11... | collective-permute-start | bytes 663560 | tf_op jit(solution)/shard_map/ppermute | solution.py:900
  467.4 0.8 copy-start.25
  467.4 12.9 %copy-start.5 = (f32[512,1152]{1,0:T(8,128)S(1)}, f32[512,1152]{1,0:T(8,128)}, u32[]{:S(2)}) copy-start(f32[512,1152]{1,0:T(8,128)} %get-tuple-element.108) | copy-start | bytes 7077892
  468.3 4.5 collective-permute-start.21
  472.8 3.6 collective-permute-start.22
  476.5 3.7 collective-permute-start.23
  480.2 1.7 collective-permute-start.24
  480.3 2.1 copy-start.21
  480.3 3.1 copy-start.4
  481.9 3.4 copy-start.11
  483.8 3.8 collective-permute-start.16
  487.6 4.9 collective-permute-start.17
  488.9 13.4 %copy-start.23 = (bf16[32,72]{1,0:T(8,128)(2,1)S(1)}, bf16[32,72]{1,0:T(8,128)(2,1)}, u32[]{:S(2)}) copy-start(bf16[32,72]{1,0:T(8,128)(2,1)} %copy-done.22) | copy-start | bytes 13828
  492.5 4.4 collective-permute-start.18
  497.0 5.1 collective-permute-start.19
  502.1 2.2 copy-start.13
  502.2 2.2 copy-start.27
  502.2 1.8 collective-permute-start.20
  504.2 33.1 %copy-start.1 = (bf16[1001,1152]{1,0:T(8,128)(2,1)S(1)}, bf16[1001,1152]{1,0:T(8,128)(2,1)}, u32[]{:S(2)}) copy-start(bf16[1001,1152]{1,0:T(8,128)(2,1)} %param.19) | copy-start | bytes 6918916
Sparse Core Ops, SparseCore 0:
  10.2 133.9 all-gather.2
  145.8 43.6 all-gather.4
  328.4 53.9 reduce-scatter.3
  384.6 82.7 reduce-scatter.5
  469.6 63.9 reduce-scatter.7

commit v6 on v5

--- a/solution.py
+++ b/solution.py
@@ -249,7 +249,7 @@
         in_specs=[pl.BlockSpec((patches, width), lambda image: (image, 0))] * len(extra)
         + [
             row(width),
-            pl.BlockSpec((1, 6, width), lambda image: (first + image, 0, 0)),
+            pl.BlockSpec((1, 8, width), lambda image: (first + image, 0, 0)),
             row(cos.shape[1]),
             row(sin.shape[1]),
             fixed(gain),
@@ -269,58 +269,53 @@
     )(*extra, x, mod, cos, sin, gain, *matrices, joined, joined, *made)
 
 
-def pack_columns(matrices, pieces):
-    rows = matrices[0].shape[0]
-    total = sum(columns for unused, first, columns in pieces)
-
-    def body(*refs):
-        at = 0
-        for which, first, columns in pieces:
-            refs[-1][:, at : at + columns] = refs[which][:, first : first + columns]
-            at += columns
-
-    if any(columns % LANES or first % LANES for unused, first, columns in pieces):
-        return jnp.concatenate(
-            [matrices[which][:, first : first + columns] for which, first, columns in pieces], axis=1
+def walk_chip(place, chips):
+    return jnp.where(place < chips // 2, 2 * place, 2 * (chips - 1 - place) + 1)
+
+
+def column_specs(joined, first, hidden, chips, step):
+    parts, rows, unused = joined.shape
+    if not chips:
+        return [pl.BlockSpec((parts, rows, step), lambda i: (0, 0, first // step + i))]
+    each = hidden // chips
+    number = step // each
+
+    def spec(which):
+        return pl.BlockSpec(
+            (parts, rows, each),
+            lambda i: (0, 0, first // each + walk_chip(i * number + which, chips)),
         )
+
+    return [spec(which) for which in range(number)]
+
+
+def step_matrix(refs, places):
+    return side_by_side([whole_rows(ref, places) for ref in refs])
+
+
+def gate_up(normed_two, joined, hidden, walked, chips):
+    tokens, width = normed_two.shape
+    step = 768
+    places = places_of(joined.shape[0], walked)
+    gate_specs = column_specs(joined, 4 * width, hidden, chips, step)
+    up_specs = column_specs(joined, 4 * width + hidden, hidden, chips, step)
+    number = len(gate_specs)
+
+    def body(normed_ref, *refs):
+        normed = normed_ref[...]
+        gate = dot(normed, step_matrix(refs[:number], places))
+        up = dot(normed, step_matrix(refs[number : 2 * number], places))
+        refs[-1][...] = (gate * (1.0 / (1.0 + jnp.exp(-gate))) * up).astype(bf16)
+
     return pl.pallas_call(
         body,
-        grid=(1,),
-        in_specs=whole_specs(matrices),
-        out_specs=pl.BlockSpec((rows, total), lambda i: (0, 0)),
-        out_shape=jax.ShapeDtypeStruct((rows, total), matrices[0].dtype),
-        compiler_params=params(),
-        cost_estimate=cost(0, 4 * rows * total),
-    )(*matrices)
-
-
-def gate_up(normed_two, joined, hidden, walked):
-    tokens, width = normed_two.shape
-    step = 512
-    base = 4 * width // step
-    count = hidden // step
-    parts, rows, unused = joined.shape
-    places = places_of(parts, walked)
-
-    def body(normed_ref, gate_ref, up_ref, act_ref):
-        normed = normed_ref[...]
-        gate = dot(normed, whole_rows(gate_ref, places))
-        up = dot(normed, whole_rows(up_ref, places))
-        act_ref[...] = (gate * (1.0 / (1.0 + jnp.exp(-gate))) * up).astype(bf16)
-
-    return pl.pallas_call(
-        body,
-        grid=(count,),
-        in_specs=[
-            pl.BlockSpec((tokens, width), lambda i: (0, 0)),
-            pl.BlockSpec((parts, rows, step), lambda i: (0, 0, base + i)),
-            pl.BlockSpec((parts, rows, step), lambda i: (0, 0, base + count + i)),
-        ],
+        grid=(hidden // step,),
+        in_specs=[pl.BlockSpec((tokens, width), lambda i: (0, 0))] + gate_specs + up_specs,
         out_specs=pl.BlockSpec((tokens, step), lambda i: (0, i)),
         out_shape=jax.ShapeDtypeStruct((tokens, hidden), bf16),
         compiler_params=params(),
         cost_estimate=cost(4 * tokens * width * hidden, 4 * width * hidden + 2 * tokens * hidden),
-    )(normed_two, joined, joined)
+    )(normed_two, *[joined] * (2 * number))
 
 
 def down_projection(active, act, down, middle, mod, first, count, keep, step):
@@ -436,28 +431,34 @@
     )(*mlp_grads, down)
 
 
-def mlp_backward(cot, backs, act_grad, forward, joined, middle, mod, walked, sums_of):
+def mlp_backward(
+    cot, backs, act_grad, forward, joined, middle, mod, walked, chips, sums_of
+):
     tokens, hidden = act_grad.shape
     images, unused, width = mod.shape
     patches = tokens // images
     parts, rows, unused = joined.shape
     places = places_of(parts, walked)
-    step = 512
-    base = 4 * width // step
+    step = 768
     count = hidden // step
+    gate_specs = column_specs(joined, 4 * width, hidden, chips, step)
+    up_specs = column_specs(joined, 4 * width + hidden, hidden, chips, step)
+    number = len(gate_specs)
     fresh, keep = len(forward) == 1, sums_of is not None
     whole = pl.BlockSpec((tokens, width), lambda i: (0, 0))
     block = pl.BlockSpec((tokens, step), lambda i: (0, i))
     anywhere = pl.BlockSpec(memory_space=pl.ANY)
     late = [cot, middle] + (list(sums_of) if keep else [])
 
-    def body(act_grad_ref, gate_weight_ref, up_weight_ref, mod_ref, joined_ref, *refs):
+    def body(act_grad_ref, mod_ref, joined_ref, *refs):
         refs = list(refs)
 
-        def taken(number):
-            first = refs[:number]
-            del refs[:number]
+        def taken(size):
+            first = refs[:size]
+            del refs[:size]
             return first
+
+        gate_refs, up_refs = taken(number), taken(number)
 
         forward_refs, back_refs, sources = taken(len(forward)), taken(len(backs)), taken(len(late))
         middle_grad_ref, mixed_grad_ref = taken(2)
@@ -479,8 +480,8 @@
             for fetch in fetches:
                 fetch.start()
 
-        gate_weight = whole_rows(gate_weight_ref, places)
-        up_weight = whole_rows(up_weight_ref, places)
+        gate_weight = step_matrix(gate_refs, places)
+        up_weight = step_matrix(up_refs, places)
         if fresh:
             normed = forward_refs[0][...]
             gate, up = dot(normed, gate_weight), dot(normed, up_weight)
@@ -543,18 +544,14 @@
     if keep:
         out_shapes += [jax.ShapeDtypeStruct((tokens, hidden), bf16)] * 2
         out_shapes += [jax.ShapeDtypeStruct((tokens, width), bf16)]
-        out_shapes += [jax.ShapeDtypeStruct((images, 4, width), f32)]
-        out_specs += [block, block, whole, pl.BlockSpec((images, 4, width), lambda i: (0, 0, 0))]
+        out_shapes += [jax.ShapeDtypeStruct((images, 8, width), f32)]
+        out_specs += [block, block, whole, pl.BlockSpec((images, 8, width), lambda i: (0, 0, 0))]
     return pl.pallas_call(
         body,
         grid=(count,),
-        in_specs=[
-            block,
-            pl.BlockSpec((parts, rows, step), lambda i: (0, 0, base + i)),
-            pl.BlockSpec((parts, rows, step), lambda i: (0, 0, base + count + i)),
-            pl.BlockSpec(mod.shape, lambda i: (0, 0, 0)),
-            anywhere,
-        ]
+        in_specs=[block, pl.BlockSpec(mod.shape, lambda i: (0, 0, 0)), anywhere]
+        + gate_specs
+        + up_specs
         + [whole if fresh else block] * len(forward)
         + [pl.BlockSpec((patches, width), lambda i: (0, 0))] * len(backs)
         + [anywhere] * len(late),
@@ -571,7 +568,7 @@
         cost_estimate=cost(
             2 * tokens * width * (4 * hidden + width), 4 * width * hidden + 6 * tokens * hidden
         ),
-    )(act_grad, joined, joined, mod, joined, *forward, *backs, *late)
+    )(act_grad, mod, joined, *[joined] * (2 * number), *forward, *backs, *late)
 
 
 def attention_backward_kernel(heads, places, first, keep, refs):
@@ -717,12 +714,12 @@
         out_shapes = [
             jax.ShapeDtypeStruct((tokens, width), f32),
             jax.ShapeDtypeStruct((tokens, 3 * width), bf16),
-            jax.ShapeDtypeStruct((count, 4, width), f32),
+            jax.ShapeDtypeStruct((count, 8, width), f32),
         ]
         out_specs = [
             token(width),
             token(3 * width),
-            pl.BlockSpec((1, 4, width), lambda image: (image, 0, 0)),
+            pl.BlockSpec((1, 8, width), lambda image: (image, 0, 0)),
         ]
 
     def body(*refs):
@@ -733,7 +730,7 @@
         grid=(count,),
         in_specs=[anywhere] * 5
         + [
-            pl.BlockSpec((1, 6, width), lambda image: (first + image, 0, 0)),
+            pl.BlockSpec((1, 8, width), lambda image: (first + image, 0, 0)),
             row(cos.shape[1]),
             row(sin.shape[1]),
             fixed(gain),
@@ -859,9 +856,10 @@
     return jnp.concatenate([blocks[place] for place in places], axis=0)
 
 
-def walk_columns(which, columns, count):
-    each = columns // (count // 2)
-    return [(which, device // 2 * each, each) for device in walk_of(count)[::2]]
+def columns_to_walk(matrix, count):
+    each = matrix.shape[1] // (count // 2)
+    chips = [device // 2 for device in walk_of(count)[::2]]
+    return jnp.concatenate([matrix[:, chip * each : (chip + 1) * each] for chip in chips], axis=1)
 
 
 def columns_from_walk(matrix, count):
@@ -881,11 +879,23 @@
     return lax.all_gather(rows, "dp", axis=0, tiled=True, axis_index_groups=[walk_of(count)])
 
 
-def scatter_walk(rows, count):
+def scatter_walk(rows, groups):
     part = lax.psum_scatter(
-        rows, "dp", scatter_dimension=0, tiled=True, axis_index_groups=[walk_of(count)]
+        rows, "dp", scatter_dimension=0, tiled=True, axis_index_groups=groups
     )
     return lax.optimization_barrier(part)
+
+
+def scatter_cores(rows, count):
+    me = lax.axis_index("dp")
+    width = rows.shape[-1]
+    pairs = rows.reshape(count // 2, 2, -1, width)
+    give = lax.dynamic_index_in_dim(pairs, 1 - me % 2, 1, keepdims=False)
+    keep = lax.dynamic_index_in_dim(pairs, me % 2, 1, keepdims=False)
+    both = keep.astype(f32) + swapped(give, 1, count).astype(f32)
+    both = both.astype(bf16).reshape(-1, width)
+    walk = walk_of(count)
+    return both, [walk[0::2], walk[1::2]]
 
 
 def as_parts(rows, count):
@@ -986,10 +996,12 @@
     rows = ada_weight.shape[1]
     classes = label_table.shape[0]
 
-    pieces = [(0, 0, 3 * width), (1, 0, width)]
-    pieces += walk_columns(2, hidden, count) + walk_columns(3, hidden, count)
+    gate_matrix, up_matrix, chips = gate_weight[0], up_weight[0], count // 2
+    if hidden // chips % LANES:
+        gate_matrix, up_matrix = columns_to_walk(gate_matrix, count), columns_to_walk(up_matrix, count)
+        chips = 0
     joined = gather_walk(
-        pack_columns([qkv_weight[0], out_weight[0], gate_weight[0], up_weight[0]], pieces), count
+        jnp.concatenate([qkv_weight[0], out_weight[0], gate_matrix, up_matrix], axis=1), count
     )
 
     ids = gather_small(jnp.stack([labels, timesteps]), count)
@@ -1002,6 +1014,7 @@
     silu_rows = lax.dynamic_slice_in_dim(silu_cond, me * rows, rows, 1)
     mod_part = dot(silu_rows, ada_weight[0])
     mod = scatter_small(mod_part.reshape(count, images, -1), count).reshape(images, 6, width)
+    mod = jnp.pad(mod, ((0, 0), (0, 2), (0, 0)))
     tables = rotation_tables(positions, width, head_size)
     flat = tokens.reshape(images * patches, width)
     own = jnp.where(first_section, flat, jnp.zeros_like(flat))
@@ -1012,13 +1025,13 @@
     down = gather_walk(down, count)
     joined, walked = as_parts(joined, count)
     tables = (*tables, head_size)
-    gain = jnp.tile(jnp.concatenate([q_gain, k_gain]), (1, heads))
+    gain = jnp.pad(jnp.tile(jnp.concatenate([q_gain, k_gain]), (1, heads)), ((0, 6), (0, 0)))
 
     cot = cotangent[0].reshape(images * patches, width)
     middle, normed_two = attention_forward(
         flat, None, mod, tables, gain, joined, walked, 0, images
     )
-    act = gate_up(normed_two, joined, hidden, walked)
+    act = gate_up(normed_two, joined, hidden, walked, chips)
     received = []
     for image in range(images):
         (early,) = down_projection(
@@ -1036,7 +1049,7 @@
     normed, raw, values, attended, branch, middle, normed_two, layer_in = kept
 
     middle_grad, mixed_grad, act, gate, up = mlp_backward(
-        cot, [], act_grad, [normed_two], joined, middle, mod, walked, None
+        cot, [], act_grad, [normed_two], joined, middle, mod, walked, chips, None
     )
     backs = []
     for image in range(images):
@@ -1068,21 +1081,19 @@
     down_term, mlp_grad = down_grad(mlp_grads, late_cot, backs[-1], act, mod, hidden // 4)
     mlp_grads = [*mlp_grads, mlp_grad]
     down_term, mlp_grads = lax.optimization_barrier((down_term, mlp_grads))
-    down_part = scatter_walk(down_term, count)
+    down_part = scatter_walk(down_term, [walk_of(count)])
     act_grad = act_backward(mlp_grads, down, hidden // 2)
     middle_grad, mixed_grad, gate_grad, up_grad, branch_grad, mlp_sums = mlp_backward(
-        cot, backs, act_grad, [gate, up], joined, middle, mod, walked, [mlp, branch]
-    )
-
-    def matrix_part(inputs, grads, step, before):
+        cot, backs, act_grad, [gate, up], joined, middle, mod, walked, chips, [mlp, branch]
+    )
+
+    def matrix_term(inputs, grads, step):
         term = matrix_grad(inputs, grads, step, joined.shape[0], walked).reshape(width, -1)
-        term = term if walked else to_walk(term, count)
-        term, *before = lax.optimization_barrier((term, *before))
-        return scatter_walk(term, count), *before
-
-    gate_up_part, down_part = matrix_part(
-        [normed_two, normed_two], [gate_grad, up_grad], hidden // 2, [down_part]
-    )
+        return term if walked else to_walk(term, count)
+
+    gate_up_term = matrix_term([normed_two, normed_two], [gate_grad, up_grad], hidden // 2)
+    gate_up_term, down_part = lax.optimization_barrier((gate_up_term, down_part))
+    gate_up_part = scatter_walk(gate_up_term, [walk_of(count)])
     flow_grad, qkv_grad, attention_sums = attention_backward(
         raw,
         values,
@@ -1098,15 +1109,18 @@
         images,
         True,
     )
-    mod_grad = jnp.concatenate([attention_sums[:, :2], mlp_sums], axis=1).reshape(images, -1)
-    mod_all = gather_small(mod_grad.astype(bf16), count).reshape(-1, mod_grad.shape[1])
-    rest_part, gate_up_part, mod_all = matrix_part(
-        [normed, attended], [qkv_grad, branch_grad], width, [gate_up_part, mod_all]
-    )
+    rest_term = matrix_term([normed, attended], [qkv_grad, branch_grad], width)
+    rest_term, attention_sums = lax.optimization_barrier((rest_term, attention_sums))
+    rest_term, groups = scatter_cores(rest_term, count)
+    mod_grad = jnp.concatenate([attention_sums[:, :2], mlp_sums[:, :4]], axis=1)
+    mod_grad = mod_grad.reshape(images, -1).astype(bf16)
+    mod_all = gather_small(mod_grad, count).reshape(-1, mod_grad.shape[1])
+    rest_term, gate_up_part, mod_all = lax.optimization_barrier((rest_term, gate_up_part, mod_all))
+    rest_part = scatter_walk(rest_term, groups)
     flow_grad = flow_grad.reshape(images, patches, width)
     input_grads = jnp.where(first_section, flow_grad, flow_grad.astype(bf16).astype(f32))
 
-    head_sums = jnp.sum(attention_sums[:, 2:], axis=0).reshape(2, heads, head_size)
+    head_sums = jnp.sum(attention_sums[:, 2:4], axis=0).reshape(2, heads, head_size)
     ada_part = dot_left(silu_rows, mod_all)
     silu_grad = dot_right(mod_all, ada_weight[0])
     silu_grad = silu_grad + lax.ppermute(silu_grad, "section", [(0, 1), (1, 0)])

time: 550 us -> 548 us (level)
  waiting for transfers between devices: 218 us -> 193 us
  other arithmetic: 20.1 us -> 34.3 us
  starting transfers between devices: 24.6 us -> 32.5 us
  local copies, waits for them, and re-layouts: 10.1 us -> 15.6 us
    reduce_scatter x3, waiting for transfers between devices: 56.6 us -> 39.1 us  [scatter_walk(): lax.psum_scatter(rows, 'dp', scatter_dimension=0, tiled=True, axis_index_...]
    ppermute x20 -> x21, waiting for transfers between devices: 63.9 us -> 55.7 us  [swapped(): lax.ppermute(block, 'dp', [(device, device ^ bit) for device in range(cou...]
    convert_element_type x0 -> x1, other arithmetic: none -> 7.93 us  [scatter_cores(): both = both.astype(bf16).reshape(-1, width)]
    ppermute x20 -> x21, starting transfers between devices: 16.7 us -> 24.5 us  [swapped(): lax.ppermute(block, 'dp', [(device, device ^ bit) for device in range(cou...]
    pallas_call x4 -> x3, Pallas kernels: 65.9 us -> 62.8 us  [the longest x2 50 us: mlp_backward(): pl.pallas_call(body, grid=(count,), in_specs=[block, pl.BlockSpec(mod.sha...]
  transfers between devices with their start and end apart: 30 -> 31, of which waited for: 23 -> 23; matrix products, arithmetic and copies ran while one was open for 5% -> 9% of each run, Pallas kernels for 32% -> 32%
where the time goes in v6:
time: 548 us; the launch traced here: 543 us
  Pallas kernels  245 us (45%)
  waiting for transfers between devices  193 us (35%)
  other arithmetic  34.3 us (6%)
  starting transfers between devices  32.5 us (6%)
  local copies, waits for them, and re-layouts  15.6 us (3%)
  between operations  14.9 us (3%)
  matrix products  7.2 us (1%)
    all_gather x2, waiting for transfers between devices, gather_walk(): lax.all_gather(rows, 'dp', axis=0, tiled=True, axis_index_groups=[walk_of...  92.3 us
    pallas_call x3, Pallas kernels, attention_backward(): pl.pallas_call(body, grid=(count,), in_specs=[anywhere] * 5 + [pl.BlockSp...  60.6 us
    ppermute x21, waiting for transfers between devices, swapped(): lax.ppermute(block, 'dp', [(device, device ^ bit) for device in range(cou...  55.7 us
    pallas_call x2, Pallas kernels, mlp_backward(): pl.pallas_call(body, grid=(count,), in_specs=[block, pl.BlockSpec(mod.sha...  50 us
    pallas_call x3, Pallas kernels, attention_forward(): pl.pallas_call(body, grid=(count,), in_specs=[pl.BlockSpec((patches, widt...  45 us
    reduce_scatter x3, waiting for transfers between devices, scatter_walk(): lax.psum_scatter(rows, 'dp', scatter_dimension=0, tiled=True, axis_index_...  39.1 us
    pallas_call x2, Pallas kernels, matrix_grad(): pl.pallas_call(functools.partial(matrix_grad_kernel, places_of(parts, wal...  25.3 us
    ppermute x21, starting transfers between devices, swapped(): lax.ppermute(block, 'dp', [(device, device ^ bit) for device in range(cou...  24.5 us
  transfers between devices with their start and end apart: 31, of which 23 were waited for; matrix products, arithmetic and copies ran while one was open for 9% of the time, Pallas kernels for 32%

profile of v6, /device:TPU:0, one launch (start us, length us, event | category | flops | bytes accessed | tf_op | source)
XLA Modules:
  0.0 542.7 jit_solution(1217673952707392616)
XLA Ops:
  7.3 2.7 pad_maximum_fusion
  10.1 4.1 collective-permute-start
  14.3 1.9 fusion.18
  21.7 1.6 collective-permute-start.1
  23.4 2.0 collective-permute-done.1
  25.6 1.5 collective-permute-start.2
  27.1 2.1 collective-permute-done.2
  32.9 1.5 collective-permute-done.4
  34.8 1.8 collective-permute-start.5
  37.8 9.9 %collective-permute-done.5 = f32[4,2,6912]{2,1,0:T(2,128)S(1)} collective-permute-done((f32[4,2,6912]{2,1,0:T(2,128)S(1)}, f32[4,2,6912]{2,1,0:T(2,128)S(1)}, u32[]{:S(2)}, u32[]{:S(2)}) %collective-permute-start.5) | collective-permute-done | bytes 221216 | tf_op jit(solution)/shard_map/ppermute | solution.py:910
  48.1 7.5 %collective-permute-done.6 = f32[2,2,6912]{2,1,0:T(2,128)S(1)} collective-permute-done((f32[2,2,6912]{2,1,0:T(2,128)S(1)}, f32[2,2,6912]{2,1,0:T(2,128)S(1)}, u32[]{:S(2)}, u32[]{:S(2)}) %collective-permute-start.6) | collective-permute-done | bytes 110624 | tf_op jit(solution)/shard_map/ppermute | solution.py:910
  56.8 5.7 %collective-permute-done.7 = f32[1,2,6912]{2,1,0:T(2,128)S(1)} collective-permute-done((f32[1,2,6912]{2,1,0:T(2,128)S(1)}, f32[1,2,6912]{2,1,0:T(2,128)S(1)}, u32[]{:S(2)}, u32[]{:S(2)}) %collective-permute-start.7) | collective-permute-done | bytes 55328 | tf_op jit(solution)/shard_map/ppermute | solution.py:910
  63.2 81.0 %all-gather.3.cloned.1.call-done = bf16[1152,10752]{1,0:T(8,128)(2,1)} async-done(((bf16[72,10752]{1,0:T(8,128)(2,1)}), bf16[1152,10752]{1,0:T(8,128)(2,1)}) %all-gather.3.cloned.1.call-update) | async-done | bytes 24772624 | tf_op jit(solution)/shard_map/all_gather | solution.py:879
  145.5 19.9 %shard_map.222 = (f32[512,1152]{1,0:T(8,128)}, bf16[512,1152]{1,0:T(8,128)(2,1)}) custom-call(bf16[512,1152]{1,0:T(8,128)(2,1)} %bitcast.256, f32[2,8,1152]{2,1,0:T(8,128)} %pad.15.mod_ref.refs_1_.refs_2_.refs_5_, bf16[512,256]{1,0:T(8,128)(2,1)} %get-tuple-element.70.refs_2_.refs_3_.refs_6_, bf16[512,256]{1,0:T(8,128)(2,1)} %get-tuple-element.71.refs_3_.refs_4_.refs_7_, ...), custom_call_target="tpu_custom_call" | custom-call | flops 6039797760 | bytes 22413312 | tf_op jit(solution)/shard_map/pallas_call | solution.py:246
  165.4 12.8 %shard_map.223.act_ref = bf16[512,3072]{1,0:T(8,128)(2,1)} custom-call(bf16[512,1152]{1,0:T(8,128)(2,1)} %get-tuple-element.76.normed_ref, bf16[8,144,10752]{2,1,0:T(8,128)(2,1)} %bitcast.226, bf16[8,144,10752]{2,1,0:T(8,128)(2,1)} %bitcast.227, bf16[8,144,10752]{2,1,0:T(8,128)(2,1)} %bitcast.228, bf16[8,144,10752]{2,1,0:T(8,128)(2,1)} %bitcast.229), custom_call_target="tpu_custom_call" | custom-call | flops 7247757312 | bytes 17301504 | tf_op jit(solution)/shard_map/pallas_call | solution.py:310
  178.2 11.3 %all-gather.5.cloned.1.call-done.down_ref.refs_1_.refs_2_ = bf16[3072,1152]{1,0:T(8,128)(2,1)} async-done(((bf16[192,1152]{1,0:T(8,128)(2,1)}), bf16[3072,1152]{1,0:T(8,128)(2,1)}) %all-gather.5.cloned.1.call-update) | async-done | bytes 7077904 | tf_op jit(solution)/shard_map/all_gather | solution.py:879
  189.5 6.1 %shard_map.226 = bf16[256,1152]{1,0:T(8,128)(2,1)} custom-call(s32[1]{0:T(128)} %bitcast.31.active_ref, bf16[512,3072]{1,0:T(8,128)(2,1)} %shard_map.223.act_ref, f32[512,1152]{1,0:T(8,128)} %get-tuple-element.77.middle_ref, f32[2,8,1152]{2,1,0:T(8,128)} %pad.15.mod_ref.refs_1_.refs_2_.refs_5_, ...), custom_call_target="tpu_custom_call" | custom-call | flops 1811939328 | bytes 9437184 | tf_op jit(solution)/shard_map/pallas_call | solution.py:358
  197.0 2.5 shard_map.221.refs_0_
  199.5 6.1 %shard_map.224 = bf16[256,1152]{1,0:T(8,128)(2,1)} custom-call(s32[1]{0:T(128)} %bitcast.31.active_ref, bf16[512,3072]{1,0:T(8,128)(2,1)} %shard_map.223.act_ref, f32[512,1152]{1,0:T(8,128)} %get-tuple-element.77.middle_ref, f32[2,8,1152]{2,1,0:T(8,128)} %pad.15.mod_ref.refs_1_.refs_2_.refs_5_, ...), custom_call_target="tpu_custom_call" | custom-call | flops 1811939328 | bytes 9437184 | tf_op jit(solution)/shard_map/pallas_call | solution.py:358
  206.9 8.1 %shard_map.225.act_grad_ref = bf16[512,3072]{1,0:T(8,128)(2,1)} custom-call(bf16[512,1152]{1,0:T(8,128)(2,1)} %shard_map.221.refs_0_, bf16[3072,1152]{1,0:T(8,128)(2,1)} %all-gather.5.cloned.1.call-done.down_ref.refs_1_.refs_2_), custom_call_target="tpu_custom_call" | custom-call | flops 3623878656 | bytes 9437184 | tf_op jit(solution)/shard_map/pallas_call | solution.py:423
  215.9 12.4 %shard_map.227 = (bf16[512,1152]{1,0:T(8,128)(2,1)}, f32[512,2304]{1,0:T(8,128)}, bf16[512,1152]{1,0:T(8,128)(2,1)}, bf16[512,1152]{1,0:T(8,128)(2,1)}, f32[512,...) custom-call(bf16[256,1152]{1,0:T(8,128)(2,1)} %copy-done.15, ...), custom_call_target="tpu_custom_call" | custom-call | flops 3019898880 | bytes 16515072 | tf_op jit(solution)/shard_map/pallas_call | solution.py:246
  229.1 12.6 %shard_map.228 = (bf16[512,1152]{1,0:T(8,128)(2,1)}, f32[512,2304]{1,0:T(8,128)}, bf16[512,1152]{1,0:T(8,128)(2,1)}, bf16[512,1152]{1,0:T(8,128)(2,1)}, f32[512,...) custom-call(bf16[256,1152]{1,0:T(8,128)(2,1)} %copy-done.16, ...), custom_call_target="tpu_custom_call", output_to_operand_aliasing={{0}: (11, {}), {1}: (12, {}), {2}: (13, {}), {3}: (14, {}),... | custom-call | flops 3019898880 | bytes 16515072 | tf_op jit(solution)/shard_map/pallas_call | solution.py:246
  241.8 26.9 %shard_map.229 = (f32[512,1152]{1,0:T(8,128)}, bf16[512,1152]{1,0:T(8,128)(2,1)}, bf16[512,3072]{1,0:T(8,128)(2,1)}, bf16[512,3072]{1,0:T(8,128)(2,1)}, bf16[512,3072]{1,0:T(8,128)(2,1)}) custom-call(bf16[512,3072]{1,0:T(8,128)(2,1)} %shard_map.225.act_grad_ref, f32[2,8,1152]{2,1,0:T(8,128)} %pad.15.mod_ref.refs_1_.refs_2_.refs_5_, ...), custom_call_target="tpu_custom_call" | custom-call | flops 15854469120 | bytes 23592960 | tf_op jit(solution)/shard_map/pallas_call | solution.py:549
  268.7 15.3 %shard_map.232 = bf16[256,1152]{1,0:T(8,128)(2,1)} custom-call(f32[512,2304]{1,0:T(8,128)} %get-tuple-element.92.refs_0_, bf16[512,1152]{1,0:T(8,128)(2,1)} %get-tuple-element.93.refs_1_, bf16[512,1152]{1,0:T(8,128)(2,1)} %get-tuple-element.94.refs_2_, f32[512,1152]{1,0:T(8,128)} %get-tuple-element.95.refs_3_, bf16[512,1152]{1,0:T(8,128)(2,1)} %get-tuple-element.96.refs_4_, ...), custom_call_target="tpu_custom_call" | custom-call | flops 2793406464 | bytes 13860864 | tf_op jit(solution)/shard_map/pallas_call | solution.py:728
  284.0 1.5 collective-permute-start.11
  285.5 15.3 %shard_map.230 = bf16[256,1152]{1,0:T(8,128)(2,1)} custom-call(f32[512,2304]{1,0:T(8,128)} %get-tuple-element.92.refs_0_, bf16[512,1152]{1,0:T(8,128)(2,1)} %get-tuple-element.93.refs_1_, bf16[512,1152]{1,0:T(8,128)(2,1)} %get-tuple-element.94.refs_2_, f32[512,1152]{1,0:T(8,128)} %get-tuple-element.95.refs_3_, bf16[512,1152]{1,0:T(8,128)(2,1)} %get-tuple-element.96.refs_4_, ...), custom_call_target="tpu_custom_call" | custom-call | flops 2793406464 | bytes 13860864 | tf_op jit(solution)/shard_map/pallas_call | solution.py:728
  300.9 1.5 collective-permute-start.10
  302.4 10.0 %shard_map.231 = (bf16[512,1152]{1,0:T(8,128)(2,1)}, f32[512,1152]{1,0:T(8,128)}) custom-call(s32[1]{0:T(128)} %constant.118.clone.1.active_ref, bf16[512,3072]{1,0:T(8,128)(2,1)} %get-tuple-element.97.act_ref, f32[512,1152]{1,0:T(8,128)} %get-tuple-element.90.refs_6_.middle_ref.refs_9_, f32[2,8,1152]{2,1,0:T(8,128)} %pad.15.mod_ref.refs_1_.refs_2_.refs_5_, ...), custom_call_target="tpu_custom_call" | custom-call | flops 3623878656 | bytes 11796480 | tf_op jit(solution)/shard_map/pallas_call | solution.py:358
  313.2 2.3 shard_map.233.refs_0_
  315.5 3.0 collective-permute-done.10.back_ref.refs_7_
  319.3 8.7 %shard_map.234 = (bf16[3072,1152]{1,0:T(8,128)(2,1)}, bf16[256,1152]{1,0:T(8,128)(2,1)}) custom-call(bf16[512,3072]{1,0:T(8,128)(2,1)} %get-tuple-element.97.act_ref, bf16[512,1152]{1,0:T(8,128)(2,1)} %bitcast.251, bf16[256,1152]{1,0:T(8,128)(2,1)} %copy-done.13, f32[2,8,1152]{2,1,0:T(8,128)} %pad.15.mod_ref.refs_1_.refs_2_.refs_5_, ...), custom_call_target="tpu_custom_call" | custom-call | flops 3623878656 | bytes 7077888 | tf_op jit(solution)/shard_map/pallas_call | solution.py:783
  328.1 7.9 %shard_map.235.act_grad_ref = bf16[512,3072]{1,0:T(8,128)(2,1)} custom-call(bf16[256,1152]{1,0:T(8,128)(2,1)} %shard_map.233.refs_0_, bf16[256,1152]{1,0:T(8,128)(2,1)} %get-tuple-element.104.refs_1_, bf16[3072,1152]{1,0:T(8,128)(2,1)} %all-gather.5.cloned.1.call-done.down_ref.refs_1_.refs_2_), custom_call_target="tpu_custom_call" | custom-call | flops 3623878656 | bytes 9437184 | tf_op jit(solution)/shard_map/pallas_call | solution.py:423
  336.0 23.2 %shard_map.236 = (f32[512,1152]{1,0:T(8,128)}, bf16[512,1152]{1,0:T(8,128)(2,1)}, bf16[512,3072]{1,0:T(8,128)(2,1)}, bf16[512,3072]{1,0:T(8,128)(2,1)}, bf16[512...) custom-call(bf16[512,3072]{1,0:T(8,128)(2,1)} %shard_map.235.act_grad_ref, f32[2,8,1152]{2,1,0:T(8,128)} %pad.15.mod_ref.refs_1_.refs_2_.refs_5_, ...), custom_call_target="tpu_custom_call" | custom-call | flops 15854469120 | bytes 23592960 | tf_op jit(solution)/shard_map/pallas_call | solution.py:549
  359.2 13.7 %shard_map.239 = bf16[8,144,6144]{2,1,0:T(8,128)(2,1)} custom-call(bf16[512,1152]{1,0:T(8,128)(2,1)} %get-tuple-element.89.refs_4_.refs_0_.refs_1_, bf16[512,1152]{1,0:T(8,128)(2,1)} %get-tuple-element.89.refs_4_.refs_0_.refs_1_, bf16[512,3072]{1,0:T(8,128)(2,1)} %get-tuple-element.117.refs_2_, bf16[512,3072]{1,0:T(8,128)(2,1)} %get-tuple-element.118.refs_3_), custom_call_target="tpu_custom_call" | custom-call | flops 7247757312 | bytes 14155776 | tf_op jit(solution)/shard_map/pallas_call | solution.py:834
  372.9 9.3 %reduce-scatter.4.cloned.1.call-done = bf16[192,1152]{1,0:T(8,128)(2,1)} async-done(((bf16[3072,1152]{1,0:T(8,128)(2,1)}), bf16[192,1152]{1,0:T(8,128)(2,1)}) %reduce-scatter.4.cloned.1.call-update) | async-done | bytes 442384 | tf_op jit(solution)/shard_map/reduce_scatter | solution.py:883
  382.7 29.9 %shard_map.237 = (f32[512,1152]{1,0:T(8,128)}, bf16[512,3456]{1,0:T(8,128)(2,1)}, f32[2,8,1152]{2,1,0:T(8,128)}) custom-call(f32[512,2304]{1,0:T(8,128)} %get-tuple-element.92.refs_0_, bf16[512,1152]{1,0:T(8,128)(2,1)} %get-tuple-element.93.refs_1_, bf16[512,1152]{1,0:T(8,128)(2,1)} %get-tuple-element.108.refs_2_, f32[512,1152]{1,0:T(8,128)} %get-tuple-element.109.refs_3_, ...), custom_call_target="tpu_custom_call" | custom-call | flops 5586812928 | bytes 19759104 | tf_op jit(solution)/shard_map/pallas_call | solution.py:728
  412.5 11.6 %shard_map.238 = bf16[8,144,4608]{2,1,0:T(8,128)(2,1)} custom-call(bf16[512,1152]{1,0:T(8,128)(2,1)} %get-tuple-element.111.refs_0_, bf16[512,1152]{1,0:T(8,128)(2,1)} %get-tuple-element.112.refs_1_, bf16[512,3456]{1,0:T(8,128)(2,1)} %get-tuple-element.113.refs_2_, bf16[512,1152]{1,0:T(8,128)(2,1)} %get-tuple-element.114.refs_3_), custom_call_target="tpu_custom_call" | custom-call | flops 5435817984 | bytes 10616832 | tf_op jit(solution)/shard_map/pallas_call | solution.py:834
  426.1 1.8 collective-permute-start.13
  427.8 4.0 collective-permute-done.13
  432.3 5.3 dynamic-slice_bitcast_fusion
  438.0 2.0 collective-permute-start.15
  440.0 5.1 collective-permute-done.15
  445.9 1.4 collective-permute-done.16
  448.8 7.9 %fusion = bf16[8,72,4608]{2,1,0:T(8,128)(2,1)} fusion(bf16[8,72,4608]{2,1,0:T(8,128)(2,1)} %collective-permute-done.12, bf16[8,2,72,4608]{3,2,1,0:T(8,128)(2,1)} %bitcast.255, s32[]{:T(128)S(6)} %select_n.357), kind=kLoop, calls=%fused_computation.1 | loop fusion | flops 10616832 | bytes 15925252 | tf_op jit(solution)/shard_map/convert_element_type | solution.py:896
  456.7 12.1 %reduce-scatter.6.cloned.1.call-done = bf16[72,6144]{1,0:T(8,128)(2,1)} async-done(((bf16[1152,6144]{1,0:T(8,128)(2,1)}), bf16[72,6144]{1,0:T(8,128)(2,1)}) %reduce-scatter.6.cloned.1.call-update) | async-done | bytes 884752 | tf_op jit(solution)/shard_map/reduce_scatter | solution.py:883
  469.9 2.0 collective-permute-start.22
  471.9 2.6 collective-permute-done.22
  474.4 1.7 collective-permute-start.23
  476.1 2.0 collective-permute-done.23
  478.1 1.7 collective-permute-start.24
  479.8 2.0 collective-permute-done.24
  481.9 4.2 convert_select_fusion
  489.3 2.5 collective-permute-done.17
  491.8 1.9 collective-permute-start.18
  493.7 3.4 collective-permute-done.18
  497.1 1.5 collective-permute-start.19
  498.7 3.3 collective-permute-done.19
  502.0 1.7 collective-permute-start.20
  505.7 2.2 collective-permute-done.20
  508.1 1.7 convolution_bitcast_fusion
  510.2 4.3 fusion.10
  514.5 17.8 %reduce-scatter.8.cloned.1.call-done = bf16[72,4608]{1,0:T(8,128)(2,1)} async-done(((bf16[576,4608]{1,0:T(8,128)(2,1)}), bf16[72,4608]{1,0:T(8,128)(2,1)}) %reduce-scatter.8.cloned.1.call-update) | async-done | bytes 663568 | tf_op jit(solution)/shard_map/reduce_scatter | solution.py:883
  532.2 2.0 fusion.6
  534.3 1.7 fusion.9
  (200 shorter events, 32.7 us)
Async XLA Ops:
  7.2 24.3 %copy-start = (bf16[1001,1152]{1,0:T(8,128)(2,1)S(1)}, bf16[1001,1152]{1,0:T(8,128)(2,1)}, u32[]{:S(2)}) copy-start(bf16[1001,1152]{1,0:T(8,128)(2,1)} %param.19) | copy-start | bytes 6918916
  7.2 2.9 copy-start.26
  7.2 2.9 copy-start.27
  7.2 137.0 %all-gather.3.cloned.1.call-start = ((), (), s32[]{:S(2)}) async-start(), calls=%async_computation.3 | async-start | bytes 26320896 | tf_op jit(solution)/shard_map/all_gather | solution.py:879
  7.3 7.0 %copy-start.25 = (s32[2,256]{1,0:T(2,128)S(1)}, s32[2,256]{1,0:T(2,128)}, u32[]{:S(2)}) copy-start(s32[2,256]{1,0:T(2,128)} %param.18) | copy-start | bytes 6148
  10.0 10.5 %copy-start.2 = (bf16[2,256,1152]{2,1,0:T(8,128)(2,1)S(1)}, bf16[2,256,1152]{2,1,0:T(8,128)(2,1)}, u32[]{:S(2)}) copy-start(bf16[2,256,1152]{2,1,0:T(8,128)(2,1)} %param.14) | copy-start | bytes 3538948
  10.0 179.5 %all-gather.5.cloned.1.call-start = ((), (), s32[]{:S(2)}) async-start(), calls=%async_computation.4 | async-start | bytes 7520256 | tf_op jit(solution)/shard_map/all_gather | solution.py:879
  10.1 11.6 %collective-permute-start = (s32[1,2,2]{2,1,0:T(2,128)S(1)}, s32[1,2,2]{2,1,0:T(2,128)S(1)}, u32[]{:S(2)}, u32[]{:S(2)}) collective-permute-start(s32[1,2,2]{2,1,0:T(2,128)S(1)} %add_bitcast_fusion.2), channel_id=1, source_target_pairs={{0,8},{1,9},{2,10},{3,11},{4,12},{5,13},{6,14},{7,15},{8,0},{9,1},... | collective-permute-start | bytes 56 | tf_op jit(solution)/shard_map/ppermute | solution.py:910
  16.2 0.7 copy-start.6
  16.2 1.6 copy-start.8
  21.7 10.5 %copy-start.3 = (bf16[1,72,6912]{2,1,0:T(8,128)(2,1)S(1)}, bf16[1,72,6912]{2,1,0:T(8,128)(2,1)}, u32[]{:S(2)}) copy-start(bf16[1,72,6912]{2,1,0:T(8,128)(2,1)} %param.20) | copy-start | bytes 2985988
  21.7 3.7 collective-permute-start.1
  25.6 3.6 collective-permute-start.2
  29.4 1.2 collective-permute-start.3
  31.1 1.4 copy-start.23
  32.1 2.7 copy-start.11
  32.2 2.6 copy-start.21
  32.2 4.5 copy-start.14
  32.6 1.9 collective-permute-start.4
  32.9 15.0 %copy-start.7 = (f32[512,18]{1,0:T(8,128)S(1)}, f32[512,18]{1,0:T(8,128)}, u32[]{:S(2)}) copy-start(f32[512,18]{1,0:T(8,128)} %copy-done.6) | copy-start | bytes 110596
  32.9 15.0 %copy-start.9 = (f32[512,18]{1,0:T(8,128)S(1)}, f32[512,18]{1,0:T(8,128)}, u32[]{:S(2)}) copy-start(f32[512,18]{1,0:T(8,128)} %copy-done.8) | copy-start | bytes 110596
  34.5 21.4 %copy-start.17 = (bf16[512,128]{1,0:T(8,128)(2,1)S(1)}, bf16[512,128]{1,0:T(8,128)(2,1)}, u32[]{:S(2)}) copy-start(bf16[512,128]{1,0:T(8,128)(2,1)} %subtract_convert_fusion.1) | copy-start | bytes 393220
  34.5 21.4 %copy-start.18 = (bf16[512,128]{1,0:T(8,128)(2,1)S(1)}, bf16[512,128]{1,0:T(8,128)(2,1)}, u32[]{:S(2)}) copy-start(bf16[512,128]{1,0:T(8,128)(2,1)} %get-tuple-element.129) | copy-start | bytes 393220
  34.5 21.4 %copy-start.19 = (bf16[512,128]{1,0:T(8,128)(2,1)S(1)}, bf16[512,128]{1,0:T(8,128)(2,1)}, u32[]{:S(2)}) copy-start(bf16[512,128]{1,0:T(8,128)(2,1)} %get-tuple-element.130) | copy-start | bytes 393220
  34.8 109.9 %copy-start.28 = (f32[1,72]{1,0:T(1,128)S(1)}, f32[1,72]{1,0:T(1,128)}, u32[]{:S(2)}) copy-start(f32[1,72]{1,0:T(1,128)} %param.27) | copy-start | bytes 868
  34.8 109.9 %copy-start.29 = (f32[1,72]{1,0:T(1,128)S(1)}, f32[1,72]{1,0:T(1,128)}, u32[]{:S(2)}) copy-start(f32[1,72]{1,0:T(1,128)} %param.26) | copy-start | bytes 868
  34.8 12.8 %collective-permute-start.5 = (f32[4,2,6912]{2,1,0:T(2,128)S(1)}, f32[4,2,6912]{2,1,0:T(2,128)S(1)}, u32[]{:S(2)}, u32[]{:S(2)}) collective-permute-start(f32[4,2,6912]{2,1,0:T(2,128)S(1)} %dynamic-slice_bitcast_fusion.2), channel_id=1, source_target_pairs={{0,2},{1,3},{2,0},{3,1},{4,6},{5,7},{6,4},{7,5},{8,10},{9,11},{10,... | collective-permute-start | bytes 663560 | tf_op jit(solution)/shard_map/ppermute | solution.py:910
  47.8 7.8 %collective-permute-start.6 = (f32[2,2,6912]{2,1,0:T(2,128)S(1)}, f32[2,2,6912]{2,1,0:T(2,128)S(1)}, u32[]{:S(2)}, u32[]{:S(2)}) collective-permute-start(f32[2,2,6912]{2,1,0:T(2,128)S(1)} %dynamic-slice_bitcast_fusion.3), channel_id=1, source_target_pairs={{0,4},{1,5},{2,6},{3,7},{4,0},{5,1},{6,2},{7,3},{8,12},{9,13},{10,... | collective-permute-start | bytes 331784 | tf_op jit(solution)/shard_map/ppermute | solution.py:910
  55.7 6.8 %collective-permute-start.7 = (f32[1,2,6912]{2,1,0:T(2,128)S(1)}, f32[1,2,6912]{2,1,0:T(2,128)S(1)}, u32[]{:S(2)}, u32[]{:S(2)}) collective-permute-start(f32[1,2,6912]{2,1,0:T(2,128)S(1)} %constant_dynamic-slice_fusion), channel_id=1, source_target_pairs={{0,8},{1,9},{2,10},{3,11},{4,12},{5,13},{6,14},{7,15},{8,0},{9,1},... | collective-permute-start | bytes 165896 | tf_op jit(solution)/shard_map/ppermute | solution.py:910
  144.2 237.9 %reduce-scatter.4.cloned.1.call-start = ((), (), s32[]{:S(2)}) async-start(), calls=%async_computation.5 | async-start | bytes 7520256 | tf_op jit(solution)/shard_map/reduce_scatter | solution.py:883
  195.6 19.4 %collective-permute-start.9 = (bf16[256,1152]{1,0:T(8,128)(2,1)}, bf16[256,1152]{1,0:T(8,128)(2,1)S(1)}, u32[]{:S(2)}, u32[]{:S(2)}) collective-permute-start(bf16[256,1152]{1,0:T(8,128)(2,1)} %shard_map.226), channel_id=1, source_target_pairs={{0,16},{1,17},{2,18},{3,19},{4,20},{5,21},{6,22},{7,23},{8,24},{9,... | collective-permute-start | bytes 1769480 | tf_op jit(solution)/shard_map/ppermute | solution.py:1040
  205.6 22.7 %collective-permute-start.8 = (bf16[256,1152]{1,0:T(8,128)(2,1)}, bf16[256,1152]{1,0:T(8,128)(2,1)S(1)}, u32[]{:S(2)}, u32[]{:S(2)}) collective-permute-start(bf16[256,1152]{1,0:T(8,128)(2,1)} %shard_map.224), channel_id=1, source_target_pairs={{0,16},{1,17},{2,18},{3,19},{4,20},{5,21},{6,22},{7,23},{8,24},{9,... | collective-permute-start | bytes 1769480 | tf_op jit(solution)/shard_map/ppermute | solution.py:1040
  215.1 0.8 copy-start.15
  228.3 0.8 copy-start.16
  284.0 28.3 %collective-permute-start.11 = (bf16[256,1152]{1,0:T(8,128)(2,1)}, bf16[256,1152]{1,0:T(8,128)(2,1)S(1)}, u32[]{:S(2)}, u32[]{:S(2)}) collective-permute-start(bf16[256,1152]{1,0:T(8,128)(2,1)} %shard_map.232), channel_id=1, source_target_pairs={{16,0},{17,1},{18,2},{19,3},{20,4},{21,5},{22,6},{23,7},{24,8},{25... | collective-permute-start | bytes 1769480 | tf_op jit(solution)/shard_map/ppermute | solution.py:1071
  300.9 17.6 %collective-permute-start.10 = (bf16[256,1152]{1,0:T(8,128)(2,1)}, bf16[256,1152]{1,0:T(8,128)(2,1)S(1)}, u32[]{:S(2)}, u32[]{:S(2)}) collective-permute-start(bf16[256,1152]{1,0:T(8,128)(2,1)} %shard_map.230), channel_id=1, source_target_pairs={{16,0},{17,1},{18,2},{19,3},{20,4},{21,5},{22,6},{23,7},{24,8},{25... | collective-permute-start | bytes 1769480 | tf_op jit(solution)/shard_map/ppermute | solution.py:1071
  312.4 0.8 copy-start.5
  318.5 0.8 copy-start.13
  328.0 140.8 %reduce-scatter.6.cloned.1.call-start = ((), (), s32[]{:S(2)}) async-start(), calls=%async_computation.6 | async-start | bytes 15040512 | tf_op jit(solution)/shard_map/reduce_scatter | solution.py:883
  382.1 150.1 %reduce-scatter.8.cloned.1.call-start = ((), (), s32[]{:S(2)}) async-start(), calls=%async_computation.7 | async-start | bytes 5971968 | tf_op jit(solution)/shard_map/reduce_scatter | solution.py:883
  426.1 5.8 %collective-permute-start.13 = (bf16[1,2,6912]{2,1,0:T(2,128)(2,1)S(1)}, bf16[1,2,6912]{2,1,0:T(2,128)(2,1)S(1)}, u32[]{:S(2)}, u32[]{:S(2)}) collective-permute-start(bf16[1,2,6912]{2,1,0:T(2,128)(2,1)S(1)} %convert_element_type.163), channel_id=1, source_target_pairs={{0,8},{1,9},{2,10},{3,11},{4,12},{5,13},{6,14},{7,15},{8,0},{9,1},... | collective-permute-start | bytes 82952 | tf_op jit(solution)/shard_map/ppermute | solution.py:910
  432.0 5.6 %collective-permute-start.14 = (bf16[2,2,6912]{2,1,0:T(2,128)(2,1)S(1)}, bf16[2,2,6912]{2,1,0:T(2,128)(2,1)S(1)}, u32[]{:S(2)}, u32[]{:S(2)}) collective-permute-start(bf16[2,2,6912]{2,1,0:T(2,128)(2,1)S(1)} %maximum_bitcast_fusion), channel_id=1, source_target_pairs={{0,4},{1,5},{2,6},{3,7},{4,0},{5,1},{6,2},{7,3},{8,12},{9,13},{10,... | collective-permute-start | bytes 165896 | tf_op jit(solution)/shard_map/ppermute | solution.py:910
  437.6 11.2 %collective-permute-start.12 = (bf16[8,72,4608]{2,1,0:T(8,128)(2,1)}, bf16[8,72,4608]{2,1,0:T(8,128)(2,1)}, u32[]{:S(2)}, u32[]{:S(2)}) collective-permute-start(bf16[8,72,4608]{2,1,0:T(8,128)(2,1)} %dynamic-slice_bitcast_fusion), channel_id=1, source_target_pairs={{0,1},{1,0},{2,3},{3,2},{4,5},{5,4},{6,7},{7,6},{8,9},{9,8},{10,11... | collective-permute-start | bytes 15925256 | tf_op jit(solution)/shard_map/ppermute | solution.py:910
  438.0 7.1 %collective-permute-start.15 = (bf16[4,2,6912]{2,1,0:T(2,128)(2,1)S(1)}, bf16[4,2,6912]{2,1,0:T(2,128)(2,1)S(1)}, u32[]{:S(2)}, u32[]{:S(2)}) collective-permute-start(bf16[4,2,6912]{2,1,0:T(2,128)(2,1)S(1)} %bitcast.269), channel_id=1, source_target_pairs={{0,2},{1,3},{2,0},{3,1},{4,6},{5,7},{6,4},{7,5},{8,10},{9,11},{10,... | collective-permute-start | bytes 331784 | tf_op jit(solution)/shard_map/ppermute | solution.py:910
  445.8 1.5 collective-permute-start.16
  469.9 4.5 collective-permute-start.22
  474.4 3.6 collective-permute-start.23
  478.1 3.7 collective-permute-start.24
  481.8 4.3 collective-permute-start.25
  481.9 4.8 copy-start.20
  481.9 5.7 %copy-start.4 = (bf16[1,72,6912]{2,1,0:T(8,128)(2,1)S(1)}, bf16[1,72,6912]{2,1,0:T(8,128)(2,1)}, u32[]{:S(2)}) copy-start(bf16[1,72,6912]{2,1,0:T(8,128)(2,1)} %param.20) | copy-start | bytes 2985988
  486.1 3.1 copy-start.10
  488.0 3.8 collective-permute-start.17
  491.8 5.3 collective-permute-start.18
  493.7 14.4 %copy-start.22 = (bf16[32,72]{1,0:T(8,128)(2,1)S(1)}, bf16[32,72]{1,0:T(8,128)(2,1)}, u32[]{:S(2)}) copy-start(bf16[32,72]{1,0:T(8,128)(2,1)} %copy-done.21) | copy-start | bytes 13828
  497.1 4.8 collective-permute-start.19
  502.0 5.9 %collective-permute-start.20 = (f32[4,32,72]{2,1,0:T(8,128)S(1)}, f32[4,32,72]{2,1,0:T(8,128)S(1)}, u32[]{:S(2)}, u32[]{:S(2)}) collective-permute-start(f32[4,32,72]{2,1,0:T(8,128)S(1)} %bitcast.270), channel_id=1, source_target_pairs={{0,2},{1,3},{2,0},{3,1},{4,6},{5,7},{6,4},{7,5},{8,10},{9,11},{10,... | collective-permute-start | bytes 110600 | tf_op jit(solution)/shard_map/ppermute | solution.py:910
  507.9 2.2 copy-start.12
  508.0 2.2 copy-start.24
  508.0 1.8 collective-permute-start.21
  510.0 25.9 %copy-start.1 = (bf16[1001,1152]{1,0:T(8,128)(2,1)S(1)}, bf16[1001,1152]{1,0:T(8,128)(2,1)}, u32[]{:S(2)}) copy-start(bf16[1001,1152]{1,0:T(8,128)(2,1)} %param.19) | copy-start | bytes 6918916
Sparse Core Ops, SparseCore 0:
  10.2 133.9 all-gather.2
  145.8 43.6 all-gather.4
  328.1 53.9 reduce-scatter.3
  384.4 84.3 reduce-scatter.5
  471.1 61.0 reduce-scatter.7

commit v7 on v6

--- a/solution.py
+++ b/solution.py
@@ -413,22 +413,32 @@
     return [pl.BlockSpec(array.shape, lambda i: (0, 0)) for array in arrays]
 
 
-def act_backward(mlp_grads, down, step):
+def act_backward(active, mlp_grads, down, step):
     hidden, width = down.shape
     tokens = sum(grad.shape[0] for grad in mlp_grads)
 
-    def body(*refs):
-        refs[-1][...] = dot_right(stacked(refs[:-2]), refs[-2][...]).astype(bf16)
+    def body(active_ref, *refs):
+        @pl.when(active_ref[0] == 0)
+        def _():
+            refs[-1][...] = jnp.zeros_like(refs[-1])
+
+        @pl.when(active_ref[0] != 0)
+        def _():
+            refs[-1][...] = dot_right(stacked(refs[:-2]), refs[-2][...]).astype(bf16)
 
     return pl.pallas_call(
         body,
-        grid=(hidden // step,),
-        in_specs=whole_specs(mlp_grads) + [pl.BlockSpec((step, width), lambda i: (i, 0))],
-        out_specs=pl.BlockSpec((tokens, step), lambda i: (0, i)),
+        grid_spec=pltpu.PrefetchScalarGridSpec(
+            num_scalar_prefetch=1,
+            grid=(hidden // step,),
+            in_specs=[pl.BlockSpec(grad.shape, lambda i, active: (0, 0)) for grad in mlp_grads]
+            + [pl.BlockSpec((step, width), lambda i, active: (i * active[0], 0))],
+            out_specs=pl.BlockSpec((tokens, step), lambda i, active: (0, i)),
+        ),
         out_shape=jax.ShapeDtypeStruct((tokens, hidden), bf16),
         compiler_params=params(),
         cost_estimate=cost(2 * tokens * width * hidden, 2 * width * hidden + 4 * tokens * width),
-    )(*mlp_grads, down)
+    )(active, *mlp_grads, down)
 
 
 def mlp_backward(
@@ -986,6 +996,7 @@
 ):
     first_section = lax.axis_index("section") == 0
     first_only = first_section.astype(jnp.int32).reshape(1)
+    second_only = 1 - first_only
     always = jnp.ones((1,), jnp.int32)
     count = lax.axis_size("dp")
     me = lax.axis_index("dp")
@@ -1040,7 +1051,7 @@
         received.append(lax.ppermute(early, "section", [(0, 1)]))
     mlp_grad, unused = lax.optimization_barrier((mlp_gradient(cot, [], mod, 0, images), early))
     mlp_grads = [mlp_grad]
-    act_grad = act_backward(mlp_grads, down, hidden // 2)
+    act_grad = act_backward(second_only, mlp_grads, down, hidden // 2)
     kept = None
     for image in range(images):
         kept = attention_forward(
@@ -1082,7 +1093,7 @@
     mlp_grads = [*mlp_grads, mlp_grad]
     down_term, mlp_grads = lax.optimization_barrier((down_term, mlp_grads))
     down_part = scatter_walk(down_term, [walk_of(count)])
-    act_grad = act_backward(mlp_grads, down, hidden // 2)
+    act_grad = act_backward(always, mlp_grads, down, hidden // 2)
     middle_grad, mixed_grad, gate_grad, up_grad, branch_grad, mlp_sums = mlp_backward(
         cot, backs, act_grad, [gate, up], joined, middle, mod, walked, chips, [mlp, branch]
     )

time: 548 us -> 545 us (level)
  no operation moved by 1% of the time
where the time goes in v7:
time: 545 us; the launch traced here: 539 us
  Pallas kernels  242 us (44%)
  waiting for transfers between devices  192 us (35%)
  other arithmetic  34.3 us (6%)
  starting transfers between devices  33.7 us (6%)
  local copies, waits for them, and re-layouts  15.6 us (3%)
  between operations  14.9 us (3%)
  matrix products  7.2 us (1%)
    all_gather x2, waiting for transfers between devices, gather_walk(): lax.all_gather(rows, 'dp', axis=0, tiled=True, axis_index_groups=[walk_of...  92.3 us
    pallas_call x3, Pallas kernels, attention_backward(): pl.pallas_call(body, grid=(count,), in_specs=[anywhere] * 5 + [pl.BlockSp...  60.6 us
    ppermute x21, waiting for transfers between devices, swapped(): lax.ppermute(block, 'dp', [(device, device ^ bit) for device in range(cou...  55.2 us
    pallas_call x2, Pallas kernels, mlp_backward(): pl.pallas_call(body, grid=(count,), in_specs=[block, pl.BlockSpec(mod.sha...  50 us
    pallas_call x3, Pallas kernels, attention_forward(): pl.pallas_call(body, grid=(count,), in_specs=[pl.BlockSpec((patches, widt...  45 us
    reduce_scatter x3, waiting for transfers between devices, scatter_walk(): lax.psum_scatter(rows, 'dp', scatter_dimension=0, tiled=True, axis_index_...  39.1 us
    pallas_call x2, Pallas kernels, matrix_grad(): pl.pallas_call(functools.partial(matrix_grad_kernel, places_of(parts, wal...  25.3 us
    ppermute x21, starting transfers between devices, swapped(): lax.ppermute(block, 'dp', [(device, device ^ bit) for device in range(cou...  25 us
  transfers between devices with their start and end apart: 31, of which 23 were waited for; matrix products, arithmetic and copies ran while one was open for 9% of the time, Pallas kernels for 32%

profile of v7, /device:TPU:0, one launch (start us, length us, event | category | flops | bytes accessed | tf_op | source)
XLA Modules:
  0.0 538.9 jit_solution(14776582137058849324)
XLA Ops:
  7.3 2.7 pad_maximum_fusion
  10.1 4.1 collective-permute-start
  14.3 1.9 fusion.18
  21.7 1.6 collective-permute-start.1
  23.4 2.0 collective-permute-done.1
  25.6 1.5 collective-permute-start.2
  27.1 2.1 collective-permute-done.2
  32.9 1.5 collective-permute-done.4
  34.8 1.8 collective-permute-start.5
  37.8 9.9 %collective-permute-done.5 = f32[4,2,6912]{2,1,0:T(2,128)S(1)} collective-permute-done((f32[4,2,6912]{2,1,0:T(2,128)S(1)}, f32[4,2,6912]{2,1,0:T(2,128)S(1)}, u32[]{:S(2)}, u32[]{:S(2)}) %collective-permute-start.5) | collective-permute-done | bytes 221216 | tf_op jit(solution)/shard_map/ppermute | solution.py:920
  48.1 7.5 %collective-permute-done.6 = f32[2,2,6912]{2,1,0:T(2,128)S(1)} collective-permute-done((f32[2,2,6912]{2,1,0:T(2,128)S(1)}, f32[2,2,6912]{2,1,0:T(2,128)S(1)}, u32[]{:S(2)}, u32[]{:S(2)}) %collective-permute-start.6) | collective-permute-done | bytes 110624 | tf_op jit(solution)/shard_map/ppermute | solution.py:920
  56.8 5.7 %collective-permute-done.7 = f32[1,2,6912]{2,1,0:T(2,128)S(1)} collective-permute-done((f32[1,2,6912]{2,1,0:T(2,128)S(1)}, f32[1,2,6912]{2,1,0:T(2,128)S(1)}, u32[]{:S(2)}, u32[]{:S(2)}) %collective-permute-start.7) | collective-permute-done | bytes 55328 | tf_op jit(solution)/shard_map/ppermute | solution.py:920
  63.2 81.0 %all-gather.3.cloned.1.call-done = bf16[1152,10752]{1,0:T(8,128)(2,1)} async-done(((bf16[72,10752]{1,0:T(8,128)(2,1)}), bf16[1152,10752]{1,0:T(8,128)(2,1)}) %all-gather.3.cloned.1.call-update) | async-done | bytes 24772624 | tf_op jit(solution)/shard_map/all_gather | solution.py:889
  145.5 19.9 %shard_map.222 = (f32[512,1152]{1,0:T(8,128)}, bf16[512,1152]{1,0:T(8,128)(2,1)}) custom-call(bf16[512,1152]{1,0:T(8,128)(2,1)} %bitcast.256, f32[2,8,1152]{2,1,0:T(8,128)} %pad.15.mod_ref.refs_1_.refs_2_.refs_5_, bf16[512,256]{1,0:T(8,128)(2,1)} %get-tuple-element.70.refs_2_.refs_3_.refs_6_, bf16[512,256]{1,0:T(8,128)(2,1)} %get-tuple-element.71.refs_3_.refs_4_.refs_7_, ...), custom_call_target="tpu_custom_call" | custom-call | flops 6039797760 | bytes 22413312 | tf_op jit(solution)/shard_map/pallas_call | solution.py:246
  165.4 12.8 %shard_map.223.act_ref = bf16[512,3072]{1,0:T(8,128)(2,1)} custom-call(bf16[512,1152]{1,0:T(8,128)(2,1)} %get-tuple-element.76.normed_ref, bf16[8,144,10752]{2,1,0:T(8,128)(2,1)} %bitcast.226, bf16[8,144,10752]{2,1,0:T(8,128)(2,1)} %bitcast.227, bf16[8,144,10752]{2,1,0:T(8,128)(2,1)} %bitcast.228, bf16[8,144,10752]{2,1,0:T(8,128)(2,1)} %bitcast.229), custom_call_target="tpu_custom_call" | custom-call | flops 7247757312 | bytes 17301504 | tf_op jit(solution)/shard_map/pallas_call | solution.py:310
  178.2 11.3 %all-gather.5.cloned.1.call-done.down_ref.refs_1_.refs_2_ = bf16[3072,1152]{1,0:T(8,128)(2,1)} async-done(((bf16[192,1152]{1,0:T(8,128)(2,1)}), bf16[3072,1152]{1,0:T(8,128)(2,1)}) %all-gather.5.cloned.1.call-update) | async-done | bytes 7077904 | tf_op jit(solution)/shard_map/all_gather | solution.py:889
  189.5 6.1 %shard_map.226 = bf16[256,1152]{1,0:T(8,128)(2,1)} custom-call(s32[1]{0:T(128)} %bitcast.active_ref, bf16[512,3072]{1,0:T(8,128)(2,1)} %shard_map.223.act_ref, f32[512,1152]{1,0:T(8,128)} %get-tuple-element.77.middle_ref, f32[2,8,1152]{2,1,0:T(8,128)} %pad.15.mod_ref.refs_1_.refs_2_.refs_5_, ...), custom_call_target="tpu_custom_call" | custom-call | flops 1811939328 | bytes 9437184 | tf_op jit(solution)/shard_map/pallas_call | solution.py:358
  197.0 2.5 shard_map.221.refs_0_
  199.5 6.1 %shard_map.224 = bf16[256,1152]{1,0:T(8,128)(2,1)} custom-call(s32[1]{0:T(128)} %bitcast.active_ref, bf16[512,3072]{1,0:T(8,128)(2,1)} %shard_map.223.act_ref, f32[512,1152]{1,0:T(8,128)} %get-tuple-element.77.middle_ref, f32[2,8,1152]{2,1,0:T(8,128)} %pad.15.mod_ref.refs_1_.refs_2_.refs_5_, ...), custom_call_target="tpu_custom_call" | custom-call | flops 1811939328 | bytes 9437184 | tf_op jit(solution)/shard_map/pallas_call | solution.py:358
  206.9 4.3 shard_map.225.act_grad_ref
  212.0 12.4 %shard_map.227 = (bf16[512,1152]{1,0:T(8,128)(2,1)}, f32[512,2304]{1,0:T(8,128)}, bf16[512,1152]{1,0:T(8,128)(2,1)}, bf16[512,1152]{1,0:T(8,128)(2,1)}, f32[512,...) custom-call(bf16[256,1152]{1,0:T(8,128)(2,1)} %copy-done.15, ...), custom_call_target="tpu_custom_call" | custom-call | flops 3019898880 | bytes 16515072 | tf_op jit(solution)/shard_map/pallas_call | solution.py:246
  225.3 12.6 %shard_map.228 = (bf16[512,1152]{1,0:T(8,128)(2,1)}, f32[512,2304]{1,0:T(8,128)}, bf16[512,1152]{1,0:T(8,128)(2,1)}, bf16[512,1152]{1,0:T(8,128)(2,1)}, f32[512,...) custom-call(bf16[256,1152]{1,0:T(8,128)(2,1)} %copy-done.16, ...), custom_call_target="tpu_custom_call", output_to_operand_aliasing={{0}: (11, {}), {1}: (12, {}), {2}: (13, {}), {3}: (14, {}),... | custom-call | flops 3019898880 | bytes 16515072 | tf_op jit(solution)/shard_map/pallas_call | solution.py:246
  238.0 26.9 %shard_map.229 = (f32[512,1152]{1,0:T(8,128)}, bf16[512,1152]{1,0:T(8,128)(2,1)}, bf16[512,3072]{1,0:T(8,128)(2,1)}, bf16[512,3072]{1,0:T(8,128)(2,1)}, bf16[512,3072]{1,0:T(8,128)(2,1)}) custom-call(bf16[512,3072]{1,0:T(8,128)(2,1)} %shard_map.225.act_grad_ref, f32[2,8,1152]{2,1,0:T(8,128)} %pad.15.mod_ref.refs_1_.refs_2_.refs_5_, ...), custom_call_target="tpu_custom_call" | custom-call | flops 15854469120 | bytes 23592960 | tf_op jit(solution)/shard_map/pallas_call | solution.py:559
  264.8 15.3 %shard_map.232 = bf16[256,1152]{1,0:T(8,128)(2,1)} custom-call(f32[512,2304]{1,0:T(8,128)} %get-tuple-element.92.refs_0_, bf16[512,1152]{1,0:T(8,128)(2,1)} %get-tuple-element.93.refs_1_, bf16[512,1152]{1,0:T(8,128)(2,1)} %get-tuple-element.94.refs_2_, f32[512,1152]{1,0:T(8,128)} %get-tuple-element.95.refs_3_, bf16[512,1152]{1,0:T(8,128)(2,1)} %get-tuple-element.96.refs_4_, ...), custom_call_target="tpu_custom_call" | custom-call | flops 2793406464 | bytes 13860864 | tf_op jit(solution)/shard_map/pallas_call | solution.py:738
  280.2 1.5 collective-permute-start.11
  281.7 15.3 %shard_map.230 = bf16[256,1152]{1,0:T(8,128)(2,1)} custom-call(f32[512,2304]{1,0:T(8,128)} %get-tuple-element.92.refs_0_, bf16[512,1152]{1,0:T(8,128)(2,1)} %get-tuple-element.93.refs_1_, bf16[512,1152]{1,0:T(8,128)(2,1)} %get-tuple-element.94.refs_2_, f32[512,1152]{1,0:T(8,128)} %get-tuple-element.95.refs_3_, bf16[512,1152]{1,0:T(8,128)(2,1)} %get-tuple-element.96.refs_4_, ...), custom_call_target="tpu_custom_call" | custom-call | flops 2793406464 | bytes 13860864 | tf_op jit(solution)/shard_map/pallas_call | solution.py:738
  297.0 1.5 collective-permute-start.10
  298.5 10.0 %shard_map.231 = (bf16[512,1152]{1,0:T(8,128)(2,1)}, f32[512,1152]{1,0:T(8,128)}) custom-call(s32[1]{0:T(128)} %constant.118.clone.1.active_ref, bf16[512,3072]{1,0:T(8,128)(2,1)} %get-tuple-element.97.act_ref, f32[512,1152]{1,0:T(8,128)} %get-tuple-element.90.refs_6_.middle_ref.refs_9_, f32[2,8,1152]{2,1,0:T(8,128)} %pad.15.mod_ref.refs_1_.refs_2_.refs_5_, ...), custom_call_target="tpu_custom_call" | custom-call | flops 3623878656 | bytes 11796480 | tf_op jit(solution)/shard_map/pallas_call | solution.py:358
  309.3 2.3 shard_map.233.refs_0_
  311.6 3.0 collective-permute-done.10.back_ref.refs_7_
  315.5 8.7 %shard_map.234 = (bf16[3072,1152]{1,0:T(8,128)(2,1)}, bf16[256,1152]{1,0:T(8,128)(2,1)}) custom-call(bf16[512,3072]{1,0:T(8,128)(2,1)} %get-tuple-element.97.act_ref, bf16[512,1152]{1,0:T(8,128)(2,1)} %bitcast.251, bf16[256,1152]{1,0:T(8,128)(2,1)} %copy-done.13, f32[2,8,1152]{2,1,0:T(8,128)} %pad.15.mod_ref.refs_1_.refs_2_.refs_5_, ...), custom_call_target="tpu_custom_call" | custom-call | flops 3623878656 | bytes 7077888 | tf_op jit(solution)/shard_map/pallas_call | solution.py:793
  324.2 8.0 %shard_map.235.act_grad_ref = bf16[512,3072]{1,0:T(8,128)(2,1)} custom-call(s32[1]{0:T(128)} %constant.118.clone.1.active_ref, bf16[256,1152]{1,0:T(8,128)(2,1)} %shard_map.233.refs_0_, bf16[256,1152]{1,0:T(8,128)(2,1)} %get-tuple-element.104.refs_1_, bf16[3072,1152]{1,0:T(8,128)(2,1)} %all-gather.5.cloned.1.call-done.down_ref.refs_1_.refs_2_), custom_call_target="tpu_custom_call" | custom-call | flops 3623878656 | bytes 9437184 | tf_op jit(solution)/shard_map/pallas_call | solution.py:429
  332.2 23.1 %shard_map.236 = (f32[512,1152]{1,0:T(8,128)}, bf16[512,1152]{1,0:T(8,128)(2,1)}, bf16[512,3072]{1,0:T(8,128)(2,1)}, bf16[512,3072]{1,0:T(8,128)(2,1)}, bf16[512...) custom-call(bf16[512,3072]{1,0:T(8,128)(2,1)} %shard_map.235.act_grad_ref, f32[2,8,1152]{2,1,0:T(8,128)} %pad.15.mod_ref.refs_1_.refs_2_.refs_5_, ...), custom_call_target="tpu_custom_call" | custom-call | flops 15854469120 | bytes 23592960 | tf_op jit(solution)/shard_map/pallas_call | solution.py:559
  355.4 13.7 %shard_map.239 = bf16[8,144,6144]{2,1,0:T(8,128)(2,1)} custom-call(bf16[512,1152]{1,0:T(8,128)(2,1)} %get-tuple-element.89.refs_4_.refs_0_.refs_1_, bf16[512,1152]{1,0:T(8,128)(2,1)} %get-tuple-element.89.refs_4_.refs_0_.refs_1_, bf16[512,3072]{1,0:T(8,128)(2,1)} %get-tuple-element.117.refs_2_, bf16[512,3072]{1,0:T(8,128)(2,1)} %get-tuple-element.118.refs_3_), custom_call_target="tpu_custom_call" | custom-call | flops 7247757312 | bytes 14155776 | tf_op jit(solution)/shard_map/pallas_call | solution.py:844
  369.0 9.2 %reduce-scatter.4.cloned.1.call-done = bf16[192,1152]{1,0:T(8,128)(2,1)} async-done(((bf16[3072,1152]{1,0:T(8,128)(2,1)}), bf16[192,1152]{1,0:T(8,128)(2,1)}) %reduce-scatter.4.cloned.1.call-update) | async-done | bytes 442384 | tf_op jit(solution)/shard_map/reduce_scatter | solution.py:893
  378.8 29.9 %shard_map.237 = (f32[512,1152]{1,0:T(8,128)}, bf16[512,3456]{1,0:T(8,128)(2,1)}, f32[2,8,1152]{2,1,0:T(8,128)}) custom-call(f32[512,2304]{1,0:T(8,128)} %get-tuple-element.92.refs_0_, bf16[512,1152]{1,0:T(8,128)(2,1)} %get-tuple-element.93.refs_1_, bf16[512,1152]{1,0:T(8,128)(2,1)} %get-tuple-element.108.refs_2_, f32[512,1152]{1,0:T(8,128)} %get-tuple-element.109.refs_3_, ...), custom_call_target="tpu_custom_call" | custom-call | flops 5586812928 | bytes 19759104 | tf_op jit(solution)/shard_map/pallas_call | solution.py:738
  408.7 11.7 %shard_map.238 = bf16[8,144,4608]{2,1,0:T(8,128)(2,1)} custom-call(bf16[512,1152]{1,0:T(8,128)(2,1)} %get-tuple-element.111.refs_0_, bf16[512,1152]{1,0:T(8,128)(2,1)} %get-tuple-element.112.refs_1_, bf16[512,3456]{1,0:T(8,128)(2,1)} %get-tuple-element.113.refs_2_, bf16[512,1152]{1,0:T(8,128)(2,1)} %get-tuple-element.114.refs_3_), custom_call_target="tpu_custom_call" | custom-call | flops 5435817984 | bytes 10616832 | tf_op jit(solution)/shard_map/pallas_call | solution.py:844
  422.2 1.8 collective-permute-start.13
  424.0 4.0 collective-permute-done.13
  428.4 5.3 dynamic-slice_bitcast_fusion
  434.1 2.1 collective-permute-start.15
  436.2 5.0 collective-permute-done.15
  445.0 7.9 %fusion = bf16[8,72,4608]{2,1,0:T(8,128)(2,1)} fusion(bf16[8,72,4608]{2,1,0:T(8,128)(2,1)} %collective-permute-done.12, bf16[8,2,72,4608]{3,2,1,0:T(8,128)(2,1)} %bitcast.255, s32[]{:T(128)S(6)} %select_n.357), kind=kLoop, calls=%fused_computation.1 | loop fusion | flops 10616832 | bytes 15925252 | tf_op jit(solution)/shard_map/convert_element_type | solution.py:906
  452.9 11.9 %reduce-scatter.6.cloned.1.call-done = bf16[72,6144]{1,0:T(8,128)(2,1)} async-done(((bf16[1152,6144]{1,0:T(8,128)(2,1)}), bf16[72,6144]{1,0:T(8,128)(2,1)}) %reduce-scatter.6.cloned.1.call-update) | async-done | bytes 884752 | tf_op jit(solution)/shard_map/reduce_scatter | solution.py:893
  465.8 1.7 collective-permute-start.22
  467.5 2.8 collective-permute-done.22
  470.4 1.8 collective-permute-start.23
  472.2 1.8 collective-permute-done.23
  474.1 2.0 collective-permute-start.24
  476.0 1.7 collective-permute-done.24
  477.9 4.2 convert_select_fusion
  483.9 1.9 collective-permute-start.17
  486.0 1.8 collective-permute-done.17
  487.7 1.6 collective-permute-start.18
  489.4 3.7 collective-permute-done.18
  493.1 1.8 collective-permute-start.19
  494.9 3.0 collective-permute-done.19
  498.0 2.0 collective-permute-start.20
  502.0 1.9 collective-permute-done.20
  504.0 1.7 convolution_bitcast_fusion
  506.2 4.3 fusion.10
  510.4 18.0 %reduce-scatter.8.cloned.1.call-done = bf16[72,4608]{1,0:T(8,128)(2,1)} async-done(((bf16[576,4608]{1,0:T(8,128)(2,1)}), bf16[72,4608]{1,0:T(8,128)(2,1)}) %reduce-scatter.8.cloned.1.call-update) | async-done | bytes 663568 | tf_op jit(solution)/shard_map/reduce_scatter | solution.py:893
  528.4 2.0 fusion.6
  530.5 1.7 fusion.9
  (200 shorter events, 32.9 us)
Async XLA Ops:
  7.2 24.3 %copy-start = (bf16[1001,1152]{1,0:T(8,128)(2,1)S(1)}, bf16[1001,1152]{1,0:T(8,128)(2,1)}, u32[]{:S(2)}) copy-start(bf16[1001,1152]{1,0:T(8,128)(2,1)} %param.19) | copy-start | bytes 6918916
  7.2 2.9 copy-start.26
  7.2 2.9 copy-start.27
  7.2 137.0 %all-gather.3.cloned.1.call-start = ((), (), s32[]{:S(2)}) async-start(), calls=%async_computation.3 | async-start | bytes 26320896 | tf_op jit(solution)/shard_map/all_gather | solution.py:889
  7.3 7.0 %copy-start.25 = (s32[2,256]{1,0:T(2,128)S(1)}, s32[2,256]{1,0:T(2,128)}, u32[]{:S(2)}) copy-start(s32[2,256]{1,0:T(2,128)} %param.18) | copy-start | bytes 6148
  10.0 10.5 %copy-start.2 = (bf16[2,256,1152]{2,1,0:T(8,128)(2,1)S(1)}, bf16[2,256,1152]{2,1,0:T(8,128)(2,1)}, u32[]{:S(2)}) copy-start(bf16[2,256,1152]{2,1,0:T(8,128)(2,1)} %param.14) | copy-start | bytes 3538948
  10.0 179.5 %all-gather.5.cloned.1.call-start = ((), (), s32[]{:S(2)}) async-start(), calls=%async_computation.4 | async-start | bytes 7520256 | tf_op jit(solution)/shard_map/all_gather | solution.py:889
  10.1 11.6 %collective-permute-start = (s32[1,2,2]{2,1,0:T(2,128)S(1)}, s32[1,2,2]{2,1,0:T(2,128)S(1)}, u32[]{:S(2)}, u32[]{:S(2)}) collective-permute-start(s32[1,2,2]{2,1,0:T(2,128)S(1)} %add_bitcast_fusion.2), channel_id=1, source_target_pairs={{0,8},{1,9},{2,10},{3,11},{4,12},{5,13},{6,14},{7,15},{8,0},{9,1},... | collective-permute-start | bytes 56 | tf_op jit(solution)/shard_map/ppermute | solution.py:920
  16.2 0.7 copy-start.6
  16.2 1.6 copy-start.8
  21.7 10.5 %copy-start.3 = (bf16[1,72,6912]{2,1,0:T(8,128)(2,1)S(1)}, bf16[1,72,6912]{2,1,0:T(8,128)(2,1)}, u32[]{:S(2)}) copy-start(bf16[1,72,6912]{2,1,0:T(8,128)(2,1)} %param.20) | copy-start | bytes 2985988
  21.7 3.7 collective-permute-start.1
  25.6 3.6 collective-permute-start.2
  29.4 1.2 collective-permute-start.3
  31.1 1.4 copy-start.23
  32.1 2.7 copy-start.11
  32.2 2.6 copy-start.21
  32.2 4.5 copy-start.14
  32.6 1.9 collective-permute-start.4
  32.9 15.0 %copy-start.7 = (f32[512,18]{1,0:T(8,128)S(1)}, f32[512,18]{1,0:T(8,128)}, u32[]{:S(2)}) copy-start(f32[512,18]{1,0:T(8,128)} %copy-done.6) | copy-start | bytes 110596
  32.9 15.0 %copy-start.9 = (f32[512,18]{1,0:T(8,128)S(1)}, f32[512,18]{1,0:T(8,128)}, u32[]{:S(2)}) copy-start(f32[512,18]{1,0:T(8,128)} %copy-done.8) | copy-start | bytes 110596
  34.5 21.4 %copy-start.17 = (bf16[512,128]{1,0:T(8,128)(2,1)S(1)}, bf16[512,128]{1,0:T(8,128)(2,1)}, u32[]{:S(2)}) copy-start(bf16[512,128]{1,0:T(8,128)(2,1)} %subtract_convert_fusion.1) | copy-start | bytes 393220
  34.5 21.4 %copy-start.18 = (bf16[512,128]{1,0:T(8,128)(2,1)S(1)}, bf16[512,128]{1,0:T(8,128)(2,1)}, u32[]{:S(2)}) copy-start(bf16[512,128]{1,0:T(8,128)(2,1)} %get-tuple-element.129) | copy-start | bytes 393220
  34.5 21.4 %copy-start.19 = (bf16[512,128]{1,0:T(8,128)(2,1)S(1)}, bf16[512,128]{1,0:T(8,128)(2,1)}, u32[]{:S(2)}) copy-start(bf16[512,128]{1,0:T(8,128)(2,1)} %get-tuple-element.130) | copy-start | bytes 393220
  34.8 109.9 %copy-start.28 = (f32[1,72]{1,0:T(1,128)S(1)}, f32[1,72]{1,0:T(1,128)}, u32[]{:S(2)}) copy-start(f32[1,72]{1,0:T(1,128)} %param.27) | copy-start | bytes 868
  34.8 109.9 %copy-start.29 = (f32[1,72]{1,0:T(1,128)S(1)}, f32[1,72]{1,0:T(1,128)}, u32[]{:S(2)}) copy-start(f32[1,72]{1,0:T(1,128)} %param.26) | copy-start | bytes 868
  34.8 12.8 %collective-permute-start.5 = (f32[4,2,6912]{2,1,0:T(2,128)S(1)}, f32[4,2,6912]{2,1,0:T(2,128)S(1)}, u32[]{:S(2)}, u32[]{:S(2)}) collective-permute-start(f32[4,2,6912]{2,1,0:T(2,128)S(1)} %dynamic-slice_bitcast_fusion.2), channel_id=1, source_target_pairs={{0,2},{1,3},{2,0},{3,1},{4,6},{5,7},{6,4},{7,5},{8,10},{9,11},{10,... | collective-permute-start | bytes 663560 | tf_op jit(solution)/shard_map/ppermute | solution.py:920
  47.8 7.8 %collective-permute-start.6 = (f32[2,2,6912]{2,1,0:T(2,128)S(1)}, f32[2,2,6912]{2,1,0:T(2,128)S(1)}, u32[]{:S(2)}, u32[]{:S(2)}) collective-permute-start(f32[2,2,6912]{2,1,0:T(2,128)S(1)} %dynamic-slice_bitcast_fusion.3), channel_id=1, source_target_pairs={{0,4},{1,5},{2,6},{3,7},{4,0},{5,1},{6,2},{7,3},{8,12},{9,13},{10,... | collective-permute-start | bytes 331784 | tf_op jit(solution)/shard_map/ppermute | solution.py:920
  55.7 6.8 %collective-permute-start.7 = (f32[1,2,6912]{2,1,0:T(2,128)S(1)}, f32[1,2,6912]{2,1,0:T(2,128)S(1)}, u32[]{:S(2)}, u32[]{:S(2)}) collective-permute-start(f32[1,2,6912]{2,1,0:T(2,128)S(1)} %constant_dynamic-slice_fusion), channel_id=1, source_target_pairs={{0,8},{1,9},{2,10},{3,11},{4,12},{5,13},{6,14},{7,15},{8,0},{9,1},... | collective-permute-start | bytes 165896 | tf_op jit(solution)/shard_map/ppermute | solution.py:920
  144.2 234.0 %reduce-scatter.4.cloned.1.call-start = ((), (), s32[]{:S(2)}) async-start(), calls=%async_computation.5 | async-start | bytes 7520256 | tf_op jit(solution)/shard_map/reduce_scatter | solution.py:893
  195.6 15.6 %collective-permute-start.9 = (bf16[256,1152]{1,0:T(8,128)(2,1)}, bf16[256,1152]{1,0:T(8,128)(2,1)S(1)}, u32[]{:S(2)}, u32[]{:S(2)}) collective-permute-start(bf16[256,1152]{1,0:T(8,128)(2,1)} %shard_map.226), channel_id=1, source_target_pairs={{0,16},{1,17},{2,18},{3,19},{4,20},{5,21},{6,22},{7,23},{8,24},{9,... | collective-permute-start | bytes 1769480 | tf_op jit(solution)/shard_map/ppermute | solution.py:1051
  205.6 18.9 %collective-permute-start.8 = (bf16[256,1152]{1,0:T(8,128)(2,1)}, bf16[256,1152]{1,0:T(8,128)(2,1)S(1)}, u32[]{:S(2)}, u32[]{:S(2)}) collective-permute-start(bf16[256,1152]{1,0:T(8,128)(2,1)} %shard_map.224), channel_id=1, source_target_pairs={{0,16},{1,17},{2,18},{3,19},{4,20},{5,21},{6,22},{7,23},{8,24},{9,... | collective-permute-start | bytes 1769480 | tf_op jit(solution)/shard_map/ppermute | solution.py:1051
  211.2 0.8 copy-start.15
  224.5 0.8 copy-start.16
  280.2 28.3 %collective-permute-start.11 = (bf16[256,1152]{1,0:T(8,128)(2,1)}, bf16[256,1152]{1,0:T(8,128)(2,1)S(1)}, u32[]{:S(2)}, u32[]{:S(2)}) collective-permute-start(bf16[256,1152]{1,0:T(8,128)(2,1)} %shard_map.232), channel_id=1, source_target_pairs={{16,0},{17,1},{18,2},{19,3},{20,4},{21,5},{22,6},{23,7},{24,8},{25... | collective-permute-start | bytes 1769480 | tf_op jit(solution)/shard_map/ppermute | solution.py:1082
  297.0 17.6 %collective-permute-start.10 = (bf16[256,1152]{1,0:T(8,128)(2,1)}, bf16[256,1152]{1,0:T(8,128)(2,1)S(1)}, u32[]{:S(2)}, u32[]{:S(2)}) collective-permute-start(bf16[256,1152]{1,0:T(8,128)(2,1)} %shard_map.230), channel_id=1, source_target_pairs={{16,0},{17,1},{18,2},{19,3},{20,4},{21,5},{22,6},{23,7},{24,8},{25... | collective-permute-start | bytes 1769480 | tf_op jit(solution)/shard_map/ppermute | solution.py:1082
  308.5 0.8 copy-start.5
  314.6 0.8 copy-start.13
  324.2 140.6 %reduce-scatter.6.cloned.1.call-start = ((), (), s32[]{:S(2)}) async-start(), calls=%async_computation.6 | async-start | bytes 15040512 | tf_op jit(solution)/shard_map/reduce_scatter | solution.py:893
  378.3 150.1 %reduce-scatter.8.cloned.1.call-start = ((), (), s32[]{:S(2)}) async-start(), calls=%async_computation.7 | async-start | bytes 5971968 | tf_op jit(solution)/shard_map/reduce_scatter | solution.py:893
  422.2 5.8 %collective-permute-start.13 = (bf16[1,2,6912]{2,1,0:T(2,128)(2,1)S(1)}, bf16[1,2,6912]{2,1,0:T(2,128)(2,1)S(1)}, u32[]{:S(2)}, u32[]{:S(2)}) collective-permute-start(bf16[1,2,6912]{2,1,0:T(2,128)(2,1)S(1)} %convert_element_type.163), channel_id=1, source_target_pairs={{0,8},{1,9},{2,10},{3,11},{4,12},{5,13},{6,14},{7,15},{8,0},{9,1},... | collective-permute-start | bytes 82952 | tf_op jit(solution)/shard_map/ppermute | solution.py:920
  428.1 5.6 %collective-permute-start.14 = (bf16[2,2,6912]{2,1,0:T(2,128)(2,1)S(1)}, bf16[2,2,6912]{2,1,0:T(2,128)(2,1)S(1)}, u32[]{:S(2)}, u32[]{:S(2)}) collective-permute-start(bf16[2,2,6912]{2,1,0:T(2,128)(2,1)S(1)} %maximum_bitcast_fusion), channel_id=1, source_target_pairs={{0,4},{1,5},{2,6},{3,7},{4,0},{5,1},{6,2},{7,3},{8,12},{9,13},{10,... | collective-permute-start | bytes 165896 | tf_op jit(solution)/shard_map/ppermute | solution.py:920
  433.7 11.3 %collective-permute-start.12 = (bf16[8,72,4608]{2,1,0:T(8,128)(2,1)}, bf16[8,72,4608]{2,1,0:T(8,128)(2,1)}, u32[]{:S(2)}, u32[]{:S(2)}) collective-permute-start(bf16[8,72,4608]{2,1,0:T(8,128)(2,1)} %dynamic-slice_bitcast_fusion), channel_id=1, source_target_pairs={{0,1},{1,0},{2,3},{3,2},{4,5},{5,4},{6,7},{7,6},{8,9},{9,8},{10,11... | collective-permute-start | bytes 15925256 | tf_op jit(solution)/shard_map/ppermute | solution.py:920
  434.1 7.2 %collective-permute-start.15 = (bf16[4,2,6912]{2,1,0:T(2,128)(2,1)S(1)}, bf16[4,2,6912]{2,1,0:T(2,128)(2,1)S(1)}, u32[]{:S(2)}, u32[]{:S(2)}) collective-permute-start(bf16[4,2,6912]{2,1,0:T(2,128)(2,1)S(1)} %bitcast.269), channel_id=1, source_target_pairs={{0,2},{1,3},{2,0},{3,1},{4,6},{5,7},{6,4},{7,5},{8,10},{9,11},{10,... | collective-permute-start | bytes 331784 | tf_op jit(solution)/shard_map/ppermute | solution.py:920
  441.9 1.5 collective-permute-start.16
  465.8 4.5 collective-permute-start.22
  470.4 3.6 collective-permute-start.23
  474.1 3.7 collective-permute-start.24
  477.8 4.3 collective-permute-start.25
  477.9 4.8 copy-start.20
  477.9 5.7 %copy-start.4 = (bf16[1,72,6912]{2,1,0:T(8,128)(2,1)S(1)}, bf16[1,72,6912]{2,1,0:T(8,128)(2,1)}, u32[]{:S(2)}) copy-start(bf16[1,72,6912]{2,1,0:T(8,128)(2,1)} %param.20) | copy-start | bytes 2985988
  482.0 3.8 copy-start.10
  483.9 3.8 collective-permute-start.17
  487.7 5.3 collective-permute-start.18
  489.4 14.6 %copy-start.22 = (bf16[32,72]{1,0:T(8,128)(2,1)S(1)}, bf16[32,72]{1,0:T(8,128)(2,1)}, u32[]{:S(2)}) copy-start(bf16[32,72]{1,0:T(8,128)(2,1)} %copy-done.21) | copy-start | bytes 13828
  493.1 4.8 collective-permute-start.19
  498.0 5.9 %collective-permute-start.20 = (f32[4,32,72]{2,1,0:T(8,128)S(1)}, f32[4,32,72]{2,1,0:T(8,128)S(1)}, u32[]{:S(2)}, u32[]{:S(2)}) collective-permute-start(f32[4,32,72]{2,1,0:T(8,128)S(1)} %bitcast.270), channel_id=1, source_target_pairs={{0,2},{1,3},{2,0},{3,1},{4,6},{5,7},{6,4},{7,5},{8,10},{9,11},{10,... | collective-permute-start | bytes 110600 | tf_op jit(solution)/shard_map/ppermute | solution.py:920
  503.9 2.2 copy-start.12
  503.9 2.2 copy-start.24
  503.9 1.8 collective-permute-start.21
  506.0 26.1 %copy-start.1 = (bf16[1001,1152]{1,0:T(8,128)(2,1)S(1)}, bf16[1001,1152]{1,0:T(8,128)(2,1)}, u32[]{:S(2)}) copy-start(bf16[1001,1152]{1,0:T(8,128)(2,1)} %param.19) | copy-start | bytes 6918916
Sparse Core Ops, SparseCore 0:
  10.2 133.9 all-gather.2
  145.8 43.6 all-gather.4
  324.3 53.9 reduce-scatter.3
  380.5 84.2 reduce-scatter.5
  467.1 61.3 reduce-scatter.7

commit v8 on v7

--- a/solution.py
+++ b/solution.py
@@ -706,7 +706,7 @@
 
 
 def attention_backward(
-    raw, value, mixed_grad, middle_grad, x, mod, tables, gain, joined, walked, first, count, keep
+    active, raw, value, mixed_grad, middle_grad, x, mod, tables, gain, joined, walked, first, count, keep
 ):
     images, unused, width = mod.shape
     patches = x.shape[0] // images
@@ -732,13 +732,21 @@
             pl.BlockSpec((1, 8, width), lambda image: (image, 0, 0)),
         ]
 
-    def body(*refs):
-        attention_backward_kernel(heads, places_of(parts, walked), first, keep, refs)
+    def body(active_ref, *refs):
+        @pl.when(active_ref[0] == 0)
+        def _():
+            for ref in refs[13 : 13 + len(out_shapes)]:
+                ref[...] = jnp.zeros_like(ref)
+
+        @pl.when(active_ref[0] != 0)
+        def _():
+            attention_backward_kernel(heads, places_of(parts, walked), first, keep, refs)
 
     return pl.pallas_call(
         body,
         grid=(count,),
-        in_specs=[anywhere] * 5
+        in_specs=[pl.BlockSpec(memory_space=pltpu.SMEM)]
+        + [anywhere] * 5
         + [
             pl.BlockSpec((1, 8, width), lambda image: (first + image, 0, 0)),
             row(cos.shape[1]),
@@ -767,7 +775,7 @@
             2 * tokens * width * (3 * width + 5 * patches),
             6 * width * width + tokens * width * 20,
         ),
-    )(raw, value, mixed_grad, middle_grad, x, mod, cos, sin, gain, *matrices, joined)
+    )(active, raw, value, mixed_grad, middle_grad, x, mod, cos, sin, gain, *matrices, joined)
 
 
 def down_grad(mlp_grads, cot, back, act, mod, step):
@@ -1065,6 +1073,7 @@
     backs = []
     for image in range(images):
         (early,) = attention_backward(
+            second_only,
             raw,
             values,
             mixed_grad,
@@ -1106,6 +1115,7 @@
     gate_up_term, down_part = lax.optimization_barrier((gate_up_term, down_part))
     gate_up_part = scatter_walk(gate_up_term, [walk_of(count)])
     flow_grad, qkv_grad, attention_sums = attention_backward(
+        always,
         raw,
         values,
         mixed_grad,

time: 545 us -> 543 us (level)
  Pallas kernels: 242 us -> 217 us
  waiting for transfers between devices: 192 us -> 213 us
    pallas_call x3, Pallas kernels: 60.6 us -> 35.8 us  [attention_backward(): pl.pallas_call(body, grid=(count,), in_specs=[pl.BlockSpec(memory_space=p...]
    ppermute x2, waiting for transfers between devices: 3.03 us -> 24.4 us  [per_device(): backs.append(lax.ppermute(early, 'section', [(1, 0)]))]
  transfers between devices with their start and end apart: 31 -> 31, of which waited for: 23 -> 24; matrix products, arithmetic and copies ran while one was open for 9% -> 9% of each run, Pallas kernels for 32% -> 30%
where the time goes in v8:
time: 543 us; the launch traced here: 537 us
  Pallas kernels  217 us (40%)
  waiting for transfers between devices  213 us (39%)
  starting transfers between devices  35.1 us (6%)
  other arithmetic  34.3 us (6%)
  local copies, waits for them, and re-layouts  15.6 us (3%)
  between operations  14.9 us (3%)
  matrix products  7.2 us (1%)
    all_gather x2, waiting for transfers between devices, gather_walk(): lax.all_gather(rows, 'dp', axis=0, tiled=True, axis_index_groups=[walk_of...  92.3 us
    ppermute x21, waiting for transfers between devices, swapped(): lax.ppermute(block, 'dp', [(device, device ^ bit) for device in range(cou...  56.6 us
    pallas_call x2, Pallas kernels, mlp_backward(): pl.pallas_call(body, grid=(count,), in_specs=[block, pl.BlockSpec(mod.sha...  49.7 us
    pallas_call x3, Pallas kernels, attention_forward(): pl.pallas_call(body, grid=(count,), in_specs=[pl.BlockSpec((patches, widt...  45.2 us
    reduce_scatter x3, waiting for transfers between devices, scatter_walk(): lax.psum_scatter(rows, 'dp', scatter_dimension=0, tiled=True, axis_index_...  37.9 us
    pallas_call x3, Pallas kernels, attention_backward(): pl.pallas_call(body, grid=(count,), in_specs=[pl.BlockSpec(memory_space=p...  35.8 us
    pallas_call x2, Pallas kernels, matrix_grad(): pl.pallas_call(functools.partial(matrix_grad_kernel, places_of(parts, wal...  25.3 us
    ppermute x2, waiting for transfers between devices, per_device(): backs.append(lax.ppermute(early, 'section', [(1, 0)]))  24.4 us
  transfers between devices with their start and end apart: 31, of which 24 were waited for; matrix products, arithmetic and copies ran while one was open for 9% of the time, Pallas kernels for 30%

profile of v8, /device:TPU:0, one launch (start us, length us, event | category | flops | bytes accessed | tf_op | source)
XLA Modules:
  0.0 537.2 jit_solution(3766719579459786822)
XLA Ops:
  7.3 2.7 pad_maximum_fusion
  10.1 4.1 collective-permute-start
  14.3 1.9 fusion.18
  21.7 1.6 collective-permute-start.1
  23.4 2.0 collective-permute-done.1
  25.6 1.5 collective-permute-start.2
  27.1 2.1 collective-permute-done.2
  32.9 1.5 collective-permute-done.4
  34.8 1.8 collective-permute-start.5
  37.8 9.9 %collective-permute-done.5 = f32[4,2,6912]{2,1,0:T(2,128)S(1)} collective-permute-done((f32[4,2,6912]{2,1,0:T(2,128)S(1)}, f32[4,2,6912]{2,1,0:T(2,128)S(1)}, u32[]{:S(2)}, u32[]{:S(2)}) %collective-permute-start.5) | collective-permute-done | bytes 221216 | tf_op jit(solution)/shard_map/ppermute | solution.py:928
  48.1 7.5 %collective-permute-done.6 = f32[2,2,6912]{2,1,0:T(2,128)S(1)} collective-permute-done((f32[2,2,6912]{2,1,0:T(2,128)S(1)}, f32[2,2,6912]{2,1,0:T(2,128)S(1)}, u32[]{:S(2)}, u32[]{:S(2)}) %collective-permute-start.6) | collective-permute-done | bytes 110624 | tf_op jit(solution)/shard_map/ppermute | solution.py:928
  56.8 5.7 %collective-permute-done.7 = f32[1,2,6912]{2,1,0:T(2,128)S(1)} collective-permute-done((f32[1,2,6912]{2,1,0:T(2,128)S(1)}, f32[1,2,6912]{2,1,0:T(2,128)S(1)}, u32[]{:S(2)}, u32[]{:S(2)}) %collective-permute-start.7) | collective-permute-done | bytes 55328 | tf_op jit(solution)/shard_map/ppermute | solution.py:928
  63.2 81.0 %all-gather.3.cloned.1.call-done = bf16[1152,10752]{1,0:T(8,128)(2,1)} async-done(((bf16[72,10752]{1,0:T(8,128)(2,1)}), bf16[1152,10752]{1,0:T(8,128)(2,1)}) %all-gather.3.cloned.1.call-update) | async-done | bytes 24772624 | tf_op jit(solution)/shard_map/all_gather | solution.py:897
  145.5 19.9 %shard_map.222 = (f32[512,1152]{1,0:T(8,128)}, bf16[512,1152]{1,0:T(8,128)(2,1)}) custom-call(bf16[512,1152]{1,0:T(8,128)(2,1)} %bitcast.256, f32[2,8,1152]{2,1,0:T(8,128)} %pad.15.mod_ref.refs_1_.refs_2_.refs_5_, bf16[512,256]{1,0:T(8,128)(2,1)} %get-tuple-element.70.refs_2_.refs_3_.refs_6_, bf16[512,256]{1,0:T(8,128)(2,1)} %get-tuple-element.71.refs_3_.refs_4_.refs_7_, ...), custom_call_target="tpu_custom_call" | custom-call | flops 6039797760 | bytes 22413312 | tf_op jit(solution)/shard_map/pallas_call | solution.py:246
  165.4 12.8 %shard_map.223.act_ref = bf16[512,3072]{1,0:T(8,128)(2,1)} custom-call(bf16[512,1152]{1,0:T(8,128)(2,1)} %get-tuple-element.76.normed_ref, bf16[8,144,10752]{2,1,0:T(8,128)(2,1)} %bitcast.226, bf16[8,144,10752]{2,1,0:T(8,128)(2,1)} %bitcast.227, bf16[8,144,10752]{2,1,0:T(8,128)(2,1)} %bitcast.228, bf16[8,144,10752]{2,1,0:T(8,128)(2,1)} %bitcast.229), custom_call_target="tpu_custom_call" | custom-call | flops 7247757312 | bytes 17301504 | tf_op jit(solution)/shard_map/pallas_call | solution.py:310
  178.2 11.3 %all-gather.5.cloned.1.call-done.down_ref.refs_1_.refs_2_ = bf16[3072,1152]{1,0:T(8,128)(2,1)} async-done(((bf16[192,1152]{1,0:T(8,128)(2,1)}), bf16[3072,1152]{1,0:T(8,128)(2,1)}) %all-gather.5.cloned.1.call-update) | async-done | bytes 7077904 | tf_op jit(solution)/shard_map/all_gather | solution.py:897
  189.5 6.1 %shard_map.226 = bf16[256,1152]{1,0:T(8,128)(2,1)} custom-call(s32[1]{0:T(128)} %bitcast.active_ref, bf16[512,3072]{1,0:T(8,128)(2,1)} %shard_map.223.act_ref, f32[512,1152]{1,0:T(8,128)} %get-tuple-element.77.middle_ref, f32[2,8,1152]{2,1,0:T(8,128)} %pad.15.mod_ref.refs_1_.refs_2_.refs_5_, ...), custom_call_target="tpu_custom_call" | custom-call | flops 1811939328 | bytes 9437184 | tf_op jit(solution)/shard_map/pallas_call | solution.py:358
  197.0 2.5 shard_map.221.refs_0_
  199.5 6.1 %shard_map.224 = bf16[256,1152]{1,0:T(8,128)(2,1)} custom-call(s32[1]{0:T(128)} %bitcast.active_ref, bf16[512,3072]{1,0:T(8,128)(2,1)} %shard_map.223.act_ref, f32[512,1152]{1,0:T(8,128)} %get-tuple-element.77.middle_ref, f32[2,8,1152]{2,1,0:T(8,128)} %pad.15.mod_ref.refs_1_.refs_2_.refs_5_, ...), custom_call_target="tpu_custom_call" | custom-call | flops 1811939328 | bytes 9437184 | tf_op jit(solution)/shard_map/pallas_call | solution.py:358
  206.9 4.3 shard_map.225.act_grad_ref
  212.0 12.4 %shard_map.227 = (bf16[512,1152]{1,0:T(8,128)(2,1)}, f32[512,2304]{1,0:T(8,128)}, bf16[512,1152]{1,0:T(8,128)(2,1)}, bf16[512,1152]{1,0:T(8,128)(2,1)}, f32[512,...) custom-call(bf16[256,1152]{1,0:T(8,128)(2,1)} %copy-done.15, ...), custom_call_target="tpu_custom_call" | custom-call | flops 3019898880 | bytes 16515072 | tf_op jit(solution)/shard_map/pallas_call | solution.py:246
  225.3 12.8 %shard_map.228 = (bf16[512,1152]{1,0:T(8,128)(2,1)}, f32[512,2304]{1,0:T(8,128)}, bf16[512,1152]{1,0:T(8,128)(2,1)}, bf16[512,1152]{1,0:T(8,128)(2,1)}, f32[512,...) custom-call(bf16[256,1152]{1,0:T(8,128)(2,1)} %copy-done.16, ...), custom_call_target="tpu_custom_call", output_to_operand_aliasing={{0}: (11, {}), {1}: (12, {}), {2}: (13, {}), {3}: (14, {}),... | custom-call | flops 3019898880 | bytes 16515072 | tf_op jit(solution)/shard_map/pallas_call | solution.py:246
  238.2 26.5 %shard_map.229 = (f32[512,1152]{1,0:T(8,128)}, bf16[512,1152]{1,0:T(8,128)(2,1)}, bf16[512,3072]{1,0:T(8,128)(2,1)}, bf16[512,3072]{1,0:T(8,128)(2,1)}, bf16[512,3072]{1,0:T(8,128)(2,1)}) custom-call(bf16[512,3072]{1,0:T(8,128)(2,1)} %shard_map.225.act_grad_ref, f32[2,8,1152]{2,1,0:T(8,128)} %pad.15.mod_ref.refs_1_.refs_2_.refs_5_, ...), custom_call_target="tpu_custom_call" | custom-call | flops 15854469120 | bytes 23592960 | tf_op jit(solution)/shard_map/pallas_call | solution.py:559
  264.7 2.6 shard_map.232
  268.6 2.4 shard_map.230
  271.0 4.6 collective-permute-start.10
  275.7 10.0 %shard_map.231 = (bf16[512,1152]{1,0:T(8,128)(2,1)}, f32[512,1152]{1,0:T(8,128)}) custom-call(s32[1]{0:T(128)} %constant.118.clone.1.active_ref, bf16[512,3072]{1,0:T(8,128)(2,1)} %get-tuple-element.97.act_ref, f32[512,1152]{1,0:T(8,128)} %get-tuple-element.90.refs_6_.middle_ref.refs_9_, f32[2,8,1152]{2,1,0:T(8,128)} %pad.15.mod_ref.refs_1_.refs_2_.refs_5_, ...), custom_call_target="tpu_custom_call" | custom-call | flops 3623878656 | bytes 11796480 | tf_op jit(solution)/shard_map/pallas_call | solution.py:358
  285.6 10.9 %collective-permute-done.11.refs_0_.refs_6_ = bf16[256,1152]{1,0:T(8,128)(2,1)S(1)} collective-permute-done((bf16[256,1152]{1,0:T(8,128)(2,1)}, bf16[256,1152]{1,0:T(8,128)(2,1)S(1)}, u32[]{:S(2)}, u32[]{:S(2)}) %collective-permute-start.11) | collective-permute-done | bytes 589856 | tf_op jit(solution)/shard_map/ppermute | solution.py:1091
  297.3 2.3 shard_map.233.refs_0_
  299.6 13.5 %collective-permute-done.10.back_ref.refs_7_ = bf16[256,1152]{1,0:T(8,128)(2,1)S(1)} collective-permute-done((bf16[256,1152]{1,0:T(8,128)(2,1)}, bf16[256,1152]{1,0:T(8,128)(2,1)S(1)}, u32[]{:S(2)}, u32[]{:S(2)}) %collective-permute-start.10) | collective-permute-done | bytes 589856 | tf_op jit(solution)/shard_map/ppermute | solution.py:1091
  314.0 8.7 %shard_map.234 = (bf16[3072,1152]{1,0:T(8,128)(2,1)}, bf16[256,1152]{1,0:T(8,128)(2,1)}) custom-call(bf16[512,3072]{1,0:T(8,128)(2,1)} %get-tuple-element.97.act_ref, bf16[512,1152]{1,0:T(8,128)(2,1)} %bitcast.251, bf16[256,1152]{1,0:T(8,128)(2,1)} %copy-done.13, f32[2,8,1152]{2,1,0:T(8,128)} %pad.15.mod_ref.refs_1_.refs_2_.refs_5_, ...), custom_call_target="tpu_custom_call" | custom-call | flops 3623878656 | bytes 7077888 | tf_op jit(solution)/shard_map/pallas_call | solution.py:801
  322.8 8.0 %shard_map.235.act_grad_ref = bf16[512,3072]{1,0:T(8,128)(2,1)} custom-call(s32[1]{0:T(128)} %constant.118.clone.1.active_ref, bf16[256,1152]{1,0:T(8,128)(2,1)} %shard_map.233.refs_0_, bf16[256,1152]{1,0:T(8,128)(2,1)} %get-tuple-element.104.refs_1_, bf16[3072,1152]{1,0:T(8,128)(2,1)} %all-gather.5.cloned.1.call-done.down_ref.refs_1_.refs_2_), custom_call_target="tpu_custom_call" | custom-call | flops 3623878656 | bytes 9437184 | tf_op jit(solution)/shard_map/pallas_call | solution.py:429
  330.7 23.2 %shard_map.236 = (f32[512,1152]{1,0:T(8,128)}, bf16[512,1152]{1,0:T(8,128)(2,1)}, bf16[512,3072]{1,0:T(8,128)(2,1)}, bf16[512,3072]{1,0:T(8,128)(2,1)}, bf16[512...) custom-call(bf16[512,3072]{1,0:T(8,128)(2,1)} %shard_map.235.act_grad_ref, f32[2,8,1152]{2,1,0:T(8,128)} %pad.15.mod_ref.refs_1_.refs_2_.refs_5_, ...), custom_call_target="tpu_custom_call" | custom-call | flops 15854469120 | bytes 23592960 | tf_op jit(solution)/shard_map/pallas_call | solution.py:559
  353.9 13.7 %shard_map.239 = bf16[8,144,6144]{2,1,0:T(8,128)(2,1)} custom-call(bf16[512,1152]{1,0:T(8,128)(2,1)} %get-tuple-element.89.refs_4_.refs_0_.refs_1_, bf16[512,1152]{1,0:T(8,128)(2,1)} %get-tuple-element.89.refs_4_.refs_0_.refs_1_, bf16[512,3072]{1,0:T(8,128)(2,1)} %get-tuple-element.117.refs_2_, bf16[512,3072]{1,0:T(8,128)(2,1)} %get-tuple-element.118.refs_3_), custom_call_target="tpu_custom_call" | custom-call | flops 7247757312 | bytes 14155776 | tf_op jit(solution)/shard_map/pallas_call | solution.py:852
  367.6 9.3 %reduce-scatter.4.cloned.1.call-done = bf16[192,1152]{1,0:T(8,128)(2,1)} async-done(((bf16[3072,1152]{1,0:T(8,128)(2,1)}), bf16[192,1152]{1,0:T(8,128)(2,1)}) %reduce-scatter.4.cloned.1.call-update) | async-done | bytes 442384 | tf_op jit(solution)/shard_map/reduce_scatter | solution.py:901
  377.4 30.8 %shard_map.237 = (f32[512,1152]{1,0:T(8,128)}, bf16[512,3456]{1,0:T(8,128)(2,1)}, f32[2,8,1152]{2,1,0:T(8,128)}) custom-call(s32[1]{0:T(128)} %constant.118.clone.1.active_ref, f32[512,2304]{1,0:T(8,128)} %get-tuple-element.92.refs_0_, bf16[512,1152]{1,0:T(8,128)(2,1)} %get-tuple-element.93.refs_1_, bf16[512,1152]{1,0:T(8,128)(2,1)} %get-tuple-element.108.refs_2_, ...), custom_call_target="tpu_custom_call" | custom-call | flops 5586812928 | bytes 19759104 | tf_op jit(solution)/shard_map/pallas_call | solution.py:745
  408.2 11.7 %shard_map.238 = bf16[8,144,4608]{2,1,0:T(8,128)(2,1)} custom-call(bf16[512,1152]{1,0:T(8,128)(2,1)} %get-tuple-element.111.refs_0_, bf16[512,1152]{1,0:T(8,128)(2,1)} %get-tuple-element.112.refs_1_, bf16[512,3456]{1,0:T(8,128)(2,1)} %get-tuple-element.113.refs_2_, bf16[512,1152]{1,0:T(8,128)(2,1)} %get-tuple-element.114.refs_3_), custom_call_target="tpu_custom_call" | custom-call | flops 5435817984 | bytes 10616832 | tf_op jit(solution)/shard_map/pallas_call | solution.py:852
  421.7 1.7 collective-permute-start.13
  423.4 4.0 collective-permute-done.13
  427.9 5.3 dynamic-slice_bitcast_fusion
  433.6 2.1 collective-permute-start.15
  435.6 5.1 collective-permute-done.15
  441.5 1.4 collective-permute-done.16
  444.5 7.9 %fusion = bf16[8,72,4608]{2,1,0:T(8,128)(2,1)} fusion(bf16[8,72,4608]{2,1,0:T(8,128)(2,1)} %collective-permute-done.12, bf16[8,2,72,4608]{3,2,1,0:T(8,128)(2,1)} %bitcast.255, s32[]{:T(128)S(6)} %select_n.357), kind=kLoop, calls=%fused_computation.1 | loop fusion | flops 10616832 | bytes 15925252 | tf_op jit(solution)/shard_map/convert_element_type | solution.py:914
  452.4 11.1 %reduce-scatter.6.cloned.1.call-done = bf16[72,6144]{1,0:T(8,128)(2,1)} async-done(((bf16[1152,6144]{1,0:T(8,128)(2,1)}), bf16[72,6144]{1,0:T(8,128)(2,1)}) %reduce-scatter.6.cloned.1.call-update) | async-done | bytes 884752 | tf_op jit(solution)/shard_map/reduce_scatter | solution.py:901
  464.5 1.3 collective-permute-start.22
  465.9 3.2 collective-permute-done.22
  469.1 1.5 collective-permute-start.23
  470.6 2.1 collective-permute-done.23
  472.7 2.0 collective-permute-start.24
  474.7 1.7 collective-permute-done.24
  476.6 4.2 convert_select_fusion
  482.7 1.7 collective-permute-start.17
  484.5 2.0 collective-permute-done.17
  487.8 3.9 collective-permute-done.18
  491.8 1.5 collective-permute-start.19
  493.3 3.3 collective-permute-done.19
  496.7 2.0 collective-permute-start.20
  500.7 1.9 collective-permute-done.20
  502.7 1.7 convolution_bitcast_fusion
  504.9 4.3 fusion.10
  509.1 17.6 %reduce-scatter.8.cloned.1.call-done = bf16[72,4608]{1,0:T(8,128)(2,1)} async-done(((bf16[576,4608]{1,0:T(8,128)(2,1)}), bf16[72,4608]{1,0:T(8,128)(2,1)}) %reduce-scatter.8.cloned.1.call-update) | async-done | bytes 663568 | tf_op jit(solution)/shard_map/reduce_scatter | solution.py:901
  526.7 2.0 fusion.6
  528.8 1.7 fusion.9
  (200 shorter events, 34.2 us)
Async XLA Ops:
  7.2 24.3 %copy-start = (bf16[1001,1152]{1,0:T(8,128)(2,1)S(1)}, bf16[1001,1152]{1,0:T(8,128)(2,1)}, u32[]{:S(2)}) copy-start(bf16[1001,1152]{1,0:T(8,128)(2,1)} %param.19) | copy-start | bytes 6918916
  7.2 2.9 copy-start.26
  7.2 2.9 copy-start.27
  7.2 137.0 %all-gather.3.cloned.1.call-start = ((), (), s32[]{:S(2)}) async-start(), calls=%async_computation.3 | async-start | bytes 26320896 | tf_op jit(solution)/shard_map/all_gather | solution.py:897
  7.3 7.0 %copy-start.25 = (s32[2,256]{1,0:T(2,128)S(1)}, s32[2,256]{1,0:T(2,128)}, u32[]{:S(2)}) copy-start(s32[2,256]{1,0:T(2,128)} %param.18) | copy-start | bytes 6148
  10.0 10.5 %copy-start.2 = (bf16[2,256,1152]{2,1,0:T(8,128)(2,1)S(1)}, bf16[2,256,1152]{2,1,0:T(8,128)(2,1)}, u32[]{:S(2)}) copy-start(bf16[2,256,1152]{2,1,0:T(8,128)(2,1)} %param.14) | copy-start | bytes 3538948
  10.0 179.5 %all-gather.5.cloned.1.call-start = ((), (), s32[]{:S(2)}) async-start(), calls=%async_computation.4 | async-start | bytes 7520256 | tf_op jit(solution)/shard_map/all_gather | solution.py:897
  10.1 11.6 %collective-permute-start = (s32[1,2,2]{2,1,0:T(2,128)S(1)}, s32[1,2,2]{2,1,0:T(2,128)S(1)}, u32[]{:S(2)}, u32[]{:S(2)}) collective-permute-start(s32[1,2,2]{2,1,0:T(2,128)S(1)} %add_bitcast_fusion.2), channel_id=1, source_target_pairs={{0,8},{1,9},{2,10},{3,11},{4,12},{5,13},{6,14},{7,15},{8,0},{9,1},... | collective-permute-start | bytes 56 | tf_op jit(solution)/shard_map/ppermute | solution.py:928
  16.2 0.7 copy-start.6
  16.2 1.6 copy-start.8
  21.7 10.5 %copy-start.3 = (bf16[1,72,6912]{2,1,0:T(8,128)(2,1)S(1)}, bf16[1,72,6912]{2,1,0:T(8,128)(2,1)}, u32[]{:S(2)}) copy-start(bf16[1,72,6912]{2,1,0:T(8,128)(2,1)} %param.20) | copy-start | bytes 2985988
  21.7 3.7 collective-permute-start.1
  25.6 3.6 collective-permute-start.2
  29.4 1.2 collective-permute-start.3
  31.1 1.4 copy-start.23
  32.1 2.7 copy-start.11
  32.2 2.6 copy-start.21
  32.2 4.5 copy-start.14
  32.6 1.9 collective-permute-start.4
  32.9 15.0 %copy-start.7 = (f32[512,18]{1,0:T(8,128)S(1)}, f32[512,18]{1,0:T(8,128)}, u32[]{:S(2)}) copy-start(f32[512,18]{1,0:T(8,128)} %copy-done.6) | copy-start | bytes 110596
  32.9 15.0 %copy-start.9 = (f32[512,18]{1,0:T(8,128)S(1)}, f32[512,18]{1,0:T(8,128)}, u32[]{:S(2)}) copy-start(f32[512,18]{1,0:T(8,128)} %copy-done.8) | copy-start | bytes 110596
  34.5 21.4 %copy-start.17 = (bf16[512,128]{1,0:T(8,128)(2,1)S(1)}, bf16[512,128]{1,0:T(8,128)(2,1)}, u32[]{:S(2)}) copy-start(bf16[512,128]{1,0:T(8,128)(2,1)} %subtract_convert_fusion.1) | copy-start | bytes 393220
  34.5 21.4 %copy-start.18 = (bf16[512,128]{1,0:T(8,128)(2,1)S(1)}, bf16[512,128]{1,0:T(8,128)(2,1)}, u32[]{:S(2)}) copy-start(bf16[512,128]{1,0:T(8,128)(2,1)} %get-tuple-element.129) | copy-start | bytes 393220
  34.5 21.4 %copy-start.19 = (bf16[512,128]{1,0:T(8,128)(2,1)S(1)}, bf16[512,128]{1,0:T(8,128)(2,1)}, u32[]{:S(2)}) copy-start(bf16[512,128]{1,0:T(8,128)(2,1)} %get-tuple-element.130) | copy-start | bytes 393220
  34.8 109.9 %copy-start.28 = (f32[1,72]{1,0:T(1,128)S(1)}, f32[1,72]{1,0:T(1,128)}, u32[]{:S(2)}) copy-start(f32[1,72]{1,0:T(1,128)} %param.27) | copy-start | bytes 868
  34.8 109.9 %copy-start.29 = (f32[1,72]{1,0:T(1,128)S(1)}, f32[1,72]{1,0:T(1,128)}, u32[]{:S(2)}) copy-start(f32[1,72]{1,0:T(1,128)} %param.26) | copy-start | bytes 868
  34.8 12.8 %collective-permute-start.5 = (f32[4,2,6912]{2,1,0:T(2,128)S(1)}, f32[4,2,6912]{2,1,0:T(2,128)S(1)}, u32[]{:S(2)}, u32[]{:S(2)}) collective-permute-start(f32[4,2,6912]{2,1,0:T(2,128)S(1)} %dynamic-slice_bitcast_fusion.2), channel_id=1, source_target_pairs={{0,2},{1,3},{2,0},{3,1},{4,6},{5,7},{6,4},{7,5},{8,10},{9,11},{10,... | collective-permute-start | bytes 663560 | tf_op jit(solution)/shard_map/ppermute | solution.py:928
  47.8 7.8 %collective-permute-start.6 = (f32[2,2,6912]{2,1,0:T(2,128)S(1)}, f32[2,2,6912]{2,1,0:T(2,128)S(1)}, u32[]{:S(2)}, u32[]{:S(2)}) collective-permute-start(f32[2,2,6912]{2,1,0:T(2,128)S(1)} %dynamic-slice_bitcast_fusion.3), channel_id=1, source_target_pairs={{0,4},{1,5},{2,6},{3,7},{4,0},{5,1},{6,2},{7,3},{8,12},{9,13},{10,... | collective-permute-start | bytes 331784 | tf_op jit(solution)/shard_map/ppermute | solution.py:928
  55.7 6.8 %collective-permute-start.7 = (f32[1,2,6912]{2,1,0:T(2,128)S(1)}, f32[1,2,6912]{2,1,0:T(2,128)S(1)}, u32[]{:S(2)}, u32[]{:S(2)}) collective-permute-start(f32[1,2,6912]{2,1,0:T(2,128)S(1)} %constant_dynamic-slice_fusion), channel_id=1, source_target_pairs={{0,8},{1,9},{2,10},{3,11},{4,12},{5,13},{6,14},{7,15},{8,0},{9,1},... | collective-permute-start | bytes 165896 | tf_op jit(solution)/shard_map/ppermute | solution.py:928
  144.2 232.6 %reduce-scatter.4.cloned.1.call-start = ((), (), s32[]{:S(2)}) async-start(), calls=%async_computation.5 | async-start | bytes 7520256 | tf_op jit(solution)/shard_map/reduce_scatter | solution.py:901
  195.6 15.6 %collective-permute-start.9 = (bf16[256,1152]{1,0:T(8,128)(2,1)}, bf16[256,1152]{1,0:T(8,128)(2,1)S(1)}, u32[]{:S(2)}, u32[]{:S(2)}) collective-permute-start(bf16[256,1152]{1,0:T(8,128)(2,1)} %shard_map.226), channel_id=1, source_target_pairs={{0,16},{1,17},{2,18},{3,19},{4,20},{5,21},{6,22},{7,23},{8,24},{9,... | collective-permute-start | bytes 1769480 | tf_op jit(solution)/shard_map/ppermute | solution.py:1059
  205.6 18.9 %collective-permute-start.8 = (bf16[256,1152]{1,0:T(8,128)(2,1)}, bf16[256,1152]{1,0:T(8,128)(2,1)S(1)}, u32[]{:S(2)}, u32[]{:S(2)}) collective-permute-start(bf16[256,1152]{1,0:T(8,128)(2,1)} %shard_map.224), channel_id=1, source_target_pairs={{0,16},{1,17},{2,18},{3,19},{4,20},{5,21},{6,22},{7,23},{8,24},{9,... | collective-permute-start | bytes 1769480 | tf_op jit(solution)/shard_map/ppermute | solution.py:1059
  211.2 0.8 copy-start.15
  224.5 0.8 copy-start.16
  267.3 29.2 %collective-permute-start.11 = (bf16[256,1152]{1,0:T(8,128)(2,1)}, bf16[256,1152]{1,0:T(8,128)(2,1)S(1)}, u32[]{:S(2)}, u32[]{:S(2)}) collective-permute-start(bf16[256,1152]{1,0:T(8,128)(2,1)} %shard_map.232), channel_id=1, source_target_pairs={{16,0},{17,1},{18,2},{19,3},{20,4},{21,5},{22,6},{23,7},{24,8},{25... | collective-permute-start | bytes 1769480 | tf_op jit(solution)/shard_map/ppermute | solution.py:1091
  271.0 42.1 %collective-permute-start.10 = (bf16[256,1152]{1,0:T(8,128)(2,1)}, bf16[256,1152]{1,0:T(8,128)(2,1)S(1)}, u32[]{:S(2)}, u32[]{:S(2)}) collective-permute-start(bf16[256,1152]{1,0:T(8,128)(2,1)} %shard_map.230), channel_id=1, source_target_pairs={{16,0},{17,1},{18,2},{19,3},{20,4},{21,5},{22,6},{23,7},{24,8},{25... | collective-permute-start | bytes 1769480 | tf_op jit(solution)/shard_map/ppermute | solution.py:1091
  296.5 0.8 copy-start.5
  313.2 0.8 copy-start.13
  322.7 140.8 %reduce-scatter.6.cloned.1.call-start = ((), (), s32[]{:S(2)}) async-start(), calls=%async_computation.6 | async-start | bytes 15040512 | tf_op jit(solution)/shard_map/reduce_scatter | solution.py:901
  376.9 149.9 %reduce-scatter.8.cloned.1.call-start = ((), (), s32[]{:S(2)}) async-start(), calls=%async_computation.7 | async-start | bytes 5971968 | tf_op jit(solution)/shard_map/reduce_scatter | solution.py:901
  421.7 5.8 %collective-permute-start.13 = (bf16[1,2,6912]{2,1,0:T(2,128)(2,1)S(1)}, bf16[1,2,6912]{2,1,0:T(2,128)(2,1)S(1)}, u32[]{:S(2)}, u32[]{:S(2)}) collective-permute-start(bf16[1,2,6912]{2,1,0:T(2,128)(2,1)S(1)} %convert_element_type.163), channel_id=1, source_target_pairs={{0,8},{1,9},{2,10},{3,11},{4,12},{5,13},{6,14},{7,15},{8,0},{9,1},... | collective-permute-start | bytes 82952 | tf_op jit(solution)/shard_map/ppermute | solution.py:928
  427.6 5.6 %collective-permute-start.14 = (bf16[2,2,6912]{2,1,0:T(2,128)(2,1)S(1)}, bf16[2,2,6912]{2,1,0:T(2,128)(2,1)S(1)}, u32[]{:S(2)}, u32[]{:S(2)}) collective-permute-start(bf16[2,2,6912]{2,1,0:T(2,128)(2,1)S(1)} %maximum_bitcast_fusion), channel_id=1, source_target_pairs={{0,4},{1,5},{2,6},{3,7},{4,0},{5,1},{6,2},{7,3},{8,12},{9,13},{10,... | collective-permute-start | bytes 165896 | tf_op jit(solution)/shard_map/ppermute | solution.py:928
  433.2 11.3 %collective-permute-start.12 = (bf16[8,72,4608]{2,1,0:T(8,128)(2,1)}, bf16[8,72,4608]{2,1,0:T(8,128)(2,1)}, u32[]{:S(2)}, u32[]{:S(2)}) collective-permute-start(bf16[8,72,4608]{2,1,0:T(8,128)(2,1)} %dynamic-slice_bitcast_fusion), channel_id=1, source_target_pairs={{0,1},{1,0},{2,3},{3,2},{4,5},{5,4},{6,7},{7,6},{8,9},{9,8},{10,11... | collective-permute-start | bytes 15925256 | tf_op jit(solution)/shard_map/ppermute | solution.py:928
  433.6 7.1 %collective-permute-start.15 = (bf16[4,2,6912]{2,1,0:T(2,128)(2,1)S(1)}, bf16[4,2,6912]{2,1,0:T(2,128)(2,1)S(1)}, u32[]{:S(2)}, u32[]{:S(2)}) collective-permute-start(bf16[4,2,6912]{2,1,0:T(2,128)(2,1)S(1)} %bitcast.269), channel_id=1, source_target_pairs={{0,2},{1,3},{2,0},{3,1},{4,6},{5,7},{6,4},{7,5},{8,10},{9,11},{10,... | collective-permute-start | bytes 331784 | tf_op jit(solution)/shard_map/ppermute | solution.py:928
  441.4 1.6 collective-permute-start.16
  464.5 4.5 collective-permute-start.22
  469.1 3.6 collective-permute-start.23
  472.7 3.7 collective-permute-start.24
  476.5 4.3 collective-permute-start.25
  476.6 4.8 copy-start.20
  476.6 5.7 %copy-start.4 = (bf16[1,72,6912]{2,1,0:T(8,128)(2,1)S(1)}, bf16[1,72,6912]{2,1,0:T(8,128)(2,1)}, u32[]{:S(2)}) copy-start(bf16[1,72,6912]{2,1,0:T(8,128)(2,1)} %param.20) | copy-start | bytes 2985988
  480.8 3.6 copy-start.10
  482.7 3.8 collective-permute-start.17
  486.5 5.3 collective-permute-start.18
  487.8 14.9 %copy-start.22 = (bf16[32,72]{1,0:T(8,128)(2,1)S(1)}, bf16[32,72]{1,0:T(8,128)(2,1)}, u32[]{:S(2)}) copy-start(bf16[32,72]{1,0:T(8,128)(2,1)} %copy-done.21) | copy-start | bytes 13828
  491.8 4.8 collective-permute-start.19
  496.7 5.9 %collective-permute-start.20 = (f32[4,32,72]{2,1,0:T(8,128)S(1)}, f32[4,32,72]{2,1,0:T(8,128)S(1)}, u32[]{:S(2)}, u32[]{:S(2)}) collective-permute-start(f32[4,32,72]{2,1,0:T(8,128)S(1)} %bitcast.270), channel_id=1, source_target_pairs={{0,2},{1,3},{2,0},{3,1},{4,6},{5,7},{6,4},{7,5},{8,10},{9,11},{10,... | collective-permute-start | bytes 110600 | tf_op jit(solution)/shard_map/ppermute | solution.py:928
  502.6 2.2 copy-start.12
  502.6 2.2 copy-start.24
  502.6 1.8 collective-permute-start.21
  504.7 25.8 %copy-start.1 = (bf16[1001,1152]{1,0:T(8,128)(2,1)S(1)}, bf16[1001,1152]{1,0:T(8,128)(2,1)}, u32[]{:S(2)}) copy-start(bf16[1001,1152]{1,0:T(8,128)(2,1)} %param.19) | copy-start | bytes 6918916
Sparse Core Ops, SparseCore 0:
  10.2 133.9 all-gather.2
  145.8 43.6 all-gather.4
  322.8 53.9 reduce-scatter.3
  379.1 84.3 reduce-scatter.5
  465.7 60.9 reduce-scatter.7

commit v9 on v8

--- a/solution.py
+++ b/solution.py
@@ -508,7 +508,7 @@
         if keep:
             kept_refs[0][...] = gate_grad
             kept_refs[1][...] = up_grad
-        term = dot_right(gate_grad, gate_weight) + dot_right(up_grad, up_weight)
+        term = dot_right(side_by_side([gate_grad, up_grad]), side_by_side([gate_weight, up_weight]))
 
         @pl.when(index == 0)
         def _():

time: 543 us -> 545 us (level)
  no operation moved by 1% of the time
where the time goes in v9:
time: 545 us; the launch traced here: 540 us
  Pallas kernels  220 us (40%)
  waiting for transfers between devices  215 us (39%)
  other arithmetic  34.3 us (6%)
  starting transfers between devices  32.2 us (6%)
  local copies, waits for them, and re-layouts  15.6 us (3%)
  between operations  14.9 us (3%)
  matrix products  7.2 us (1%)
    all_gather x2, waiting for transfers between devices, gather_walk(): lax.all_gather(rows, 'dp', axis=0, tiled=True, axis_index_groups=[walk_of...  92.6 us
    ppermute x21, waiting for transfers between devices, swapped(): lax.ppermute(block, 'dp', [(device, device ^ bit) for device in range(cou...  58.5 us
    pallas_call x2, Pallas kernels, mlp_backward(): pl.pallas_call(body, grid=(count,), in_specs=[block, pl.BlockSpec(mod.sha...  53 us
    pallas_call x3, Pallas kernels, attention_forward(): pl.pallas_call(body, grid=(count,), in_specs=[pl.BlockSpec((patches, widt...  45 us
    reduce_scatter x3, waiting for transfers between devices, scatter_walk(): lax.psum_scatter(rows, 'dp', scatter_dimension=0, tiled=True, axis_index_...  37.3 us
    pallas_call x3, Pallas kernels, attention_backward(): pl.pallas_call(body, grid=(count,), in_specs=[pl.BlockSpec(memory_space=p...  36.1 us
    pallas_call x2, Pallas kernels, matrix_grad(): pl.pallas_call(functools.partial(matrix_grad_kernel, places_of(parts, wal...  25.3 us
    ppermute x2, waiting for transfers between devices, per_device(): backs.append(lax.ppermute(early, 'section', [(1, 0)]))  24.1 us
  transfers between devices with their start and end apart: 31, of which 24 were waited for; matrix products, arithmetic and copies ran while one was open for 9% of the time, Pallas kernels for 30%

profile of v9, /device:TPU:0, one launch (start us, length us, event | category | flops | bytes accessed | tf_op | source)
XLA Modules:
  0.0 539.6 jit_solution(5275340089824698736)
XLA Ops:
  7.3 2.7 pad_maximum_fusion
  10.1 4.1 collective-permute-start
  14.3 1.9 fusion.18
  21.7 1.6 collective-permute-start.1
  23.4 2.0 collective-permute-done.1
  25.6 1.5 collective-permute-start.2
  27.1 2.1 collective-permute-done.2
  32.9 1.5 collective-permute-done.4
  34.8 1.8 collective-permute-start.5
  37.8 9.9 %collective-permute-done.5 = f32[4,2,6912]{2,1,0:T(2,128)S(1)} collective-permute-done((f32[4,2,6912]{2,1,0:T(2,128)S(1)}, f32[4,2,6912]{2,1,0:T(2,128)S(1)}, u32[]{:S(2)}, u32[]{:S(2)}) %collective-permute-start.5) | collective-permute-done | bytes 221216 | tf_op jit(solution)/shard_map/ppermute | solution.py:928
  48.1 7.5 %collective-permute-done.6 = f32[2,2,6912]{2,1,0:T(2,128)S(1)} collective-permute-done((f32[2,2,6912]{2,1,0:T(2,128)S(1)}, f32[2,2,6912]{2,1,0:T(2,128)S(1)}, u32[]{:S(2)}, u32[]{:S(2)}) %collective-permute-start.6) | collective-permute-done | bytes 110624 | tf_op jit(solution)/shard_map/ppermute | solution.py:928
  56.8 5.7 %collective-permute-done.7 = f32[1,2,6912]{2,1,0:T(2,128)S(1)} collective-permute-done((f32[1,2,6912]{2,1,0:T(2,128)S(1)}, f32[1,2,6912]{2,1,0:T(2,128)S(1)}, u32[]{:S(2)}, u32[]{:S(2)}) %collective-permute-start.7) | collective-permute-done | bytes 55328 | tf_op jit(solution)/shard_map/ppermute | solution.py:928
  63.2 81.0 %all-gather.3.cloned.1.call-done = bf16[1152,10752]{1,0:T(8,128)(2,1)} async-done(((bf16[72,10752]{1,0:T(8,128)(2,1)}), bf16[1152,10752]{1,0:T(8,128)(2,1)}) %all-gather.3.cloned.1.call-update) | async-done | bytes 24772624 | tf_op jit(solution)/shard_map/all_gather | solution.py:897
  145.2 19.9 %shard_map.222 = (f32[512,1152]{1,0:T(8,128)}, bf16[512,1152]{1,0:T(8,128)(2,1)}) custom-call(bf16[512,1152]{1,0:T(8,128)(2,1)} %bitcast.256, f32[2,8,1152]{2,1,0:T(8,128)} %pad.15.mod_ref.refs_1_.refs_2_.refs_5_, bf16[512,256]{1,0:T(8,128)(2,1)} %get-tuple-element.70.refs_2_.refs_3_.refs_6_, bf16[512,256]{1,0:T(8,128)(2,1)} %get-tuple-element.71.refs_3_.refs_4_.refs_7_, ...), custom_call_target="tpu_custom_call" | custom-call | flops 6039797760 | bytes 22413312 | tf_op jit(solution)/shard_map/pallas_call | solution.py:246
  165.1 12.8 %shard_map.223.act_ref = bf16[512,3072]{1,0:T(8,128)(2,1)} custom-call(bf16[512,1152]{1,0:T(8,128)(2,1)} %get-tuple-element.76.normed_ref, bf16[8,144,10752]{2,1,0:T(8,128)(2,1)} %bitcast.226, bf16[8,144,10752]{2,1,0:T(8,128)(2,1)} %bitcast.227, bf16[8,144,10752]{2,1,0:T(8,128)(2,1)} %bitcast.228, bf16[8,144,10752]{2,1,0:T(8,128)(2,1)} %bitcast.229), custom_call_target="tpu_custom_call" | custom-call | flops 7247757312 | bytes 17301504 | tf_op jit(solution)/shard_map/pallas_call | solution.py:310
  177.9 11.6 %all-gather.5.cloned.1.call-done.down_ref.refs_1_.refs_2_ = bf16[3072,1152]{1,0:T(8,128)(2,1)} async-done(((bf16[192,1152]{1,0:T(8,128)(2,1)}), bf16[3072,1152]{1,0:T(8,128)(2,1)}) %all-gather.5.cloned.1.call-update) | async-done | bytes 7077904 | tf_op jit(solution)/shard_map/all_gather | solution.py:897
  189.5 6.1 %shard_map.226 = bf16[256,1152]{1,0:T(8,128)(2,1)} custom-call(s32[1]{0:T(128)} %bitcast.active_ref, bf16[512,3072]{1,0:T(8,128)(2,1)} %shard_map.223.act_ref, f32[512,1152]{1,0:T(8,128)} %get-tuple-element.77.middle_ref, f32[2,8,1152]{2,1,0:T(8,128)} %pad.15.mod_ref.refs_1_.refs_2_.refs_5_, ...), custom_call_target="tpu_custom_call" | custom-call | flops 1811939328 | bytes 9437184 | tf_op jit(solution)/shard_map/pallas_call | solution.py:358
  195.7 1.3 collective-permute-start.9
  197.0 2.5 shard_map.221.refs_0_
  199.5 6.1 %shard_map.224 = bf16[256,1152]{1,0:T(8,128)(2,1)} custom-call(s32[1]{0:T(128)} %bitcast.active_ref, bf16[512,3072]{1,0:T(8,128)(2,1)} %shard_map.223.act_ref, f32[512,1152]{1,0:T(8,128)} %get-tuple-element.77.middle_ref, f32[2,8,1152]{2,1,0:T(8,128)} %pad.15.mod_ref.refs_1_.refs_2_.refs_5_, ...), custom_call_target="tpu_custom_call" | custom-call | flops 1811939328 | bytes 9437184 | tf_op jit(solution)/shard_map/pallas_call | solution.py:358
  205.6 1.3 collective-permute-start.8
  206.9 4.5 shard_map.225.act_grad_ref
  212.3 12.4 %shard_map.227 = (bf16[512,1152]{1,0:T(8,128)(2,1)}, f32[512,2304]{1,0:T(8,128)}, bf16[512,1152]{1,0:T(8,128)(2,1)}, bf16[512,1152]{1,0:T(8,128)(2,1)}, f32[512,...) custom-call(bf16[256,1152]{1,0:T(8,128)(2,1)} %copy-done.15, ...), custom_call_target="tpu_custom_call" | custom-call | flops 3019898880 | bytes 16515072 | tf_op jit(solution)/shard_map/pallas_call | solution.py:246
  225.6 12.6 %shard_map.228 = (bf16[512,1152]{1,0:T(8,128)(2,1)}, f32[512,2304]{1,0:T(8,128)}, bf16[512,1152]{1,0:T(8,128)(2,1)}, bf16[512,1152]{1,0:T(8,128)(2,1)}, f32[512,...) custom-call(bf16[256,1152]{1,0:T(8,128)(2,1)} %copy-done.16, ...), custom_call_target="tpu_custom_call", output_to_operand_aliasing={{0}: (11, {}), {1}: (12, {}), {2}: (13, {}), {3}: (14, {}),... | custom-call | flops 3019898880 | bytes 16515072 | tf_op jit(solution)/shard_map/pallas_call | solution.py:246
  238.2 28.9 %shard_map.229 = (f32[512,1152]{1,0:T(8,128)}, bf16[512,1152]{1,0:T(8,128)(2,1)}, bf16[512,3072]{1,0:T(8,128)(2,1)}, bf16[512,3072]{1,0:T(8,128)(2,1)}, bf16[512,3072]{1,0:T(8,128)(2,1)}) custom-call(bf16[512,3072]{1,0:T(8,128)(2,1)} %shard_map.225.act_grad_ref, f32[2,8,1152]{2,1,0:T(8,128)} %pad.15.mod_ref.refs_1_.refs_2_.refs_5_, ...), custom_call_target="tpu_custom_call" | custom-call | flops 15854469120 | bytes 23592960 | tf_op jit(solution)/shard_map/pallas_call | solution.py:559
  267.1 2.8 shard_map.232
  269.9 1.3 collective-permute-start.11
  271.2 2.4 shard_map.230
  273.7 4.8 collective-permute-start.10
  278.5 10.0 %shard_map.231 = (bf16[512,1152]{1,0:T(8,128)(2,1)}, f32[512,1152]{1,0:T(8,128)}) custom-call(s32[1]{0:T(128)} %constant.118.clone.1.active_ref, bf16[512,3072]{1,0:T(8,128)(2,1)} %get-tuple-element.97.act_ref, f32[512,1152]{1,0:T(8,128)} %get-tuple-element.90.refs_6_.middle_ref.refs_9_, f32[2,8,1152]{2,1,0:T(8,128)} %pad.15.mod_ref.refs_1_.refs_2_.refs_5_, ...), custom_call_target="tpu_custom_call" | custom-call | flops 3623878656 | bytes 11796480 | tf_op jit(solution)/shard_map/pallas_call | solution.py:358
  288.4 10.5 %collective-permute-done.11.refs_0_.refs_6_ = bf16[256,1152]{1,0:T(8,128)(2,1)S(1)} collective-permute-done((bf16[256,1152]{1,0:T(8,128)(2,1)}, bf16[256,1152]{1,0:T(8,128)(2,1)S(1)}, u32[]{:S(2)}, u32[]{:S(2)}) %collective-permute-start.11) | collective-permute-done | bytes 589856 | tf_op jit(solution)/shard_map/ppermute | solution.py:1091
  299.8 2.3 shard_map.233.refs_0_
  302.1 13.5 %collective-permute-done.10.back_ref.refs_7_ = bf16[256,1152]{1,0:T(8,128)(2,1)S(1)} collective-permute-done((bf16[256,1152]{1,0:T(8,128)(2,1)}, bf16[256,1152]{1,0:T(8,128)(2,1)S(1)}, u32[]{:S(2)}, u32[]{:S(2)}) %collective-permute-start.10) | collective-permute-done | bytes 589856 | tf_op jit(solution)/shard_map/ppermute | solution.py:1091
  316.4 8.7 %shard_map.234 = (bf16[3072,1152]{1,0:T(8,128)(2,1)}, bf16[256,1152]{1,0:T(8,128)(2,1)}) custom-call(bf16[512,3072]{1,0:T(8,128)(2,1)} %get-tuple-element.97.act_ref, bf16[512,1152]{1,0:T(8,128)(2,1)} %bitcast.251, bf16[256,1152]{1,0:T(8,128)(2,1)} %copy-done.13, f32[2,8,1152]{2,1,0:T(8,128)} %pad.15.mod_ref.refs_1_.refs_2_.refs_5_, ...), custom_call_target="tpu_custom_call" | custom-call | flops 3623878656 | bytes 7077888 | tf_op jit(solution)/shard_map/pallas_call | solution.py:801
  325.2 8.0 %shard_map.235.act_grad_ref = bf16[512,3072]{1,0:T(8,128)(2,1)} custom-call(s32[1]{0:T(128)} %constant.118.clone.1.active_ref, bf16[256,1152]{1,0:T(8,128)(2,1)} %shard_map.233.refs_0_, bf16[256,1152]{1,0:T(8,128)(2,1)} %get-tuple-element.104.refs_1_, bf16[3072,1152]{1,0:T(8,128)(2,1)} %all-gather.5.cloned.1.call-done.down_ref.refs_1_.refs_2_), custom_call_target="tpu_custom_call" | custom-call | flops 3623878656 | bytes 9437184 | tf_op jit(solution)/shard_map/pallas_call | solution.py:429
  333.2 24.0 %shard_map.236 = (f32[512,1152]{1,0:T(8,128)}, bf16[512,1152]{1,0:T(8,128)(2,1)}, bf16[512,3072]{1,0:T(8,128)(2,1)}, bf16[512,3072]{1,0:T(8,128)(2,1)}, bf16[512...) custom-call(bf16[512,3072]{1,0:T(8,128)(2,1)} %shard_map.235.act_grad_ref, f32[2,8,1152]{2,1,0:T(8,128)} %pad.15.mod_ref.refs_1_.refs_2_.refs_5_, ...), custom_call_target="tpu_custom_call" | custom-call | flops 15854469120 | bytes 23592960 | tf_op jit(solution)/shard_map/pallas_call | solution.py:559
  357.2 13.7 %shard_map.239 = bf16[8,144,6144]{2,1,0:T(8,128)(2,1)} custom-call(bf16[512,1152]{1,0:T(8,128)(2,1)} %get-tuple-element.89.refs_4_.refs_0_.refs_1_, bf16[512,1152]{1,0:T(8,128)(2,1)} %get-tuple-element.89.refs_4_.refs_0_.refs_1_, bf16[512,3072]{1,0:T(8,128)(2,1)} %get-tuple-element.117.refs_2_, bf16[512,3072]{1,0:T(8,128)(2,1)} %get-tuple-element.118.refs_3_), custom_call_target="tpu_custom_call" | custom-call | flops 7247757312 | bytes 14155776 | tf_op jit(solution)/shard_map/pallas_call | solution.py:852
  370.9 8.4 %reduce-scatter.4.cloned.1.call-done = bf16[192,1152]{1,0:T(8,128)(2,1)} async-done(((bf16[3072,1152]{1,0:T(8,128)(2,1)}), bf16[192,1152]{1,0:T(8,128)(2,1)}) %reduce-scatter.4.cloned.1.call-update) | async-done | bytes 442384 | tf_op jit(solution)/shard_map/reduce_scatter | solution.py:901
  379.7 30.8 %shard_map.237 = (f32[512,1152]{1,0:T(8,128)}, bf16[512,3456]{1,0:T(8,128)(2,1)}, f32[2,8,1152]{2,1,0:T(8,128)}) custom-call(s32[1]{0:T(128)} %constant.118.clone.1.active_ref, f32[512,2304]{1,0:T(8,128)} %get-tuple-element.92.refs_0_, bf16[512,1152]{1,0:T(8,128)(2,1)} %get-tuple-element.93.refs_1_, bf16[512,1152]{1,0:T(8,128)(2,1)} %get-tuple-element.108.refs_2_, ...), custom_call_target="tpu_custom_call" | custom-call | flops 5586812928 | bytes 19759104 | tf_op jit(solution)/shard_map/pallas_call | solution.py:745
  410.5 11.6 %shard_map.238 = bf16[8,144,4608]{2,1,0:T(8,128)(2,1)} custom-call(bf16[512,1152]{1,0:T(8,128)(2,1)} %get-tuple-element.111.refs_0_, bf16[512,1152]{1,0:T(8,128)(2,1)} %get-tuple-element.112.refs_1_, bf16[512,3456]{1,0:T(8,128)(2,1)} %get-tuple-element.113.refs_2_, bf16[512,1152]{1,0:T(8,128)(2,1)} %get-tuple-element.114.refs_3_), custom_call_target="tpu_custom_call" | custom-call | flops 5435817984 | bytes 10616832 | tf_op jit(solution)/shard_map/pallas_call | solution.py:852
  424.0 1.5 collective-permute-start.13
  425.6 4.3 collective-permute-done.13
  430.3 5.3 dynamic-slice_bitcast_fusion
  436.0 2.0 collective-permute-start.15
  438.0 5.1 collective-permute-done.15
  443.9 1.4 collective-permute-done.16
  446.8 7.9 %fusion = bf16[8,72,4608]{2,1,0:T(8,128)(2,1)} fusion(bf16[8,72,4608]{2,1,0:T(8,128)(2,1)} %collective-permute-done.12, bf16[8,2,72,4608]{3,2,1,0:T(8,128)(2,1)} %bitcast.255, s32[]{:T(128)S(6)} %select_n.357), kind=kLoop, calls=%fused_computation.1 | loop fusion | flops 10616832 | bytes 15925252 | tf_op jit(solution)/shard_map/convert_element_type | solution.py:914
  454.7 11.4 %reduce-scatter.6.cloned.1.call-done = bf16[72,6144]{1,0:T(8,128)(2,1)} async-done(((bf16[1152,6144]{1,0:T(8,128)(2,1)}), bf16[72,6144]{1,0:T(8,128)(2,1)}) %reduce-scatter.6.cloned.1.call-update) | async-done | bytes 884752 | tf_op jit(solution)/shard_map/reduce_scatter | solution.py:901
  468.2 3.5 collective-permute-done.22
  471.7 1.2 collective-permute-start.23
  472.9 2.4 collective-permute-done.23
  475.4 1.7 collective-permute-start.24
  477.1 2.0 collective-permute-done.24
  479.2 4.2 convert_select_fusion
  486.4 2.6 collective-permute-done.17
  490.0 4.3 collective-permute-done.18
  495.5 3.6 collective-permute-done.19
  499.2 1.8 collective-permute-start.20
  503.0 2.1 collective-permute-done.20
  505.2 1.7 convolution_bitcast_fusion
  507.4 4.3 fusion.10
  511.6 17.5 %reduce-scatter.8.cloned.1.call-done = bf16[72,4608]{1,0:T(8,128)(2,1)} async-done(((bf16[576,4608]{1,0:T(8,128)(2,1)}), bf16[72,4608]{1,0:T(8,128)(2,1)}) %reduce-scatter.8.cloned.1.call-update) | async-done | bytes 663568 | tf_op jit(solution)/shard_map/reduce_scatter | solution.py:901
  529.2 2.0 fusion.6
  531.2 1.7 fusion.9
  (200 shorter events, 32.7 us)
Async XLA Ops:
  7.2 24.3 %copy-start = (bf16[1001,1152]{1,0:T(8,128)(2,1)S(1)}, bf16[1001,1152]{1,0:T(8,128)(2,1)}, u32[]{:S(2)}) copy-start(bf16[1001,1152]{1,0:T(8,128)(2,1)} %param.19) | copy-start | bytes 6918916
  7.2 2.9 copy-start.26
  7.2 2.9 copy-start.27
  7.2 137.0 %all-gather.3.cloned.1.call-start = ((), (), s32[]{:S(2)}) async-start(), calls=%async_computation.3 | async-start | bytes 26320896 | tf_op jit(solution)/shard_map/all_gather | solution.py:897
  7.3 7.0 %copy-start.25 = (s32[2,256]{1,0:T(2,128)S(1)}, s32[2,256]{1,0:T(2,128)}, u32[]{:S(2)}) copy-start(s32[2,256]{1,0:T(2,128)} %param.18) | copy-start | bytes 6148
  10.0 10.5 %copy-start.2 = (bf16[2,256,1152]{2,1,0:T(8,128)(2,1)S(1)}, bf16[2,256,1152]{2,1,0:T(8,128)(2,1)}, u32[]{:S(2)}) copy-start(bf16[2,256,1152]{2,1,0:T(8,128)(2,1)} %param.14) | copy-start | bytes 3538948
  10.0 179.5 %all-gather.5.cloned.1.call-start = ((), (), s32[]{:S(2)}) async-start(), calls=%async_computation.4 | async-start | bytes 7520256 | tf_op jit(solution)/shard_map/all_gather | solution.py:897
  10.1 11.6 %collective-permute-start = (s32[1,2,2]{2,1,0:T(2,128)S(1)}, s32[1,2,2]{2,1,0:T(2,128)S(1)}, u32[]{:S(2)}, u32[]{:S(2)}) collective-permute-start(s32[1,2,2]{2,1,0:T(2,128)S(1)} %add_bitcast_fusion.2), channel_id=1, source_target_pairs={{0,8},{1,9},{2,10},{3,11},{4,12},{5,13},{6,14},{7,15},{8,0},{9,1},... | collective-permute-start | bytes 56 | tf_op jit(solution)/shard_map/ppermute | solution.py:928
  16.2 0.7 copy-start.6
  16.2 1.6 copy-start.8
  21.7 10.5 %copy-start.3 = (bf16[1,72,6912]{2,1,0:T(8,128)(2,1)S(1)}, bf16[1,72,6912]{2,1,0:T(8,128)(2,1)}, u32[]{:S(2)}) copy-start(bf16[1,72,6912]{2,1,0:T(8,128)(2,1)} %param.20) | copy-start | bytes 2985988
  21.7 3.7 collective-permute-start.1
  25.6 3.6 collective-permute-start.2
  29.4 1.2 collective-permute-start.3
  31.1 1.4 copy-start.23
  32.1 2.7 copy-start.11
  32.2 2.6 copy-start.21
  32.2 4.5 copy-start.14
  32.6 1.9 collective-permute-start.4
  32.9 15.0 %copy-start.7 = (f32[512,18]{1,0:T(8,128)S(1)}, f32[512,18]{1,0:T(8,128)}, u32[]{:S(2)}) copy-start(f32[512,18]{1,0:T(8,128)} %copy-done.6) | copy-start | bytes 110596
  32.9 15.0 %copy-start.9 = (f32[512,18]{1,0:T(8,128)S(1)}, f32[512,18]{1,0:T(8,128)}, u32[]{:S(2)}) copy-start(f32[512,18]{1,0:T(8,128)} %copy-done.8) | copy-start | bytes 110596
  34.5 21.5 %copy-start.17 = (bf16[512,128]{1,0:T(8,128)(2,1)S(1)}, bf16[512,128]{1,0:T(8,128)(2,1)}, u32[]{:S(2)}) copy-start(bf16[512,128]{1,0:T(8,128)(2,1)} %subtract_convert_fusion.1) | copy-start | bytes 393220
  34.5 21.4 %copy-start.18 = (bf16[512,128]{1,0:T(8,128)(2,1)S(1)}, bf16[512,128]{1,0:T(8,128)(2,1)}, u32[]{:S(2)}) copy-start(bf16[512,128]{1,0:T(8,128)(2,1)} %get-tuple-element.129) | copy-start | bytes 393220
  34.5 21.4 %copy-start.19 = (bf16[512,128]{1,0:T(8,128)(2,1)S(1)}, bf16[512,128]{1,0:T(8,128)(2,1)}, u32[]{:S(2)}) copy-start(bf16[512,128]{1,0:T(8,128)(2,1)} %get-tuple-element.130) | copy-start | bytes 393220
  34.8 109.6 %copy-start.28 = (f32[1,72]{1,0:T(1,128)S(1)}, f32[1,72]{1,0:T(1,128)}, u32[]{:S(2)}) copy-start(f32[1,72]{1,0:T(1,128)} %param.27) | copy-start | bytes 868
  34.8 109.6 %copy-start.29 = (f32[1,72]{1,0:T(1,128)S(1)}, f32[1,72]{1,0:T(1,128)}, u32[]{:S(2)}) copy-start(f32[1,72]{1,0:T(1,128)} %param.26) | copy-start | bytes 868
  34.8 12.8 %collective-permute-start.5 = (f32[4,2,6912]{2,1,0:T(2,128)S(1)}, f32[4,2,6912]{2,1,0:T(2,128)S(1)}, u32[]{:S(2)}, u32[]{:S(2)}) collective-permute-start(f32[4,2,6912]{2,1,0:T(2,128)S(1)} %dynamic-slice_bitcast_fusion.2), channel_id=1, source_target_pairs={{0,2},{1,3},{2,0},{3,1},{4,6},{5,7},{6,4},{7,5},{8,10},{9,11},{10,... | collective-permute-start | bytes 663560 | tf_op jit(solution)/shard_map/ppermute | solution.py:928
  47.8 7.8 %collective-permute-start.6 = (f32[2,2,6912]{2,1,0:T(2,128)S(1)}, f32[2,2,6912]{2,1,0:T(2,128)S(1)}, u32[]{:S(2)}, u32[]{:S(2)}) collective-permute-start(f32[2,2,6912]{2,1,0:T(2,128)S(1)} %dynamic-slice_bitcast_fusion.3), channel_id=1, source_target_pairs={{0,4},{1,5},{2,6},{3,7},{4,0},{5,1},{6,2},{7,3},{8,12},{9,13},{10,... | collective-permute-start | bytes 331784 | tf_op jit(solution)/shard_map/ppermute | solution.py:928
  55.7 6.8 %collective-permute-start.7 = (f32[1,2,6912]{2,1,0:T(2,128)S(1)}, f32[1,2,6912]{2,1,0:T(2,128)S(1)}, u32[]{:S(2)}, u32[]{:S(2)}) collective-permute-start(f32[1,2,6912]{2,1,0:T(2,128)S(1)} %constant_dynamic-slice_fusion), channel_id=1, source_target_pairs={{0,8},{1,9},{2,10},{3,11},{4,12},{5,13},{6,14},{7,15},{8,0},{9,1},... | collective-permute-start | bytes 165896 | tf_op jit(solution)/shard_map/ppermute | solution.py:928
  144.2 235.0 %reduce-scatter.4.cloned.1.call-start = ((), (), s32[]{:S(2)}) async-start(), calls=%async_computation.5 | async-start | bytes 7520256 | tf_op jit(solution)/shard_map/reduce_scatter | solution.py:901
  195.7 15.8 %collective-permute-start.9 = (bf16[256,1152]{1,0:T(8,128)(2,1)}, bf16[256,1152]{1,0:T(8,128)(2,1)S(1)}, u32[]{:S(2)}, u32[]{:S(2)}) collective-permute-start(bf16[256,1152]{1,0:T(8,128)(2,1)} %shard_map.226), channel_id=1, source_target_pairs={{0,16},{1,17},{2,18},{3,19},{4,20},{5,21},{6,22},{7,23},{8,24},{9,... | collective-permute-start | bytes 1769480 | tf_op jit(solution)/shard_map/ppermute | solution.py:1059
  205.6 19.1 %collective-permute-start.8 = (bf16[256,1152]{1,0:T(8,128)(2,1)}, bf16[256,1152]{1,0:T(8,128)(2,1)S(1)}, u32[]{:S(2)}, u32[]{:S(2)}) collective-permute-start(bf16[256,1152]{1,0:T(8,128)(2,1)} %shard_map.224), channel_id=1, source_target_pairs={{0,16},{1,17},{2,18},{3,19},{4,20},{5,21},{6,22},{7,23},{8,24},{9,... | collective-permute-start | bytes 1769480 | tf_op jit(solution)/shard_map/ppermute | solution.py:1059
  211.5 0.8 copy-start.15
  224.7 0.8 copy-start.16
  269.9 29.0 %collective-permute-start.11 = (bf16[256,1152]{1,0:T(8,128)(2,1)}, bf16[256,1152]{1,0:T(8,128)(2,1)S(1)}, u32[]{:S(2)}, u32[]{:S(2)}) collective-permute-start(bf16[256,1152]{1,0:T(8,128)(2,1)} %shard_map.232), channel_id=1, source_target_pairs={{16,0},{17,1},{18,2},{19,3},{20,4},{21,5},{22,6},{23,7},{24,8},{25... | collective-permute-start | bytes 1769480 | tf_op jit(solution)/shard_map/ppermute | solution.py:1091
  273.7 41.9 %collective-permute-start.10 = (bf16[256,1152]{1,0:T(8,128)(2,1)}, bf16[256,1152]{1,0:T(8,128)(2,1)S(1)}, u32[]{:S(2)}, u32[]{:S(2)}) collective-permute-start(bf16[256,1152]{1,0:T(8,128)(2,1)} %shard_map.230), channel_id=1, source_target_pairs={{16,0},{17,1},{18,2},{19,3},{20,4},{21,5},{22,6},{23,7},{24,8},{25... | collective-permute-start | bytes 1769480 | tf_op jit(solution)/shard_map/ppermute | solution.py:1091
  299.0 0.8 copy-start.5
  315.6 0.8 copy-start.13
  325.1 140.9 %reduce-scatter.6.cloned.1.call-start = ((), (), s32[]{:S(2)}) async-start(), calls=%async_computation.6 | async-start | bytes 15040512 | tf_op jit(solution)/shard_map/reduce_scatter | solution.py:901
  379.3 149.9 %reduce-scatter.8.cloned.1.call-start = ((), (), s32[]{:S(2)}) async-start(), calls=%async_computation.7 | async-start | bytes 5971968 | tf_op jit(solution)/shard_map/reduce_scatter | solution.py:901
  424.0 5.8 %collective-permute-start.13 = (bf16[1,2,6912]{2,1,0:T(2,128)(2,1)S(1)}, bf16[1,2,6912]{2,1,0:T(2,128)(2,1)S(1)}, u32[]{:S(2)}, u32[]{:S(2)}) collective-permute-start(bf16[1,2,6912]{2,1,0:T(2,128)(2,1)S(1)} %convert_element_type.163), channel_id=1, source_target_pairs={{0,8},{1,9},{2,10},{3,11},{4,12},{5,13},{6,14},{7,15},{8,0},{9,1},... | collective-permute-start | bytes 82952 | tf_op jit(solution)/shard_map/ppermute | solution.py:928
  430.0 5.6 %collective-permute-start.14 = (bf16[2,2,6912]{2,1,0:T(2,128)(2,1)S(1)}, bf16[2,2,6912]{2,1,0:T(2,128)(2,1)S(1)}, u32[]{:S(2)}, u32[]{:S(2)}) collective-permute-start(bf16[2,2,6912]{2,1,0:T(2,128)(2,1)S(1)} %maximum_bitcast_fusion), channel_id=1, source_target_pairs={{0,4},{1,5},{2,6},{3,7},{4,0},{5,1},{6,2},{7,3},{8,12},{9,13},{10,... | collective-permute-start | bytes 165896 | tf_op jit(solution)/shard_map/ppermute | solution.py:928
  435.6 11.2 %collective-permute-start.12 = (bf16[8,72,4608]{2,1,0:T(8,128)(2,1)}, bf16[8,72,4608]{2,1,0:T(8,128)(2,1)}, u32[]{:S(2)}, u32[]{:S(2)}) collective-permute-start(bf16[8,72,4608]{2,1,0:T(8,128)(2,1)} %dynamic-slice_bitcast_fusion), channel_id=1, source_target_pairs={{0,1},{1,0},{2,3},{3,2},{4,5},{5,4},{6,7},{7,6},{8,9},{9,8},{10,11... | collective-permute-start | bytes 15925256 | tf_op jit(solution)/shard_map/ppermute | solution.py:928
  436.0 7.1 %collective-permute-start.15 = (bf16[4,2,6912]{2,1,0:T(2,128)(2,1)S(1)}, bf16[4,2,6912]{2,1,0:T(2,128)(2,1)S(1)}, u32[]{:S(2)}, u32[]{:S(2)}) collective-permute-start(bf16[4,2,6912]{2,1,0:T(2,128)(2,1)S(1)} %bitcast.269), channel_id=1, source_target_pairs={{0,2},{1,3},{2,0},{3,1},{4,6},{5,7},{6,4},{7,5},{8,10},{9,11},{10,... | collective-permute-start | bytes 331784 | tf_op jit(solution)/shard_map/ppermute | solution.py:928
  443.7 1.6 collective-permute-start.16
  467.1 4.5 collective-permute-start.22
  471.7 3.6 collective-permute-start.23
  475.4 3.7 collective-permute-start.24
  479.1 4.3 collective-permute-start.25
  479.2 4.8 copy-start.20
  479.2 5.7 %copy-start.4 = (bf16[1,72,6912]{2,1,0:T(8,128)(2,1)S(1)}, bf16[1,72,6912]{2,1,0:T(8,128)(2,1)}, u32[]{:S(2)}) copy-start(bf16[1,72,6912]{2,1,0:T(8,128)(2,1)} %param.20) | copy-start | bytes 2985988
  483.4 2.9 copy-start.10
  485.3 3.8 collective-permute-start.17
  489.1 5.2 collective-permute-start.18
  490.0 15.3 %copy-start.22 = (bf16[32,72]{1,0:T(8,128)(2,1)S(1)}, bf16[32,72]{1,0:T(8,128)(2,1)}, u32[]{:S(2)}) copy-start(bf16[32,72]{1,0:T(8,128)(2,1)} %copy-done.21) | copy-start | bytes 13828
  494.3 4.9 collective-permute-start.19
  499.2 5.9 %collective-permute-start.20 = (f32[4,32,72]{2,1,0:T(8,128)S(1)}, f32[4,32,72]{2,1,0:T(8,128)S(1)}, u32[]{:S(2)}, u32[]{:S(2)}) collective-permute-start(f32[4,32,72]{2,1,0:T(8,128)S(1)} %bitcast.270), channel_id=1, source_target_pairs={{0,2},{1,3},{2,0},{3,1},{4,6},{5,7},{6,4},{7,5},{8,10},{9,11},{10,... | collective-permute-start | bytes 110600 | tf_op jit(solution)/shard_map/ppermute | solution.py:928
  505.1 2.2 copy-start.12
  505.1 2.2 copy-start.24
  505.1 1.8 collective-permute-start.21
  507.2 25.7 %copy-start.1 = (bf16[1001,1152]{1,0:T(8,128)(2,1)S(1)}, bf16[1001,1152]{1,0:T(8,128)(2,1)}, u32[]{:S(2)}) copy-start(bf16[1001,1152]{1,0:T(8,128)(2,1)} %param.19) | copy-start | bytes 6918916
Sparse Core Ops, SparseCore 0:
  10.2 133.9 all-gather.2
  145.8 43.6 all-gather.4
  325.3 53.9 reduce-scatter.3
  381.5 84.5 reduce-scatter.5
  468.4 60.7 reduce-scatter.7
